TPU v7x, 32 devices: a whole 2x2x4 slice. The times are simulated.
32 devices in a mesh: dp: 4 (over y, x), seq: 8 (over z, core).
Axes of the slice: x: 2, y: 2, z: 4, core: 2. Of those that a mesh axis runs over, the one named last changes fastest.
Arguments:
- tokens: bfloat16 [4, 1024, 1024], P('dp', 'seq'), may hold values from -6 to 6
- cotangent: bfloat16 [4, 1024, 1024], P('dp', 'seq'), may hold values from -6 to 6
- doc_starts: int32 [4, 4], P('dp'), may hold values from 0 to 1023, as said below
- in_weight: bfloat16 [1024, 4096], replicated, may hold values from -0.1875 to 0.1875
- conv_weight: bfloat16 [2048, 4], replicated, may hold values from -3 to 3
- conv_bias: bfloat16 [2048], replicated, may hold values from -3 to 3
- xproj_weight: bfloat16 [2048, 96], replicated, may hold values from -0.125 to 0.125
- dt_weight: bfloat16 [64, 2048], replicated, may hold values from -0.75 to 0.75
- dt_bias: bfloat16 [2048], replicated, may hold values from -3.6875 to -2.296875
- a_log: float32 [2048, 16], replicated
- skip_scale: bfloat16 [2048], replicated, may hold values from 0.5 to 1.5
- out_weight: bfloat16 [2048, 1024], replicated, may hold values from -0.125 to 0.125
- norm_gain: bfloat16 [1024], replicated, may hold values from 0.5 to 1.5
Outputs:
- mixed: bfloat16 [4, 1024, 1024], P('dp', 'seq')
- tokens_grad: bfloat16 [4, 1024, 1024], P('dp', 'seq')
- in_weight_grad: float32 [1024, 4096], P(None, ('dp', 'seq'))
- conv_weight_grad: float32 [2048, 4], replicated
- conv_bias_grad: float32 [2048], replicated
- xproj_weight_grad: float32 [2048, 96], replicated
- dt_weight_grad: float32 [64, 2048], replicated
- dt_bias_grad: float32 [2048], replicated
- a_log_grad: float32 [2048, 16], replicated
- skip_scale_grad: float32 [2048], replicated
- out_weight_grad: float32 [2048, 1024], P(None, ('dp', 'seq'))
- norm_gain_grad: float32 [1024], replicated
Inputs may be any that keep to these rules, and one draw needn't show every extreme that they name: `doc_starts`: the first entry of each row is 0 and the entries of a row increase strictly.
All inputs are finite; a program needn't handle non-finite values.
Results may differ from a plain program's by a relative error of at most 0.012.
Values may be sent and summed in bfloat16 or wider, within the bound.
No kernel may reach another device: no remote copies, remote signals or barrier semaphores. Data moves between devices by JAX's collectives and lax.ppermute only.
A program may use at most 320 MiB of HBM per device.

v0:
```python
import jax
import jax.numpy as jnp
from jax import lax
from jax.sharding import PartitionSpec as P

epsilon = 1e-05


def shifted(x, axis, by):
    peers = lax.axis_size(axis)
    pairs = [(i, i + by) for i in range(peers) if 0 <= i + by < peers]
    return lax.ppermute(x, axis, pairs)


def carried_in(x, axis, combine, identity, reverse):
    peers, position = (lax.axis_size(axis), lax.axis_index(axis))
    everything = jax.tree.map(
        lambda part, kind: lax.all_gather(part.astype(kind), axis), x, (jnp.bfloat16, jnp.bfloat16)
    )
    start = jax.tree.map(
        lambda part, zero: jnp.broadcast_to(jnp.asarray(zero, part.dtype), part.shape), x, identity
    )

    def lap(k, before):
        at = peers - 1 - k if reverse else k
        reached = at > position if reverse else at < position
        new = combine(
            before, jax.tree.map(lambda part, own: part[at].astype(own.dtype), everything, x)
        )
        return jax.tree.map(lambda a, b: jnp.where(reached, a, b), new, before)

    return lax.fori_loop(0, peers, lap, start)


def silu_slope(values):
    sigma = jax.nn.sigmoid(values)
    return sigma * (1.0 + values * (1.0 - sigma))


def pair_combine(earlier, later):
    return (earlier[0] * later[0], later[0] * earlier[1] + later[1])


def body(
    tokens,
    cotangent,
    doc_starts,
    in_weight,
    conv_weight,
    conv_bias,
    xproj_weight,
    dt_weight,
    dt_bias,
    a_log,
    skip_scale,
    out_weight,
    norm_gain,
):
    length = tokens.shape[1]
    inner_width = conv_bias.shape[0]
    states = a_log.shape[1]
    low_rank = dt_weight.shape[0]
    tap_count = conv_weight.shape[1]
    rim_width = tap_count - 1
    places = lax.axis_index("seq") * length + jnp.arange(length, dtype=jnp.int32)
    hits = doc_starts[:, :, None] <= places[None, None, :]
    doc_begin = jnp.max(jnp.where(hits, doc_starts[:, :, None], 0), axis=1)
    doc_reset = jnp.any(doc_starts[:, :, None] == places[None, None, :], axis=1).astype(jnp.float32)
    persist = 1.0 - doc_reset
    resets_seen = jnp.cumsum(doc_reset, axis=1)
    resets_total = resets_seen[:, -1:]
    clear_before = (resets_seen == 0.0).astype(jnp.float32)
    clear_after = (resets_seen == resets_total).astype(jnp.float32)
    clear_whole = clear_before[:, -1]
    tok_f = tokens.astype(jnp.float32)
    inv_rms = lax.rsqrt(jnp.mean(tok_f * tok_f, axis=-1, keepdims=True) + epsilon)
    scaled = tok_f * inv_rms
    normed = (scaled * norm_gain).astype(jnp.bfloat16)
    joined = jnp.einsum("rld,df->rlf", normed, in_weight, preferred_element_type=jnp.float32)
    conv_in = joined[..., :inner_width].astype(jnp.bfloat16)
    gate_in = joined[..., inner_width:]
    left_rim = shifted(conv_in[:, length - rim_width :, :], "seq", 1)
    extended = jnp.concatenate([left_rim, conv_in], axis=1).astype(jnp.float32)
    conv_f = conv_weight.astype(jnp.float32)
    tap_masks = []
    pre_conv = jnp.zeros(conv_in.shape, jnp.float32) + conv_bias.astype(jnp.float32)
    for offset in range(tap_count):
        usable = (doc_begin <= places[None, :] - offset).astype(jnp.float32)[..., None]
        tap_masks.append(usable)
        window = extended[:, rim_width - offset : rim_width - offset + length]
        pre_conv = pre_conv + conv_f[:, tap_count - 1 - offset] * window * usable
    inner_act = jax.nn.silu(pre_conv).astype(jnp.bfloat16)
    inner_f = inner_act.astype(jnp.float32)
    projected = jnp.einsum(
        "rle,ek->rlk", inner_act, xproj_weight, preferred_element_type=jnp.float32
    )
    dt_low = projected[..., :low_rank].astype(jnp.bfloat16)
    input_map = projected[..., low_rank : low_rank + states]
    output_map = projected[..., low_rank + states :]
    dt_raw = jnp.einsum(
        "rlk,ke->rle", dt_low, dt_weight, preferred_element_type=jnp.float32
    ) + dt_bias.astype(jnp.float32)
    time_step = jax.nn.softplus(dt_raw)
    rates_t = -jnp.exp(a_log).T
    time_sum = jnp.cumsum(time_step, axis=1)
    whole_decay = jnp.exp(time_sum[:, -1, None, :] * rates_t[None]) * clear_whole[:, None, None]
    drive = time_step * inner_f
    skip_f = skip_scale.astype(jnp.float32)
    identity_pair = (jnp.ones_like(whole_decay), jnp.zeros_like(whole_decay))

    def states_from(step_row, drive_row, in_row, keep_row, initial):
        decay_now = jnp.exp(step_row[:, None, :] * rates_t[None]) * keep_row[:, None, None]
        inflow = in_row[:, :, None] * drive_row[:, None, :]
        carried, hidden_state = lax.associative_scan(pair_combine, (decay_now, inflow), axis=0)
        return (decay_now, hidden_state + carried * initial[None])

    def start_reach(sum_row, before_row):
        return jnp.exp(sum_row[:, None, :] * rates_t[None]) * before_row[:, None, None]

    def end_state(column_item):
        sum_row, after_row, drive_row, in_row = column_item
        toward = (
            jnp.exp((sum_row[-1:] - sum_row)[:, None, :] * rates_t[None]) * after_row[:, None, None]
        )
        return jnp.sum(toward * in_row[:, :, None] * drive_row[:, None, :], axis=0)

    end_values = lax.map(end_state, (time_sum, clear_after, drive, input_map))
    entry = carried_in((whole_decay, end_values), "seq", pair_combine, identity_pair, False)[1]

    def core_row(column_item):
        step_row, drive_row, in_row, out_row, keep_row, initial = column_item
        decay_now, hidden_state = states_from(step_row, drive_row, in_row, keep_row, initial)
        return jnp.sum(hidden_state * out_row[:, :, None], axis=1)

    scan_core = lax.map(core_row, (time_step, drive, input_map, output_map, persist, entry))
    scanned = scan_core + skip_f * inner_f
    gate_act = jax.nn.silu(gate_in)
    gated_out = (scanned * gate_act).astype(jnp.bfloat16)
    outgoing = jnp.einsum("rle,ed->rld", gated_out, out_weight, preferred_element_type=jnp.float32)
    mixed = (tok_f + outgoing).astype(jnp.bfloat16)
    out_full = jnp.einsum("rle,rld->ed", gated_out, cotangent, preferred_element_type=jnp.float32)
    g_gated = jnp.einsum("rld,ed->rle", cotangent, out_weight, preferred_element_type=jnp.float32)
    g_scanned = g_gated * gate_act
    g_gate_in = g_gated * scanned * silu_slope(gate_in)

    def back_source(column_item):
        sum_row, before_row, gscan_row, out_row = column_item
        reach_now = start_reach(sum_row, before_row)
        return jnp.sum(reach_now * out_row[:, :, None] * gscan_row[:, None, :], axis=0)

    sources = lax.map(back_source, (time_sum, clear_before, g_scanned, output_map))
    incoming = carried_in((whole_decay, sources), "seq", pair_combine, identity_pair, True)[1]

    def row_backward(column_item):
        step_row, drive_row, inner_row, in_row, out_row, keep_row, gscan_row, initial, arriving = (
            column_item
        )
        decay_now, hidden_state = states_from(step_row, drive_row, in_row, keep_row, initial)
        source_now = out_row[:, :, None] * gscan_row[:, None, :]
        following = jnp.concatenate([decay_now[1:], jnp.ones_like(decay_now[:1])], axis=0)
        reach_decay, adjoint_zero = lax.associative_scan(
            pair_combine, (following, source_now), axis=0, reverse=True
        )
        adjoint = adjoint_zero + reach_decay * arriving[None]
        previous = jnp.concatenate([initial[None], hidden_state[:-1]], axis=0)
        decay_flow = adjoint * previous * decay_now
        out_map_grad = jnp.sum(hidden_state * gscan_row[:, None, :], axis=2)
        in_map_grad = jnp.sum(adjoint * drive_row[:, None, :], axis=2)
        adjoint_in = jnp.sum(adjoint * in_row[:, :, None], axis=1)
        step_grad = adjoint_in * inner_row + jnp.sum(decay_flow * rates_t[None], axis=1)
        inner_scan_grad = adjoint_in * step_row + gscan_row * skip_f
        rate_part = jnp.sum(decay_flow * step_row[:, None, :], axis=0)
        return (step_grad, inner_scan_grad, in_map_grad, out_map_grad, rate_part)

    step_grad, inner_scan_grad, in_map_grad, out_map_grad, rate_parts = lax.map(
        row_backward,
        (time_step, drive, inner_f, input_map, output_map, persist, g_scanned, entry, incoming),
    )
    a_log_part = (rates_t * jnp.sum(rate_parts, axis=0)).T
    skip_part = jnp.sum(g_scanned * inner_f, axis=(0, 1))
    raw_grad = step_grad * jax.nn.sigmoid(dt_raw)
    dt_bias_part = jnp.sum(raw_grad, axis=(0, 1))
    raw_low = raw_grad.astype(jnp.bfloat16)
    dt_weight_part = jnp.einsum("rlk,rle->ke", dt_low, raw_low, preferred_element_type=jnp.float32)
    low_grad = jnp.einsum("rle,ke->rlk", raw_low, dt_weight, preferred_element_type=jnp.float32)
    proj_grad = jnp.concatenate([low_grad, in_map_grad, out_map_grad], axis=-1).astype(jnp.bfloat16)
    xproj_part = jnp.einsum("rle,rlk->ek", inner_act, proj_grad, preferred_element_type=jnp.float32)
    inner_grad = inner_scan_grad + jnp.einsum(
        "rlk,ek->rle", proj_grad, xproj_weight, preferred_element_type=jnp.float32
    )
    pre_grad = inner_grad * silu_slope(pre_conv)
    conv_bias_part = jnp.sum(pre_grad, axis=(0, 1))
    ext_grad = jnp.zeros(extended.shape, jnp.float32)
    tap_columns = []
    for offset in range(tap_count):
        masked = pre_grad * tap_masks[offset]
        window = extended[:, rim_width - offset : rim_width - offset + length]
        tap_columns.append(jnp.sum(masked * window, axis=(0, 1)))
        ext_grad = ext_grad + jnp.pad(
            conv_f[:, tap_count - 1 - offset] * masked,
            ((0, 0), (rim_width - offset, offset), (0, 0)),
        )
    conv_weight_part = jnp.stack(tap_columns[::-1], axis=1)
    rim_back = shifted(ext_grad[:, :rim_width], "seq", -1)
    conv_grad = ext_grad[:, rim_width:] + jnp.pad(
        rim_back, ((0, 0), (length - rim_width, 0), (0, 0))
    )
    joined_grad = jnp.concatenate([conv_grad, g_gate_in], axis=-1).astype(jnp.bfloat16)
    in_full = jnp.einsum("rld,rlf->df", normed, joined_grad, preferred_element_type=jnp.float32)
    normed_grad = jnp.einsum(
        "rlf,df->rld", joined_grad, in_weight, preferred_element_type=jnp.float32
    )
    gain_part = jnp.sum(normed_grad * scaled, axis=(0, 1))
    hat_grad = normed_grad * norm_gain.astype(jnp.float32)
    tokens_grad = (
        cotangent.astype(jnp.float32)
        + inv_rms * (hat_grad - scaled * jnp.mean(hat_grad * scaled, axis=-1, keepdims=True))
    ).astype(jnp.bfloat16)
    small_sums = lax.psum(
        (
            xproj_part,
            dt_weight_part,
            dt_bias_part,
            a_log_part,
            skip_part,
            conv_weight_part,
            conv_bias_part,
            gain_part,
        ),
        ("dp", "seq"),
    )
    in_share, out_share = (
        lax.psum_scatter(in_full, ("dp", "seq"), scatter_dimension=1, tiled=True),
        lax.psum_scatter(out_full, ("dp", "seq"), scatter_dimension=1, tiled=True),
    )
    return (
        mixed,
        tokens_grad,
        in_share,
        small_sums[5],
        small_sums[6],
        small_sums[0],
        small_sums[1],
        small_sums[2],
        small_sums[3],
        small_sums[4],
        out_share,
        small_sums[7],
    )


def solution(mesh):
    placed = (
        P("dp", "seq", None),
        P("dp", "seq", None),
        P("dp", None),
        P(),
        P(),
        P(),
        P(),
        P(),
        P(),
        P(),
        P(),
        P(),
        P(),
    )
    return jax.shard_map(
        body,
        mesh=mesh,
        in_specs=placed,
        out_specs=(
            P("dp", "seq", None),
            P("dp", "seq", None),
            P(None, ("dp", "seq")),
            P(),
            P(),
            P(),
            P(),
            P(),
            P(),
            P(),
            P(None, ("dp", "seq")),
            P(),
        ),
        check_vma=False,
    )
```

profile of v0, /device:TPU:0, one launch (start us, length us, event | category | flops | bytes accessed | tf_op | source)
XLA Modules:
  0.0 1737.5 jit_solution(16986197351270098208)
XLA Ops:
  44.8 14.8 broadcast_multiply_fusion.1
  59.6 19.1 %slice_add_fusion = (f32[64,16,2048]{2,1,0:T(8,128)}, f32[64,16,2048]{2,1,0:T(8,128)}) fusion(f32[128,16,2048]{2,1,0:T(8,128)} %get-tuple-element.504, f32[128,16,2048]{2,1,0:T(8,128)} %get-tuple-element.540), kind=kLoop, calls=%fused_computation.29 | loop fusion | flops 6291456 | bytes 50331648 | tf_op jit(solution)/shard_map/while/body/eval_jaxpr/add | solution.py:41
  78.6 10.2 slice_add_fusion.2
  146.1 6.6 pad.312
  176.1 11.6 pad.314
  187.7 7.4 pad.315
  195.1 11.4 pad.329
  208.2 7.3 pad.328
  215.5 6.8 add.676
  224.1 8.0 fusion.6
  237.7 21.1 %pad.317 = f32[64,16,2048]{2,1,0:T(8,128)} pad(f32[32,16,2048]{2,1,0:T(8,128)} %add.676, f32[]{:T(128)} %constant.164.clone.1), padding=1_0_1x0_0_0x0_0_0 | pad | bytes 12582916 | tf_op jit(solution)/shard_map/while/body/eval_jaxpr/pad | solution.py:114
  263.4 21.0 %pad.316 = f32[64,16,2048]{2,1,0:T(8,128)} pad(f32[32,16,2048]{2,1,0:T(8,128)} %pad_maximum_fusion.3, f32[]{:T(128)} %constant.164.clone.1), padding=0_1_1x0_0_0x0_0_0 | pad | bytes 12582916 | tf_op jit(solution)/shard_map/while/body/eval_jaxpr/pad | solution.py:114
  284.4 21.0 %pad.331 = f32[64,16,2048]{2,1,0:T(8,128)} pad(f32[32,16,2048]{2,1,0:T(8,128)} %add.685, f32[]{:T(128)} %constant.164.clone.1), padding=1_0_1x0_0_0x0_0_0 | pad | bytes 12582916 | tf_op jit(solution)/shard_map/while/body/eval_jaxpr/pad | solution.py:114
  310.0 21.0 %pad.330 = f32[64,16,2048]{2,1,0:T(8,128)} pad(f32[32,16,2048]{2,1,0:T(8,128)} %pad_maximum_fusion.4, f32[]{:T(128)} %constant.164.clone.1), padding=0_1_1x0_0_0x0_0_0 | pad | bytes 12582916 | tf_op jit(solution)/shard_map/while/body/eval_jaxpr/pad | solution.py:114
  331.0 11.7 add.686
  342.7 24.6 %fusion.4 = (f32[63,16,2048]{2,1,0:T(8,128)}, f32[63,16,2048]{2,1,0:T(8,128)}) fusion(f32[64,16,2048]{2,1,0:T(8,128)} %pad.317, f32[64,16,2048]{2,1,0:T(8,128)} %pad.316, f32[128,16,2048]{2,1,0:T(8,128)} %get-tuple-element.504, f32[128,16,2048]{2,1,0:T(8,128)} %get-tuple-element.540, f32[64,16,2048]{2,1,0:T(8,128)} %pad.331, f32[64,16,2048]{2,1,0:T(8,128)} %pad.330), kind=kLoop, calls=%fused_computation.36 | loop fusion | flops 10321920 | bytes 66060288 | tf_op jit(solution)/shard_map/while/body/eval_jaxpr/add | solution.py:41
  367.3 11.7 add.678
  379.0 11.9 slice.974
  391.1 16.0 all-gather
  407.0 14.8 all-gather.1
  422.7 8.0 pad_maximum_fusion.1
  430.7 40.4 %pad.332 = f32[128,16,2048]{2,1,0:T(8,128)} pad(f32[64,16,2048]{2,1,0:T(8,128)} %pad_maximum_fusion.1, f32[]{:T(128)} %constant.164.clone.1), padding=0_1_1x0_0_0x0_0_0 | pad | bytes 25165828 | tf_op jit(solution)/shard_map/while/body/eval_jaxpr/pad | solution.py:114
  471.1 40.3 %pad.333 = f32[128,16,2048]{2,1,0:T(8,128)} pad(f32[64,16,2048]{2,1,0:T(8,128)} %add.686, f32[]{:T(128)} %constant.164.clone.1), padding=1_0_1x0_0_0x0_0_0 | pad | bytes 25165828 | tf_op jit(solution)/shard_map/while/body/eval_jaxpr/pad | solution.py:114
  511.3 7.7 pad_maximum_fusion
  519.0 40.3 %pad.318 = f32[128,16,2048]{2,1,0:T(8,128)} pad(f32[64,16,2048]{2,1,0:T(8,128)} %pad_maximum_fusion, f32[]{:T(128)} %constant.164.clone.1), padding=0_1_1x0_0_0x0_0_0 | pad | bytes 25165828 | tf_op jit(solution)/shard_map/while/body/eval_jaxpr/pad | solution.py:114
  559.3 40.5 %pad.319 = f32[128,16,2048]{2,1,0:T(8,128)} pad(f32[64,16,2048]{2,1,0:T(8,128)} %add.678, f32[]{:T(128)} %constant.164.clone.1), padding=1_0_1x0_0_0x0_0_0 | pad | bytes 25165828 | tf_op jit(solution)/shard_map/while/body/eval_jaxpr/pad | solution.py:114
  599.9 34.4 %multiply_reduce_fusion.1 = (bf16[128,16]{1,0:T(8,128)(2,1)}, f32[128,2048]{1,0:T(8,128)}, bf16[16,2048]{1,0:T(8,128)(2,1)}, f32[128,16,2048]{2,1,0:T(8,128)}, f32[128,16,2048]{2,1,0:T(8,128)}) fusion(f32[128,2048]{1,0:T(8,128)S(1)} %copy-done.48, f32[128,16]{1,0:T(8,128)S(1)} %copy.32, f32[128]{0:T(128)S(1)} %copy-done.99, f32[16,2048]{1,0:T(8,128)S(1)} %copy-done.60, ...), kind=kLoop, calls=%fused_computation.9 | loop fusion | flops 58423296 | bytes 104149504 | tf_op jit(solution)/shard_map/while/body/eval_jaxpr/reduce_sum | solution.py:167
  634.2 10.8 fusion.76
  645.0 10.9 pad_slice_fusion.1
  656.0 19.1 %reverse_add_fusion = (f32[64,16,2048]{2,1,0:T(8,128)}, f32[64,16,2048]{2,1,0:T(8,128)}) fusion(f32[64,16,2048]{2,1,0:T(8,128)} %get-tuple-element.465, f32[64,16,2048]{2,1,0:T(8,128)} %get-tuple-element.464, f32[64,16,2048]{2,1,0:T(8,128)} %get-tuple-element.470, f32[64,16,2048]{2,1,0:T(8,128)} %get-tuple-element.471), kind=kLoop, calls=%fused_computation.26 | loop fusion | flops 6291456 | bytes 50331648 | tf_op jit(solution)/shard_map/while/body/eval_jaxpr/add | solution.py:41
  675.1 10.2 slice_add_fusion.1
  740.6 6.5 pad.340
  771.9 7.8 slice.899
  785.6 11.5 pad.342
  797.1 7.3 pad.343
  804.3 11.4 pad.357
  817.4 7.3 pad.356
  824.7 6.6 add.707
  831.3 9.5 fusion.5
  840.9 7.3 add.716
  850.1 6.3 slice.1015
  856.3 14.7 all-gather.2
  871.1 7.7 while.21
  878.7 21.0 %pad.345 = f32[64,16,2048]{2,1,0:T(8,128)} pad(f32[32,16,2048]{2,1,0:T(8,128)} %add.707, f32[]{:T(128)} %constant.164.clone.1), padding=1_0_1x0_0_0x0_0_0 | pad | bytes 12582916 | tf_op jit(solution)/shard_map/while/body/eval_jaxpr/pad | solution.py:161
  904.4 21.0 %pad.344 = f32[64,16,2048]{2,1,0:T(8,128)} pad(f32[32,16,2048]{2,1,0:T(8,128)} %pad_maximum_fusion.5, f32[]{:T(128)} %constant.164.clone.1), padding=0_1_1x0_0_0x0_0_0 | pad | bytes 12582916 | tf_op jit(solution)/shard_map/while/body/eval_jaxpr/pad | solution.py:161
  925.3 21.1 %pad.359 = f32[64,16,2048]{2,1,0:T(8,128)} pad(f32[32,16,2048]{2,1,0:T(8,128)} %add.716, f32[]{:T(128)} %constant.164.clone.1), padding=1_0_1x0_0_0x0_0_0 | pad | bytes 12582916 | tf_op jit(solution)/shard_map/while/body/eval_jaxpr/pad | solution.py:161
  951.0 21.0 %pad.358 = f32[64,16,2048]{2,1,0:T(8,128)} pad(f32[32,16,2048]{2,1,0:T(8,128)} %pad_maximum_fusion.6, f32[]{:T(128)} %constant.164.clone.1), padding=0_1_1x0_0_0x0_0_0 | pad | bytes 12582916 | tf_op jit(solution)/shard_map/while/body/eval_jaxpr/pad | solution.py:161
  972.0 11.7 add.717
  983.6 11.7 add.709
  995.3 21.2 %fusion.3 = (f32[63,16,2048]{2,1,0:T(8,128)}, f32[63,16,2048]{2,1,0:T(8,128)S(1)}) fusion(f32[64,16,2048]{2,1,0:T(8,128)} %pad.345, f32[64,16,2048]{2,1,0:T(8,128)} %pad.344, f32[63,16,2048]{2,1,0:T(8,128)} %slice.899, f32[63,16,2048]{2,1,0:T(8,128)} %pad_slice_fusion.2, f32[64,16,2048]{2,1,0:T(8,128)} %pad.359, f32[64,16,2048]{2,1,0:T(8,128)} %pad.358), kind=kLoop, calls=%fused_computation.33 | loop fusion | flops 10321920 | bytes 66060288 | tf_op jit(solution)/shard_map/while/body/eval_jaxpr/add | solution.py:41
  1020.9 40.3 %pad.360 = f32[128,16,2048]{2,1,0:T(8,128)} pad(f32[64,16,2048]{2,1,0:T(8,128)} %concatenate.184, f32[]{:T(128)} %constant.164.clone.1), padding=0_1_1x0_0_0x0_0_0 | pad | bytes 25165828 | tf_op jit(solution)/shard_map/while/body/eval_jaxpr/pad | solution.py:161
  1061.2 40.3 %pad.361 = f32[128,16,2048]{2,1,0:T(8,128)} pad(f32[64,16,2048]{2,1,0:T(8,128)} %add.717, f32[]{:T(128)} %constant.164.clone.1), padding=1_0_1x0_0_0x0_0_0 | pad | bytes 25165828 | tf_op jit(solution)/shard_map/while/body/eval_jaxpr/pad | solution.py:161
  1101.5 7.7 pad_maximum_fusion.2
  1109.3 40.3 %pad.346 = f32[128,16,2048]{2,1,0:T(8,128)} pad(f32[64,16,2048]{2,1,0:T(8,128)} %pad_maximum_fusion.2, f32[]{:T(128)} %constant.164.clone.1), padding=0_1_1x0_0_0x0_0_0 | pad | bytes 25165828 | tf_op jit(solution)/shard_map/while/body/eval_jaxpr/pad | solution.py:161
  1149.6 40.3 %pad.347 = f32[128,16,2048]{2,1,0:T(8,128)} pad(f32[64,16,2048]{2,1,0:T(8,128)} %add.709, f32[]{:T(128)} %constant.164.clone.1), padding=1_0_1x0_0_0x0_0_0 | pad | bytes 25165828 | tf_op jit(solution)/shard_map/while/body/eval_jaxpr/pad | solution.py:161
  1189.9 17.8 %add.718 = f32[128,16,2048]{2,1,0:T(8,128)} add(f32[128,16,2048]{2,1,0:T(8,128)} %pad.360, f32[128,16,2048]{2,1,0:T(8,128)} %pad.361) | non-fusion elementwise | flops 4194304 | bytes 50331648 | tf_op jit(solution)/shard_map/while/body/eval_jaxpr/add | solution.py:161
  1211.4 12.4 add.711
  1223.8 21.4 %multiply_reduce_fusion = (f32[16,2048]{1,0:T(8,128)S(1)}, f32[128,2048]{1,0:T(8,128)S(1)}, bf16[128,16]{1,0:T(8,128)(2,1)S(1)}, f32[128,2048]{1,0:T(8,128)S(1)}) fusion(f32[128,2048]{1,0:T(8,128)S(1)} %copy-done.27, f32[128]{0:T(128)S(1)} %copy-done.98, f32[16,2048]{1,0:T(8,128)S(1)} %copy-done.61, f32[127,16,2048]{2,1,0:T(8,128)} %slice.1015, ...), kind=kLoop, calls=%fused_computation.8 | loop fusion | flops 62355456 | bytes 54931968 | tf_op jit(solution)/shard_map/while/body/eval_jaxpr/reduce_sum | solution.py:172
  1267.1 8.2 fusion.27
  1279.1 6.4 fusion.35
  1285.5 42.9 %all-reduce.63 = (f32[2048,4]{0,1:T(4,128)}, f32[2048]{0:T(1024)}, f32[2048]{0:T(1024)}, f32[2048]{0:T(1024)}, f32[1024]{0:T(1024)}) all-reduce(f32[2048,4]{0,1:T(4,128)S(1)} %pad_maximum_fusion.26, f32[2048]{0:T(1024)S(1)} %get-tuple-element.427, f32[2048]{0:T(1024)S(1)} %get-tuple-element.461, ...), channel_id=1, replica_groups=mesh['dp'=4,'seq'=8] {'dp','seq'}, use_global_device_ids=true, to_apply=%region_22.23 | all-reduce | flops 15360 | bytes 122880 | tf_op jit(solution)/shard_map/psum | solution.py:219
  1329.4 54.2 %all-reduce.67.cloned.1.call-done = (f32[2048,96]{0,1:T(8,128)}, f32[64,2048]{1,0:T(8,128)}, f32[2048,16]{0,1:T(8,128)}) async-done(((f32[2048,96]{0,1:T(8,128)}, f32[64,2048]{1,0:T(8,128)}, f32[2048,16]{0,1:T(8,128)}), (f32[2048,96]{0,1:T(8,128)}, f32[64,2048]{1,0:T(8,128)}, f32[2048,16]{0,1:T(8,128)})) %all-reduce.67.cloned.1.call-update) | async-done | bytes 1441808 | tf_op jit(solution)/shard_map/psum | solution.py:219
  1383.6 154.6 %reduce-scatter.5.cloned.1.call-done = f32[2048,32]{0,1:T(8,128)} async-done(((f32[2048,1024]{0,1:T(8,128)}), f32[2048,32]{0,1:T(8,128)}) %reduce-scatter.5.cloned.1.call-update) | async-done | bytes 262160 | tf_op jit(solution)/shard_map/reduce_scatter | solution.py:234
  1538.2 187.1 %reduce-scatter.3.cloned.1.call-done = f32[1024,128]{1,0:T(8,128)} async-done(((f32[1024,4096]{1,0:T(8,128)}), f32[1024,128]{1,0:T(8,128)}) %reduce-scatter.3.cloned.1.call-update) | async-done | bytes 524304 | tf_op jit(solution)/shard_map/reduce_scatter | solution.py:233
  (404 shorter events, 283.0 us)
Async XLA Ops:
  7.2 30.6 %copy-start = (bf16[2048,96]{0,1:T(8,128)(2,1)S(1)}, bf16[2048,96]{0,1:T(8,128)(2,1)}, u32[]{:S(2)}) copy-start(bf16[2048,96]{0,1:T(8,128)(2,1)} %param.23) | copy-start | bytes 1179652
  7.2 1376.4 %all-reduce.67.cloned.1.call-start = ((), (), s32[]{:S(2)}) async-start(), calls=%async_computation.4 | async-start | bytes 2883584 | tf_op jit(solution)/shard_map/psum | solution.py:219
  8.0 6.0 copy-start.72
  9.1 9.5 copy-start.100
  9.1 10.3 copy-start.82
  9.1 13.0 copy-start.67
  14.0 19.8 %copy-start.37 = (f32[1,128,4096]{2,1,0:T(8,128)}, f32[1,128,4096]{2,1,0:T(8,128)S(1)}, u32[]{:S(2)}) copy-start(f32[1,128,4096]{2,1,0:T(8,128)S(1)} %get-tuple-element.555) | copy-start | bytes 6291460
  15.6 16.9 collective-permute-start
  20.0 13.8 copy-start.85
  20.0 13.8 copy-start.87
  20.3 6.9 copy-start.58
  26.5 11.3 copy-start.30
  33.8 4.9 copy-start.70
  40.6 19.0 %copy-start.26 = (f32[128,2048]{1,0:T(8,128)}, f32[128,2048]{1,0:T(8,128)S(1)}, u32[]{:S(2)}) copy-start(f32[128,2048]{1,0:T(8,128)S(1)} %get-tuple-element.518) | copy-start | bytes 3145732
  41.3 18.3 %copy-start.28 = (f32[128,2048]{1,0:T(8,128)}, f32[128,2048]{1,0:T(8,128)S(1)}, u32[]{:S(2)}) copy-start(f32[128,2048]{1,0:T(8,128)S(1)} %fusion.13) | copy-start | bytes 3145732
  43.8 15.8 copy-start.24
  109.8 10.0 copy-start.65
  139.8 12.8 copy-start.49
  166.6 5.4 copy-start.17
  166.6 5.4 copy-start.19
  176.1 11.6 copy-start.36
  215.5 6.8 copy-start.2
  215.5 6.8 copy-start.4
  215.5 8.6 copy-start.5
  224.1 8.0 copy-start.7
  379.0 11.9 copy-start.91
  379.0 12.0 copy-start.68
  379.0 28.1 %copy-start.79 = (bf16[16,2048]{1,0:T(8,128)(2,1)S(1)}, bf16[16,2048]{1,0:T(8,128)(2,1)}, u32[]{:S(2)}) copy-start(bf16[16,2048]{1,0:T(8,128)(2,1)} %get-tuple-element.505) | copy-start | bytes 196612
  379.0 42.9 %copy-start.44 = (f32[1,16,2048]{2,1,0:T(8,128)S(1)}, f32[1,16,2048]{2,1,0:T(8,128)}, u32[]{:S(2)}) copy-start(f32[1,16,2048]{2,1,0:T(8,128)} %custom-call) | copy-start | bytes 393220
  422.6 8.0 copy-start.56
  422.6 177.2 %copy-start.45 = (f32[1,16,2048]{2,1,0:T(8,128)}, f32[1,16,2048]{2,1,0:T(8,128)S(1)}, u32[]{:S(2)}) copy-start(f32[1,16,2048]{2,1,0:T(8,128)S(1)} %get-tuple-element.358) | copy-start | bytes 393220
  559.3 40.5 %copy-start.25 = (f32[1,128,2048]{2,1,0:T(8,128)S(1)}, f32[1,128,2048]{2,1,0:T(8,128)}, u32[]{:S(2)}) copy-start(f32[1,128,2048]{2,1,0:T(8,128)} %copy-done.24) | copy-start | bytes 3145732
  559.3 40.5 %copy-start.48 = (f32[128,2048]{1,0:T(8,128)S(1)}, f32[128,2048]{1,0:T(8,128)}, u32[]{:S(2)}) copy-start(f32[128,2048]{1,0:T(8,128)} %get-tuple-element.494) | copy-start | bytes 3145732
  559.3 40.5 %copy-start.60 = (f32[16,2048]{1,0:T(8,128)S(1)}, f32[16,2048]{1,0:T(8,128)}, u32[]{:S(2)}) copy-start(f32[16,2048]{1,0:T(8,128)} %fusion.62) | copy-start | bytes 393220
  559.3 40.5 %copy-start.99 = (f32[128]{0:T(128)S(1)}, f32[128]{0:T(128)}, u32[]{:S(2)}) copy-start(f32[128]{0:T(128)} %get-tuple-element.548) | copy-start | bytes 1540
  704.5 9.9 copy-start.66
  734.4 12.8 copy-start.50
  760.7 19.0 %slice-start = ((s8[16646144]{0:T(1024)(128)(4,1)}), s8[4194304]{0:T(1024)(128)(4,1)S(1)}, s32[]{:S(2)}) async-start(s8[16646144]{0:T(1024)(128)(4,1)} %bitcast.147), calls=%async_computation.5 | async-start | bytes 8388608
  760.7 19.0 %slice-start.1 = ((s8[16646144]{0:T(1024)(128)(4,1)}), s8[4194304]{0:T(1024)(128)(4,1)S(1)}, s32[]{:S(2)}) async-start(s8[16646144]{0:T(1024)(128)(4,1)} %bitcast.147), calls=%async_computation.6 | async-start | bytes 8388608
  766.9 12.8 slice-start.2
  771.9 7.8 slice-start.3
  785.5 11.5 copy-start.35
  824.7 6.6 copy-start.3
  824.7 6.6 copy-start.6
  831.3 18.7 %slice-start.4 = ((s8[16777216]{0:T(1024)(128)(4,1)}), s8[4194304]{0:T(1024)(128)(4,1)S(1)}, s32[]{:S(2)}) async-start(s8[16777216]{0:T(1024)(128)(4,1)} %bitcast.149), calls=%async_computation.9 | async-start | bytes 8388608
  831.3 18.7 %slice-start.5 = ((s8[16777216]{0:T(1024)(128)(4,1)}), s8[4194304]{0:T(1024)(128)(4,1)S(1)}, s32[]{:S(2)}) async-start(s8[16777216]{0:T(1024)(128)(4,1)} %bitcast.149), calls=%async_computation.10 | async-start | bytes 8388608
  831.3 18.7 %slice-start.6 = ((s8[16777216]{0:T(1024)(128)(4,1)}), s8[4194304]{0:T(1024)(128)(4,1)S(1)}, s32[]{:S(2)}) async-start(s8[16777216]{0:T(1024)(128)(4,1)} %bitcast.149), calls=%async_computation.11 | async-start | bytes 8388608
  840.8 9.2 slice-start.7
  850.1 6.3 copy-start.80
  850.1 21.0 %copy-start.47 = (f32[1,16,2048]{2,1,0:T(8,128)S(1)}, f32[1,16,2048]{2,1,0:T(8,128)}, u32[]{:S(2)}) copy-start(f32[1,16,2048]{2,1,0:T(8,128)} %custom-call.1) | copy-start | bytes 393220
  1189.9 21.4 %copy-start.1 = (f32[128,16,2048]{2,1,0:T(8,128)S(1)}, f32[128,16,2048]{2,1,0:T(8,128)}, u32[]{:S(2)}) copy-start(f32[128,16,2048]{2,1,0:T(8,128)} %pad.346) | copy-start | bytes 50331652
  1211.4 12.4 copy-start.27
  1211.4 12.4 copy-start.29
  1211.4 12.4 copy-start.46
  1211.4 12.4 copy-start.61
  1211.4 12.4 copy-start.74
  1211.4 12.4 copy-start.98
  1223.8 21.5 %copy-start.15 = (bf16[1,128,2048]{2,1,0:T(8,128)(2,1)S(1)}, bf16[1,128,2048]{2,1,0:T(8,128)(2,1)}, u32[]{:S(2)}) copy-start(bf16[1,128,2048]{2,1,0:T(8,128)(2,1)} %copy-done.14) | copy-start | bytes 1572868
  1223.8 21.5 %copy-start.21 = (f32[128,2048]{1,0:T(8,128)S(1)}, f32[128,2048]{1,0:T(8,128)}, u32[]{:S(2)}) copy-start(f32[128,2048]{1,0:T(8,128)} %copy-done.20) | copy-start | bytes 3145732
  1247.7 5.3 copy-start.59
  1249.7 288.4 %reduce-scatter.5.cloned.1.call-start = ((), (), s32[]{:S(2)}) async-start(), calls=%async_computation.3 | async-start | bytes 8650752 | tf_op jit(solution)/shard_map/reduce_scatter | solution.py:234
  1257.7 467.6 %reduce-scatter.3.cloned.1.call-start = ((), (), s32[]{:S(2)}) async-start(), calls=%async_computation.2 | async-start | bytes 17301504 | tf_op jit(solution)/shard_map/reduce_scatter | solution.py:233
  1262.9 3.2 collective-permute-start.1
  1279.1 6.4 copy-start.83
  (52 other events, 149.7 us)
Sparse Core Ops, SparseCore 0:
  1249.9 133.6 all-reduce.66
  1386.4 151.7 reduce-scatter.4
  1541.1 184.1 reduce-scatter.2
where the time goes:
time: 1760 us; the launch traced here: 1740 us
  local copies, waits for them, and re-layouts  742 us (42%)
  other arithmetic  451 us (26%)
  waiting for transfers between devices  397 us (23%)
  blocking collectives  88.4 us (5%)
  matrix products  38.6 us (2%)
    pad x24, local copies, waits for them, and re-layouts, states_from(): lax.associative_scan(pair_combine, (decay_now, inflow), axis=0)  323 us
    pad x24, local copies, waits for them, and re-layouts, row_backward(): lax.associative_scan(pair_combine, (following, source_now), axis=0, rever...  320 us
    reduce_scatter x1, waiting for transfers between devices, body(): lax.psum_scatter(in_full, ('dp', 'seq'), scatter_dimension=1, tiled=True)  187 us
    add x24, other arithmetic, pair_combine(): return (earlier[0] * later[0], later[0] * earlier[1] + later[1])  155 us
    reduce_scatter x1, waiting for transfers between devices, body(): lax.psum_scatter(out_full, ('dp', 'seq'), scatter_dimension=1, tiled=True)  155 us
    add x14, other arithmetic, row_backward(): lax.associative_scan(pair_combine, (following, source_now), axis=0, rever...  82.2 us
    psum x1, waiting for transfers between devices, body(): lax.psum((xproj_part, dt_weight_part, dt_bias_part, a_log_part, skip_part...  54.2 us
    all_gather x3, blocking collectives, carried_in(): lax.all_gather(part.astype(kind), axis)  45.5 us
  transfers between devices with their start and end apart: 5, of which 4 were waited for; matrix products, arithmetic and copies ran while one was open for 3% of the time, Pallas kernels for 0%

commit v1 on v0

v1 whole, which is shorter than its diff:
```python
import functools

import jax
import jax.numpy as jnp
from jax import lax
from jax.experimental import pallas as pl
from jax.experimental.pallas import tpu as pltpu
from jax.sharding import PartitionSpec as P

epsilon = 1e-05
LANES = 128
SUBS = 8
FAR = 1e36
LEAST_RATE = 1e-33
LN2 = 0.6931471805599453
bf16, f32 = jnp.bfloat16, jnp.float32


def spread_maps(maps_ref, table_ref, steps, width):
    def lap(t, _):
        v = maps_ref[pl.ds(pl.multiple_of(t * SUBS, SUBS), SUBS), :]
        for n in range(width):
            table_ref[t, n] = jnp.broadcast_to(v[:, n : n + 1], (SUBS, LANES))
        return 0
    lax.fori_loop(0, steps, lap, 0)


def sub_scan(decay, value, forward):
    row = lax.broadcasted_iota(jnp.int32, decay.shape, 0)
    if not forward:
        row = SUBS - 1 - row
    def moved(x, by, fill):
        return jnp.where(row < by, fill, pltpu.roll(x, by if forward else SUBS - by, 0))
    by = 1
    while by < SUBS:
        d, v = moved(decay, by, 1.0), moved(value, by, 0.0)
        value = decay * v + value
        decay = decay * d
        by *= 2
    return decay, value, moved(decay, 1, 1.0), moved(value, 1, 0.0)


def ends_kernel(states, dtm_ref, dtx_ref, gs_ref, maps_ref, rates_ref,
                s_ref, f_ref, dx_ref, ex_ref, db_ref, fx_ref, table):
    steps = dtm_ref.shape[0] // SUBS
    @pl.when(pl.program_id(0) == 0)
    def _():
        spread_maps(maps_ref, table, steps, 2 * states)
    half = states // 2
    for tile in range(dtm_ref.shape[1] // LANES):
        at = pl.ds(tile * LANES, LANES)
        for first in range(0, states, half):
            rates = [jnp.broadcast_to(rates_ref[pl.ds(first + k, 1), at], (SUBS, LANES)) for k in range(half)]
            def lap(t, carry):
                h, f, p = carry
                rows = pl.ds(pl.multiple_of(t * SUBS, SUBS), SUBS)
                d, u, g = dtm_ref[rows, at], dtx_ref[rows, at], gs_ref[rows, at]
                hn, fn, pn = [], [], []
                for k in range(half):
                    a = jnp.exp2(d * rates[k])
                    hn.append(a * h[k] + u * table[t, first + k])
                    q = p[k] * a
                    pn.append(q)
                    fn.append(f[k] + q * (g * table[t, states + first + k]))
                return tuple(hn), tuple(fn), tuple(pn)
            zero = jnp.zeros((SUBS, LANES), jnp.float32)
            one = jnp.ones((SUBS, LANES), jnp.float32)
            h, f, p = lax.fori_loop(0, steps, lap, ((zero,) * half, (zero,) * half, (one,) * half), unroll=4)
            for k in range(half):
                n = first + k
                _, e_in, d_ex, e_ex = sub_scan(p[k], h[k], True)
                _, f_in, b_ex, f_ex = sub_scan(p[k], f[k], False)
                s_ref[pl.ds(n, 1), at] = e_in[SUBS - 1 :, :]
                f_ref[pl.ds(n, 1), at] = f_in[:1, :]
                dx_ref[n, :, at] = d_ex
                ex_ref[n, :, at] = e_ex
                db_ref[n, :, at] = b_ex
                fx_ref[n, :, at] = f_ex


def scan_ends(dtm, dtx, gs, maps, rates, block):
    length, width = dtm.shape
    states = rates.shape[0]
    f32 = jnp.float32
    wide = pl.BlockSpec((length, block), lambda i: (0, i))
    thin = pl.BlockSpec((states, block), lambda i: (0, i))
    deep = pl.BlockSpec((states, SUBS, block), lambda i: (0, 0, i))
    return pl.pallas_call(
        functools.partial(ends_kernel, states),
        grid=(width // block,),
        in_specs=[wide, wide, wide, pl.BlockSpec(maps.shape, lambda i: (0, 0)), thin],
        out_specs=[thin, thin] + [deep] * 4,
        out_shape=[jax.ShapeDtypeStruct((states, width), f32)] * 2 + [jax.ShapeDtypeStruct((states, SUBS, width), f32)] * 4,
        scratch_shapes=[pltpu.VMEM((length // SUBS, 2 * states, SUBS, LANES), f32)],
        compiler_params=pltpu.CompilerParams(vmem_limit_bytes=48 << 20),
        name="scan_ends",
    )(dtm, dtx, gs, maps, rates)


def core_kernel(states, dtm_ref, dt_ref, x_ref, gs_ref, maps_ref, rates_ref, entry_ref, arrive_ref,
                dx_ref, ex_ref, db_ref, fx_ref,
                y_ref, s1_ref, s2_ref, rate_ref, mapg_ref, table, acc, hs, decays):
    steps = dtm_ref.shape[0] // SUBS
    step_id = pl.program_id(0)
    f32 = jnp.float32
    @pl.when(step_id == 0)
    def _():
        spread_maps(maps_ref, table, steps, 2 * states)
        acc[...] = jnp.zeros_like(acc)
    half = states // 2
    zero = jnp.zeros((SUBS, LANES), f32)
    for tile in range(dtm_ref.shape[1] // LANES):
        at = pl.ds(tile * LANES, LANES)
        def wide(ref, n):
            return jnp.broadcast_to(ref[pl.ds(n, 1), at], (SUBS, LANES))
        rates = [wide(rates_ref, n) for n in range(states)]
        start = []
        for n in range(states):
            h0 = dx_ref[n, :, at] * wide(entry_ref, n) + ex_ref[n, :, at]
            hs[0, n] = h0
            start.append(h0)
        def lap(t, h):
            rows = pl.ds(pl.multiple_of(t * SUBS, SUBS), SUBS)
            d = dtm_ref[rows, at]
            u = dt_ref[rows, at] * x_ref[rows, at]
            new, y = [], [zero, zero]
            for n in range(states):
                a = jnp.exp2(d * rates[n])
                decays[t, n] = a
                now = a * h[n] + u * table[t, n]
                hs[t + 1, n] = now
                y[n % 2] = y[n % 2] + now * table[t, states + n]
                new.append(now)
            y_ref[rows, at] = y[0] + y[1]
            return tuple(new)
        lax.fori_loop(0, steps, lap, tuple(start), unroll=4)
        for first in range(0, states, half):
            some = rates[first : first + half]
            def back(i, carry):
                f, r = carry
                t = steps - 1 - i
                rows = pl.ds(pl.multiple_of(t * SUBS, SUBS), SUBS)
                dt, g = dt_ref[rows, at], gs_ref[rows, at]
                u = dt * x_ref[rows, at]
                fn, rn, s1, s2 = [], [], zero, zero
                for k in range(half):
                    n = first + k
                    adj = g * table[t, states + n] + f[k]
                    acc[t, n] += adj * u
                    acc[t, states + n] += g * hs[t + 1, n]
                    s1 = s1 + adj * table[t, n]
                    flow = decays[t, n] * adj
                    fn.append(flow)
                    flow = flow * hs[t, n]
                    s2 = s2 + flow * some[k]
                    rn.append(r[k] + flow * dt)
                if first == 0:
                    s1_ref[rows, at] = s1
                    s2_ref[rows, at] = s2
                else:
                    s1_ref[rows, at] += s1
                    s2_ref[rows, at] += s2
                return tuple(fn), tuple(rn)
            f0 = tuple(db_ref[first + k, :, at] * wide(arrive_ref, first + k) + fx_ref[first + k, :, at] for k in range(half))
            _, r = lax.fori_loop(0, steps, back, (f0, (zero,) * half), unroll=4)
            for k in range(half):
                rate_ref[pl.ds(first + k, 1), at] = jnp.sum(r[k], axis=0, keepdims=True)
    @pl.when(step_id == pl.num_programs(0) - 1)
    def _():
        lane = lax.broadcasted_iota(jnp.int32, (SUBS, LANES), 1)
        def lap(t, _):
            out = zero
            for n in range(2 * states):
                out = jnp.where(lane == n, jnp.sum(acc[t, n], axis=1, keepdims=True), out)
            mapg_ref[pl.ds(pl.multiple_of(t * SUBS, SUBS), SUBS), :] = out
            return 0
        lax.fori_loop(0, steps, lap, 0)


def scan_core(dtm, dt, x, gs, maps, rates, entry, arrive, deep4, block):
    length, width = dtm.shape
    states = rates.shape[0]
    steps = length // SUBS
    f32 = jnp.float32
    wide = pl.BlockSpec((length, block), lambda i: (0, i))
    thin = pl.BlockSpec((states, block), lambda i: (0, i))
    deep = pl.BlockSpec((states, SUBS, block), lambda i: (0, 0, i))
    full = pl.BlockSpec(maps.shape, lambda i: (0, 0))
    big = jax.ShapeDtypeStruct((length, width), f32)
    return pl.pallas_call(
        functools.partial(core_kernel, states),
        grid=(width // block,),
        in_specs=[wide] * 4 + [full] + [thin] * 3 + [deep] * 4,
        out_specs=[wide] * 3 + [thin, full],
        out_shape=[big] * 3 + [jax.ShapeDtypeStruct((states, width), f32), jax.ShapeDtypeStruct(maps.shape, f32)],
        scratch_shapes=[
            pltpu.VMEM((steps, 2 * states, SUBS, LANES), f32),
            pltpu.VMEM((steps, 2 * states, SUBS, LANES), f32),
            pltpu.VMEM((steps + 1, states, SUBS, LANES), f32),
            pltpu.VMEM((steps, states, SUBS, LANES), f32),
        ],
        compiler_params=pltpu.CompilerParams(vmem_limit_bytes=56 << 20),
        name="scan_core",
    )(dtm, dt, x, gs, maps, rates, entry, arrive, *deep4)


class Group:
    def __init__(self, axis, size, stride):
        self.axis, self.size, self.stride = axis, size, stride
        self.direct = size <= 4
        self.place = (lax.axis_index(axis) // stride) % size

    def lists(self):
        n = lax.axis_size(self.axis)
        span = self.stride * self.size
        return [
            [base + low + self.stride * k for k in range(self.size)]
            for base in range(0, n, span)
            for low in range(self.stride)
        ]

    def swap(self, x, k):
        n = lax.axis_size(self.axis)
        return lax.ppermute(x, self.axis, [(i, i ^ (k * self.stride)) for i in range(n)])

    def exchange(self, blocks):
        if not self.direct:
            got = lax.all_to_all(blocks, self.axis, 0, 0, axis_index_groups=self.lists(), tiled=True)
            return [got[k] for k in range(self.size)]
        pick = lambda k: lax.dynamic_index_in_dim(blocks, self.place ^ k, 0, keepdims=False)
        return [pick(0)] + [self.swap(pick(k), k) for k in range(1, self.size)]

    def gather(self, x):
        if not self.direct:
            got = lax.all_gather(x, self.axis, axis_index_groups=self.lists())
            return [got[k] for k in range(self.size)]
        return [x] + [self.swap(x, k) for k in range(1, self.size)]

    def in_order(self, parts):
        if not self.direct:
            return jnp.stack(parts)
        stacked = jnp.stack(parts)
        return jnp.stack(
            [lax.dynamic_index_in_dim(stacked, self.place ^ q, 0, keepdims=False) for q in range(self.size)]
        )


def total(parts):
    return functools.reduce(lambda a, b: a + b, [part.astype(f32) for part in parts])


def silu_slope(values):
    sigma = jax.nn.sigmoid(values)
    return sigma * (1.0 + values * (1.0 - sigma))


def pack(state, flow, span):
    high = span.astype(bf16)
    rest = span - high.astype(f32)
    middle = rest.astype(bf16)
    low = (rest - middle.astype(f32)).astype(bf16)
    return jnp.concatenate([state.astype(bf16), flow.astype(bf16), high, middle, low], axis=0)


def unpack(packed, states):
    wide = packed.astype(f32)
    span = wide[2 * states : 2 * states + 1] + wide[2 * states + 1 : 2 * states + 2] + wide[2 * states + 2 :]
    return wide[:states], wide[states : 2 * states], span


def carried(state, flow, span, rates, core, outer):
    states = state.shape[0]
    mine = pack(state, flow, span)
    pair = core.in_order(core.gather(mine))
    (s0, f0, d0), (s1, f1, d1) = unpack(pair[0], states), unpack(pair[1], states)
    whole0, whole1 = jnp.exp2(rates * d0), jnp.exp2(rates * d1)
    chips = outer.in_order(outer.gather(pack(whole1 * s0 + s1, f0 + whole0 * f1, d0 + d1)))
    entry, arrive = jnp.zeros_like(state), jnp.zeros_like(flow)
    for q in range(outer.size):
        s, f, d = unpack(chips[q], states)
        entry = jnp.where(q < outer.place, jnp.exp2(rates * d) * entry + s, entry)
        r = outer.size - 1 - q
        s, f, d = unpack(chips[r], states)
        arrive = jnp.where(r > outer.place, jnp.exp2(rates * d) * arrive + f, arrive)
    entry = jnp.where(core.place == 1, whole0 * entry + s0, entry)
    arrive = jnp.where(core.place == 0, whole1 * arrive + f1, arrive)
    return entry, arrive


def matmul(a, b):
    return jnp.dot(a, b, preferred_element_type=f32)


def body(
    tokens,
    cotangent,
    doc_starts,
    in_weight,
    conv_weight,
    conv_bias,
    xproj_weight,
    dt_weight,
    dt_bias,
    a_log,
    skip_scale,
    out_weight,
    norm_gain,
):
    length, model = tokens.shape[1:]
    inner_width, states = a_log.shape
    low_rank = dt_weight.shape[0]
    tap_count = conv_weight.shape[1]
    rim = tap_count - 1
    steps = length // SUBS
    dp_size, seq_size = lax.axis_size("dp"), lax.axis_size("seq")
    core, outer = Group("seq", 2, 1), Group("seq", seq_size // 2, 2)
    rows_group = Group("dp", dp_size, 1)
    row_at = lax.axis_index("dp")

    def mixed_order(x):
        return x.reshape(SUBS, steps, -1).swapaxes(0, 1).reshape(length, -1)

    def plain_order(x):
        return x.reshape(steps, SUBS, -1).swapaxes(0, 1).reshape(length, -1)

    base = lax.axis_index("seq") * length
    order = jnp.arange(length, dtype=jnp.int32)
    places = (base + (order % SUBS) * steps + order // SUBS)[:, None]
    doc_begin = jnp.max(jnp.where(doc_starts <= places, doc_starts, 0), axis=1, keepdims=True)
    reset = jnp.any(doc_starts == places, axis=1, keepdims=True)

    tok_row = tokens[0]
    left = lax.ppermute(tok_row[length - rim :], "seq", [(i, i + 1) for i in range(seq_size - 1)])
    tok_all = jnp.concatenate([mixed_order(tok_row), left, jnp.zeros((SUBS - rim, model), bf16)], axis=0)
    all_f = tok_all.astype(f32)
    inv_all = lax.rsqrt(jnp.mean(all_f * all_f, axis=-1, keepdims=True) + epsilon)
    scaled_all = all_f * inv_all
    normed_all = (scaled_all * norm_gain.astype(f32)).astype(bf16)
    normed = normed_all[:length]
    cot = mixed_order(cotangent[0])

    conv_all = matmul(normed_all, in_weight[:, :inner_width]).astype(bf16)
    gate_in = matmul(normed, in_weight[:, inner_width:])
    conv_in = conv_all[:length]
    tail_blocks = conv_in[length - rim * SUBS :].reshape(rim, SUBS, inner_width)
    head = jnp.concatenate([conv_all[length : length + rim][:, None], tail_blocks[:, : SUBS - 1]], axis=1)
    extended = jnp.concatenate([head.reshape(rim * SUBS, inner_width), conv_in], axis=0).astype(f32)
    conv_f = conv_weight.astype(f32)
    pre_conv = jnp.zeros((length, inner_width), f32) + conv_bias.astype(f32)
    masks, windows = [], []
    for offset in range(tap_count):
        masks.append((doc_begin <= places - offset).astype(f32))
        windows.append(extended[(rim - offset) * SUBS : (rim - offset) * SUBS + length])
        pre_conv = pre_conv + conv_f[:, tap_count - 1 - offset] * windows[offset] * masks[offset]
    inner_act = jax.nn.silu(pre_conv).astype(bf16)
    inner_f = inner_act.astype(f32)
    projected = matmul(inner_act, xproj_weight)
    dt_low = projected[:, :low_rank].astype(bf16)
    maps = jnp.pad(projected[:, low_rank:], ((0, 0), (0, LANES - 2 * states)))
    dt_raw = matmul(dt_low, dt_weight) + dt_bias.astype(f32)
    time_step = jax.nn.softplus(dt_raw)
    masked_step = jnp.where(reset, FAR, time_step)
    decay_rates = -jnp.exp(a_log).T
    rates = jnp.minimum(decay_rates, -LEAST_RATE) / LN2
    skip_f = skip_scale.astype(f32)
    g_gated = lax.dot_general(cot, out_weight, (((1,), (1,)), ((), ())), preferred_element_type=f32)
    gate_act = jax.nn.silu(gate_in)
    g_scanned = g_gated * gate_act

    block = min(512, inner_width)
    state_end, flow_end, *deep = scan_ends(masked_step, time_step * inner_f, g_scanned, maps, rates, block)
    span = jnp.sum(masked_step, axis=0, keepdims=True)
    entry, arrive = carried(state_end, flow_end, span, rates, core, outer)
    scan_out, adjoint_in, flow_rates, rate_part, map_grads = scan_core(
        masked_step, time_step, inner_f, g_scanned, maps, rates, entry, arrive, deep, block
    )
    scanned = scan_out + skip_f * inner_f
    gated_out = (scanned * gate_act).astype(bf16)
    mixed = (all_f[:length] + matmul(gated_out, out_weight)).astype(bf16)
    g_gate_in = g_gated * scanned * silu_slope(gate_in)

    step_grad = adjoint_in * inner_f + LN2 * flow_rates
    inner_scan_grad = adjoint_in * time_step + g_scanned * skip_f
    a_log_part = decay_rates * rate_part
    skip_part = jnp.sum(g_scanned * inner_f, axis=0)
    raw_grad = step_grad * jax.nn.sigmoid(dt_raw)
    dt_bias_part = jnp.sum(raw_grad, axis=0)
    raw_low = raw_grad.astype(bf16)
    dt_weight_part = matmul(dt_low.T, raw_low)
    low_grad = lax.dot_general(raw_low, dt_weight, (((1,), (1,)), ((), ())), preferred_element_type=f32)
    proj_grad = jnp.concatenate([low_grad, map_grads[:, : 2 * states]], axis=-1).astype(bf16)
    xproj_part = matmul(proj_grad.T, inner_act)
    inner_grad = inner_scan_grad + lax.dot_general(
        proj_grad, xproj_weight, (((1,), (1,)), ((), ())), preferred_element_type=f32
    )
    pre_grad = inner_grad * silu_slope(pre_conv)
    conv_bias_part = jnp.sum(pre_grad, axis=0)
    ext_grad = jnp.zeros(extended.shape, f32)
    taps = []
    for offset in range(tap_count):
        masked = pre_grad * masks[offset]
        taps.append(jnp.sum(masked * windows[offset], axis=0))
        ext_grad = ext_grad + jnp.pad(
            conv_f[:, tap_count - 1 - offset] * masked,
            (((rim - offset) * SUBS, offset * SUBS), (0, 0)),
        )
    head_grad = ext_grad[: rim * SUBS].reshape(rim, SUBS, inner_width)
    rim_grad = head_grad[:, 0]
    moved = jnp.pad(head_grad[:, 1:], ((0, 0), (0, 1), (0, 0))).reshape(rim * SUBS, inner_width)
    near_grad = ext_grad[rim * SUBS :] + jnp.pad(moved, ((length - rim * SUBS, 0), (0, 0)))
    rim_back = lax.ppermute(rim_grad, "seq", [(i, i - 1) for i in range(1, seq_size)])
    far_grad = jnp.pad(rim_back[:, None], ((0, 0), (SUBS - 1, 0), (0, 0))).reshape(rim * SUBS, inner_width)
    conv_grad = near_grad + jnp.pad(far_grad, ((length - rim * SUBS, 0), (0, 0)))

    width = in_weight.shape[1] // (dp_size * seq_size)
    half_rows = dp_size // 2

    def by_chip(x):
        rows = x.shape[0]
        blocks = x.reshape(rows, half_rows, outer.size, 2, width)
        return blocks.transpose(2, 0, 3, 1, 4).reshape(outer.size, rows, 2 * half_rows * width)

    normed_parts = outer.gather(normed_all)
    cot_parts = outer.gather(cot)
    sent = jnp.concatenate([near_grad, rim_grad, jnp.zeros((SUBS - rim, inner_width), f32)], axis=0).astype(bf16)
    conv_got = outer.exchange(by_chip(sent))
    gate_got = outer.exchange(by_chip(g_gate_in.astype(bf16)))
    out_got = outer.exchange(gated_out.reshape(length, outer.size, -1).swapaxes(0, 1))

    def summed(lefts, rights):
        return functools.reduce(
            lambda a, b: a + b,
            [
                lax.dot_general(a, b, (((0,), (0,)), ((), ())), preferred_element_type=f32)
                for a, b in zip(lefts, rights, strict=True)
            ],
        )

    conv_sum = summed(normed_parts, conv_got).reshape(model, 2, half_rows, width)
    gate_sum = summed([part[:length] for part in normed_parts], gate_got).reshape(model, 2, half_rows, width)
    in_sum = jnp.concatenate([conv_sum, gate_sum], axis=2).transpose(1, 2, 0, 3)
    in_core = total(core.exchange(in_sum.astype(bf16)))
    in_share = total(rows_group.exchange(in_core.astype(bf16)))

    out_sum = summed(out_got, cot_parts)
    thin = model // (dp_size * seq_size)
    out_sum = out_sum.reshape(-1, dp_size, outer.size, 2, thin).transpose(3, 1, 2, 0, 4)
    out_core = total(core.exchange(out_sum.astype(bf16)))
    out_row = total(rows_group.exchange(out_core.astype(bf16)))
    out_share = outer.in_order(outer.exchange(out_row.astype(bf16))).reshape(inner_width, thin).astype(f32)

    joined_grad = jnp.concatenate([conv_grad, g_gate_in], axis=-1).astype(bf16)
    normed_grad = lax.dot_general(joined_grad, in_weight, (((1,), (1,)), ((), ())), preferred_element_type=f32)
    scaled = scaled_all[:length]
    gain_part = jnp.sum(normed_grad * scaled, axis=0)
    hat_grad = normed_grad * norm_gain.astype(f32)
    tokens_grad = (
        cot.astype(f32)
        + inv_all[:length] * (hat_grad - scaled * jnp.mean(hat_grad * scaled, axis=-1, keepdims=True))
    ).astype(bf16)

    small = jnp.concatenate(
        [
            xproj_part,
            dt_weight_part,
            a_log_part,
            jnp.stack(taps[::-1], axis=0),
            dt_bias_part[None],
            skip_part[None],
            conv_bias_part[None],
            jnp.pad(gain_part, (0, inner_width - model))[None],
        ],
        axis=0,
    )
    rows = small.shape[0]
    small = small.reshape(rows, 2, dp_size, -1).transpose(1, 2, 0, 3)
    small = total(core.exchange(small.astype(bf16)))
    small = total(rows_group.exchange(small.astype(bf16)))
    small = total(list(outer.in_order(outer.gather(small.astype(bf16)))))
    small = rows_group.in_order(rows_group.gather(small))
    small = core.in_order(core.gather(small))
    small = small.transpose(2, 0, 1, 3).reshape(rows, inner_width)
    edges = [0, low_rank + 2 * states, low_rank, states, tap_count, 1, 1, 1, 1]
    cuts = [sum(edges[: k + 1]) for k in range(len(edges))]
    parts = [small[a:b] for a, b in zip(cuts[:-1], cuts[1:], strict=True)]
    return (
        plain_order(mixed)[None],
        plain_order(tokens_grad)[None],
        in_share,
        parts[3].T,
        parts[6][0],
        parts[0].T,
        parts[1],
        parts[4][0],
        parts[2].T,
        parts[5][0],
        out_share,
        parts[7][0, :model],
    )


def solution(mesh):
    whole = (P(),) * 10
    row = P("dp", "seq", None)
    columns = P(None, ("dp", "seq"))
    return jax.shard_map(
        body,
        mesh=mesh,
        in_specs=(row, row, P("dp", None)) + whole,
        out_specs=(row, row, columns) + (P(),) * 7 + (columns, P()),
        check_vma=False,
    )
```

time: 1760 us -> 294 us (0.17); the launches traced: 1740 us -> 292 us
  local copies, waits for them, and re-layouts: 742 us -> 48.7 us
  other arithmetic: 451 us -> 26.7 us
  waiting for transfers between devices: 397 us -> 48.4 us
  blocking collectives: 88.4 us -> 0 us
  starting transfers between devices: 4.65 us -> 77.5 us
  Pallas kernels: 0 us -> 33 us
    pad x48 -> x2, local copies, waits for them, and re-layouts: 643 us -> 0.01 us  [the longest x1 0.01 us: body(): maps = jnp.pad(projected[:, low_rank:], ((0, 0), (0, LANES - 2 * states)))]
    reduce_scatter x2 -> x0, waiting for transfers between devices: 342 us -> none  [the longest x1 187 us: body(): lax.psum_scatter(in_full, ('dp', 'seq'), scatter_dimension=1, tiled=True)]
    add x51 -> x5, other arithmetic: 283 us -> 2.38 us  [the longest x1 1.34 us: body(): ext_grad + jnp.pad(conv_f[:, tap_count - 1 - offset] * masked, (((rim - o...]
    ppermute x2 -> x43, starting transfers between devices: 4.53 us -> 77.5 us  [the longest x41 73.9 us: swap(): lax.ppermute(x, self.axis, [(i, i ^ k * self.stride) for i in range(n)])]
    concatenate x24 -> x0, other arithmetic: 67.7 us -> none  [the longest x11 36.1 us: states_from(): lax.associative_scan(pair_combine, (decay_now, inflow), axis=0)]
    slice x31 -> x23, local copies, waits for them, and re-layouts: 74.4 us -> 8.63 us  [the longest x12 5.53 us: body(): parts = [small[a:b] for a, b in zip(cuts[:-1], cuts[1:], strict=True)]]
    reduce_sum x5 -> x2, other arithmetic: 61.2 us -> 3.02 us  [the longest x1 2.8 us: body(): dt_bias_part = jnp.sum(raw_grad, axis=0)]
    psum x1 -> x0, waiting for transfers between devices: 54.2 us -> none  [body(): lax.psum((xproj_part, dt_weight_part, dt_bias_part, a_log_part, skip_part...]
  transfers between devices with their start and end apart: 5 -> 43, of which waited for: 4 -> 11; matrix products, arithmetic and copies ran while one was open for 3% -> 35% of each run, Pallas kernels for 0% -> 7%
where the time goes in v1:
time: 294 us; the launch traced here: 292 us
  starting transfers between devices  77.5 us (26%)
  matrix products  55.8 us (19%)
  local copies, waits for them, and re-layouts  48.7 us (17%)
  waiting for transfers between devices  48.4 us (16%)
  Pallas kernels  33 us (11%)
  other arithmetic  26.7 us (9%)
    ppermute x41, starting transfers between devices, swap(): lax.ppermute(x, self.axis, [(i, i ^ k * self.stride) for i in range(n)])  73.9 us
    ppermute x41, waiting for transfers between devices, swap(): lax.ppermute(x, self.axis, [(i, i ^ k * self.stride) for i in range(n)])  48.4 us
    dot_general x12, matrix products, summed(): lax.dot_general(a, b, (((0,), (0,)), ((), ())), preferred_element_type=f32)  25.9 us
    pallas_call x1, Pallas kernels, scan_core(): pl.pallas_call(functools.partial(core_kernel, states), grid=(width // blo...  21.2 us
    dot_general x7, matrix products, matmul(): return jnp.dot(a, b, preferred_element_type=f32)  12.8 us
    pallas_call x1, Pallas kernels, scan_ends(): pl.pallas_call(functools.partial(ends_kernel, states), grid=(width // blo...  11.8 us
    unnamed x173, local copies, waits for them, and re-layouts  9.37 us
    concatenate x15, local copies, waits for them, and re-layouts, body(): jnp.concatenate([xproj_part, dt_weight_part, a_log_part, jnp.stack(taps[:...  8.39 us
  transfers between devices with their start and end apart: 43, of which 11 were waited for; matrix products, arithmetic and copies ran while one was open for 35% of the time, Pallas kernels for 7%

profile of v1, /device:TPU:0, one launch (start us, length us, event | category | flops | bytes accessed | tf_op | source)
XLA Modules:
  0.0 292.4 jit_solution(11308135929595243491)
XLA Ops:
  1.4 2.3 collective-permute-start
  10.8 3.2 %fusion.5 = bf16[136,2048]{1,0:T(8,128)(2,1)S(1)} fusion(bf16[1024,4096]{1,0:T(8,128)(2,1)} %param.16, f32[1024]{0:T(1024)S(1)} %convert_element_type.368, f32[136]{0:T(256)S(1)} %add_rsqrt_fusion, bf16[136]{0:T(256)(128)(2,1)S(1)} %pad.95.clone, bf16[3,1024]{1,0:T(4,128)(2,1)S(1)} %collective-permute-done, bf16[128,1024]{1,0:T(8,128)(2,1)S(1)} %bitcast.342), kind=kOutput, calls=%fused_computation.8 | convolution fusion | flops 571957248 | bytes 5024560 | tf_op jit(solution)/shard_map/dot_general | solution.py:291
  15.6 1.8 fusion
  18.6 4.3 %multiply_reduce_fusion = (bf16[2048]{0:T(1024)(128)(2,1)}, f32[128,2048]{1,0:T(8,128)}, bf16[128,2048]{1,0:T(8,128)(2,1)S(1)}, f32[128,2048]{1,0:T(8,128)}, f32[128,2048]{1,0:T(8,128)}) fusion(f32[128,2048]{1,0:T(8,128)S(1)} %fusion, f32[128]{0:T(128)S(1)} %get-tuple-element.123, f32[152,2048]{1,0:T(8,128)S(1)} %maximum_convert_fusion, ...), kind=kOutput, calls=%fused_computation.37 | convolution fusion | flops 543422464 | bytes 13416448 | tf_op jit(solution)/shard_map/dot_general | solution.py:366
  23.3 2.6 fusion.96
  27.3 11.8 %scan_ends.1 = (f32[16,2048]{1,0:T(8,128)S(1)}, f32[16,2048]{1,0:T(8,128)S(1)}, f32[16,8,2048]{2,1,0:T(8,128)S(1)}, f32[16,8,2048]{2,1,0:T(8,128)S(1)}, f32[16,8...) custom-call(f32[128,2048]{1,0:T(8,128)S(1)} %get-tuple-element.51.dtm_ref, f32[128,2048]{1,0:T(8,128)} %get-tuple-element.69.dtx_ref, ...), custom_call_target="tpu_custom_call" | custom-call | tf_op jit(solution)/shard_map/scan_ends/pallas_call | solution.py:88
  44.1 2.8 collective-permute-start.1
  47.7 1.6 collective-permute-start.31
  54.6 2.1 collective-permute-start.2
  57.0 2.1 collective-permute-start.4
  60.0 8.6 %collective-permute-done.2 = bf16[35,2048]{1,0:T(8,128)(2,1)S(1)} collective-permute-done((bf16[35,2048]{1,0:T(8,128)(2,1)S(1)}, bf16[35,2048]{1,0:T(8,128)(2,1)S(1)}, u32[]{:S(2)}, u32[]{:S(2)}) %collective-permute-start.2) | collective-permute-done | bytes 143392 | tf_op jit(solution)/shard_map/ppermute | solution.py:224
  69.9 10.3 %collective-permute-done.3 = bf16[35,2048]{1,0:T(8,128)(2,1)S(1)} collective-permute-done((bf16[35,2048]{1,0:T(8,128)(2,1)S(1)}, bf16[35,2048]{1,0:T(8,128)(2,1)S(1)}, u32[]{:S(2)}, u32[]{:S(2)}) %collective-permute-start.3) | collective-permute-done | bytes 143392 | tf_op jit(solution)/shard_map/ppermute | solution.py:224
  80.5 1.8 add_select_fusion.arrive_ref
  83.2 21.2 %scan_core.1 = (f32[128,2048]{1,0:T(8,128)}, f32[128,2048]{1,0:T(8,128)}, f32[128,2048]{1,0:T(8,128)}, f32[16,2048]{1,0:T(8,128)}, f32[128,128]{1,0:T(8,128)}) custom-call(f32[128,2048]{1,0:T(8,128)} %copy-done.2, f32[128,2048]{1,0:T(8,128)} %get-tuple-element.70.dt_ref, f32[128,2048]{1,0:T(8,128)} %convert_element_type.378.x_ref, ...), custom_call_target="tpu_custom_call" | custom-call | tf_op jit(solution)/shard_map/scan_core/pallas_call | solution.py:190
  104.4 2.8 fusion.95
  109.0 6.1 %multiply_reduce_fusion.1 = (bf16[2048]{0:T(1024)(128)(2,1)}, bf16[2048]{0:T(1024)(128)(2,1)}, bf16[2048]{0:T(1024)(128)(2,1)}, bf16[2048]{0:T(1024)(128)(2,1)},...) fusion(f32[152,2048]{1,0:T(8,128)} %copy-done.28, ...), kind=kOutput, calls=%fused_computation.38 | convolution fusion | flops 59545600 | bytes 13064192 | tf_op jit(solution)/shard_map/dot_general | solution.py:393
  117.5 1.9 constant_dynamic-slice_fusion.4
  119.4 1.8 fusion.74
  124.3 1.5 copy.106
  125.8 2.7 fusion.40
  128.5 3.7 %fusion.26 = bf16[8,16,1024]{2,0,1:T(8,128)(2,1)} fusion(f32[136,1024]{1,0:T(8,128)S(1)} %copy-done.25, bf16[128,2048]{1,0:T(8,128)(2,1)S(1)} %get-tuple-element.96, bf16[2048,1024]{1,0:T(8,128)(2,1)} %param.24), kind=kOutput, calls=%fused_computation.88 | convolution fusion | flops 537133056 | bytes 5505024 | tf_op jit(solution)/shard_map/dot_general | solution.py:291
  141.7 10.9 %collective-permute-start.30 = (bf16[128,512]{1,0:T(8,128)(2,1)}, bf16[128,512]{1,0:T(8,128)(2,1)}, u32[]{:S(2)}, u32[]{:S(2)}) collective-permute-start(bf16[128,512]{1,0:T(8,128)(2,1)} %bitcast.338), channel_id=1, source_target_pairs={{0,2},{1,3},{2,0},{3,1},{4,6},{5,7},{6,4},{7,5},{8,10},{9,11},{10,... | collective-permute-start | bytes 393224 | tf_op jit(solution)/shard_map/ppermute | solution.py:224
  157.7 6.4 %multiply_reduce_fusion.6 = (bf16[1024]{0:T(1024)(128)(2,1)S(1)}, f32[128]{0:T(128)S(1)}, f32[128,1024]{1,0:T(8,128)S(1)}) fusion(f32[136,1024]{1,0:T(8,128)S(1)} %get-tuple-element.103, f32[1024]{0:T(1024)S(1)} %convert_element_type.368, bf16[1024,4096]{1,0:T(8,128)(2,1)} %param.16, bf16[128,2048]{1,0:T(8,128)(2,1)S(1)} %get-tuple-element.97, ...), kind=kOutput, calls=%fused_computation.75 | convolution fusion | flops 1076493184 | bytes 10492416 | tf_op jit(solution)/shard_map/dot_general | solution.py:453
  164.2 1.6 fusion.51
  166.2 2.1 concatenate.85
  169.9 1.8 dynamic-slice_bitcast_fusion.7
  171.8 4.0 %collective-permute-start.32 = (bf16[128,512]{1,0:T(8,128)(2,1)S(1)}, bf16[128,512]{1,0:T(8,128)(2,1)S(1)}, u32[]{:S(2)}, u32[]{:S(2)}) collective-permute-start(bf16[128,512]{1,0:T(8,128)(2,1)S(1)} %bitcast.373), channel_id=1, source_target_pairs={{0,4},{1,5},{2,6},{3,7},{4,0},{5,1},{6,2},{7,3},{8,12},{9,13},{10,... | collective-permute-start | bytes 393224 | tf_op jit(solution)/shard_map/ppermute | solution.py:224
  175.7 1.5 fusion.102
  177.7 4.0 %collective-permute-done.32 = bf16[128,512]{1,0:T(8,128)(2,1)S(1)} collective-permute-done((bf16[128,512]{1,0:T(8,128)(2,1)S(1)}, bf16[128,512]{1,0:T(8,128)(2,1)S(1)}, u32[]{:S(2)}, u32[]{:S(2)}) %collective-permute-start.32) | collective-permute-done | bytes 131104 | tf_op jit(solution)/shard_map/ppermute | solution.py:224
  181.8 3.4 %collective-permute-start.34 = (bf16[128,512]{1,0:T(8,128)(2,1)S(1)}, bf16[128,512]{1,0:T(8,128)(2,1)S(1)}, u32[]{:S(2)}, u32[]{:S(2)}) collective-permute-start(bf16[128,512]{1,0:T(8,128)(2,1)S(1)} %bitcast.372), channel_id=1, source_target_pairs={{0,6},{1,7},{2,4},{3,5},{4,2},{5,3},{6,0},{7,1},{8,14},{9,15},{10,... | collective-permute-start | bytes 393224 | tf_op jit(solution)/shard_map/ppermute | solution.py:224
  185.1 1.4 fusion.103
  186.5 2.6 collective-permute-start.13
  189.2 5.3 %collective-permute-done.34 = bf16[128,512]{1,0:T(8,128)(2,1)S(1)} collective-permute-done((bf16[128,512]{1,0:T(8,128)(2,1)S(1)}, bf16[128,512]{1,0:T(8,128)(2,1)S(1)}, u32[]{:S(2)}, u32[]{:S(2)}) %collective-permute-start.34) | collective-permute-done | bytes 131104 | tf_op jit(solution)/shard_map/ppermute | solution.py:224
  194.4 9.8 %collective-permute-start.12 = (bf16[128,512]{0,1:T(8,128)(2,1)S(1)}, bf16[128,512]{0,1:T(8,128)(2,1)S(1)}, u32[]{:S(2)}, u32[]{:S(2)}) collective-permute-start(bf16[128,512]{0,1:T(8,128)(2,1)S(1)} %copy-done.46), channel_id=1, source_target_pairs={{0,2},{1,3},{2,0},{3,1},{4,6},{5,7},{6,4},{7,5},{8,10},{9,11},{10,... | collective-permute-start | bytes 393224 | tf_op jit(solution)/shard_map/ppermute | solution.py:224
  204.3 2.4 add_convert_fusion
  206.7 1.9 collective-permute-start.14
  208.6 2.7 fusion.31
  211.3 2.5 collective-permute-start.9
  213.8 1.8 fusion.33
  215.6 1.5 copy.127
  218.0 1.9 collective-permute-start.11
  219.9 4.4 %add_convert_fusion.1 = bf16[1024,512]{0,1:T(8,128)(2,1)} fusion(f32[1024,512]{0,1:T(8,128)} %fusion.31, f32[1024,512]{0,1:T(8,128)} %fusion.40, f32[1024,512]{0,1:T(8,128)} %fusion.33, bf16[128,512]{0,1:T(8,128)(2,1)} %collective-permute-done.14, bf16[136,1024]{1,0:T(8,128)(2,1)} %collective-permute-done.10), kind=kOutput, calls=%fused_computation.18 | convolution fusion | flops 136314880 | bytes 7733248 | tf_op jit(solution)/shard_map/dot_general | solution.py:434
  224.3 1.9 copy.108
  226.2 1.5 fusion.100
  227.7 1.5 fusion.101
  231.0 1.5 collective-permute-start.20
  232.5 1.5 collective-permute-start.21
  234.5 2.6 add_convert_fusion.2
  237.1 1.6 copy.107
  241.0 2.5 collective-permute-start.24
  243.5 1.9 collective-permute-start.25
  245.5 4.9 %collective-permute-done.24 = bf16[184,256]{1,0:T(8,128)(2,1)S(1)} collective-permute-done((bf16[184,256]{1,0:T(8,128)(2,1)S(1)}, bf16[184,256]{1,0:T(8,128)(2,1)S(1)}, u32[]{:S(2)}, u32[]{:S(2)}) %collective-permute-start.24) | collective-permute-done | bytes 94240 | tf_op jit(solution)/shard_map/ppermute | solution.py:224
  250.5 2.0 collective-permute-start.26
  255.4 2.0 collective-permute-start.37
  258.2 1.9 collective-permute-start.38
  260.1 3.4 %collective-permute-done.27 = f32[184,256]{1,0:T(8,128)S(1)} collective-permute-done((f32[184,256]{1,0:T(8,128)S(1)}, f32[184,256]{1,0:T(8,128)S(1)}, u32[]{:S(2)}, u32[]{:S(2)}) %collective-permute-start.27) | collective-permute-done | bytes 188448 | tf_op jit(solution)/shard_map/ppermute | solution.py:224
  263.5 1.5 collective-permute-start.39
  265.4 4.0 %collective-permute-done.39 = bf16[4,512,32]{1,2,0:T(8,128)(2,1)S(1)} collective-permute-done((bf16[4,512,32]{1,2,0:T(8,128)(2,1)S(1)}, bf16[4,512,32]{1,2,0:T(8,128)(2,1)S(1)}, u32[]{:S(2)}, u32[]{:S(2)}) %collective-permute-start.39) | collective-permute-done | bytes 131104 | tf_op jit(solution)/shard_map/ppermute | solution.py:224
  269.5 2.3 collective-permute-start.40
  272.4 1.8 collective-permute-start.42
  274.7 1.9 collective-permute-start.17
  276.6 1.5 collective-permute-start.18
  279.0 2.5 collective-permute-done.16
  281.5 3.4 %collective-permute-done.17 = bf16[1024,128]{1,0:T(8,128)(2,1)S(1)} collective-permute-done((bf16[1024,128]{1,0:T(8,128)(2,1)S(1)}, bf16[1024,128]{1,0:T(8,128)(2,1)S(1)}, u32[]{:S(2)}, u32[]{:S(2)}) %collective-permute-start.17) | collective-permute-done | bytes 262176 | tf_op jit(solution)/shard_map/ppermute | solution.py:224
  (351 shorter events, 69.9 us)
Async XLA Ops:
  0.6 22.4 %copy-start = (bf16[2048,96]{0,1:T(8,128)(2,1)S(1)}, bf16[2048,96]{0,1:T(8,128)(2,1)}, u32[]{:S(2)}) copy-start(bf16[2048,96]{0,1:T(8,128)(2,1)} %param.19) | copy-start | bytes 1179652
  1.4 9.1 %collective-permute-start = (bf16[3,1024]{1,0:T(4,128)(2,1)S(1)}, bf16[3,1024]{1,0:T(4,128)(2,1)S(1)}, u32[]{:S(2)}, u32[]{:S(2)}) collective-permute-start(bf16[3,1024]{1,0:T(4,128)(2,1)S(1)} %slice_bitcast_fusion.14), channel_id=1, source_target_pairs={{0,1},{1,2},{2,3},{3,4},{4,5},{5,6},{6,7},{8,9},{9,10},{10,11},{11... | collective-permute-start | bytes 18440 | tf_op jit(solution)/shard_map/ppermute | solution.py:333
  4.6 13.0 %copy-start.75 = (f32[128]{0:T(128)}, f32[128]{0:T(128)S(1)}, u32[]{:S(2)}) copy-start(f32[128]{0:T(128)S(1)} %get-tuple-element.122) | copy-start | bytes 1540
  4.6 13.0 %copy-start.77 = (f32[128]{0:T(128)}, f32[128]{0:T(128)S(1)}, u32[]{:S(2)}) copy-start(f32[128]{0:T(128)S(1)} %get-tuple-element.123) | copy-start | bytes 1540
  4.6 13.0 %copy-start.79 = (f32[128]{0:T(128)}, f32[128]{0:T(128)S(1)}, u32[]{:S(2)}) copy-start(f32[128]{0:T(128)S(1)} %get-tuple-element.124) | copy-start | bytes 1540
  4.6 13.0 %copy-start.81 = (f32[128]{0:T(128)}, f32[128]{0:T(128)S(1)}, u32[]{:S(2)}) copy-start(f32[128]{0:T(128)S(1)} %get-tuple-element.125) | copy-start | bytes 1540
  6.5 20.8 %copy-start.3 = (f32[16,2048]{1,0:T(8,128)}, f32[16,2048]{1,0:T(8,128)S(1)}, u32[]{:S(2)}) copy-start(f32[16,2048]{1,0:T(8,128)S(1)} %broadcast_multiply_fusion.1.rates_ref) | copy-start | bytes 393220
  8.4 50.7 %copy-start.11 = (bf16[8,16,1024]{2,0,1:T(8,128)(2,1)}, bf16[8,16,1024]{2,0,1:T(8,128)(2,1)S(1)}, u32[]{:S(2)}) copy-start(bf16[8,16,1024]{2,0,1:T(8,128)(2,1)S(1)} %copy.154) | copy-start | bytes 786436
  10.6 48.6 %copy-start.57 = (bf16[136]{0:T(256)(128)(2,1)}, bf16[136]{0:T(256)(128)(2,1)S(1)}, u32[]{:S(2)}) copy-start(bf16[136]{0:T(256)(128)(2,1)S(1)} %pad.95.clone) | copy-start | bytes 820
  15.1 142.6 %copy-start.14 = (f32[136,1024]{1,0:T(8,128)}, f32[136,1024]{1,0:T(8,128)S(1)}, u32[]{:S(2)}) copy-start(f32[136,1024]{1,0:T(8,128)S(1)} %get-tuple-element.103) | copy-start | bytes 1671172
  25.9 18.1 %copy-start.2 = (f32[128,2048]{1,0:T(8,128)}, f32[128,2048]{1,0:T(8,128)S(1)}, u32[]{:S(2)}) copy-start(f32[128,2048]{1,0:T(8,128)S(1)} %get-tuple-element.51.dtm_ref) | copy-start | bytes 3145732
  27.3 20.3 %copy-start.8 = (f32[128,128]{1,0:T(8,128)}, f32[128,128]{1,0:T(8,128)S(1)}, u32[]{:S(2)}) copy-start(f32[128,128]{1,0:T(8,128)S(1)} %pad.40.maps_ref) | copy-start | bytes 196612
  44.1 9.2 %collective-permute-start.1 = (bf16[35,2048]{1,0:T(8,128)(2,1)S(1)}, bf16[35,2048]{1,0:T(8,128)(2,1)}, u32[]{:S(2)}, u32[]{:S(2)}) collective-permute-start(bf16[35,2048]{1,0:T(8,128)(2,1)S(1)} %concatenate.66), channel_id=1, source_target_pairs={{0,1},{1,0},{2,3},{3,2},{4,5},{5,4},{6,7},{7,6},{8,9},{9,8},{10,11... | collective-permute-start | bytes 430088 | tf_op jit(solution)/shard_map/ppermute | solution.py:224
  47.7 124.0 %collective-permute-start.31 = (bf16[128,1024]{1,0:T(8,128)(2,1)}, bf16[128,1024]{1,0:T(8,128)(2,1)}, u32[]{:S(2)}, u32[]{:S(2)}) collective-permute-start(bf16[128,1024]{1,0:T(8,128)(2,1)} %bitcast.334), channel_id=1, source_target_pairs={{0,2},{1,3},{2,0},{3,1},{4,6},{5,7},{6,4},{7,5},{8,10},{9,11},{10,... | collective-permute-start | bytes 786440 | tf_op jit(solution)/shard_map/ppermute | solution.py:224
  49.2 128.0 %collective-permute-start.33 = (bf16[128,1024]{1,0:T(8,128)(2,1)}, bf16[128,1024]{1,0:T(8,128)(2,1)}, u32[]{:S(2)}, u32[]{:S(2)}) collective-permute-start(bf16[128,1024]{1,0:T(8,128)(2,1)} %bitcast.334), channel_id=1, source_target_pairs={{0,4},{1,5},{2,6},{3,7},{4,0},{5,1},{6,2},{7,3},{8,12},{9,13},{10,... | collective-permute-start | bytes 786440 | tf_op jit(solution)/shard_map/ppermute | solution.py:224
  54.3 25.9 %copy-start.27 = (f32[1,35,2048]{2,1,0:T(8,128)}, f32[1,35,2048]{2,1,0:T(8,128)S(1)}, u32[]{:S(2)}) copy-start(f32[1,35,2048]{2,1,0:T(8,128)S(1)} %get-tuple-element.102) | copy-start | bytes 860164
  54.6 14.0 %collective-permute-start.2 = (bf16[35,2048]{1,0:T(8,128)(2,1)S(1)}, bf16[35,2048]{1,0:T(8,128)(2,1)S(1)}, u32[]{:S(2)}, u32[]{:S(2)}) collective-permute-start(bf16[35,2048]{1,0:T(8,128)(2,1)S(1)} %concatenate.67), channel_id=1, source_target_pairs={{0,2},{1,3},{2,0},{3,1},{4,6},{5,7},{6,4},{7,5},{8,10},{9,11},{10,... | collective-permute-start | bytes 430088 | tf_op jit(solution)/shard_map/ppermute | solution.py:224
  56.7 23.5 %collective-permute-start.3 = (bf16[35,2048]{1,0:T(8,128)(2,1)S(1)}, bf16[35,2048]{1,0:T(8,128)(2,1)S(1)}, u32[]{:S(2)}, u32[]{:S(2)}) collective-permute-start(bf16[35,2048]{1,0:T(8,128)(2,1)S(1)} %concatenate.67), channel_id=1, source_target_pairs={{0,4},{1,5},{2,6},{3,7},{4,0},{5,1},{6,2},{7,3},{8,12},{9,13},{10,... | collective-permute-start | bytes 430088 | tf_op jit(solution)/shard_map/ppermute | solution.py:224
  57.0 23.2 %collective-permute-start.4 = (bf16[35,2048]{1,0:T(8,128)(2,1)S(1)}, bf16[35,2048]{1,0:T(8,128)(2,1)S(1)}, u32[]{:S(2)}, u32[]{:S(2)}) collective-permute-start(bf16[35,2048]{1,0:T(8,128)(2,1)S(1)} %concatenate.67), channel_id=1, source_target_pairs={{0,6},{1,7},{2,4},{3,5},{4,2},{5,3},{6,0},{7,1},{8,14},{9,15},{10,... | collective-permute-start | bytes 430088 | tf_op jit(solution)/shard_map/ppermute | solution.py:224
  68.6 117.9 %collective-permute-start.35 = (bf16[128,1024]{1,0:T(8,128)(2,1)}, bf16[128,1024]{1,0:T(8,128)(2,1)}, u32[]{:S(2)}, u32[]{:S(2)}) collective-permute-start(bf16[128,1024]{1,0:T(8,128)(2,1)} %bitcast.334), channel_id=1, source_target_pairs={{0,6},{1,7},{2,4},{3,5},{4,2},{5,3},{6,0},{7,1},{8,14},{9,15},{10,... | collective-permute-start | bytes 786440 | tf_op jit(solution)/shard_map/ppermute | solution.py:224
  80.2 126.5 %collective-permute-start.8 = (bf16[136,1024]{1,0:T(8,128)(2,1)}, bf16[136,1024]{1,0:T(8,128)(2,1)}, u32[]{:S(2)}, u32[]{:S(2)}) collective-permute-start(bf16[136,1024]{1,0:T(8,128)(2,1)} %get-tuple-element.104), channel_id=1, source_target_pairs={{0,4},{1,5},{2,6},{3,7},{4,0},{5,1},{6,2},{7,3},{8,12},{9,13},{10,... | collective-permute-start | bytes 835592 | tf_op jit(solution)/shard_map/ppermute | solution.py:224
  83.1 21.2 %copy-start.17 = (f32[128,2048]{1,0:T(8,128)S(1)}, f32[128,2048]{1,0:T(8,128)}, u32[]{:S(2)}) copy-start(f32[128,2048]{1,0:T(8,128)} %get-tuple-element.127) | copy-start | bytes 3145732
  83.1 21.2 %copy-start.30 = (f32[128,2048]{1,0:T(8,128)S(1)}, f32[128,2048]{1,0:T(8,128)}, u32[]{:S(2)}) copy-start(f32[128,2048]{1,0:T(8,128)} %copy-done.29) | copy-start | bytes 3145732
  83.1 21.2 %copy-start.31 = (f32[128,2048]{1,0:T(8,128)S(1)}, f32[128,2048]{1,0:T(8,128)}, u32[]{:S(2)}) copy-start(f32[128,2048]{1,0:T(8,128)} %get-tuple-element.126) | copy-start | bytes 3145732
  83.1 21.2 %copy-start.49 = (f32[2048]{0:T(1024)S(1)}, f32[2048]{0:T(1024)}, u32[]{:S(2)}) copy-start(f32[2048]{0:T(1024)} %convert_element_type.399) | copy-start | bytes 24580
  122.6 19.2 %collective-permute-start.5 = (f32[3,2048]{1,0:T(4,128)}, f32[3,2048]{1,0:T(4,128)}, u32[]{:S(2)}, u32[]{:S(2)}) collective-permute-start(f32[3,2048]{1,0:T(4,128)} %bitcast.339), channel_id=1, source_target_pairs={{1,0},{2,1},{3,2},{4,3},{5,4},{6,5},{7,6},{9,8},{10,9},{11,10},{12... | collective-permute-start | bytes 73736 | tf_op jit(solution)/shard_map/ppermute | solution.py:411
  134.4 19.1 %copy-start.39 = (f32[24,2048]{1,0:T(8,128)S(1)}, f32[24,2048]{1,0:T(8,128)}, u32[]{:S(2)}) copy-start(f32[24,2048]{1,0:T(8,128)} %pad_bitcast_fusion.1) | copy-start | bytes 589828
  141.7 30.0 %collective-permute-start.30 = (bf16[128,512]{1,0:T(8,128)(2,1)}, bf16[128,512]{1,0:T(8,128)(2,1)}, u32[]{:S(2)}, u32[]{:S(2)}) collective-permute-start(bf16[128,512]{1,0:T(8,128)(2,1)} %bitcast.338), channel_id=1, source_target_pairs={{0,2},{1,3},{2,0},{3,1},{4,6},{5,7},{6,4},{7,5},{8,10},{9,11},{10,... | collective-permute-start | bytes 393224 | tf_op jit(solution)/shard_map/ppermute | solution.py:224
  171.7 39.6 %collective-permute-start.6 = (bf16[136,1024]{1,0:T(8,128)(2,1)}, bf16[136,1024]{1,0:T(8,128)(2,1)S(1)}, u32[]{:S(2)}, u32[]{:S(2)}) collective-permute-start(bf16[136,1024]{1,0:T(8,128)(2,1)} %get-tuple-element.104), channel_id=1, source_target_pairs={{0,2},{1,3},{2,0},{3,1},{4,6},{5,7},{6,4},{7,5},{8,10},{9,11},{10,... | collective-permute-start | bytes 835592 | tf_op jit(solution)/shard_map/ppermute | solution.py:224
  171.7 14.8 %copy-start.47 = (bf16[128,512]{0,1:T(8,128)(2,1)S(1)}, bf16[128,512]{0,1:T(8,128)(2,1)}, u32[]{:S(2)}) copy-start(bf16[128,512]{0,1:T(8,128)(2,1)} %get-tuple-element.94) | copy-start | bytes 393220
  171.7 22.7 %copy-start.46 = (bf16[128,512]{0,1:T(8,128)(2,1)S(1)}, bf16[128,512]{0,1:T(8,128)(2,1)}, u32[]{:S(2)}) copy-start(bf16[128,512]{0,1:T(8,128)(2,1)} %get-tuple-element.95) | copy-start | bytes 393220
  171.7 32.5 %copy-start.10 = (f32[512,1024]{1,0:T(8,128)S(1)}, f32[512,1024]{1,0:T(8,128)}, u32[]{:S(2)}) copy-start(f32[512,1024]{1,0:T(8,128)} %fusion.74) | copy-start | bytes 6291460
  171.8 10.0 %collective-permute-start.32 = (bf16[128,512]{1,0:T(8,128)(2,1)S(1)}, bf16[128,512]{1,0:T(8,128)(2,1)S(1)}, u32[]{:S(2)}, u32[]{:S(2)}) collective-permute-start(bf16[128,512]{1,0:T(8,128)(2,1)S(1)} %bitcast.373), channel_id=1, source_target_pairs={{0,4},{1,5},{2,6},{3,7},{4,0},{5,1},{6,2},{7,3},{8,12},{9,13},{10,... | collective-permute-start | bytes 393224 | tf_op jit(solution)/shard_map/ppermute | solution.py:224
  177.2 40.8 %collective-permute-start.10 = (bf16[136,1024]{1,0:T(8,128)(2,1)}, bf16[136,1024]{1,0:T(8,128)(2,1)}, u32[]{:S(2)}, u32[]{:S(2)}) collective-permute-start(bf16[136,1024]{1,0:T(8,128)(2,1)} %get-tuple-element.104), channel_id=1, source_target_pairs={{0,6},{1,7},{2,4},{3,5},{4,2},{5,3},{6,0},{7,1},{8,14},{9,15},{10,... | collective-permute-start | bytes 835592 | tf_op jit(solution)/shard_map/ppermute | solution.py:224
  181.8 12.7 %collective-permute-start.34 = (bf16[128,512]{1,0:T(8,128)(2,1)S(1)}, bf16[128,512]{1,0:T(8,128)(2,1)S(1)}, u32[]{:S(2)}, u32[]{:S(2)}) collective-permute-start(bf16[128,512]{1,0:T(8,128)(2,1)S(1)} %bitcast.372), channel_id=1, source_target_pairs={{0,6},{1,7},{2,4},{3,5},{4,2},{5,3},{6,0},{7,1},{8,14},{9,15},{10,... | collective-permute-start | bytes 393224 | tf_op jit(solution)/shard_map/ppermute | solution.py:224
  186.5 22.0 %collective-permute-start.13 = (bf16[128,512]{0,1:T(8,128)(2,1)S(1)}, bf16[128,512]{0,1:T(8,128)(2,1)S(1)}, u32[]{:S(2)}, u32[]{:S(2)}) collective-permute-start(bf16[128,512]{0,1:T(8,128)(2,1)S(1)} %copy-done.47), channel_id=1, source_target_pairs={{0,4},{1,5},{2,6},{3,7},{4,0},{5,1},{6,2},{7,3},{8,12},{9,13},{10,... | collective-permute-start | bytes 393224 | tf_op jit(solution)/shard_map/ppermute | solution.py:224
  194.4 16.9 %collective-permute-start.12 = (bf16[128,512]{0,1:T(8,128)(2,1)S(1)}, bf16[128,512]{0,1:T(8,128)(2,1)S(1)}, u32[]{:S(2)}, u32[]{:S(2)}) collective-permute-start(bf16[128,512]{0,1:T(8,128)(2,1)S(1)} %copy-done.46), channel_id=1, source_target_pairs={{0,2},{1,3},{2,0},{3,1},{4,6},{5,7},{6,4},{7,5},{8,10},{9,11},{10,... | collective-permute-start | bytes 393224 | tf_op jit(solution)/shard_map/ppermute | solution.py:224
  206.7 13.2 %collective-permute-start.14 = (bf16[128,512]{0,1:T(8,128)(2,1)}, bf16[128,512]{0,1:T(8,128)(2,1)}, u32[]{:S(2)}, u32[]{:S(2)}) collective-permute-start(bf16[128,512]{0,1:T(8,128)(2,1)} %get-tuple-element.93), channel_id=1, source_target_pairs={{0,6},{1,7},{2,4},{3,5},{4,2},{5,3},{6,0},{7,1},{8,14},{9,15},{10,... | collective-permute-start | bytes 393224 | tf_op jit(solution)/shard_map/ppermute | solution.py:224
  208.6 20.6 %collective-permute-start.19 = (bf16[4,184,256]{2,1,0:T(8,128)(2,1)}, bf16[4,184,256]{2,1,0:T(8,128)(2,1)}, u32[]{:S(2)}, u32[]{:S(2)}) collective-permute-start(bf16[4,184,256]{2,1,0:T(8,128)(2,1)} %dynamic-slice_bitcast_fusion.1), channel_id=1, source_target_pairs={{0,1},{1,0},{2,3},{3,2},{4,5},{5,4},{6,7},{7,6},{8,9},{9,8},{10,11... | collective-permute-start | bytes 1130504 | tf_op jit(solution)/shard_map/ppermute | solution.py:224
  211.3 14.9 %collective-permute-start.7 = (bf16[136,512]{1,0:T(8,128)(2,1)}, bf16[136,512]{1,0:T(8,128)(2,1)}, u32[]{:S(2)}, u32[]{:S(2)}) collective-permute-start(bf16[136,512]{1,0:T(8,128)(2,1)} %get-tuple-element.83), channel_id=1, source_target_pairs={{0,2},{1,3},{2,0},{3,1},{4,6},{5,7},{6,4},{7,5},{8,10},{9,11},{10,... | collective-permute-start | bytes 417800 | tf_op jit(solution)/shard_map/ppermute | solution.py:224
  211.3 16.4 %collective-permute-start.9 = (bf16[136,512]{1,0:T(8,128)(2,1)}, bf16[136,512]{1,0:T(8,128)(2,1)}, u32[]{:S(2)}, u32[]{:S(2)}) collective-permute-start(bf16[136,512]{1,0:T(8,128)(2,1)} %get-tuple-element.85), channel_id=1, source_target_pairs={{0,4},{1,5},{2,6},{3,7},{4,0},{5,1},{6,2},{7,3},{8,12},{9,13},{10,... | collective-permute-start | bytes 417800 | tf_op jit(solution)/shard_map/ppermute | solution.py:224
  218.0 16.5 %collective-permute-start.11 = (bf16[136,512]{1,0:T(8,128)(2,1)}, bf16[136,512]{1,0:T(8,128)(2,1)}, u32[]{:S(2)}, u32[]{:S(2)}) collective-permute-start(bf16[136,512]{1,0:T(8,128)(2,1)} %get-tuple-element.84), channel_id=1, source_target_pairs={{0,6},{1,7},{2,4},{3,5},{4,2},{5,3},{6,0},{7,1},{8,14},{9,15},{10,... | collective-permute-start | bytes 417800 | tf_op jit(solution)/shard_map/ppermute | solution.py:224
  219.9 34.2 %collective-permute-start.36 = (bf16[4,4,512,32]{2,3,1,0:T(8,128)(2,1)}, bf16[4,4,512,32]{2,3,1,0:T(8,128)(2,1)}, u32[]{:S(2)}, u32[]{:S(2)}) collective-permute-start(bf16[4,4,512,32]{2,3,1,0:T(8,128)(2,1)} %dynamic-slice_bitcast_fusion), channel_id=1, source_target_pairs={{0,1},{1,0},{2,3},{3,2},{4,5},{5,4},{6,7},{7,6},{8,9},{9,8},{10,11... | collective-permute-start | bytes 1572872 | tf_op jit(solution)/shard_map/ppermute | solution.py:224
  231.0 7.7 %collective-permute-start.20 = (bf16[184,256]{1,0:T(8,128)(2,1)}, bf16[184,256]{1,0:T(8,128)(2,1)}, u32[]{:S(2)}, u32[]{:S(2)}) collective-permute-start(bf16[184,256]{1,0:T(8,128)(2,1)} %get-tuple-element.98), channel_id=1, source_target_pairs={{0,8},{8,0},{16,24},{24,16},{1,9},{9,1},{17,25},{25,17},{2,10},{10... | collective-permute-start | bytes 282632 | tf_op jit(solution)/shard_map/ppermute | solution.py:224
  232.5 6.2 %collective-permute-start.21 = (bf16[184,256]{1,0:T(8,128)(2,1)}, bf16[184,256]{1,0:T(8,128)(2,1)}, u32[]{:S(2)}, u32[]{:S(2)}) collective-permute-start(bf16[184,256]{1,0:T(8,128)(2,1)} %get-tuple-element.100), channel_id=1, source_target_pairs={{0,16},{8,24},{16,0},{24,8},{1,17},{9,25},{17,1},{25,9},{2,18},{10... | collective-permute-start | bytes 282632 | tf_op jit(solution)/shard_map/ppermute | solution.py:224
  234.1 5.8 %collective-permute-start.22 = (bf16[184,256]{1,0:T(8,128)(2,1)}, bf16[184,256]{1,0:T(8,128)(2,1)}, u32[]{:S(2)}, u32[]{:S(2)}) collective-permute-start(bf16[184,256]{1,0:T(8,128)(2,1)} %get-tuple-element.99), channel_id=1, source_target_pairs={{0,24},{8,16},{16,8},{24,0},{1,25},{9,17},{17,9},{25,1},{2,26},{10... | collective-permute-start | bytes 282632 | tf_op jit(solution)/shard_map/ppermute | solution.py:224
  240.9 13.3 %copy-start.19 = (bf16[512,1024]{0,1:T(8,128)(2,1)S(1)}, bf16[512,1024]{0,1:T(8,128)(2,1)}, u32[]{:S(2)}) copy-start(bf16[512,1024]{0,1:T(8,128)(2,1)} %copy-done.18) | copy-start | bytes 3145732
  240.9 4.6 %collective-permute-start.23 = (bf16[184,256]{1,0:T(8,128)(2,1)S(1)}, bf16[184,256]{1,0:T(8,128)(2,1)S(1)}, u32[]{:S(2)}, u32[]{:S(2)}) collective-permute-start(bf16[184,256]{1,0:T(8,128)(2,1)S(1)} %fusion.45), channel_id=1, source_target_pairs={{0,2},{1,3},{2,0},{3,1},{4,6},{5,7},{6,4},{7,5},{8,10},{9,11},{10,... | collective-permute-start | bytes 282632 | tf_op jit(solution)/shard_map/ppermute | solution.py:224
  241.0 9.4 %collective-permute-start.24 = (bf16[184,256]{1,0:T(8,128)(2,1)S(1)}, bf16[184,256]{1,0:T(8,128)(2,1)S(1)}, u32[]{:S(2)}, u32[]{:S(2)}) collective-permute-start(bf16[184,256]{1,0:T(8,128)(2,1)S(1)} %fusion.45), channel_id=1, source_target_pairs={{0,4},{1,5},{2,6},{3,7},{4,0},{5,1},{6,2},{7,3},{8,12},{9,13},{10,... | collective-permute-start | bytes 282632 | tf_op jit(solution)/shard_map/ppermute | solution.py:224
  243.5 6.9 %collective-permute-start.25 = (bf16[184,256]{1,0:T(8,128)(2,1)S(1)}, bf16[184,256]{1,0:T(8,128)(2,1)S(1)}, u32[]{:S(2)}, u32[]{:S(2)}) collective-permute-start(bf16[184,256]{1,0:T(8,128)(2,1)S(1)} %fusion.45), channel_id=1, source_target_pairs={{0,6},{1,7},{2,4},{3,5},{4,2},{5,3},{6,0},{7,1},{8,14},{9,15},{10,... | collective-permute-start | bytes 282632 | tf_op jit(solution)/shard_map/ppermute | solution.py:224
  245.4 28.8 %collective-permute-start.15 = (bf16[4,1024,128]{2,1,0:T(8,128)(2,1)S(1)}, bf16[4,1024,128]{2,1,0:T(8,128)(2,1)S(1)}, u32[]{:S(2)}, u32[]{:S(2)}) collective-permute-start(bf16[4,1024,128]{2,1,0:T(8,128)(2,1)S(1)} %fusion.10), channel_id=1, source_target_pairs={{0,1},{1,0},{2,3},{3,2},{4,5},{5,4},{6,7},{7,6},{8,9},{9,8},{10,11... | collective-permute-start | bytes 3145736 | tf_op jit(solution)/shard_map/ppermute | solution.py:224
  250.5 7.7 %collective-permute-start.26 = (f32[184,256]{1,0:T(8,128)S(1)}, f32[184,256]{1,0:T(8,128)S(1)}, u32[]{:S(2)}, u32[]{:S(2)}) collective-permute-start(f32[184,256]{1,0:T(8,128)S(1)} %fusion.131), channel_id=1, source_target_pairs={{0,8},{8,0},{16,24},{24,16},{1,9},{9,1},{17,25},{25,17},{2,10},{10... | collective-permute-start | bytes 565256 | tf_op jit(solution)/shard_map/ppermute | solution.py:224
  252.5 11.0 %collective-permute-start.27 = (f32[184,256]{1,0:T(8,128)S(1)}, f32[184,256]{1,0:T(8,128)S(1)}, u32[]{:S(2)}, u32[]{:S(2)}) collective-permute-start(f32[184,256]{1,0:T(8,128)S(1)} %fusion.131), channel_id=1, source_target_pairs={{0,16},{8,24},{16,0},{24,8},{1,17},{9,25},{17,1},{25,9},{2,18},{10... | collective-permute-start | bytes 565256 | tf_op jit(solution)/shard_map/ppermute | solution.py:224
  253.4 11.6 %collective-permute-start.28 = (f32[184,256]{1,0:T(8,128)S(1)}, f32[184,256]{1,0:T(8,128)S(1)}, u32[]{:S(2)}, u32[]{:S(2)}) collective-permute-start(f32[184,256]{1,0:T(8,128)S(1)} %fusion.131), channel_id=1, source_target_pairs={{0,24},{8,16},{16,8},{24,0},{1,25},{9,17},{17,9},{25,1},{2,26},{10... | collective-permute-start | bytes 565256 | tf_op jit(solution)/shard_map/ppermute | solution.py:224
  255.4 9.9 %collective-permute-start.37 = (bf16[4,512,32]{1,2,0:T(8,128)(2,1)S(1)}, bf16[4,512,32]{1,2,0:T(8,128)(2,1)S(1)}, u32[]{:S(2)}, u32[]{:S(2)}) collective-permute-start(bf16[4,512,32]{1,2,0:T(8,128)(2,1)S(1)} %get-tuple-element.86), channel_id=1, source_target_pairs={{0,8},{8,0},{16,24},{24,16},{1,9},{9,1},{17,25},{25,17},{2,10},{10... | collective-permute-start | bytes 393224 | tf_op jit(solution)/shard_map/ppermute | solution.py:224
  258.2 7.2 %collective-permute-start.38 = (bf16[4,512,32]{1,2,0:T(8,128)(2,1)S(1)}, bf16[4,512,32]{1,2,0:T(8,128)(2,1)S(1)}, u32[]{:S(2)}, u32[]{:S(2)}) collective-permute-start(bf16[4,512,32]{1,2,0:T(8,128)(2,1)S(1)} %get-tuple-element.88), channel_id=1, source_target_pairs={{0,16},{8,24},{16,0},{24,8},{1,17},{9,25},{17,1},{25,9},{2,18},{10... | collective-permute-start | bytes 393224 | tf_op jit(solution)/shard_map/ppermute | solution.py:224
  263.5 5.9 %collective-permute-start.39 = (bf16[4,512,32]{1,2,0:T(8,128)(2,1)S(1)}, bf16[4,512,32]{1,2,0:T(8,128)(2,1)S(1)}, u32[]{:S(2)}, u32[]{:S(2)}) collective-permute-start(bf16[4,512,32]{1,2,0:T(8,128)(2,1)S(1)} %get-tuple-element.87), channel_id=1, source_target_pairs={{0,24},{8,16},{16,8},{24,0},{1,25},{9,17},{17,9},{25,1},{2,26},{10... | collective-permute-start | bytes 393224 | tf_op jit(solution)/shard_map/ppermute | solution.py:224
  265.3 20.5 %collective-permute-start.29 = (f32[4,184,256]{2,1,0:T(8,128)S(1)}, f32[4,184,256]{2,1,0:T(8,128)S(1)}, u32[]{:S(2)}, u32[]{:S(2)}) collective-permute-start(f32[4,184,256]{2,1,0:T(8,128)S(1)} %get-tuple-element.73), channel_id=1, source_target_pairs={{0,1},{1,0},{2,3},{3,2},{4,5},{5,4},{6,7},{7,6},{8,9},{9,8},{10,11... | collective-permute-start | bytes 2261000 | tf_op jit(solution)/shard_map/ppermute | solution.py:224
  269.5 5.2 %collective-permute-start.40 = (bf16[512,32]{0,1:T(8,128)(2,1)S(1)}, bf16[512,32]{0,1:T(8,128)(2,1)S(1)}, u32[]{:S(2)}, u32[]{:S(2)}) collective-permute-start(bf16[512,32]{0,1:T(8,128)(2,1)S(1)} %get-tuple-element.112), channel_id=1, source_target_pairs={{0,2},{1,3},{2,0},{3,1},{4,6},{5,7},{6,4},{7,5},{8,10},{9,11},{10,... | collective-permute-start | bytes 98312 | tf_op jit(solution)/shard_map/ppermute | solution.py:224
  271.8 4.8 %collective-permute-start.41 = (bf16[512,32]{0,1:T(8,128)(2,1)S(1)}, bf16[512,32]{0,1:T(8,128)(2,1)S(1)}, u32[]{:S(2)}, u32[]{:S(2)}) collective-permute-start(bf16[512,32]{0,1:T(8,128)(2,1)S(1)} %get-tuple-element.111), channel_id=1, source_target_pairs={{0,4},{1,5},{2,6},{3,7},{4,0},{5,1},{6,2},{7,3},{8,12},{9,13},{10,... | collective-permute-start | bytes 98312 | tf_op jit(solution)/shard_map/ppermute | solution.py:224
  272.4 5.8 %collective-permute-start.42 = (bf16[512,32]{0,1:T(8,128)(2,1)S(1)}, bf16[512,32]{0,1:T(8,128)(2,1)S(1)}, u32[]{:S(2)}, u32[]{:S(2)}) collective-permute-start(bf16[512,32]{0,1:T(8,128)(2,1)S(1)} %get-tuple-element.110), channel_id=1, source_target_pairs={{0,6},{1,7},{2,4},{3,5},{4,2},{5,3},{6,0},{7,1},{8,14},{9,15},{10,... | collective-permute-start | bytes 98312 | tf_op jit(solution)/shard_map/ppermute | solution.py:224
  274.6 6.9 %collective-permute-start.16 = (bf16[1024,128]{1,0:T(8,128)(2,1)S(1)}, bf16[1024,128]{1,0:T(8,128)(2,1)S(1)}, u32[]{:S(2)}, u32[]{:S(2)}) collective-permute-start(bf16[1024,128]{1,0:T(8,128)(2,1)S(1)} %get-tuple-element.66), channel_id=1, source_target_pairs={{0,8},{8,0},{16,24},{24,16},{1,9},{9,1},{17,25},{25,17},{2,10},{10... | collective-permute-start | bytes 786440 | tf_op jit(solution)/shard_map/ppermute | solution.py:224
  274.7 10.2 %collective-permute-start.17 = (bf16[1024,128]{1,0:T(8,128)(2,1)S(1)}, bf16[1024,128]{1,0:T(8,128)(2,1)S(1)}, u32[]{:S(2)}, u32[]{:S(2)}) collective-permute-start(bf16[1024,128]{1,0:T(8,128)(2,1)S(1)} %get-tuple-element.68), channel_id=1, source_target_pairs={{0,16},{8,24},{16,0},{24,8},{1,17},{9,25},{17,1},{25,9},{2,18},{10... | collective-permute-start | bytes 786440 | tf_op jit(solution)/shard_map/ppermute | solution.py:224
  276.6 8.2 %collective-permute-start.18 = (bf16[1024,128]{1,0:T(8,128)(2,1)S(1)}, bf16[1024,128]{1,0:T(8,128)(2,1)S(1)}, u32[]{:S(2)}, u32[]{:S(2)}) collective-permute-start(bf16[1024,128]{1,0:T(8,128)(2,1)S(1)} %get-tuple-element.67), channel_id=1, source_target_pairs={{0,24},{8,16},{16,8},{24,0},{1,25},{9,17},{17,9},{25,1},{2,26},{10... | collective-permute-start | bytes 786440 | tf_op jit(solution)/shard_map/ppermute | solution.py:224
  (64 other events, 273.0 us)

commit v2 on v1

v2 whole, which is shorter than its diff:
```python
import functools

import jax
import jax.numpy as jnp
from jax import lax
from jax.experimental import pallas as pl
from jax.experimental.pallas import tpu as pltpu
from jax.sharding import PartitionSpec as P

epsilon = 1e-05
LANES = 128
SUBS = 8
FAR = 1e36
LEAST_RATE = 1e-33
LN2 = 0.6931471805599453
EDGE = 16
bf16, f32 = jnp.bfloat16, jnp.float32


def nt(a, b):
    return lax.dot_general(a, b, (((1,), (1,)), ((), ())), preferred_element_type=f32)


def tn(a, b):
    return lax.dot_general(a, b, (((0,), (0,)), ((), ())), preferred_element_type=f32)


def nn(a, b):
    return jnp.dot(a, b, preferred_element_type=f32)


def softplus(v):
    return jnp.maximum(v, 0.0) + jnp.log1p(jnp.exp(-jnp.abs(v)))


def tile_at(start):
    return pl.ds(pl.multiple_of(start, LANES), LANES)


def step_rows(t):
    return pl.ds(pl.multiple_of(t * SUBS, SUBS), SUBS)


def tap_masks(info_ref, docs, taps, length):
    row = lax.broadcasted_iota(jnp.int32, (length, LANES), 0)
    place = info_ref[0] + (row % SUBS) * (length // SUBS) + row // SUBS
    begin = jnp.zeros_like(place)
    reset = jnp.zeros((length, LANES), f32)
    for k in range(docs):
        start = info_ref[1 + k]
        begin = jnp.maximum(begin, jnp.where(place >= start, start, 0))
        reset = jnp.where(place == start, 1.0, reset)
    return [reset] + [jnp.where(begin <= place - j, 1.0, 0.0) for j in range(1, taps)]


def spread_maps(maps_ref, table_ref, steps, first, width):
    def lap(t, _):
        v = maps_ref[step_rows(t), :]
        for n in range(width):
            table_ref[t, n] = jnp.broadcast_to(v[:, first + n : first + n + 1], (SUBS, LANES))
        return 0

    lax.fori_loop(0, steps, lap, 0)


def sub_scan(decay, value, forward):
    row = lax.broadcasted_iota(jnp.int32, decay.shape, 0)
    if not forward:
        row = SUBS - 1 - row

    def moved(x, by, fill):
        return jnp.where(row < by, fill, pltpu.roll(x, by if forward else SUBS - by, 0))

    by = 1
    while by < SUBS:
        d, v = moved(decay, by, 1.0), moved(value, by, 0.0)
        value = decay * v + value
        decay = decay * d
        by *= 2
    return value, moved(decay, 1, 1.0), moved(value, 1, 0.0)


def conv_windows(ext, taps, length):
    return [ext[(taps - 1 - j) * SUBS : (taps - 1 - j) * SUBS + length] for j in range(taps)]


def conv_sum(windows, masks, vec_ref, at, taps):
    out = vec_ref[pl.ds(taps, 1), at] + vec_ref[pl.ds(taps - 1, 1), at] * windows[0]
    for j in range(1, taps):
        out = out + vec_ref[pl.ds(taps - 1 - j, 1), at] * windows[j] * masks[j]
    return out


def front_kernel(
    states, rank, taps, docs, lap1, lap2,
    info_ref, tok_ref, cot_ref, gain_ref, vec_ref, rates_ref, dtw_ref, wc_ref, wg_ref, wo_ref, wx_ref,
    ext_ref, inner_ref, gate_ref, ggated_ref, proj_ref, pack_ref, dx_ref, ex_ref, db_ref, fx_ref,
    normed, masks, inner_s, gs_s, table, dtm_s, u_s, ends,
):
    i = pl.program_id(0)
    length = cot_ref.shape[0]
    steps = length // SUBS
    rim = taps - 1
    block1, block2 = wc_ref.shape[1], pack_ref.shape[1]

    @pl.when(i == 0)
    def _():
        x = tok_ref[...].astype(f32)
        inv = lax.rsqrt(jnp.mean(x * x, axis=-1, keepdims=True) + epsilon)
        normed[...] = (x * inv * gain_ref[...]).astype(bf16)
        for k, mask in enumerate(tap_masks(info_ref, docs, taps, length)):
            masks[k] = mask
        proj_ref[...] = jnp.zeros_like(proj_ref)

    @pl.when(i < lap1)
    def _():
        own = normed[pl.ds(0, length), :]
        conv = nn(normed[...], wc_ref[...]).astype(bf16)
        gate = nn(own, wg_ref[...])
        ggated = nt(cot_ref[...], wo_ref[...])
        gate_ref[...] = gate
        ggated_ref[...] = ggated
        gs_s[:, pl.ds(pl.multiple_of(i * block1, LANES), block1)] = ggated * gate * jax.nn.sigmoid(gate)
        row = lax.broadcasted_iota(jnp.int32, (SUBS, LANES), 0)
        mask = [masks[k] for k in range(taps)]
        for tile in range(block1 // LANES):
            near = pl.ds(tile * LANES, LANES)
            far = tile_at(i * block1 + tile * LANES)
            part = conv[:, tile * LANES : (tile + 1) * LANES].astype(f32)
            pieces = []
            for b in range(rim):
                first = length - (rim - b) * SUBS
                moved = pltpu.roll(part[first : first + SUBS], 1, 0)
                pieces.append(jnp.where(row == 0, part[length + b : length + b + 1], moved))
            ext = jnp.concatenate(pieces + [part[:length]], axis=0)
            ext_ref[:, near] = jnp.concatenate(
                [jnp.zeros((2 * EDGE - rim * SUBS, LANES), f32), ext], axis=0
            ).astype(bf16)
            pre = conv_sum(conv_windows(ext, taps, length), mask, vec_ref, far, taps)
            act = (pre * jax.nn.sigmoid(pre)).astype(bf16)
            inner_ref[:, near] = act
            inner_s[:, far] = act.astype(f32)
        width = rank + 2 * states
        proj_ref[:, :width] += nn(inner_ref[...], wx_ref[...])

    @pl.when(i == lap1)
    def _():
        spread_maps(proj_ref, table, steps, rank, 2 * states)

    @pl.when(i >= lap1)
    def _():
        j = i - lap1
        wide = pl.ds(pl.multiple_of(j * block2, LANES), block2)
        low = proj_ref[:, :rank].astype(bf16)
        dt = softplus(nn(low, dtw_ref[:, wide]) + vec_ref[pl.ds(taps + 1, 1), wide])
        u_s[...] = dt * inner_s[:, wide]
        for tile in range(block2 // LANES):
            near = pl.ds(tile * LANES, LANES)
            dtm = jnp.where(masks[0] > 0.0, FAR, dt[:, tile * LANES : (tile + 1) * LANES])
            dtm_s[:, near] = dtm
            span = jnp.sum(dtm, axis=0, keepdims=True)
            high = span.astype(bf16).astype(f32)
            middle = (span - high).astype(bf16).astype(f32)
            ends[pl.ds(2 * states, 1), near] = high
            ends[pl.ds(2 * states + 1, 1), near] = middle
            ends[pl.ds(2 * states + 2, 1), near] = span - high - middle
        half = states // 2
        zero = jnp.zeros((SUBS, LANES), f32)
        one = jnp.ones((SUBS, LANES), f32)
        for tile in range(block2 // LANES):
            near = pl.ds(tile * LANES, LANES)
            far = tile_at(j * block2 + tile * LANES)
            for first in range(0, states, half):
                rates = [jnp.broadcast_to(rates_ref[pl.ds(first + k, 1), far], (SUBS, LANES)) for k in range(half)]

                def lap(t, carry):
                    h, f, p = carry
                    rows = step_rows(t)
                    d, u, g = dtm_s[rows, near], u_s[rows, near], gs_s[rows, far]
                    hn, fn, pn = [], [], []
                    for k in range(half):
                        a = jnp.exp2(d * rates[k])
                        hn.append(a * h[k] + u * table[t, first + k])
                        q = p[k] * a
                        pn.append(q)
                        fn.append(f[k] + q * (g * table[t, states + first + k]))
                    return tuple(hn), tuple(fn), tuple(pn)

                h, f, p = lax.fori_loop(
                    0, steps, lap, ((zero,) * half, (zero,) * half, (one,) * half), unroll=4
                )
                for k in range(half):
                    n = first + k
                    e_in, d_ex, e_ex = sub_scan(p[k], h[k], True)
                    f_in, b_ex, f_ex = sub_scan(p[k], f[k], False)
                    ends[pl.ds(n, 1), near] = e_in[SUBS - 1 :, :]
                    ends[pl.ds(states + n, 1), near] = f_in[:1, :]
                    dx_ref[n, :, near] = d_ex
                    ex_ref[n, :, near] = e_ex
                    db_ref[n, :, near] = b_ex
                    fx_ref[n, :, near] = f_ex
        pack_ref[...] = ends[...].astype(bf16)


def front(info, tok, cot, gain, vec, rates, dtw, in_weight, out_weight, xproj, taps, docs):
    length, model = cot.shape
    states, width = rates.shape
    rank = dtw.shape[0]
    block1, block2 = min(256, width), min(512, width)
    lap1, lap2 = width // block1, width // block2
    first = lambda i: jnp.minimum(i, lap1 - 1)
    second = lambda i: jnp.maximum(i - lap1, 0)
    full = lambda x: pl.BlockSpec(x.shape, lambda i: (0,) * x.ndim)
    wide1 = pl.BlockSpec((length, block1), lambda i: (0, first(i)))
    deep = pl.BlockSpec((states, SUBS, block2), lambda i: (0, 0, second(i)))
    pack_rows = 2 * states + EDGE
    big = lambda dtype: jax.ShapeDtypeStruct((length, width), dtype)
    return pl.pallas_call(
        functools.partial(front_kernel, states, rank, taps, docs, lap1, lap2),
        grid=(lap1 + lap2,),
        in_specs=[pl.BlockSpec(memory_space=pltpu.SMEM), full(tok), full(cot), full(gain), full(vec), full(rates), full(dtw)]
        + [
            pl.BlockSpec((model, block1), lambda i: (0, first(i))),
            pl.BlockSpec((model, block1), lambda i: (0, lap1 + first(i))),
            pl.BlockSpec((block1, model), lambda i: (first(i), 0)),
            pl.BlockSpec((block1, xproj.shape[1]), lambda i: (first(i), 0)),
        ],
        out_specs=[
            pl.BlockSpec((2 * EDGE + length, block1), lambda i: (0, first(i))),
            wide1, wide1, wide1,
            pl.BlockSpec((length, LANES), lambda i: (0, 0)),
            pl.BlockSpec((pack_rows, block2), lambda i: (0, second(i))),
            deep, deep, deep, deep,
        ],
        out_shape=[
            jax.ShapeDtypeStruct((2 * EDGE + length, width), bf16),
            big(bf16), big(f32), big(f32),
            jax.ShapeDtypeStruct((length, LANES), f32),
            jax.ShapeDtypeStruct((pack_rows, width), bf16),
        ] + [jax.ShapeDtypeStruct((states, SUBS, width), f32)] * 4,
        scratch_shapes=[
            pltpu.VMEM(tok.shape, bf16),
            pltpu.VMEM((taps, length, LANES), f32),
            pltpu.VMEM((length, width), f32),
            pltpu.VMEM((length, width), f32),
            pltpu.VMEM((length // SUBS, 2 * states, SUBS, LANES), f32),
            pltpu.VMEM((length, block2), f32),
            pltpu.VMEM((length, block2), f32),
            pltpu.VMEM((pack_rows, block2), f32),
        ],
        compiler_params=pltpu.CompilerParams(vmem_limit_bytes=48 << 20),
        cost_estimate=pl.CostEstimate(flops=0, bytes_accessed=72000000, transcendentals=0),
        name="front",
    )(info, tok, cot, gain, vec, rates, dtw, in_weight, in_weight, out_weight, xproj)


def chip_spot(tile, chips, tiles):
    if chips == 1:
        return 0, tile
    half, chip, core = tile // (2 * chips), (tile // 2) % chips, tile % 2
    return chip, core * (tiles // (2 * chips)) + half


def forward_kernel(
    states, rank, taps, docs, chips, laps,
    info_ref, proj_ref, dtw_ref, vec_ref, rates_ref, entry_ref, inner_ref, gate_ref, ggated_ref, dx_ref, ex_ref,
    gated_ref, ggate_ref, *rest,
):
    blocks, (table, masks, dtm_s, u_s, y_s, held) = rest[: chips], rest[chips:]
    length = inner_ref.shape[0]
    tiles = laps * inner_ref.shape[1] // LANES
    steps = length // SUBS
    zero = jnp.zeros((SUBS, LANES), f32)

    @pl.when(pl.program_id(0) == 0)
    def _():
        spread_maps(proj_ref, table, steps, rank, 2 * states)
        masks[0] = tap_masks(info_ref, docs, 1, length)[0]

    low = proj_ref[:, :rank].astype(bf16)
    dt_all = softplus(nn(low, dtw_ref[...]) + vec_ref[pl.ds(taps + 1, 1), :])
    for tile in range(inner_ref.shape[1] // LANES):
        at = pl.ds(tile * LANES, LANES)
        dt = dt_all[:, tile * LANES : (tile + 1) * LANES]
        x = inner_ref[:, at].astype(f32)
        dtm_s[...] = jnp.where(masks[0] > 0.0, FAR, dt)
        u_s[...] = dt * x

        def wide(ref, n):
            return jnp.broadcast_to(ref[pl.ds(n, 1), at], (SUBS, LANES))

        rates = [wide(rates_ref, n) for n in range(states)]
        start = tuple(dx_ref[n, :, at] * wide(entry_ref, n) + ex_ref[n, :, at] for n in range(states))

        def lap(t, h):
            rows = step_rows(t)
            d, u = dtm_s[rows, :], u_s[rows, :]
            new, y = [], [zero, zero]
            for n in range(states):
                now = jnp.exp2(d * rates[n]) * h[n] + u * table[t, n]
                y[n % 2] = y[n % 2] + now * table[t, states + n]
                new.append(now)
            y_s[rows, :] = y[0] + y[1]
            return tuple(new)

        lax.fori_loop(0, steps, lap, start, unroll=4)
        scanned = y_s[...] + vec_ref[pl.ds(taps + 2, 1), at] * x
        gate = gate_ref[:, at]
        sig = jax.nn.sigmoid(gate)
        gated_ref[:, at] = (scanned * gate * sig).astype(bf16)
        ggate = (ggated_ref[:, at] * scanned * (sig * (1.0 + gate * (1.0 - sig)))).astype(bf16)
        ggate_ref[:, at] = ggate
        chip, spot = chip_spot(pl.program_id(0) * (inner_ref.shape[1] // LANES) + tile, chips, tiles)
        held[chip, :, tile_at(spot * LANES)] = ggate

    @pl.when(pl.program_id(0) == laps - 1)
    def _():
        for n in range(chips):
            blocks[n][...] = held[info_ref[1 + docs] ^ n] if chips > 1 else held[0]


def forward(info, proj, dtw, vec, rates, entry, inner, gate, ggated, dx, ex, taps, docs, chips):
    length, width = inner.shape
    states = rates.shape[0]
    rank = dtw.shape[0]
    block = min(512, width)
    wide = pl.BlockSpec((length, block), lambda i: (0, i))
    deep = pl.BlockSpec((states, SUBS, block), lambda i: (0, 0, i))
    thin = lambda x: pl.BlockSpec((x.shape[0], block), lambda i: (0, i))
    return pl.pallas_call(
        functools.partial(forward_kernel, states, rank, taps, docs, chips, width // block),
        grid=(width // block,),
        in_specs=[pl.BlockSpec(memory_space=pltpu.SMEM), pl.BlockSpec(proj.shape, lambda i: (0, 0))]
        + [thin(dtw), thin(vec), thin(rates), thin(entry), wide, wide, wide, deep, deep],
        out_specs=[wide, wide] + [pl.BlockSpec((length, width // chips), lambda i: (0, 0))] * chips,
        out_shape=[jax.ShapeDtypeStruct((length, width), bf16)] * 2
        + [jax.ShapeDtypeStruct((length, width // chips), bf16)] * chips,
        scratch_shapes=[
            pltpu.VMEM((length // SUBS, 2 * states, SUBS, LANES), f32),
            pltpu.VMEM((1, length, LANES), f32),
        ] + [pltpu.VMEM((length, LANES), f32)] * 3 + [pltpu.VMEM((chips, length, width // chips), bf16)],
        compiler_params=pltpu.CompilerParams(vmem_limit_bytes=48 << 20),
        cost_estimate=pl.CostEstimate(flops=0, bytes_accessed=32400000, transcendentals=0),
        name="forward",
    )(info, proj, dtw, vec, rates, entry, inner, gate, ggated, dx, ex)


def backward_kernel(
    states, rank, taps, docs, laps, chips,
    info_ref, proj_ref, tok_ref, gain_ref, dtw_ref, vec_ref, rates_ref, entry_ref, arrive_ref,
    inner_ref, gate_ref, ggated_ref, dx_ref, ex_ref, db_ref, fx_ref, gated_ref, ggate_ref, wo_ref, wg_ref,
    ext_ref, wc_ref, wx_ref,
    mine_ref, theirs_ref, ngrad_ref, mixed_ref, *rest,
):
    blocks = rest[:chips]
    (table, acc, hs, decays, masks, dtm_s, dt_s, u_s, gs_s, s1_s, s2_s,
    isg, inner_s, raw_s, sent_s, low_acc, pg, mixed_acc, ngrad, small, held) = rest[chips:]
    i = pl.program_id(0)
    length, block = inner_ref.shape
    model = tok_ref.shape[1]
    steps = length // SUBS
    rim = taps - 1
    maps = rank + 2 * states
    row_dtw = maps
    row_rate = row_dtw + rank
    row_taps = row_rate + states
    row_dtb, row_skip, row_cb, row_gain = (row_taps + taps + k for k in range(4))
    zero = jnp.zeros((SUBS, LANES), f32)
    half = states // 2

    @pl.when(i == 0)
    def _():
        spread_maps(proj_ref, table, steps, rank, 2 * states)
        for k, mask in enumerate(tap_masks(info_ref, docs, taps, length)):
            masks[k] = mask
        acc[...] = jnp.zeros_like(acc)
        low_acc[...] = jnp.zeros_like(low_acc)
        mixed_acc[...] = jnp.zeros_like(mixed_acc)
        ngrad[...] = jnp.zeros_like(ngrad)
        small[pl.ds(small.shape[0] - EDGE, EDGE), :] = jnp.zeros((EDGE, small.shape[1]), f32)

    @pl.when(i < laps)
    def _():
        mixed_acc[...] += nn(gated_ref[...], wo_ref[...])
        ngrad[pl.ds(0, length), :] += nt(ggate_ref[...], wg_ref[...])
        wide_far = pl.ds(pl.multiple_of(i * block, LANES), block)
        low = proj_ref[:, :rank].astype(bf16)
        raw_all = nn(low, dtw_ref[...]) + vec_ref[pl.ds(taps + 1, 1), wide_far]
        for tile in range(block // LANES):
            at = pl.ds(tile * LANES, LANES)
            far = tile_at(i * block + tile * LANES)
            raw = raw_all[:, tile * LANES : (tile + 1) * LANES]
            dt = softplus(raw)
            x = inner_ref[:, at].astype(f32)
            inner_s[:, far] = inner_ref[:, at]
            gate = gate_ref[:, at]
            gs = ggated_ref[:, at] * gate * jax.nn.sigmoid(gate)
            dtm_s[...] = jnp.where(masks[0] > 0.0, FAR, dt)
            dt_s[...] = dt
            u_s[...] = dt * x
            gs_s[...] = gs

            def wide(ref, n):
                return jnp.broadcast_to(ref[pl.ds(n, 1), at], (SUBS, LANES))

            rates = [wide(rates_ref, n) for n in range(states)]
            start = []
            for n in range(states):
                h0 = dx_ref[n, :, at] * wide(entry_ref, n) + ex_ref[n, :, at]
                hs[0, n] = h0
                start.append(h0)

            def lap(t, h):
                rows = step_rows(t)
                d, u = dtm_s[rows, :], u_s[rows, :]
                new = []
                for n in range(states):
                    a = jnp.exp2(d * rates[n])
                    decays[t, n] = a
                    now = a * h[n] + u * table[t, n]
                    hs[t + 1, n] = now
                    new.append(now)
                return tuple(new)

            lax.fori_loop(0, steps, lap, tuple(start), unroll=4)
            for first in range(0, states, half):
                some = rates[first : first + half]

                def back(k, carry):
                    f, r = carry
                    t = steps - 1 - k
                    rows = step_rows(t)
                    dtt, g, u = dt_s[rows, :], gs_s[rows, :], u_s[rows, :]
                    fn, rn, s1, s2 = [], [], zero, zero
                    for k in range(half):
                        n = first + k
                        adj = g * table[t, states + n] + f[k]
                        acc[t, n] += adj * u
                        acc[t, states + n] += g * hs[t + 1, n]
                        s1 = s1 + adj * table[t, n]
                        flow = decays[t, n] * adj
                        fn.append(flow)
                        flow = flow * hs[t, n]
                        s2 = s2 + flow * some[k]
                        rn.append(r[k] + flow * dtt)
                    if first == 0:
                        s1_s[rows, :] = s1
                        s2_s[rows, :] = s2
                    else:
                        s1_s[rows, :] += s1
                        s2_s[rows, :] += s2
                    return tuple(fn), tuple(rn)

                f0 = tuple(
                    db_ref[first + k, :, at] * wide(arrive_ref, first + k) + fx_ref[first + k, :, at]
                    for k in range(half)
                )
                _, r = lax.fori_loop(0, steps, back, (f0, (zero,) * half), unroll=4)
                for k in range(half):
                    small[pl.ds(row_rate + first + k, 1), far] = jnp.sum(r[k], axis=0, keepdims=True)
            s1 = s1_s[...]
            step_grad = s1 * x + LN2 * s2_s[...]
            isg[:, far] = s1 * dt + gs * vec_ref[pl.ds(taps + 2, 1), far]
            raw_grad = step_grad * jax.nn.sigmoid(raw)
            raw_s[:, at] = raw_grad.astype(bf16)
            small[pl.ds(row_dtb, 1), far] = jnp.sum(raw_grad, axis=0, keepdims=True)
            small[pl.ds(row_skip, 1), far] = jnp.sum(gs * x, axis=0, keepdims=True)
        small[pl.ds(row_dtw, rank), wide_far] = tn(low, raw_s[...])
        low_acc[:, :rank] += nt(raw_s[...], dtw_ref[...])

    @pl.when(i == laps - 1)
    def _():
        lane = lax.broadcasted_iota(jnp.int32, (SUBS, LANES), 1)

        def lap(t, _):
            out = low_acc[step_rows(t), :]
            for n in range(2 * states):
                out = jnp.where(lane == rank + n, jnp.sum(acc[t, n], axis=1, keepdims=True), out)
            low_acc[step_rows(t), :] = out
            return 0

        lax.fori_loop(0, steps, lap, 0)
        pg[...] = low_acc[...].astype(bf16)

    @pl.when(i >= laps)
    def _():
        j = i - laps
        wide_far = pl.ds(pl.multiple_of(j * block, LANES), block)
        small[pl.ds(0, maps), wide_far] = tn(pg[...], inner_s[:, wide_far])[:maps]
        inner_grad = isg[:, wide_far] + nt(pg[:, :maps], wx_ref[...])
        mask = [masks[k] for k in range(taps)]
        row = lax.broadcasted_iota(jnp.int32, (SUBS, LANES), 0)
        for tile in range(block // LANES):
            at = pl.ds(tile * LANES, LANES)
            far = tile_at(j * block + tile * LANES)
            ext = ext_ref[:, at].astype(f32)[2 * EDGE - rim * SUBS :]
            windows = conv_windows(ext, taps, length)
            pre = conv_sum(windows, mask, vec_ref, far, taps)
            sig = jax.nn.sigmoid(pre)
            grad = inner_grad[:, tile * LANES : (tile + 1) * LANES] * (sig * (1.0 + pre * (1.0 - sig)))
            small[pl.ds(row_cb, 1), far] = jnp.sum(grad, axis=0, keepdims=True)
            small[pl.ds(row_taps + rim, 1), far] = jnp.sum(grad * windows[0], axis=0, keepdims=True)
            near = [grad[step * SUBS : (step + 1) * SUBS] * vec_ref[pl.ds(rim, 1), far] for step in range(steps)]
            head = [zero] * rim
            for k in range(1, taps):
                masked = grad * mask[k]
                small[pl.ds(row_taps + rim - k, 1), far] = jnp.sum(masked * windows[k], axis=0, keepdims=True)
                masked = masked * vec_ref[pl.ds(rim - k, 1), far]
                for step in range(steps):
                    piece = masked[step * SUBS : (step + 1) * SUBS]
                    if step >= k:
                        near[step - k] = near[step - k] + piece
                    else:
                        head[rim + step - k] = head[rim + step - k] + piece
            edge = zero
            for b in range(rim):
                moved = jnp.where(row == SUBS - 1, 0.0, pltpu.roll(head[b], SUBS - 1, 0))
                near[steps - rim + b] = near[steps - rim + b] + moved
                edge = jnp.where(row == b, jnp.broadcast_to(head[b][:1], (SUBS, LANES)), edge)
            sent = jnp.concatenate(near + [edge] + [zero] * (EDGE // SUBS - 1), axis=0).astype(bf16)
            sent_s[:, at] = sent
            chip, spot = chip_spot(j * (block // LANES) + tile, chips, laps * block // LANES)
            held[chip, :, tile_at(spot * LANES)] = sent
        ngrad[...] += nt(sent_s[...], wc_ref[...])

    @pl.when(i == 2 * laps - 1)
    def _():
        x = tok_ref[...].astype(f32)
        inv = lax.rsqrt(jnp.mean(x * x, axis=-1, keepdims=True) + epsilon)
        grad = ngrad[...]
        ngrad_ref[...] = grad
        small[pl.ds(row_gain, 1), pl.ds(0, model)] = jnp.sum(grad * x * inv, axis=0, keepdims=True)
        for n in range(chips):
            blocks[n][...] = held[info_ref[1 + docs] ^ n] if chips > 1 else held[0]
        count, chunk = mine_ref.shape[0], mine_ref.shape[2]
        for c in range(2):
            @pl.when(info_ref[2 + docs] == c)
            def _():
                for n in range(count):
                    at, other = (c * count + n) * chunk, ((1 - c) * count + n) * chunk
                    mine_ref[n] = small[:, at : at + chunk]
                    theirs_ref[n] = small[:, other : other + chunk].astype(bf16)
        mixed_ref[...] = turned((x[:length] + mixed_acc[...]).astype(bf16), True)


def turned(x, plain):
    length = x.shape[0]
    steps = length // SUBS
    a = lax.broadcasted_iota(jnp.int32, (length, length), 1 - plain)
    b = lax.broadcasted_iota(jnp.int32, (length, length), plain + 0)
    turn = jnp.where(b == (a % steps) * SUBS + a // steps, 1.0, 0.0).astype(bf16)
    return nn(turn, x).astype(bf16)


def backward(info, proj, tok, gain, dtw, vec, rates, entry, arrive, inner, gate, ggated, deep4, gated, ggate,
             in_weight, out_weight, ext, xproj, taps, docs, chips, chunks):
    length, width = inner.shape
    model = tok.shape[1]
    states = rates.shape[0]
    rank = dtw.shape[0]
    block = min(512, width)
    laps = width // block
    steps = length // SUBS
    first = lambda i: jnp.minimum(i, laps - 1)
    second = lambda i: jnp.maximum(i - laps, 0)
    full = lambda x: pl.BlockSpec(x.shape, lambda i: (0,) * x.ndim)
    wide = pl.BlockSpec((length, block), lambda i: (0, first(i)))
    deep = pl.BlockSpec((states, SUBS, block), lambda i: (0, 0, first(i)))
    thin = lambda x: pl.BlockSpec((x.shape[0], block), lambda i: (0, first(i)))
    rows = 2 * rank + 3 * states + taps + 4
    rows = -(-rows // EDGE) * EDGE
    return pl.pallas_call(
        functools.partial(backward_kernel, states, rank, taps, docs, laps, chips),
        grid=(2 * laps,),
        in_specs=[pl.BlockSpec(memory_space=pltpu.SMEM), full(proj), full(tok), full(gain), thin(dtw), full(vec)]
        + [thin(rates), thin(entry), thin(arrive), wide, wide, wide, deep, deep, deep, deep, wide, wide]
        + [
            pl.BlockSpec((block, model), lambda i: (first(i), 0)),
            pl.BlockSpec((model, block), lambda i: (0, laps + first(i))),
            pl.BlockSpec((ext.shape[0], block), lambda i: (0, second(i))),
            pl.BlockSpec((model, block), lambda i: (0, second(i))),
            pl.BlockSpec((block, xproj.shape[1]), lambda i: (second(i), 0)),
        ],
        out_specs=[
            pl.BlockSpec((chunks, rows, width // (2 * chunks)), lambda i: (0, 0, 0)),
            pl.BlockSpec((chunks, rows, width // (2 * chunks)), lambda i: (0, 0, 0)),
            pl.BlockSpec((length + EDGE, model), lambda i: (0, 0)),
            pl.BlockSpec((length, model), lambda i: (0, 0)),
        ] + [pl.BlockSpec((length + EDGE, width // chips), lambda i: (0, 0))] * chips,
        out_shape=[
            jax.ShapeDtypeStruct((chunks, rows, width // (2 * chunks)), f32),
            jax.ShapeDtypeStruct((chunks, rows, width // (2 * chunks)), bf16),
            jax.ShapeDtypeStruct((length + EDGE, model), f32),
            jax.ShapeDtypeStruct((length, model), bf16),
        ] + [jax.ShapeDtypeStruct((length + EDGE, width // chips), bf16)] * chips,
        scratch_shapes=[
            pltpu.VMEM((steps, 2 * states, SUBS, LANES), f32),
            pltpu.VMEM((steps, 2 * states, SUBS, LANES), f32),
            pltpu.VMEM((steps + 1, states, SUBS, LANES), f32),
            pltpu.VMEM((steps, states, SUBS, LANES), f32),
            pltpu.VMEM((taps, length, LANES), f32),
        ] + [pltpu.VMEM((length, LANES), f32)] * 6
        + [
            pltpu.VMEM((length, width), f32),
            pltpu.VMEM((length, width), bf16),
            pltpu.VMEM((length, block), bf16),
            pltpu.VMEM((length + EDGE, block), bf16),
            pltpu.VMEM((length, LANES), f32),
            pltpu.VMEM((length, LANES), bf16),
            pltpu.VMEM((length, model), f32),
            pltpu.VMEM((length + EDGE, model), f32),
            pltpu.VMEM((rows, width), f32),
            pltpu.VMEM((chips, length + EDGE, width // chips), bf16),
        ],
        compiler_params=pltpu.CompilerParams(vmem_limit_bytes=56 << 20),
        cost_estimate=pl.CostEstimate(flops=0, bytes_accessed=100800000, transcendentals=0),
        name="backward",
    )(info, proj, tok, gain, dtw, vec, rates, entry, arrive, inner, gate, ggated, *deep4, gated, ggate,
      out_weight, in_weight, ext, in_weight, xproj)


def finish_kernel(rim, ngrad_ref, back_ref, tok_ref, cot_ref, gain_ref, out_ref):
    length = cot_ref.shape[0]
    x = tok_ref[pl.ds(0, length), :].astype(f32)
    inv = lax.rsqrt(jnp.mean(x * x, axis=-1, keepdims=True) + epsilon)
    scaled = x * inv
    row = lax.broadcasted_iota(jnp.int32, (SUBS, x.shape[1]), 0)
    pieces = [ngrad_ref[pl.ds(0, length - rim * SUBS), :]]
    for b in range(rim):
        late = jnp.where(row == SUBS - 1, back_ref[pl.ds(b, 1), :], 0.0)
        pieces.append(ngrad_ref[pl.ds(length - (rim - b) * SUBS, SUBS), :] + late)
    hat = jnp.concatenate(pieces, axis=0) * gain_ref[...]
    grad = cot_ref[...].astype(f32) + inv * (hat - scaled * jnp.mean(hat * scaled, axis=-1, keepdims=True))
    out_ref[...] = turned(grad.astype(bf16), True)


def finish(ngrad, back, tok, cot, gain, rim):
    return pl.pallas_call(
        functools.partial(finish_kernel, rim),
        out_shape=jax.ShapeDtypeStruct(cot.shape, bf16),
        compiler_params=pltpu.CompilerParams(vmem_limit_bytes=32 << 20),
        cost_estimate=pl.CostEstimate(flops=0, bytes_accessed=7200000, transcendentals=0),
        name="finish",
    )(ngrad, back, tok, cot, gain)


SMEM_SPEC = pl.BlockSpec(memory_space=pltpu.SMEM)


def plain_call(kernel, name, out_shape, args, us, scratch=()):
    full = lambda x: pl.BlockSpec(x.shape, lambda: (0,) * len(x.shape))
    return pl.pallas_call(
        kernel,
        in_specs=[SMEM_SPEC] + [full(x) for x in args[1:]],
        out_specs=[full(x) for x in out_shape],
        out_shape=out_shape,
        scratch_shapes=list(scratch),
        compiler_params=pltpu.CompilerParams(vmem_limit_bytes=40 << 20),
        cost_estimate=pl.CostEstimate(flops=0, bytes_accessed=int(us * 3.6e6), transcendentals=0),
        name=name,
    )(*args)


def prepare_kernel(rim, size, info_ref, tok_ref, left_ref, cot_ref, tok_out, cot_out, *parts):
    length = tok_ref.shape[0]
    tok_out[pl.ds(0, length), :] = turned(tok_ref[...], False)
    left = left_ref[...].astype(f32)
    tok_out[pl.ds(length, EDGE), :] = jnp.concatenate(
        [left, jnp.zeros((EDGE - rim, left.shape[1]), f32)], axis=0
    ).astype(bf16)
    cot = turned(cot_ref[...], False)
    cot_out[...] = cot
    thin = cot.shape[1] // size
    for q in range(size):
        for k in range(size):
            @pl.when((info_ref[0] ^ k) == q)
            def _():
                parts[k][...] = cot[:, q * thin : (q + 1) * thin]


def pair_kernel(states, info_ref, mine_ref, other_ref, rates_ref, out_ref):
    first = info_ref[0] == 0
    mine, other, rates = mine_ref[...].astype(f32), other_ref[...].astype(f32), rates_ref[...]
    near, far = jnp.where(first, mine, other), jnp.where(first, other, mine)

    def span(x):
        return x[2 * states : 2 * states + 1] + x[2 * states + 1 : 2 * states + 2] + x[2 * states + 2 : 2 * states + 3]

    d0, d1 = span(near), span(far)
    out_ref[pl.ds(0, states), :] = (jnp.exp2(rates * d1) * near[:states] + far[:states]).astype(bf16)
    flow = near[states : 2 * states] + jnp.exp2(rates * d0) * far[states : 2 * states]
    out_ref[pl.ds(states, states), :] = flow.astype(bf16)
    d = d0 + d1
    high = d.astype(bf16).astype(f32)
    middle = (d - high).astype(bf16).astype(f32)
    row = lax.broadcasted_iota(jnp.int32, (EDGE, d.shape[1]), 0)
    rest = jnp.where(row == 0, high, jnp.where(row == 1, middle, jnp.where(row == 2, d - high - middle, 0.0)))
    out_ref[pl.ds(2 * states, EDGE), :] = rest.astype(bf16)


def enter_kernel(states, count, info_ref, mine_ref, other_ref, rates_ref, *rest):
    chips, (entry_ref, arrive_ref, held) = rest[:count], rest[count:]
    core, place, turn = info_ref[0], info_ref[1], info_ref[2]
    rates = rates_ref[...]
    for k in range(count):
        held[(place & turn) ^ k] = chips[k][...].astype(f32)

    def split(x):
        span = x[2 * states : 2 * states + 1] + x[2 * states + 1 : 2 * states + 2] + x[2 * states + 2 : 2 * states + 3]
        return x[:states], x[states : 2 * states], jnp.exp2(rates * span)

    def lap(k, carry):
        entry, arrive = carry
        s, _, whole = split(held[k])
        entry = jnp.where(k < place, whole * entry + s, entry)
        back = count - 1 - k
        _, f, whole = split(held[back])
        arrive = jnp.where(back > place, whole * arrive + f, arrive)
        return entry, arrive

    entry, arrive = lax.fori_loop(0, count, lap, (jnp.zeros_like(rates), jnp.zeros_like(rates)))
    s, f, whole = split(other_ref[...].astype(f32))
    entry_ref[...] = jnp.where(core == 1, whole * entry + s, entry)
    arrive_ref[...] = jnp.where(core == 0, whole * arrive + f, arrive)


def enter(where, mine, other, rates, chips):
    states, width = rates.shape
    block = min(512, width)
    thin = lambda x: pl.BlockSpec((x.shape[0], block), lambda i: (0, i))
    return pl.pallas_call(
        functools.partial(enter_kernel, states, len(chips)),
        grid=(width // block,),
        in_specs=[SMEM_SPEC] + [thin(x) for x in (mine, other, rates, *chips)],
        out_specs=[thin(rates)] * 2,
        out_shape=[jax.ShapeDtypeStruct(rates.shape, f32)] * 2,
        scratch_shapes=[pltpu.VMEM((len(chips), mine.shape[0], block), f32)],
        compiler_params=pltpu.CompilerParams(vmem_limit_bytes=40 << 20),
        cost_estimate=pl.CostEstimate(flops=0, bytes_accessed=7000000, transcendentals=0),
        name="enter",
    )(where, mine, other, rates, *chips)


def split_cores(info_ref, x, mine_ref, theirs_ref):
    half = x.shape[1] // 2
    for c in range(2):
        @pl.when(info_ref[0] == c)
        def _():
            mine_ref[...] = x[:, c * half : (c + 1) * half]
            theirs_ref[...] = x[:, (1 - c) * half : (2 - c) * half].astype(bf16)


def gate_kernel(count, info_ref, gain_ref, *rest):
    toks, gots, (turned_ref, mine_ref, theirs_ref) = rest[:count], rest[count : 2 * count], rest[2 * count :]
    length = gots[0].shape[0]
    edges = []
    for k in range(count):
        x = toks[k][...].astype(f32)
        inv = lax.rsqrt(jnp.mean(x * x, axis=-1, keepdims=True) + epsilon)
        normed = x * inv * gain_ref[...]
        turned_ref[:, k * length : (k + 1) * length] = normed[:length].T.astype(bf16)
        edges.append(normed[length:])
    pad = jnp.zeros((length - count * EDGE, edges[0].shape[1]), f32)
    turned_ref[:, count * length :] = jnp.concatenate(edges + [pad], axis=0).T.astype(bf16)
    got = jnp.concatenate([got[...] for got in gots], axis=0)
    split_cores(info_ref, nn(turned_ref[:, : count * length], got), mine_ref, theirs_ref)


def conv_kernel(count, info_ref, turned_ref, *rest):
    gots, (mine_ref, theirs_ref) = rest[:count], rest[count:]
    length = gots[0].shape[0] - EDGE
    wide = gots[0].shape[1]
    pad = jnp.zeros((length - count * EDGE, wide), bf16)
    got = jnp.concatenate([got[:length, :] for got in gots] + [got[length:, :] for got in gots] + [pad], axis=0)
    split_cores(info_ref, nn(turned_ref[...], got), mine_ref, theirs_ref)


def out_kernel(count, chips, thin, info_ref, *rest):
    cots, gateds, (mine_ref, theirs_ref) = rest[:count], rest[count : 2 * count], rest[2 * count :]
    left = jnp.concatenate([cot[...].astype(f32).T for cot in cots], axis=1).astype(bf16)
    out = nn(left, jnp.concatenate([gated[...] for gated in gateds], axis=0))
    for c in range(2):
        @pl.when(info_ref[0] == c)
        def _():
            for q in range(chips):
                at = 2 * q * thin
                mine_ref[pl.ds(q * thin, thin), :] = out[at + c * thin : at + (c + 1) * thin]
                theirs_ref[pl.ds(q * thin, thin), :] = out[at + (1 - c) * thin : at + (2 - c) * thin].astype(bf16)


def in_merge_kernel(info_ref, conv_mine, conv_got, gate_mine, gate_got, own_ref, *rest):
    size = len(rest)
    parts, held = rest[: size - 1], rest[size - 1]
    width = own_ref.shape[1]
    half = held.shape[0] // 2
    for mine, got, first in ((conv_mine, conv_got, 0), (gate_mine, gate_got, half)):
        for k in range(half):
            at = pl.ds(k * width, width)
            held[first + k] = mine[:, at] + got[:, at].astype(f32)
    own_ref[...] = held[info_ref[1]]
    for k, part in enumerate(parts):
        part[...] = held[info_ref[1] ^ (k + 1)].astype(bf16)


def out_merge_kernel(chips, info_ref, mine_ref, got_ref, own_ref, *rest):
    parts, held = rest[:-1], rest[-1]
    thin = own_ref.shape[0]
    for q in range(chips):
        at = pl.ds(q * thin, thin)
        held[q] = mine_ref[at, :] + got_ref[at, :].astype(f32)
    own_ref[...] = held[info_ref[2]]
    for k, part in enumerate(parts):
        part[...] = held[info_ref[2] ^ (k + 1)].astype(bf16)


def small_merge_kernel(info_ref, mine_ref, got_ref, own_ref, *parts):
    size = mine_ref.shape[0]
    for k in range(size):
        at = info_ref[1] ^ k
        total = mine_ref[at] + got_ref[at].astype(f32)
        if k == 0:
            own_ref[...] = total
        else:
            parts[k - 1][...] = total.astype(bf16)


def small_sum_kernel(info_ref, *refs):
    parts, out_ref, held = refs[:-2], refs[-2], refs[-1]
    for k, part in enumerate(parts):
        held[info_ref[2] ^ k] = part[...].astype(f32)
    total = held[0]
    for k in range(1, len(parts)):
        total = total + held[k]
    out_ref[...] = total.astype(bf16)


def unpack_kernel(edges, info_ref, rates_ref, mine_ref, other_ref, *outs):
    size = mine_ref.shape[0]
    chunk = mine_ref.shape[2]
    for c, part in ((info_ref[0], mine_ref), (1 - info_ref[0], other_ref)):
        for k in range(size):
            at = pl.ds(pl.multiple_of((c * size + (info_ref[1] ^ k)) * chunk, LANES), chunk)
            block = part[k].astype(f32)
            for n, out in enumerate(outs):
                piece = block[edges[n] : edges[n + 1]]
                out[:, at] = piece * rates_ref[:, at] if n == 2 else piece


class Group:
    def __init__(self, axis, size, stride):
        self.axis, self.size, self.stride = axis, size, stride
        self.direct = size <= 4
        self.place = (lax.axis_index(axis) // stride) % size

    def lists(self):
        n = lax.axis_size(self.axis)
        span = self.stride * self.size
        return [
            [base + low + self.stride * k for k in range(self.size)]
            for base in range(0, n, span)
            for low in range(self.stride)
        ]

    def swap(self, x, k):
        n = lax.axis_size(self.axis)
        return lax.ppermute(x, self.axis, [(i, i ^ (k * self.stride)) for i in range(n)])

    def exchange(self, blocks):
        if not self.direct:
            got = lax.all_to_all(blocks, self.axis, 0, 0, axis_index_groups=self.lists(), tiled=True)
            return [got[k] for k in range(self.size)]
        pick = lambda k: lax.dynamic_index_in_dim(blocks, self.place ^ k, 0, keepdims=False)
        return [pick(0)] + [self.swap(pick(k), k) for k in range(1, self.size)]

    def trade(self, blocks):
        if not self.direct:
            return self.exchange(jnp.stack(blocks))
        return [blocks[0]] + [self.swap(blocks[k], k) for k in range(1, self.size)]

    def gather(self, x):
        if not self.direct:
            got = lax.all_gather(x, self.axis, axis_index_groups=self.lists())
            return [got[k] for k in range(self.size)]
        return [x] + [self.swap(x, k) for k in range(1, self.size)]

    def sender(self, k):
        return self.place ^ k if self.direct else k

    def in_order(self, parts):
        if not self.direct:
            return jnp.stack(parts)
        stacked = jnp.stack(parts)
        return jnp.stack(
            [lax.dynamic_index_in_dim(stacked, self.place ^ q, 0, keepdims=False) for q in range(self.size)]
        )


def total(parts):
    return functools.reduce(lambda a, b: a + b, [part.astype(f32) for part in parts])


def body(
    tokens,
    cotangent,
    doc_starts,
    in_weight,
    conv_weight,
    conv_bias,
    xproj_weight,
    dt_weight,
    dt_bias,
    a_log,
    skip_scale,
    out_weight,
    norm_gain,
):
    length, model = tokens.shape[1:]
    inner_width, states = a_log.shape
    low_rank = dt_weight.shape[0]
    taps = conv_weight.shape[1]
    docs = doc_starts.shape[1]
    rim = taps - 1
    dp_size, seq_size = lax.axis_size("dp"), lax.axis_size("seq")
    core, outer = Group("seq", 2, 1), Group("seq", seq_size // 2, 2)
    rows_group = Group("dp", dp_size, 1)
    width = in_weight.shape[1] // (dp_size * seq_size)
    half_rows = dp_size // 2
    thin = model // (dp_size * seq_size)
    tiled = outer.direct and width % LANES == 0 and thin % EDGE == 0
    chips = outer.size if tiled else 1
    shape = jax.ShapeDtypeStruct

    base = lax.axis_index("seq") * length
    as_int = lambda *v: jnp.stack([jnp.asarray(x, jnp.int32) for x in v])
    info = jnp.concatenate([as_int(base), doc_starts[0], as_int(outer.place, core.place)])
    where = as_int(core.place, rows_group.place, outer.place)
    gain = norm_gain.astype(f32)[None]
    vec = jnp.concatenate(
        [conv_weight.T, conv_bias[None], dt_bias[None], skip_scale[None], jnp.zeros((1, inner_width), bf16)], axis=0
    ).astype(f32)
    decay_rates = -jnp.exp(a_log).T
    rates = jnp.minimum(decay_rates, -LEAST_RATE) / LN2

    left = lax.ppermute(tokens[0, length - rim :], "seq", [(i, i + 1) for i in range(seq_size - 1)])
    slim = shape((length, model // dp_size), bf16)
    tok, cot, *cot_blocks = plain_call(
        functools.partial(prepare_kernel, rim, dp_size),
        "prepare",
        [shape((length + EDGE, model), bf16), shape((length, model), bf16)] + [slim] * dp_size,
        (as_int(rows_group.place), tokens[0], left, cotangent[0]),
        2,
    )
    tok_parts = outer.gather(tok)
    cot_got = rows_group.trade(cot_blocks)

    ext, inner, gate, ggated, proj, mine, *deep = front(
        info, tok, cot, gain, vec, rates, dt_weight, in_weight, out_weight, xproj_weight, taps, docs
    )
    mine, tok_parts, cot_got = lax.optimization_barrier((mine, tok_parts, cot_got))
    other = core.swap(mine, 1)
    (chip,) = plain_call(
        functools.partial(pair_kernel, states), "pair", [shape(mine.shape, bf16)], (where, mine, other, rates), 2
    )
    spot = as_int(core.place, outer.place, -1 if outer.direct else 0)
    entry, arrive = enter(spot, mine, other, rates, outer.gather(chip))
    gated, ggate, *gate_blocks = forward(
        info, proj, dt_weight, vec, rates, entry, inner, gate, ggated, deep[0], deep[1], taps, docs, chips
    )

    def by_chip(blocks):
        if tiled:
            return outer.trade(blocks)
        (x,) = blocks
        blocks = x.reshape(x.shape[0], half_rows, outer.size, 2, width)
        return outer.exchange(blocks.transpose(2, 0, 3, 1, 4).reshape(outer.size, x.shape[0], -1))

    gate_got = by_chip(gate_blocks)
    gated_parts = rows_group.gather(gated)

    small_mine, small_theirs, ngrad, mixed, *sent = backward(
        info, proj, tok, gain, dt_weight, vec, rates, entry, arrive, inner, gate, ggated, deep, gated, ggate,
        in_weight, out_weight, ext, xproj_weight, taps, docs, chips, dp_size,
    )
    sent, small_theirs, gate_got, gated_parts = lax.optimization_barrier((sent, small_theirs, gate_got, gated_parts))
    conv_got = by_chip(sent)
    rows = small_mine.shape[1]
    chunk = shape((rows, inner_width // (2 * dp_size)), bf16)
    small_own, *small_blocks = plain_call(
        small_merge_kernel,
        "small_merge",
        [shape(chunk.shape, f32)] + [chunk] * (dp_size - 1),
        (where, small_mine, core.swap(small_theirs, 1)),
        1.5,
    )
    small = total(rows_group.trade([small_own] + small_blocks)).astype(bf16)
    if outer.direct:
        (small,) = plain_call(
            small_sum_kernel,
            "small_sum",
            [chunk],
            (where, *outer.gather(small)),
            1,
            [pltpu.VMEM((outer.size,) + chunk.shape, f32)],
        )
    else:
        small = total(outer.gather(small)).astype(bf16)
    small = jnp.stack(rows_group.gather(small))
    sizes = [low_rank + 2 * states, low_rank, states, taps, 1, 1, 1, 1]
    edges = [sum(sizes[:k]) for k in range(len(sizes) + 1)]
    parts = plain_call(
        functools.partial(unpack_kernel, edges),
        "unpack",
        [shape((size, inner_width), f32) for size in sizes],
        (where, decay_rates, small, core.swap(small, 1)),
        2,
    )

    back = lax.ppermute(ngrad[length:], "seq", [(i, i - 1) for i in range(1, seq_size)])
    tokens_grad = finish(ngrad, back, tok, cot, gain, rim)

    if tiled:
        halves = [shape((model, half_rows * width), f32), shape((model, half_rows * width), bf16)]
        turned_over, gate_mine, gate_theirs = plain_call(
            functools.partial(gate_kernel, chips),
            "gate_columns",
            [shape((model, (chips + 1) * length), bf16)] + halves,
            (where, gain, *tok_parts, *gate_got),
            4,
        )
        gate_other = core.swap(gate_theirs, 1)
        conv_mine, conv_theirs = plain_call(
            functools.partial(conv_kernel, chips), "conv_columns", halves, (where, turned_over, *conv_got), 3
        )
        slab = (model, width)
        in_own, *in_blocks = plain_call(
            in_merge_kernel,
            "in_merge",
            [shape(slab, f32)] + [shape(slab, bf16)] * (dp_size - 1),
            (where, conv_mine, core.swap(conv_theirs, 1), gate_mine, gate_other),
            2,
            [pltpu.VMEM((dp_size,) + slab, f32)],
        )
        in_share = total(rows_group.trade([in_own] + in_blocks))
        thick = (chips * thin, inner_width)
        out_mine, out_theirs = plain_call(
            functools.partial(out_kernel, dp_size, chips, thin),
            "out_columns",
            [shape(thick, f32), shape(thick, bf16)],
            (where, *cot_got, *gated_parts),
            4,
        )
        slab = (thin, inner_width)
        out_own, *out_blocks = plain_call(
            functools.partial(out_merge_kernel, chips),
            "out_merge",
            [shape(slab, f32)] + [shape(slab, bf16)] * (chips - 1),
            (where, out_mine, core.swap(out_theirs, 1)),
            2,
            [pltpu.VMEM((chips,) + slab, f32)],
        )
        out_share = total(outer.trade([out_own] + out_blocks))
    else:

        def normalised(x):
            wide = x.astype(f32)
            inv = lax.rsqrt(jnp.mean(wide * wide, axis=-1, keepdims=True) + epsilon)
            return (wide * inv * gain).astype(bf16)

        def summed(lefts, rights):
            return functools.reduce(lambda a, b: a + b, [tn(a, b) for a, b in zip(lefts, rights, strict=True)])

        def halved(x):
            return x.astype(bf16).reshape(model, 2, -1).swapaxes(0, 1)

        normed_parts = [normalised(part) for part in tok_parts]
        gate_core = total(core.exchange(halved(summed([part[:length] for part in normed_parts], gate_got))))
        conv_core = total(core.exchange(halved(summed(normed_parts, conv_got))))
        in_core = jnp.concatenate([conv_core, gate_core], axis=1).astype(bf16)
        in_share = total(rows_group.exchange(in_core.reshape(model, dp_size, width).swapaxes(0, 1)))
        out_sum = summed(cot_got, gated_parts).astype(bf16)
        out_core = total(core.exchange(out_sum.reshape(outer.size, 2, thin, inner_width).swapaxes(0, 1)))
        out_share = total(outer.exchange(out_core.astype(bf16)))

    return (
        mixed[None],
        tokens_grad[None],
        in_share,
        parts[3].T,
        parts[6][0],
        parts[0].T,
        parts[1],
        parts[4][0],
        parts[2].T,
        parts[5][0],
        out_share.T,
        parts[7][0, :model],
    )


def solution(mesh):
    whole = (P(),) * 10
    row = P("dp", "seq", None)
    columns = P(None, ("dp", "seq"))
    return jax.shard_map(
        body,
        mesh=mesh,
        in_specs=(row, row, P("dp", None)) + whole,
        out_specs=(row, row, columns) + (P(),) * 7 + (columns, P()),
        check_vma=False,
    )
```

time: 294 us -> 197 us (0.67)
  matrix products: 55.8 us -> 0 us
  Pallas kernels: 33 us -> 79.1 us
  local copies, waits for them, and re-layouts: 48.7 us -> 16.4 us
  starting transfers between devices: 77.5 us -> 54.7 us
  other arithmetic: 26.7 us -> 4.35 us
  waiting for transfers between devices: 48.4 us -> 40.3 us
    dot_general x23 -> x0, matrix products: 55.8 us -> none  [the longest x12 25.9 us: summed(): lax.dot_general(a, b, (((0,), (0,)), ((), ())), preferred_element_type=f32)]
    pallas_call x2 -> x15, Pallas kernels: 33 us -> 79.1 us  [the longest x1 32.5 us: backward(): pl.pallas_call(functools.partial(backward_kernel, states, rank, taps, doc...]
    ppermute x41 -> x39, starting transfers between devices: 73.9 us -> 51.1 us  [swap(): lax.ppermute(x, self.axis, [(i, i ^ k * self.stride) for i in range(n)])]
    convert_element_type x23 -> x2, other arithmetic: 11.9 us -> 0.06 us  [the longest x1 0.05 us: body(): small = total(rows_group.trade([small_own] + small_blocks)).astype(bf16)]
    concatenate x22 -> x1, local copies, waits for them, and re-layouts: 10.3 us -> 0.78 us  [body(): jnp.concatenate([conv_weight.T, conv_bias[None], dt_bias[None], skip_scal...]
    ppermute x41 -> x39, waiting for transfers between devices: 48.4 us -> 39.5 us  [swap(): lax.ppermute(x, self.axis, [(i, i ^ k * self.stride) for i in range(n)])]
    slice x22 -> x1, local copies, waits for them, and re-layouts: 8.04 us -> 0.01 us  [body(): ngrad[length:]]
    reshape x9 -> x0, local copies, waits for them, and re-layouts: 7.46 us -> none  [the longest x1 1.87 us: body(): summed([part[:length] for part in normed_parts], gate_got)]
  transfers between devices with their start and end apart: 43 -> 41, of which waited for: 11 -> 12; matrix products, arithmetic and copies ran while one was open for 35% -> 4% of each run, Pallas kernels for 7% -> 33%
where the time goes in v2:
time: 197 us; the launch traced here: 196 us
  Pallas kernels  79.1 us (40%)
  starting transfers between devices  54.7 us (28%)
  waiting for transfers between devices  40.3 us (20%)
  local copies, waits for them, and re-layouts  16.4 us (8%)
  other arithmetic  4.35 us (2%)
    ppermute x39, starting transfers between devices, swap(): lax.ppermute(x, self.axis, [(i, i ^ k * self.stride) for i in range(n)])  51.1 us
    ppermute x39, waiting for transfers between devices, swap(): lax.ppermute(x, self.axis, [(i, i ^ k * self.stride) for i in range(n)])  39.5 us
    pallas_call x1, Pallas kernels, backward(): pl.pallas_call(functools.partial(backward_kernel, states, rank, taps, doc...  32.5 us
    pallas_call x1, Pallas kernels, front(): pl.pallas_call(functools.partial(front_kernel, states, rank, taps, docs,...  22.7 us
    unnamed x63, local copies, waits for them, and re-layouts  12.2 us
    pallas_call x1, Pallas kernels, forward(): pl.pallas_call(functools.partial(forward_kernel, states, rank, taps, docs...  10.6 us
    pallas_call x10, Pallas kernels, plain_call(): pl.pallas_call(kernel, in_specs=[SMEM_SPEC] + [full(x) for x in args[1:]]...  10.6 us
  transfers between devices with their start and end apart: 41, of which 12 were waited for; matrix products, arithmetic and copies ran while one was open for 4% of the time, Pallas kernels for 33%

profile of v2, /device:TPU:0, one launch (start us, length us, event | category | flops | bytes accessed | tf_op | source)
XLA Modules:
  0.0 196.1 jit_solution(10192284973337082124)
XLA Ops:
  0.6 0.7 slice_bitcast_fusion
  1.4 2.3 %collective-permute-start = (bf16[3,1024]{1,0:T(4,128)(2,1)S(1)}, bf16[3,1024]{1,0:T(4,128)(2,1)S(1)}, u32[]{:S(2)}, u32[]{:S(2)}) collective-permute-start(bf16[3,1024]{1,0:T(4,128)(2,1)S(1)} %slice_bitcast_fusion), channel_id=1, source_target_pairs={{0,1},{1,2},{2,3},{3,4},{4,5},{5,6},{6,7},{8,9},{9,10},{10,11},{11... | collective-permute-start | bytes 18440 | tf_op jit(solution)/shard_map/ppermute | solution.py:944
  3.7 0.8 collective-permute-done.left_ref
  4.5 0.9 copy-done.18
  5.5 0.9 copy-done.20
  6.9 4.9 %collective-permute-start.1 = (bf16[144,1024]{1,0:T(8,128)(2,1)S(1)}, bf16[144,1024]{1,0:T(8,128)(2,1)S(1)}, u32[]{:S(2)}, u32[]{:S(2)}) collective-permute-start(bf16[144,1024]{1,0:T(8,128)(2,1)S(1)} %get-tuple-element.116.tok_ref.rest_0_), channel_id=1, source_target_pairs={{0,2},{1,3},{2,0},{3,1},{4,6},{5,7},{6,4},{7,5},{8,10},{9,11},{10,... | collective-permute-start | bytes 884744 | tf_op jit(solution)/shard_map/ppermute | solution.py:866
  11.8 2.6 %collective-permute-start.2 = (bf16[144,1024]{1,0:T(8,128)(2,1)S(1)}, bf16[144,1024]{1,0:T(8,128)(2,1)S(1)}, u32[]{:S(2)}, u32[]{:S(2)}) collective-permute-start(bf16[144,1024]{1,0:T(8,128)(2,1)S(1)} %get-tuple-element.116.tok_ref.rest_0_), channel_id=1, source_target_pairs={{0,4},{1,5},{2,6},{3,7},{4,0},{5,1},{6,2},{7,3},{8,12},{9,13},{10,... | collective-permute-start | bytes 884744 | tf_op jit(solution)/shard_map/ppermute | solution.py:866
  14.3 1.5 collective-permute-start.4
  15.8 0.9 minimum_multiply_fusion.rates_ref
  16.8 0.7 broadcast_in_dim.31
  19.6 0.8 concatenate.7
  20.4 1.3 copy.25.wx_ref
  21.8 1.6 collective-permute-start.5
  23.8 0.7 pad_add_fusion.info_ref
  24.6 1.0 copy-done.7
  25.5 22.7 %front.1 = (bf16[160,2048]{1,0:T(8,128)(2,1)S(1)}, bf16[128,2048]{1,0:T(8,128)(2,1)S(1)}, f32[128,2048]{1,0:T(8,128)S(1)}, f32[128,2048]{1,0:T(8,128)S(1)}, f32[...) custom-call(s32[7]{0:T(128)S(1)} %pad_add_fusion.info_ref, ...), custom_call_target="tpu_custom_call" | custom-call | bytes 72000000 | tf_op jit(solution)/shard_map/front/pallas_call | solution.py:218
  48.3 0.8 copy-done.15
  49.8 1.2 copy-done.27
  51.2 1.4 collective-permute-done.7.other_ref
  53.2 3.9 %collective-permute-start.10 = (bf16[48,2048]{1,0:T(8,128)(2,1)S(1)}, bf16[48,2048]{1,0:T(8,128)(2,1)S(1)}, u32[]{:S(2)}, u32[]{:S(2)}) collective-permute-start(bf16[48,2048]{1,0:T(8,128)(2,1)S(1)} %pair.1.rest_0_), channel_id=1, source_target_pairs={{0,6},{1,7},{2,4},{3,5},{4,2},{5,3},{6,0},{7,1},{8,14},{9,15},{10,... | collective-permute-start | bytes 589832 | tf_op jit(solution)/shard_map/ppermute | solution.py:866
  57.8 5.0 %collective-permute-done.10.rest_3_ = bf16[48,2048]{1,0:T(8,128)(2,1)S(1)} collective-permute-done((bf16[48,2048]{1,0:T(8,128)(2,1)S(1)}, bf16[48,2048]{1,0:T(8,128)(2,1)S(1)}, u32[]{:S(2)}, u32[]{:S(2)}) %collective-permute-start.10) | collective-permute-done | bytes 196640 | tf_op jit(solution)/shard_map/ppermute | solution.py:866
  62.8 5.7 %collective-permute-done.8.rest_1_ = bf16[48,2048]{1,0:T(8,128)(2,1)S(1)} collective-permute-done((bf16[48,2048]{1,0:T(8,128)(2,1)S(1)}, bf16[48,2048]{1,0:T(8,128)(2,1)S(1)}, u32[]{:S(2)}, u32[]{:S(2)}) %collective-permute-start.8) | collective-permute-done | bytes 196640 | tf_op jit(solution)/shard_map/ppermute | solution.py:866
  68.5 4.7 %collective-permute-done.9.rest_2_ = bf16[48,2048]{1,0:T(8,128)(2,1)S(1)} collective-permute-done((bf16[48,2048]{1,0:T(8,128)(2,1)S(1)}, bf16[48,2048]{1,0:T(8,128)(2,1)S(1)}, u32[]{:S(2)}, u32[]{:S(2)}) %collective-permute-start.9) | collective-permute-done | bytes 196640 | tf_op jit(solution)/shard_map/ppermute | solution.py:866
  73.2 1.4 enter.1
  75.3 10.6 %forward.1 = (bf16[128,2048]{1,0:T(8,128)(2,1)S(1)}, bf16[128,2048]{1,0:T(8,128)(2,1)S(1)}, bf16[128,512]{1,0:T(8,128)(2,1)S(1)}, bf16[128,512]{1,0:T(8,128)(2,1...) custom-call(s32[7]{0:T(128)S(1)} %pad_add_fusion.info_ref, f32[128,128]{1,0:T(8,128)S(1)} %get-tuple-element.95.proj_ref, ...), custom_call_target="tpu_custom_call" | custom-call | bytes 32400000 | tf_op jit(solution)/shard_map/forward/pallas_call | solution.py:330
  85.9 0.8 copy-done.17
  86.7 1.5 collective-permute-start.15
  88.2 1.5 collective-permute-start.16
  90.2 3.0 %collective-permute-start.13 = (bf16[128,512]{1,0:T(8,128)(2,1)}, bf16[128,512]{1,0:T(8,128)(2,1)S(1)}, u32[]{:S(2)}, u32[]{:S(2)}) collective-permute-start(bf16[128,512]{1,0:T(8,128)(2,1)} %get-tuple-element.127), channel_id=1, source_target_pairs={{0,4},{1,5},{2,6},{3,7},{4,0},{5,1},{6,2},{7,3},{8,12},{9,13},{10,... | collective-permute-start | bytes 393224 | tf_op jit(solution)/shard_map/ppermute | solution.py:866
  93.2 2.4 %collective-permute-done.12.rest_5_ = bf16[128,512]{1,0:T(8,128)(2,1)S(1)} collective-permute-done((bf16[128,512]{1,0:T(8,128)(2,1)S(1)}, bf16[128,512]{1,0:T(8,128)(2,1)S(1)}, u32[]{:S(2)}, u32[]{:S(2)}) %collective-permute-start.12) | collective-permute-done | bytes 131104 | tf_op jit(solution)/shard_map/ppermute | solution.py:866
  95.6 2.5 %collective-permute-start.14 = (bf16[128,512]{1,0:T(8,128)(2,1)S(1)}, bf16[128,512]{1,0:T(8,128)(2,1)S(1)}, u32[]{:S(2)}, u32[]{:S(2)}) collective-permute-start(bf16[128,512]{1,0:T(8,128)(2,1)S(1)} %get-tuple-element.128), channel_id=1, source_target_pairs={{0,6},{1,7},{2,4},{3,5},{4,2},{5,3},{6,0},{7,1},{8,14},{9,15},{10,... | collective-permute-start | bytes 393224 | tf_op jit(solution)/shard_map/ppermute | solution.py:866
  98.2 32.5 %backward.1 = (f32[4,192,256]{2,1,0:T(8,128)}, bf16[4,192,256]{2,1,0:T(8,128)(2,1)}, f32[144,1024]{1,0:T(8,128)}, bf16[128,1024]{1,0:T(8,128)(2,1)}, bf16[144,51...) custom-call(s32[7]{0:T(128)} %copy-done.29, ...), custom_call_target="tpu_custom_call" | custom-call | bytes 100800000 | tf_op jit(solution)/shard_map/backward/pallas_call | solution.py:572
  130.9 1.9 collective-permute-start.19
  132.8 2.5 %collective-permute-start.20 = (bf16[144,512]{1,0:T(8,128)(2,1)}, bf16[144,512]{1,0:T(8,128)(2,1)S(1)}, u32[]{:S(2)}, u32[]{:S(2)}) collective-permute-start(bf16[144,512]{1,0:T(8,128)(2,1)} %get-tuple-element.137), channel_id=1, source_target_pairs={{0,6},{1,7},{2,4},{3,5},{4,2},{5,3},{6,0},{7,1},{8,14},{9,15},{10,... | collective-permute-start | bytes 442376 | tf_op jit(solution)/shard_map/ppermute | solution.py:866
  135.3 1.1 copy-done.13
  137.1 1.6 collective-permute-start.27
  138.6 1.5 collective-permute-start.28
  140.2 1.5 collective-permute-start.29
  141.7 1.0 copy-done.10
  142.7 0.8 copy-done.26
  143.6 0.8 copy-done.28
  144.4 1.4 out_columns.1
  145.8 1.9 gate_columns.1
  148.3 1.6 conv_columns.1
  150.7 2.4 %collective-permute-start.31 = (bf16[192,256]{1,0:T(8,128)(2,1)S(1)}, bf16[192,256]{1,0:T(8,128)(2,1)S(1)}, u32[]{:S(2)}, u32[]{:S(2)}) collective-permute-start(bf16[192,256]{1,0:T(8,128)(2,1)S(1)} %add_convert_fusion.refs_0_), channel_id=1, source_target_pairs={{0,4},{1,5},{2,6},{3,7},{4,0},{5,1},{6,2},{7,3},{8,12},{9,13},{10,... | collective-permute-start | bytes 294920 | tf_op jit(solution)/shard_map/ppermute | solution.py:866
  153.1 3.9 %collective-permute-done.30.refs_1_ = bf16[192,256]{1,0:T(8,128)(2,1)S(1)} collective-permute-done((bf16[192,256]{1,0:T(8,128)(2,1)S(1)}, bf16[192,256]{1,0:T(8,128)(2,1)S(1)}, u32[]{:S(2)}, u32[]{:S(2)}) %collective-permute-start.30) | collective-permute-done | bytes 98336 | tf_op jit(solution)/shard_map/ppermute | solution.py:866
  157.0 1.7 collective-permute-start.32
  158.8 4.6 %collective-permute-done.32.refs_3_ = bf16[192,256]{1,0:T(8,128)(2,1)S(1)} collective-permute-done((bf16[192,256]{1,0:T(8,128)(2,1)S(1)}, bf16[192,256]{1,0:T(8,128)(2,1)S(1)}, u32[]{:S(2)}, u32[]{:S(2)}) %collective-permute-start.32) | collective-permute-done | bytes 98336 | tf_op jit(solution)/shard_map/ppermute | solution.py:866
  164.2 1.3 collective-permute-start.11
  166.2 1.6 collective-permute-start.38
  167.8 2.4 %collective-permute-start.39 = (bf16[32,2048]{1,0:T(8,128)(2,1)S(1)}, bf16[32,2048]{1,0:T(8,128)(2,1)S(1)}, u32[]{:S(2)}, u32[]{:S(2)}) collective-permute-start(bf16[32,2048]{1,0:T(8,128)(2,1)S(1)} %get-tuple-element.171), channel_id=1, source_target_pairs={{0,4},{1,5},{2,6},{3,7},{4,0},{5,1},{6,2},{7,3},{8,12},{9,13},{10,... | collective-permute-start | bytes 393224 | tf_op jit(solution)/shard_map/ppermute | solution.py:866
  170.2 1.1 collective-permute-start.40
  171.3 1.5 collective-permute-start.34
  172.8 1.3 collective-permute-start.35
  174.2 1.2 finish.1
  175.3 0.9 in_merge.1
  176.3 1.1 collective-permute-done.34
  177.4 2.4 %collective-permute-start.23 = (bf16[1024,128]{1,0:T(8,128)(2,1)S(1)}, bf16[1024,128]{1,0:T(8,128)(2,1)S(1)}, u32[]{:S(2)}, u32[]{:S(2)}) collective-permute-start(bf16[1024,128]{1,0:T(8,128)(2,1)S(1)} %get-tuple-element.143), channel_id=1, source_target_pairs={{0,8},{8,0},{16,24},{24,16},{1,9},{9,1},{17,25},{25,17},{2,10},{10... | collective-permute-start | bytes 786440 | tf_op jit(solution)/shard_map/ppermute | solution.py:866
  180.0 1.5 collective-permute-start.25
  181.5 0.8 add_bitcast_fusion
  182.3 4.7 %collective-permute-done.23 = bf16[1024,128]{1,0:T(8,128)(2,1)S(1)} collective-permute-done((bf16[1024,128]{1,0:T(8,128)(2,1)S(1)}, bf16[1024,128]{1,0:T(8,128)(2,1)S(1)}, u32[]{:S(2)}, u32[]{:S(2)}) %collective-permute-start.23) | collective-permute-done | bytes 262176 | tf_op jit(solution)/shard_map/ppermute | solution.py:866
  186.9 5.8 %collective-permute-done.24 = bf16[1024,128]{1,0:T(8,128)(2,1)S(1)} collective-permute-done((bf16[1024,128]{1,0:T(8,128)(2,1)S(1)}, bf16[1024,128]{1,0:T(8,128)(2,1)S(1)}, u32[]{:S(2)}, u32[]{:S(2)}) %collective-permute-start.24) | collective-permute-done | bytes 262176 | tf_op jit(solution)/shard_map/ppermute | solution.py:866
  192.8 0.9 convert_add_fusion
  193.7 1.8 unpack.1
  (115 shorter events, 10.8 us)
Async XLA Ops:
  1.4 3.2 %collective-permute-start = (bf16[3,1024]{1,0:T(4,128)(2,1)S(1)}, bf16[3,1024]{1,0:T(4,128)(2,1)S(1)}, u32[]{:S(2)}, u32[]{:S(2)}) collective-permute-start(bf16[3,1024]{1,0:T(4,128)(2,1)S(1)} %slice_bitcast_fusion), channel_id=1, source_target_pairs={{0,1},{1,2},{2,3},{3,4},{4,5},{5,6},{6,7},{8,9},{9,10},{10,11},{11... | collective-permute-start | bytes 18440 | tf_op jit(solution)/shard_map/ppermute | solution.py:944
  6.9 41.4 %copy-start.2 = (bf16[144,1024]{1,0:T(8,128)(2,1)}, bf16[144,1024]{1,0:T(8,128)(2,1)S(1)}, u32[]{:S(2)}) copy-start(bf16[144,1024]{1,0:T(8,128)(2,1)S(1)} %get-tuple-element.116.tok_ref.rest_0_) | copy-start | bytes 884740
  6.9 44.1 %collective-permute-start.1 = (bf16[144,1024]{1,0:T(8,128)(2,1)S(1)}, bf16[144,1024]{1,0:T(8,128)(2,1)S(1)}, u32[]{:S(2)}, u32[]{:S(2)}) collective-permute-start(bf16[144,1024]{1,0:T(8,128)(2,1)S(1)} %get-tuple-element.116.tok_ref.rest_0_), channel_id=1, source_target_pairs={{0,2},{1,3},{2,0},{3,1},{4,6},{5,7},{6,4},{7,5},{8,10},{9,11},{10,... | collective-permute-start | bytes 884744 | tf_op jit(solution)/shard_map/ppermute | solution.py:866
  11.8 39.2 %collective-permute-start.2 = (bf16[144,1024]{1,0:T(8,128)(2,1)S(1)}, bf16[144,1024]{1,0:T(8,128)(2,1)S(1)}, u32[]{:S(2)}, u32[]{:S(2)}) collective-permute-start(bf16[144,1024]{1,0:T(8,128)(2,1)S(1)} %get-tuple-element.116.tok_ref.rest_0_), channel_id=1, source_target_pairs={{0,4},{1,5},{2,6},{3,7},{4,0},{5,1},{6,2},{7,3},{8,12},{9,13},{10,... | collective-permute-start | bytes 884744 | tf_op jit(solution)/shard_map/ppermute | solution.py:866
  14.3 36.7 %collective-permute-start.3 = (bf16[144,1024]{1,0:T(8,128)(2,1)S(1)}, bf16[144,1024]{1,0:T(8,128)(2,1)S(1)}, u32[]{:S(2)}, u32[]{:S(2)}) collective-permute-start(bf16[144,1024]{1,0:T(8,128)(2,1)S(1)} %get-tuple-element.116.tok_ref.rest_0_), channel_id=1, source_target_pairs={{0,6},{1,7},{2,4},{3,5},{4,2},{5,3},{6,0},{7,1},{8,14},{9,15},{10,... | collective-permute-start | bytes 884744 | tf_op jit(solution)/shard_map/ppermute | solution.py:866
  14.3 9.0 %collective-permute-start.4 = (bf16[128,256]{1,0:T(8,128)(2,1)S(1)}, bf16[128,256]{1,0:T(8,128)(2,1)S(1)}, u32[]{:S(2)}, u32[]{:S(2)}) collective-permute-start(bf16[128,256]{1,0:T(8,128)(2,1)S(1)} %get-tuple-element.98), channel_id=1, source_target_pairs={{0,8},{8,0},{16,24},{24,16},{1,9},{9,1},{17,25},{25,17},{2,10},{10... | collective-permute-start | bytes 196616 | tf_op jit(solution)/shard_map/ppermute | solution.py:866
  16.8 58.5 %copy-start = (f32[16,2048]{1,0:T(8,128)}, f32[16,2048]{1,0:T(8,128)S(1)}, u32[]{:S(2)}) copy-start(f32[16,2048]{1,0:T(8,128)S(1)} %minimum_multiply_fusion.rates_ref) | copy-start | bytes 393220
  17.5 30.7 %copy-start.23 = (f32[1024]{0:T(1024)}, f32[1024]{0:T(1024)S(1)}, u32[]{:S(2)}) copy-start(f32[1024]{0:T(1024)S(1)} %broadcast_in_dim.31) | copy-start | bytes 12292
  20.4 54.8 %copy-start.12 = (f32[8,2048]{1,0:T(8,128)}, f32[8,2048]{1,0:T(8,128)S(1)}, u32[]{:S(2)}) copy-start(f32[8,2048]{1,0:T(8,128)S(1)} %convert_element_type.34.vec_ref) | copy-start | bytes 196612
  21.7 26.5 %copy-start.1 = (bf16[2048,96]{1,0:T(8,128)(2,1)}, bf16[2048,96]{1,0:T(8,128)(2,1)S(1)}, u32[]{:S(2)}) copy-start(bf16[2048,96]{1,0:T(8,128)(2,1)S(1)} %copy.25.wx_ref) | copy-start | bytes 1179652
  21.8 27.4 %collective-permute-start.5 = (bf16[128,256]{1,0:T(8,128)(2,1)S(1)}, bf16[128,256]{1,0:T(8,128)(2,1)S(1)}, u32[]{:S(2)}, u32[]{:S(2)}) collective-permute-start(bf16[128,256]{1,0:T(8,128)(2,1)S(1)} %get-tuple-element.99), channel_id=1, source_target_pairs={{0,16},{8,24},{16,0},{24,8},{1,17},{9,25},{17,1},{25,9},{2,18},{10... | collective-permute-start | bytes 196616 | tf_op jit(solution)/shard_map/ppermute | solution.py:866
  23.4 26.5 %collective-permute-start.6 = (bf16[128,256]{1,0:T(8,128)(2,1)S(1)}, bf16[128,256]{1,0:T(8,128)(2,1)S(1)}, u32[]{:S(2)}, u32[]{:S(2)}) collective-permute-start(bf16[128,256]{1,0:T(8,128)(2,1)S(1)} %get-tuple-element.100), channel_id=1, source_target_pairs={{0,24},{8,16},{16,8},{24,0},{1,25},{9,17},{17,9},{25,1},{2,26},{10... | collective-permute-start | bytes 196616 | tf_op jit(solution)/shard_map/ppermute | solution.py:866
  24.6 50.7 %copy-start.29 = (s32[7]{0:T(128)}, s32[7]{0:T(128)S(1)}, u32[]{:S(2)}) copy-start(s32[7]{0:T(128)S(1)} %pad_add_fusion.info_ref) | copy-start | bytes 88
  24.6 1.0 copy-start.7
  25.5 49.7 %copy-start.8 = (bf16[64,2048]{1,0:T(8,128)(2,1)S(1)}, bf16[64,2048]{1,0:T(8,128)(2,1)}, u32[]{:S(2)}) copy-start(bf16[64,2048]{1,0:T(8,128)(2,1)} %dtw_ref.5) | copy-start | bytes 786436
  49.1 49.0 %copy-start.4 = (f32[128,2048]{1,0:T(8,128)}, f32[128,2048]{1,0:T(8,128)S(1)}, u32[]{:S(2)}) copy-start(f32[128,2048]{1,0:T(8,128)S(1)} %get-tuple-element.105.gate_ref) | copy-start | bytes 3145732
  49.1 49.0 %copy-start.5 = (f32[128,2048]{1,0:T(8,128)}, f32[128,2048]{1,0:T(8,128)S(1)}, u32[]{:S(2)}) copy-start(f32[128,2048]{1,0:T(8,128)S(1)} %get-tuple-element.106.ggated_ref) | copy-start | bytes 3145732
  49.1 49.0 %copy-start.6 = (f32[16,8,2048]{2,1,0:T(8,128)}, f32[16,8,2048]{2,1,0:T(8,128)S(1)}, u32[]{:S(2)}) copy-start(f32[16,8,2048]{2,1,0:T(8,128)S(1)} %get-tuple-element.107.dx_ref) | copy-start | bytes 3145732
  49.1 49.0 %copy-start.11 = (bf16[128,2048]{1,0:T(8,128)(2,1)}, bf16[128,2048]{1,0:T(8,128)(2,1)S(1)}, u32[]{:S(2)}) copy-start(bf16[128,2048]{1,0:T(8,128)(2,1)S(1)} %get-tuple-element.104.inner_ref) | copy-start | bytes 1572868
  49.1 49.0 %copy-start.19 = (f32[128,128]{1,0:T(8,128)}, f32[128,128]{1,0:T(8,128)S(1)}, u32[]{:S(2)}) copy-start(f32[128,128]{1,0:T(8,128)S(1)} %get-tuple-element.95.proj_ref) | copy-start | bytes 196612
  49.8 1.2 copy-start.27
  51.0 1.5 collective-permute-start.7
  53.2 9.6 %collective-permute-start.10 = (bf16[48,2048]{1,0:T(8,128)(2,1)S(1)}, bf16[48,2048]{1,0:T(8,128)(2,1)S(1)}, u32[]{:S(2)}, u32[]{:S(2)}) collective-permute-start(bf16[48,2048]{1,0:T(8,128)(2,1)S(1)} %pair.1.rest_0_), channel_id=1, source_target_pairs={{0,6},{1,7},{2,4},{3,5},{4,2},{5,3},{6,0},{7,1},{8,14},{9,15},{10,... | collective-permute-start | bytes 589832 | tf_op jit(solution)/shard_map/ppermute | solution.py:866
  57.1 11.4 %collective-permute-start.8 = (bf16[48,2048]{1,0:T(8,128)(2,1)S(1)}, bf16[48,2048]{1,0:T(8,128)(2,1)S(1)}, u32[]{:S(2)}, u32[]{:S(2)}) collective-permute-start(bf16[48,2048]{1,0:T(8,128)(2,1)S(1)} %pair.1.rest_0_), channel_id=1, source_target_pairs={{0,2},{1,3},{2,0},{3,1},{4,6},{5,7},{6,4},{7,5},{8,10},{9,11},{10,... | collective-permute-start | bytes 589832 | tf_op jit(solution)/shard_map/ppermute | solution.py:866
  57.1 16.1 %collective-permute-start.9 = (bf16[48,2048]{1,0:T(8,128)(2,1)S(1)}, bf16[48,2048]{1,0:T(8,128)(2,1)S(1)}, u32[]{:S(2)}, u32[]{:S(2)}) collective-permute-start(bf16[48,2048]{1,0:T(8,128)(2,1)S(1)} %pair.1.rest_0_), channel_id=1, source_target_pairs={{0,4},{1,5},{2,6},{3,7},{4,0},{5,1},{6,2},{7,3},{8,12},{9,13},{10,... | collective-permute-start | bytes 589832 | tf_op jit(solution)/shard_map/ppermute | solution.py:866
  75.2 22.9 %copy-start.16 = (f32[16,2048]{1,0:T(8,128)}, f32[16,2048]{1,0:T(8,128)S(1)}, u32[]{:S(2)}) copy-start(f32[16,2048]{1,0:T(8,128)S(1)} %get-tuple-element.102.entry_ref) | copy-start | bytes 393220
  86.7 11.5 %copy-start.9 = (bf16[128,2048]{1,0:T(8,128)(2,1)}, bf16[128,2048]{1,0:T(8,128)(2,1)S(1)}, u32[]{:S(2)}) copy-start(bf16[128,2048]{1,0:T(8,128)(2,1)S(1)} %get-tuple-element.163.gated_ref.rest_4_) | copy-start | bytes 1572868
  86.7 44.1 %collective-permute-start.15 = (bf16[128,2048]{1,0:T(8,128)(2,1)S(1)}, bf16[128,2048]{1,0:T(8,128)(2,1)S(1)}, u32[]{:S(2)}, u32[]{:S(2)}) collective-permute-start(bf16[128,2048]{1,0:T(8,128)(2,1)S(1)} %get-tuple-element.163.gated_ref.rest_4_), channel_id=1, source_target_pairs={{0,8},{8,0},{16,24},{24,16},{1,9},{9,1},{17,25},{25,17},{2,10},{10... | collective-permute-start | bytes 1572872 | tf_op jit(solution)/shard_map/ppermute | solution.py:866
  88.2 42.6 %collective-permute-start.16 = (bf16[128,2048]{1,0:T(8,128)(2,1)S(1)}, bf16[128,2048]{1,0:T(8,128)(2,1)S(1)}, u32[]{:S(2)}, u32[]{:S(2)}) collective-permute-start(bf16[128,2048]{1,0:T(8,128)(2,1)S(1)} %get-tuple-element.163.gated_ref.rest_4_), channel_id=1, source_target_pairs={{0,16},{8,24},{16,0},{24,8},{1,17},{9,25},{17,1},{25,9},{2,18},{10... | collective-permute-start | bytes 1572872 | tf_op jit(solution)/shard_map/ppermute | solution.py:866
  89.7 41.1 %collective-permute-start.17 = (bf16[128,2048]{1,0:T(8,128)(2,1)S(1)}, bf16[128,2048]{1,0:T(8,128)(2,1)S(1)}, u32[]{:S(2)}, u32[]{:S(2)}) collective-permute-start(bf16[128,2048]{1,0:T(8,128)(2,1)S(1)} %get-tuple-element.163.gated_ref.rest_4_), channel_id=1, source_target_pairs={{0,24},{8,16},{16,8},{24,0},{1,25},{9,17},{17,9},{25,1},{2,26},{10... | collective-permute-start | bytes 1572872 | tf_op jit(solution)/shard_map/ppermute | solution.py:866
  90.2 5.5 %collective-permute-start.12 = (bf16[128,512]{1,0:T(8,128)(2,1)S(1)}, bf16[128,512]{1,0:T(8,128)(2,1)S(1)}, u32[]{:S(2)}, u32[]{:S(2)}) collective-permute-start(bf16[128,512]{1,0:T(8,128)(2,1)S(1)} %get-tuple-element.126), channel_id=1, source_target_pairs={{0,2},{1,3},{2,0},{3,1},{4,6},{5,7},{6,4},{7,5},{8,10},{9,11},{10,... | collective-permute-start | bytes 393224 | tf_op jit(solution)/shard_map/ppermute | solution.py:866
  90.2 40.6 %collective-permute-start.13 = (bf16[128,512]{1,0:T(8,128)(2,1)}, bf16[128,512]{1,0:T(8,128)(2,1)S(1)}, u32[]{:S(2)}, u32[]{:S(2)}) collective-permute-start(bf16[128,512]{1,0:T(8,128)(2,1)} %get-tuple-element.127), channel_id=1, source_target_pairs={{0,4},{1,5},{2,6},{3,7},{4,0},{5,1},{6,2},{7,3},{8,12},{9,13},{10,... | collective-permute-start | bytes 393224 | tf_op jit(solution)/shard_map/ppermute | solution.py:866
  95.6 35.1 %collective-permute-start.14 = (bf16[128,512]{1,0:T(8,128)(2,1)S(1)}, bf16[128,512]{1,0:T(8,128)(2,1)S(1)}, u32[]{:S(2)}, u32[]{:S(2)}) collective-permute-start(bf16[128,512]{1,0:T(8,128)(2,1)S(1)} %get-tuple-element.128), channel_id=1, source_target_pairs={{0,6},{1,7},{2,4},{3,5},{4,2},{5,3},{6,0},{7,1},{8,14},{9,15},{10,... | collective-permute-start | bytes 393224 | tf_op jit(solution)/shard_map/ppermute | solution.py:866
  98.2 47.6 %copy-start.3 = (bf16[144,1024]{1,0:T(8,128)(2,1)S(1)}, bf16[144,1024]{1,0:T(8,128)(2,1)}, u32[]{:S(2)}) copy-start(bf16[144,1024]{1,0:T(8,128)(2,1)} %copy-done.2) | copy-start | bytes 884740
  98.2 47.6 %copy-start.24 = (f32[1024]{0:T(1024)S(1)}, f32[1024]{0:T(1024)}, u32[]{:S(2)}) copy-start(f32[1024]{0:T(1024)} %copy-done.23) | copy-start | bytes 12292
  130.8 4.5 %collective-permute-start.26 = (bf16[4,192,256]{2,1,0:T(8,128)(2,1)}, bf16[4,192,256]{2,1,0:T(8,128)(2,1)S(1)}, u32[]{:S(2)}, u32[]{:S(2)}) collective-permute-start(bf16[4,192,256]{2,1,0:T(8,128)(2,1)} %get-tuple-element.147), channel_id=1, source_target_pairs={{0,1},{1,0},{2,3},{3,2},{4,5},{5,4},{6,7},{7,6},{8,9},{9,8},{10,11... | collective-permute-start | bytes 1179656 | tf_op jit(solution)/shard_map/ppermute | solution.py:866
  130.9 9.3 %collective-permute-start.18 = (bf16[144,512]{1,0:T(8,128)(2,1)}, bf16[144,512]{1,0:T(8,128)(2,1)S(1)}, u32[]{:S(2)}, u32[]{:S(2)}) collective-permute-start(bf16[144,512]{1,0:T(8,128)(2,1)} %get-tuple-element.135), channel_id=1, source_target_pairs={{0,2},{1,3},{2,0},{3,1},{4,6},{5,7},{6,4},{7,5},{8,10},{9,11},{10,... | collective-permute-start | bytes 442376 | tf_op jit(solution)/shard_map/ppermute | solution.py:866
  130.9 16.8 %collective-permute-start.19 = (bf16[144,512]{1,0:T(8,128)(2,1)}, bf16[144,512]{1,0:T(8,128)(2,1)S(1)}, u32[]{:S(2)}, u32[]{:S(2)}) collective-permute-start(bf16[144,512]{1,0:T(8,128)(2,1)} %get-tuple-element.136), channel_id=1, source_target_pairs={{0,4},{1,5},{2,6},{3,7},{4,0},{5,1},{6,2},{7,3},{8,12},{9,13},{10,... | collective-permute-start | bytes 442376 | tf_op jit(solution)/shard_map/ppermute | solution.py:866
  132.8 15.0 %collective-permute-start.20 = (bf16[144,512]{1,0:T(8,128)(2,1)}, bf16[144,512]{1,0:T(8,128)(2,1)S(1)}, u32[]{:S(2)}, u32[]{:S(2)}) collective-permute-start(bf16[144,512]{1,0:T(8,128)(2,1)} %get-tuple-element.137), channel_id=1, source_target_pairs={{0,6},{1,7},{2,4},{3,5},{4,2},{5,3},{6,0},{7,1},{8,14},{9,15},{10,... | collective-permute-start | bytes 442376 | tf_op jit(solution)/shard_map/ppermute | solution.py:866
  135.3 1.1 copy-start.13
  136.5 11.9 %copy-start.21 = (bf16[144,512]{1,0:T(8,128)(2,1)S(1)}, bf16[144,512]{1,0:T(8,128)(2,1)}, u32[]{:S(2)}) copy-start(bf16[144,512]{1,0:T(8,128)(2,1)} %get-tuple-element.134.rest_0_) | copy-start | bytes 442372
  136.5 27.7 %copy-start.14 = (f32[144,1024]{1,0:T(8,128)S(1)}, f32[144,1024]{1,0:T(8,128)}, u32[]{:S(2)}) copy-start(f32[144,1024]{1,0:T(8,128)} %get-tuple-element.115.ngrad_ref) | copy-start | bytes 1769476
  137.1 12.9 %collective-permute-start.27 = (bf16[192,256]{1,0:T(8,128)(2,1)S(1)}, bf16[192,256]{1,0:T(8,128)(2,1)S(1)}, u32[]{:S(2)}, u32[]{:S(2)}) collective-permute-start(bf16[192,256]{1,0:T(8,128)(2,1)S(1)} %get-tuple-element.149), channel_id=1, source_target_pairs={{0,8},{8,0},{16,24},{24,16},{1,9},{9,1},{17,25},{25,17},{2,10},{10... | collective-permute-start | bytes 294920 | tf_op jit(solution)/shard_map/ppermute | solution.py:866
  138.6 11.5 %collective-permute-start.28 = (bf16[192,256]{1,0:T(8,128)(2,1)S(1)}, bf16[192,256]{1,0:T(8,128)(2,1)S(1)}, u32[]{:S(2)}, u32[]{:S(2)}) collective-permute-start(bf16[192,256]{1,0:T(8,128)(2,1)S(1)} %get-tuple-element.150), channel_id=1, source_target_pairs={{0,16},{8,24},{16,0},{24,8},{1,17},{9,25},{17,1},{25,9},{2,18},{10... | collective-permute-start | bytes 294920 | tf_op jit(solution)/shard_map/ppermute | solution.py:866
  140.2 10.0 %collective-permute-start.29 = (bf16[192,256]{1,0:T(8,128)(2,1)S(1)}, bf16[192,256]{1,0:T(8,128)(2,1)S(1)}, u32[]{:S(2)}, u32[]{:S(2)}) collective-permute-start(bf16[192,256]{1,0:T(8,128)(2,1)S(1)} %get-tuple-element.151), channel_id=1, source_target_pairs={{0,24},{8,16},{16,8},{24,0},{1,25},{9,17},{17,9},{25,1},{2,26},{10... | collective-permute-start | bytes 294920 | tf_op jit(solution)/shard_map/ppermute | solution.py:866
  141.7 1.0 copy-start.10
  144.4 29.7 %copy-start.30 = (f32[2048,16]{0,1:T(8,128)S(1)}, f32[2048,16]{0,1:T(8,128)}, u32[]{:S(2)}) copy-start(f32[2048,16]{0,1:T(8,128)} %param.22) | copy-start | bytes 393220
  147.8 17.7 %collective-permute-start.37 = (bf16[128,2048]{1,0:T(8,128)(2,1)S(1)}, bf16[128,2048]{1,0:T(8,128)(2,1)S(1)}, u32[]{:S(2)}, u32[]{:S(2)}) collective-permute-start(bf16[128,2048]{1,0:T(8,128)(2,1)S(1)} %get-tuple-element.168), channel_id=1, source_target_pairs={{0,1},{1,0},{2,3},{3,2},{4,5},{5,4},{6,7},{7,6},{8,9},{9,8},{10,11... | collective-permute-start | bytes 1572872 | tf_op jit(solution)/shard_map/ppermute | solution.py:866
  147.8 22.4 %collective-permute-start.22 = (bf16[1024,256]{1,0:T(8,128)(2,1)S(1)}, bf16[1024,256]{1,0:T(8,128)(2,1)S(1)}, u32[]{:S(2)}, u32[]{:S(2)}) collective-permute-start(bf16[1024,256]{1,0:T(8,128)(2,1)S(1)} %get-tuple-element.141), channel_id=1, source_target_pairs={{0,1},{1,0},{2,3},{3,2},{4,5},{5,4},{6,7},{7,6},{8,9},{9,8},{10,11... | collective-permute-start | bytes 1572872 | tf_op jit(solution)/shard_map/ppermute | solution.py:866
  149.9 21.4 %collective-permute-start.21 = (bf16[1024,256]{1,0:T(8,128)(2,1)S(1)}, bf16[1024,256]{1,0:T(8,128)(2,1)S(1)}, u32[]{:S(2)}, u32[]{:S(2)}) collective-permute-start(bf16[1024,256]{1,0:T(8,128)(2,1)S(1)} %get-tuple-element.139), channel_id=1, source_target_pairs={{0,1},{1,0},{2,3},{3,2},{4,5},{5,4},{6,7},{7,6},{8,9},{9,8},{10,11... | collective-permute-start | bytes 1572872 | tf_op jit(solution)/shard_map/ppermute | solution.py:866
  150.2 6.8 %collective-permute-start.30 = (bf16[192,256]{1,0:T(8,128)(2,1)S(1)}, bf16[192,256]{1,0:T(8,128)(2,1)S(1)}, u32[]{:S(2)}, u32[]{:S(2)}) collective-permute-start(bf16[192,256]{1,0:T(8,128)(2,1)S(1)} %add_convert_fusion.refs_0_), channel_id=1, source_target_pairs={{0,2},{1,3},{2,0},{3,1},{4,6},{5,7},{6,4},{7,5},{8,10},{9,11},{10,... | collective-permute-start | bytes 294920 | tf_op jit(solution)/shard_map/ppermute | solution.py:866
  150.7 8.2 %collective-permute-start.31 = (bf16[192,256]{1,0:T(8,128)(2,1)S(1)}, bf16[192,256]{1,0:T(8,128)(2,1)S(1)}, u32[]{:S(2)}, u32[]{:S(2)}) collective-permute-start(bf16[192,256]{1,0:T(8,128)(2,1)S(1)} %add_convert_fusion.refs_0_), channel_id=1, source_target_pairs={{0,4},{1,5},{2,6},{3,7},{4,0},{5,1},{6,2},{7,3},{8,12},{9,13},{10,... | collective-permute-start | bytes 294920 | tf_op jit(solution)/shard_map/ppermute | solution.py:866
  157.0 6.4 %collective-permute-start.32 = (bf16[192,256]{1,0:T(8,128)(2,1)S(1)}, bf16[192,256]{1,0:T(8,128)(2,1)S(1)}, u32[]{:S(2)}, u32[]{:S(2)}) collective-permute-start(bf16[192,256]{1,0:T(8,128)(2,1)S(1)} %add_convert_fusion.refs_0_), channel_id=1, source_target_pairs={{0,6},{1,7},{2,4},{3,5},{4,2},{5,3},{6,0},{7,1},{8,14},{9,15},{10,... | collective-permute-start | bytes 294920 | tf_op jit(solution)/shard_map/ppermute | solution.py:866
  164.1 8.7 %collective-permute-start.33 = (bf16[192,256]{1,0:T(8,128)(2,1)S(1)}, bf16[192,256]{1,0:T(8,128)(2,1)S(1)}, u32[]{:S(2)}, u32[]{:S(2)}) collective-permute-start(bf16[192,256]{1,0:T(8,128)(2,1)S(1)} %small_sum.1), channel_id=1, source_target_pairs={{0,8},{8,0},{16,24},{24,16},{1,9},{9,1},{17,25},{25,17},{2,10},{10... | collective-permute-start | bytes 294920 | tf_op jit(solution)/shard_map/ppermute | solution.py:866
  164.2 3.6 %collective-permute-start.11 = (f32[16,1024]{1,0:T(8,128)S(1)}, f32[16,1024]{1,0:T(8,128)S(1)}, u32[]{:S(2)}, u32[]{:S(2)}) collective-permute-start(f32[16,1024]{1,0:T(8,128)S(1)} %slice.10), channel_id=1, source_target_pairs={{1,0},{2,1},{3,2},{4,3},{5,4},{6,5},{7,6},{9,8},{10,9},{11,10},{12... | collective-permute-start | bytes 196616 | tf_op jit(solution)/shard_map/ppermute | solution.py:1018
  166.2 13.7 %collective-permute-start.38 = (bf16[32,2048]{1,0:T(8,128)(2,1)S(1)}, bf16[32,2048]{1,0:T(8,128)(2,1)S(1)}, u32[]{:S(2)}, u32[]{:S(2)}) collective-permute-start(bf16[32,2048]{1,0:T(8,128)(2,1)S(1)} %get-tuple-element.170), channel_id=1, source_target_pairs={{0,2},{1,3},{2,0},{3,1},{4,6},{5,7},{6,4},{7,5},{8,10},{9,11},{10,... | collective-permute-start | bytes 393224 | tf_op jit(solution)/shard_map/ppermute | solution.py:866
  167.8 13.7 %collective-permute-start.39 = (bf16[32,2048]{1,0:T(8,128)(2,1)S(1)}, bf16[32,2048]{1,0:T(8,128)(2,1)S(1)}, u32[]{:S(2)}, u32[]{:S(2)}) collective-permute-start(bf16[32,2048]{1,0:T(8,128)(2,1)S(1)} %get-tuple-element.171), channel_id=1, source_target_pairs={{0,4},{1,5},{2,6},{3,7},{4,0},{5,1},{6,2},{7,3},{8,12},{9,13},{10,... | collective-permute-start | bytes 393224 | tf_op jit(solution)/shard_map/ppermute | solution.py:866
  170.2 11.3 %collective-permute-start.40 = (bf16[32,2048]{1,0:T(8,128)(2,1)S(1)}, bf16[32,2048]{1,0:T(8,128)(2,1)S(1)}, u32[]{:S(2)}, u32[]{:S(2)}) collective-permute-start(bf16[32,2048]{1,0:T(8,128)(2,1)S(1)} %get-tuple-element.172), channel_id=1, source_target_pairs={{0,6},{1,7},{2,4},{3,5},{4,2},{5,3},{6,0},{7,1},{8,14},{9,15},{10,... | collective-permute-start | bytes 393224 | tf_op jit(solution)/shard_map/ppermute | solution.py:866
  171.3 6.1 %collective-permute-start.34 = (bf16[192,256]{1,0:T(8,128)(2,1)S(1)}, bf16[192,256]{1,0:T(8,128)(2,1)S(1)}, u32[]{:S(2)}, u32[]{:S(2)}) collective-permute-start(bf16[192,256]{1,0:T(8,128)(2,1)S(1)} %small_sum.1), channel_id=1, source_target_pairs={{0,16},{8,24},{16,0},{24,8},{1,17},{9,25},{17,1},{25,9},{2,18},{10... | collective-permute-start | bytes 294920 | tf_op jit(solution)/shard_map/ppermute | solution.py:866
  172.8 6.9 %collective-permute-start.35 = (bf16[192,256]{1,0:T(8,128)(2,1)S(1)}, bf16[192,256]{1,0:T(8,128)(2,1)S(1)}, u32[]{:S(2)}, u32[]{:S(2)}) collective-permute-start(bf16[192,256]{1,0:T(8,128)(2,1)S(1)} %small_sum.1), channel_id=1, source_target_pairs={{0,24},{8,16},{16,8},{24,0},{1,25},{9,17},{17,9},{25,1},{2,26},{10... | collective-permute-start | bytes 294920 | tf_op jit(solution)/shard_map/ppermute | solution.py:866
  177.4 9.5 %collective-permute-start.23 = (bf16[1024,128]{1,0:T(8,128)(2,1)S(1)}, bf16[1024,128]{1,0:T(8,128)(2,1)S(1)}, u32[]{:S(2)}, u32[]{:S(2)}) collective-permute-start(bf16[1024,128]{1,0:T(8,128)(2,1)S(1)} %get-tuple-element.143), channel_id=1, source_target_pairs={{0,8},{8,0},{16,24},{24,16},{1,9},{9,1},{17,25},{25,17},{2,10},{10... | collective-permute-start | bytes 786440 | tf_op jit(solution)/shard_map/ppermute | solution.py:866
  179.8 13.0 %collective-permute-start.24 = (bf16[1024,128]{1,0:T(8,128)(2,1)S(1)}, bf16[1024,128]{1,0:T(8,128)(2,1)S(1)}, u32[]{:S(2)}, u32[]{:S(2)}) collective-permute-start(bf16[1024,128]{1,0:T(8,128)(2,1)S(1)} %get-tuple-element.144), channel_id=1, source_target_pairs={{0,16},{8,24},{16,0},{24,8},{1,17},{9,25},{17,1},{25,9},{2,18},{10... | collective-permute-start | bytes 786440 | tf_op jit(solution)/shard_map/ppermute | solution.py:866
  180.0 12.8 %collective-permute-start.25 = (bf16[1024,128]{1,0:T(8,128)(2,1)S(1)}, bf16[1024,128]{1,0:T(8,128)(2,1)S(1)}, u32[]{:S(2)}, u32[]{:S(2)}) collective-permute-start(bf16[1024,128]{1,0:T(8,128)(2,1)S(1)} %get-tuple-element.145), channel_id=1, source_target_pairs={{0,24},{8,16},{16,8},{24,0},{1,25},{9,17},{17,9},{25,1},{2,26},{10... | collective-permute-start | bytes 786440 | tf_op jit(solution)/shard_map/ppermute | solution.py:866
  181.5 12.2 %collective-permute-start.36 = (bf16[4,192,256]{2,1,0:T(8,128)(2,1)S(1)}, bf16[4,192,256]{2,1,0:T(8,128)(2,1)S(1)}, u32[]{:S(2)}, u32[]{:S(2)}) collective-permute-start(bf16[4,192,256]{2,1,0:T(8,128)(2,1)S(1)} %pad_maximum_fusion.mine_ref), channel_id=1, source_target_pairs={{0,1},{1,0},{2,3},{3,2},{4,5},{5,4},{6,7},{7,6},{8,9},{9,8},{10,11... | collective-permute-start | bytes 1179656 | tf_op jit(solution)/shard_map/ppermute | solution.py:866
  (8 other events, 6.5 us)

commit v3 on v1

v3 whole, which is shorter than its diff:
```python
import functools

import jax
import jax.numpy as jnp
from jax import lax
from jax.experimental import pallas as pl
from jax.experimental.pallas import tpu as pltpu
from jax.sharding import PartitionSpec as P

epsilon = 1e-05
LANES = 128
SUBS = 8
FAR = 1e36
LEAST_RATE = 1e-33
LN2 = 0.6931471805599453
EDGE = 16
UNROLL = 8
bf16, f32 = jnp.bfloat16, jnp.float32
SMEM_SPEC = pl.BlockSpec(memory_space=pltpu.SMEM)


def nt(a, b):
    return lax.dot_general(a, b, (((1,), (1,)), ((), ())), preferred_element_type=f32)


def tn(a, b):
    return lax.dot_general(a, b, (((0,), (0,)), ((), ())), preferred_element_type=f32)


def nn(a, b):
    return jnp.dot(a, b, preferred_element_type=f32)


def plain_call(kernel, name, out_shape, args, us, scratch=(), limit=12):
    full = lambda x: pl.BlockSpec(x.shape, lambda: (0,) * len(x.shape))
    return pl.pallas_call(
        kernel,
        in_specs=[SMEM_SPEC] + [full(x) for x in args[1:]],
        out_specs=[full(x) for x in out_shape],
        out_shape=out_shape,
        scratch_shapes=list(scratch),
        compiler_params=pltpu.CompilerParams(vmem_limit_bytes=limit << 20),
        cost_estimate=pl.CostEstimate(flops=0, bytes_accessed=int(us * 3.6e6), transcendentals=0),
        name=name,
    )(*args)


def softplus(v):
    return jnp.maximum(v, 0.0) + jnp.log1p(jnp.exp(-jnp.abs(v)))


def tile_at(start, size=LANES):
    return pl.ds(pl.multiple_of(start, LANES), size)


def step_rows(t):
    return pl.ds(pl.multiple_of(t * SUBS, SUBS), SUBS)


def tap_masks(info_ref, docs, taps, length):
    row = lax.broadcasted_iota(jnp.int32, (length, LANES), 0)
    place = info_ref[0] + (row % SUBS) * (length // SUBS) + row // SUBS
    begin = jnp.zeros_like(place)
    reset = jnp.zeros((length, LANES), f32)
    for k in range(docs):
        start = info_ref[1 + k]
        begin = jnp.maximum(begin, jnp.where(place >= start, start, 0))
        reset = jnp.where(place == start, 1.0, reset)
    return [reset] + [jnp.where(begin <= place - j, 1.0, 0.0) for j in range(1, taps)]


def turned(x, plain):
    length = x.shape[0]
    steps = length // SUBS
    a = lax.broadcasted_iota(jnp.int32, (length, length), 1 - plain)
    b = lax.broadcasted_iota(jnp.int32, (length, length), plain + 0)
    turn = jnp.where(b == (a % steps) * SUBS + a // steps, 1.0, 0.0).astype(bf16)
    return nn(turn, x).astype(bf16)


def spread(maps, table_ref, first, width):
    high = maps.astype(bf16)
    rest = maps - high.astype(f32)
    middle = rest.astype(bf16)
    low = (rest - middle.astype(f32)).astype(bf16)
    row = lax.broadcasted_iota(jnp.int32, (LANES, width * LANES), 0)
    lane = lax.broadcasted_iota(jnp.int32, (LANES, width * LANES), 1)
    ones = jnp.where(row == first + lane // LANES, 1.0, 0.0).astype(bf16)
    table_ref[...] = nn(high, ones) + nn(middle, ones) + nn(low, ones)


def sub_scan(decay, value, forward):
    row = lax.broadcasted_iota(jnp.int32, decay.shape, 0)
    if not forward:
        row = SUBS - 1 - row

    def moved(x, by, fill):
        return jnp.where(row < by, fill, pltpu.roll(x, by if forward else SUBS - by, 0))

    by = 1
    while by < SUBS:
        d, v = moved(decay, by, 1.0), moved(value, by, 0.0)
        value = decay * v + value
        decay = decay * d
        by *= 2
    return value, moved(decay, 1, 1.0), moved(value, 1, 0.0)


def conv_windows(ext, taps, length):
    return [ext[(taps - 1 - j) * SUBS : (taps - 1 - j) * SUBS + length] for j in range(taps)]


def conv_sum(windows, masks, vec_ref, at, taps):
    out = vec_ref[pl.ds(taps, 1), at] + vec_ref[pl.ds(taps - 1, 1), at] * windows[0]
    for j in range(1, taps):
        out = out + vec_ref[pl.ds(taps - 1 - j, 1), at] * windows[j] * masks[j]
    return out


def normalise(x, gain):
    wide = x.astype(f32)
    inv = lax.rsqrt(jnp.mean(wide * wide, axis=-1, keepdims=True) + epsilon)
    return (wide * inv * gain).astype(bf16)


def front_kernel(
    states, rank, taps, docs, rows_size,
    info_ref, tok_ref, left_ref, cot_ref, gain_ref, vec_ref, rates_ref, dtw_ref, win_ref, wo_ref, wx_ref,
    tok_out, cot_out, ext_ref, inner_ref, gate_ref, ggated_ref, gs_ref, dt_ref, proj_ref, table, pack_ref,
    dx_ref, ex_ref, db_ref, fx_ref, *rest,
):
    blocks, (normed, masks, dtm_s, u_s, ends) = rest[:rows_size], rest[rows_size:]
    length, model = cot_ref.shape
    width = rates_ref.shape[1]
    steps = length // SUBS
    rim = taps - 1
    maps = rank + 2 * states

    tok_out[pl.ds(0, length), :] = turned(tok_ref[...], False)
    left = left_ref[...].astype(f32)
    tok_out[pl.ds(length, EDGE), :] = jnp.concatenate([left, jnp.zeros((EDGE - rim, model), f32)], axis=0).astype(bf16)
    cot = turned(cot_ref[...], False)
    cot_out[...] = cot
    thin = model // rows_size
    for k in range(rows_size):
        blocks[k][:, :model] = tok_out[pl.ds(0, length), :]
        for q in range(rows_size):

            @pl.when((info_ref[3 + docs] ^ k) == q)
            def _():
                blocks[k][:, model:] = cot[:, q * thin : (q + 1) * thin]

    normed[...] = normalise(tok_out[...], gain_ref[...])
    for k, mask in enumerate(tap_masks(info_ref, docs, taps, length)):
        masks[k] = mask
    proj_ref[...] = jnp.zeros_like(proj_ref)
    block = min(512, width)

    def project(j, _):
        wide = tile_at(j * block, block)
        conv = nn(normed[...], win_ref[:, wide]).astype(bf16)
        gate = nn(normed[pl.ds(0, length), :], win_ref[:, tile_at(width + j * block, block)])
        ggated = nt(cot_out[...], wo_ref[wide, :])
        gate_ref[:, wide] = gate
        ggated_ref[:, wide] = ggated
        gs_ref[:, wide] = ggated * gate * jax.nn.sigmoid(gate)
        row = lax.broadcasted_iota(jnp.int32, (SUBS, LANES), 0)
        mask = [masks[k] for k in range(taps)]
        for tile in range(block // LANES):
            far = tile_at(j * block + tile * LANES)
            part = conv[:, tile * LANES : (tile + 1) * LANES].astype(f32)
            pieces = []
            for b in range(rim):
                first = length - (rim - b) * SUBS
                moved = pltpu.roll(part[first : first + SUBS], 1, 0)
                pieces.append(jnp.where(row == 0, part[length + b : length + b + 1], moved))
            ext = jnp.concatenate(pieces + [part[:length]], axis=0)
            pad = jnp.zeros((2 * EDGE - rim * SUBS, LANES), f32)
            ext_ref[:, far] = jnp.concatenate([pad, ext], axis=0).astype(bf16)
            pre = conv_sum(conv_windows(ext, taps, length), mask, vec_ref, far, taps)
            inner_ref[:, far] = (pre * jax.nn.sigmoid(pre)).astype(bf16)
        proj_ref[:, :maps] += nt(inner_ref[:, wide], wx_ref[:, wide])
        return 0

    lax.fori_loop(0, width // block, project, 0)
    spread(proj_ref[...], table, rank, 2 * states)
    ends[...] = jnp.zeros_like(ends)
    half = states // 2
    zero = jnp.zeros((SUBS, LANES), f32)
    one = jnp.ones((SUBS, LANES), f32)
    low = proj_ref[:, :rank].astype(bf16)

    def scan(tile, _):
        at = tile_at(tile * LANES)
        dt = softplus(nn(low, dtw_ref[:, at]) + vec_ref[pl.ds(taps + 1, 1), at])
        dt_ref[:, at] = dt
        u_s[...] = dt * inner_ref[:, at].astype(f32)
        dtm = jnp.where(masks[0] > 0.0, FAR, dt)
        dtm_s[...] = dtm
        span = jnp.sum(dtm, axis=0, keepdims=True)
        high = span.astype(bf16).astype(f32)
        middle = (span - high).astype(bf16).astype(f32)
        ends[pl.ds(2 * states, 1), at] = high
        ends[pl.ds(2 * states + 1, 1), at] = middle
        ends[pl.ds(2 * states + 2, 1), at] = span - high - middle
        for first in range(0, states, half):
            rates = [jnp.broadcast_to(rates_ref[pl.ds(first + k, 1), at], (SUBS, LANES)) for k in range(half)]

            def lap(t, carry):
                h, f, p = carry
                rows = step_rows(t)
                d, u, g = dtm_s[rows, :], u_s[rows, :], gs_ref[rows, at]
                hn, fn, pn = [], [], []
                for k in range(half):
                    n = first + k
                    a = jnp.exp2(d * rates[k])
                    hn.append(a * h[k] + u * table[rows, n * LANES : (n + 1) * LANES])
                    q = p[k] * a
                    pn.append(q)
                    n += states
                    fn.append(f[k] + q * (g * table[rows, n * LANES : (n + 1) * LANES]))
                return tuple(hn), tuple(fn), tuple(pn)

            start = ((zero,) * half, (zero,) * half, (one,) * half)
            h, f, p = lax.fori_loop(0, steps, lap, start, unroll=UNROLL)
            for k in range(half):
                n = first + k
                e_in, d_ex, e_ex = sub_scan(p[k], h[k], True)
                f_in, b_ex, f_ex = sub_scan(p[k], f[k], False)
                ends[pl.ds(n, 1), at] = e_in[SUBS - 1 :, :]
                ends[pl.ds(states + n, 1), at] = f_in[:1, :]
                dx_ref[n, :, at] = d_ex
                ex_ref[n, :, at] = e_ex
                db_ref[n, :, at] = b_ex
                fx_ref[n, :, at] = f_ex
        return 0

    lax.fori_loop(0, width // LANES, scan, 0)
    pack_ref[...] = ends[...].astype(bf16)


def front(info, tok, left, cot, gain, vec, rates, dtw, in_weight, out_weight, wx, taps, docs, rows_size):
    length, model = cot.shape
    states, width = rates.shape
    rank = dtw.shape[0]
    pack_rows = 2 * states + EDGE
    shape = jax.ShapeDtypeStruct
    big = lambda dtype: shape((length, width), dtype)
    out = [
        shape((length + EDGE, model), bf16), shape((length, model), bf16), shape((length + 2 * EDGE, width), bf16),
        big(bf16), big(f32), big(f32), big(f32), big(f32),
        shape((length, LANES), f32), shape((length, 2 * states * LANES), f32), shape((pack_rows, width), bf16),
    ] + [shape((states, SUBS, width), f32)] * 4 + [shape((length, model + model // rows_size), bf16)] * rows_size
    scratch = [
        pltpu.VMEM((length + EDGE, model), bf16),
        pltpu.VMEM((taps, length, LANES), f32),
        pltpu.VMEM((length, LANES), f32),
        pltpu.VMEM((length, LANES), f32),
        pltpu.VMEM((pack_rows, width), f32),
    ]
    return plain_call(
        functools.partial(front_kernel, states, rank, taps, docs, rows_size), "front", out,
        (info, tok, left, cot, gain, vec, rates, dtw, in_weight, out_weight, wx), 18, scratch, 10,
    )


def halves_of(near, far):
    lane = lax.broadcasted_iota(jnp.int32, near.shape, 1)
    half = LANES // 2
    low = jnp.where(lane < half, near, pltpu.roll(far, half, 1))
    high = jnp.where(lane < half, pltpu.roll(near, half, 1), far)
    return low.astype(bf16), high.astype(bf16)


def forward_kernel(
    states, taps, docs, slices,
    info_ref, vec_ref, rates_ref, entry_ref, table, dt_ref, inner_ref, gate_ref, ggated_ref, dx_ref, ex_ref,
    gated_ref, ggate_ref, *rest,
):
    blocks, (reset, dtm_s, u_s, y_s, held) = rest[:slices], rest[slices:]
    length, width = inner_ref.shape
    tiles, steps = width // LANES, length // SUBS
    zero = jnp.zeros((SUBS, LANES), f32)
    reset[...] = tap_masks(info_ref, docs, 1, length)[0]

    def scan(tile, _):
        at = tile_at(tile * LANES)
        dt = dt_ref[:, at]
        x = inner_ref[:, at].astype(f32)
        dtm_s[...] = jnp.where(reset[...] > 0.0, FAR, dt)
        u_s[...] = dt * x

        def wide(ref, n):
            return jnp.broadcast_to(ref[pl.ds(n, 1), at], (SUBS, LANES))

        rates = [wide(rates_ref, n) for n in range(states)]
        start = tuple(dx_ref[n, :, at] * wide(entry_ref, n) + ex_ref[n, :, at] for n in range(states))

        def lap(t, h):
            rows = step_rows(t)
            d, u = dtm_s[rows, :], u_s[rows, :]
            new, y = [], [zero, zero]
            for n in range(states):
                now = jnp.exp2(d * rates[n]) * h[n] + u * table[rows, n * LANES : (n + 1) * LANES]
                y[n % 2] = y[n % 2] + now * table[rows, (states + n) * LANES : (states + n + 1) * LANES]
                new.append(now)
            y_s[rows, :] = y[0] + y[1]
            return tuple(new)

        lax.fori_loop(0, steps, lap, start, unroll=UNROLL)
        scanned = y_s[...] + vec_ref[pl.ds(taps + 2, 1), at] * x
        gate = gate_ref[:, at]
        sig = jax.nn.sigmoid(gate)
        gated_ref[:, at] = (scanned * gate * sig).astype(bf16)
        ggate = (ggated_ref[:, at] * scanned * (sig * (1.0 + gate * (1.0 - sig)))).astype(bf16)
        ggate_ref[:, at] = ggate
        return 0

    lax.fori_loop(0, tiles, scan, 0)
    if not slices:
        return
    for pair in range(tiles // 2):
        side, spot = pair // (tiles // 4), pair % (tiles // 4)
        near, far = (ggate_ref[:, (2 * pair + n) * LANES : (2 * pair + n + 1) * LANES].astype(f32) for n in range(2))
        at = pl.ds(spot * LANES, LANES)
        held[side, :, at], held[side + 2, :, at] = halves_of(near, far)
    for n in range(slices):
        blocks[n][:, :width] = gated_ref[...]
        blocks[n][:, width:] = held[info_ref[3 + docs] ^ n]


def forward(info, vec, rates, entry, table, dt, inner, gate, ggated, dx, ex, taps, docs, slices):
    length, width = inner.shape
    states = rates.shape[0]
    shape = jax.ShapeDtypeStruct
    return plain_call(
        functools.partial(forward_kernel, states, taps, docs, slices),
        "forward",
        [shape((length, width), bf16)] * 2 + [shape((length, width + width // max(slices, 1)), bf16)] * slices,
        (info, vec, rates, entry, table, dt, inner, gate, ggated, dx, ex),
        8,
        [pltpu.VMEM((length, LANES), f32)] * 4 + [pltpu.VMEM((max(slices, 1), length, width // max(slices, 1)), bf16)],
        8,
    )


def backward_kernel(
    states, rank, taps, docs, slices,
    info_ref, proj_ref, tok_ref, gain_ref, dtw_ref, vec_ref, rates_ref, entry_ref, arrive_ref, table,
    dt_ref, inner_ref, gs_ref, dx_ref, ex_ref, db_ref, fx_ref, ggate_ref, ext_ref, win_ref, wx_ref,
    mine_ref, theirs_ref, ngrad, *rest,
):
    blocks = rest[: max(slices, 1)]
    (acc, hs, decays, masks, dtm_s, u_s, s1_s, s2_s, isg, raw_s, sent_s, low_acc, pg, small, held) = rest[max(slices, 1) :]
    length, width = inner_ref.shape
    model = tok_ref.shape[1]
    steps, tiles = length // SUBS, width // LANES
    rim = taps - 1
    maps = rank + 2 * states
    row_dtw = maps
    row_rate = row_dtw + rank
    row_taps = row_rate + states
    row_dtb, row_skip, row_cb, row_gain = (row_taps + taps + k for k in range(4))
    zero = jnp.zeros((SUBS, LANES), f32)
    half = states // 2
    block = min(512, width)

    for k, mask in enumerate(tap_masks(info_ref, docs, taps, length)):
        masks[k] = mask
    low_acc[...] = jnp.zeros_like(low_acc)
    small[pl.ds(small.shape[0] - EDGE, EDGE), :] = jnp.zeros((EDGE, width), f32)
    low = proj_ref[:, :rank].astype(bf16)

    def clear(t, _):
        acc[step_rows(t), :] = jnp.zeros((SUBS, acc.shape[1]), f32)
        return 0

    lax.fori_loop(0, steps, clear, 0)

    def scan(tile, _):
        at = tile_at(tile * LANES)
        dt = dt_ref[:, at]
        x = inner_ref[:, at].astype(f32)
        dtm_s[...] = jnp.where(masks[0] > 0.0, FAR, dt)
        u_s[...] = dt * x

        def wide(ref, n):
            return jnp.broadcast_to(ref[pl.ds(n, 1), at], (SUBS, LANES))

        rates = [wide(rates_ref, n) for n in range(states)]
        start = []
        for n in range(states):
            h0 = dx_ref[n, :, at] * wide(entry_ref, n) + ex_ref[n, :, at]
            hs[0, n] = h0
            start.append(h0)

        def lap(t, h):
            rows = step_rows(t)
            d, u = dtm_s[rows, :], u_s[rows, :]
            new = []
            for n in range(states):
                a = jnp.exp2(d * rates[n])
                decays[t, n] = a
                now = a * h[n] + u * table[rows, n * LANES : (n + 1) * LANES]
                hs[t + 1, n] = now
                new.append(now)
            return tuple(new)

        lax.fori_loop(0, steps, lap, tuple(start), unroll=UNROLL)
        for first in range(0, states, half):
            some = rates[first : first + half]

            def back(k, carry):
                f, r = carry
                t = steps - 1 - k
                rows = step_rows(t)
                dtt, g, u = dt_ref[rows, at], gs_ref[rows, at], u_s[rows, :]
                fn, rn, s1, s2 = [], [], zero, zero
                for k in range(half):
                    n = first + k
                    into, out = (slice(m * LANES, (m + 1) * LANES) for m in (n, states + n))
                    adj = g * table[rows, out] + f[k]
                    acc[rows, into] += adj * u
                    acc[rows, out] += g * hs[t + 1, n]
                    s1 = s1 + adj * table[rows, into]
                    flow = decays[t, n] * adj
                    fn.append(flow)
                    flow = flow * hs[t, n]
                    s2 = s2 + flow * some[k]
                    rn.append(r[k] + flow * dtt)
                if first == 0:
                    s1_s[rows, :] = s1
                    s2_s[rows, :] = s2
                else:
                    s1_s[rows, :] += s1
                    s2_s[rows, :] += s2
                return tuple(fn), tuple(rn)

            f0 = tuple(
                db_ref[first + k, :, at] * wide(arrive_ref, first + k) + fx_ref[first + k, :, at] for k in range(half)
            )
            _, r = lax.fori_loop(0, steps, back, (f0, (zero,) * half), unroll=UNROLL)
            for k in range(half):
                small[pl.ds(row_rate + first + k, 1), at] = jnp.sum(r[k], axis=0, keepdims=True)
        s1, gs = s1_s[...], gs_ref[:, at]
        step_grad = s1 * x + LN2 * s2_s[...]
        isg[:, at] = s1 * dt + gs * vec_ref[pl.ds(taps + 2, 1), at]
        raw = nn(low, dtw_ref[:, at]) + vec_ref[pl.ds(taps + 1, 1), at]
        raw_grad = step_grad * jax.nn.sigmoid(raw)
        raw_s[:, at] = raw_grad.astype(bf16)
        small[pl.ds(row_dtb, 1), at] = jnp.sum(raw_grad, axis=0, keepdims=True)
        small[pl.ds(row_skip, 1), at] = jnp.sum(gs * x, axis=0, keepdims=True)
        return 0

    lax.fori_loop(0, tiles, scan, 0)

    def low_part(j, _):
        wide = tile_at(j * block, block)
        small[pl.ds(row_dtw, rank), wide] = tn(low, raw_s[:, wide])
        low_acc[:, :rank] += nt(raw_s[:, wide], dtw_ref[:, wide])
        return 0

    lax.fori_loop(0, width // block, low_part, 0)
    lane = lax.broadcasted_iota(jnp.int32, (SUBS, LANES), 1)

    def gather_maps(t, _):
        rows = step_rows(t)
        out = low_acc[rows, :]
        for n in range(2 * states):
            part = jnp.sum(acc[rows, n * LANES : (n + 1) * LANES], axis=1, keepdims=True)
            out = jnp.where(lane == rank + n, part, out)
        low_acc[rows, :] = out
        return 0

    lax.fori_loop(0, steps, gather_maps, 0)
    pg[...] = low_acc[...].astype(bf16)
    ngrad[...] = jnp.zeros_like(ngrad)

    def close(j, _):
        wide = tile_at(j * block, block)
        ngrad[pl.ds(0, length), :] += nt(ggate_ref[:, wide], win_ref[:, tile_at(width + j * block, block)])
        small[pl.ds(0, maps), wide] = tn(pg[...], inner_ref[:, wide])[:maps]
        inner_grad = isg[:, wide] + nn(pg[:, :maps], wx_ref[:, wide])
        mask = [masks[k] for k in range(taps)]
        row = lax.broadcasted_iota(jnp.int32, (SUBS, LANES), 0)
        for tile in range(block // LANES):
            far = tile_at(j * block + tile * LANES)
            ext = ext_ref[:, far].astype(f32)[2 * EDGE - rim * SUBS :]
            windows = conv_windows(ext, taps, length)
            pre = conv_sum(windows, mask, vec_ref, far, taps)
            sig = jax.nn.sigmoid(pre)
            grad = inner_grad[:, tile * LANES : (tile + 1) * LANES] * (sig * (1.0 + pre * (1.0 - sig)))
            small[pl.ds(row_cb, 1), far] = jnp.sum(grad, axis=0, keepdims=True)
            small[pl.ds(row_taps + rim, 1), far] = jnp.sum(grad * windows[0], axis=0, keepdims=True)
            near = [grad[step * SUBS : (step + 1) * SUBS] * vec_ref[pl.ds(rim, 1), far] for step in range(steps)]
            head = [zero] * rim
            for k in range(1, taps):
                masked = grad * mask[k]
                small[pl.ds(row_taps + rim - k, 1), far] = jnp.sum(masked * windows[k], axis=0, keepdims=True)
                masked = masked * vec_ref[pl.ds(rim - k, 1), far]
                for step in range(steps):
                    piece = masked[step * SUBS : (step + 1) * SUBS]
                    if step >= k:
                        near[step - k] = near[step - k] + piece
                    else:
                        head[rim + step - k] = head[rim + step - k] + piece
            edge = zero
            for b in range(rim):
                moved = jnp.where(row == SUBS - 1, 0.0, pltpu.roll(head[b], SUBS - 1, 0))
                near[steps - rim + b] = near[steps - rim + b] + moved
                edge = jnp.where(row == b, jnp.broadcast_to(head[b][:1], (SUBS, LANES)), edge)
            sent = jnp.concatenate(near + [edge, zero], axis=0)
            sent_s[:, tile * LANES : (tile + 1) * LANES] = sent.astype(bf16)
            if not slices:
                blocks[0][:, far] = sent.astype(bf16)
            elif tile % 2 == 1:
                pair = j * (block // LANES // 2) + tile // 2
                side, spot = pair // (tiles // 4), tile_at(pair % (tiles // 4) * LANES)
                held[side, :, spot], held[side + 2, :, spot] = halves_of(last, sent)
            last = sent
        ngrad[...] += nt(sent_s[...], win_ref[:, wide])
        return 0

    lax.fori_loop(0, width // block, close, 0)
    x = tok_ref[...].astype(f32)
    inv = lax.rsqrt(jnp.mean(x * x, axis=-1, keepdims=True) + epsilon)
    small[pl.ds(row_gain, 1), pl.ds(0, model)] = jnp.sum(ngrad[...] * (x * inv), axis=0, keepdims=True)
    if slices:
        part = width // slices
        row = lax.broadcasted_iota(jnp.int32, (EDGE, part), 0)
        extra = jnp.zeros((EDGE, part), f32)
        normed = x[length:] * inv[length:] * gain_ref[...]
        count = model // part
        for b in range(rim):
            for c in range(count):
                piece = jnp.broadcast_to(normed[b : b + 1, c * part : (c + 1) * part], (EDGE, part))
                extra = jnp.where(row == rim + b * count + c, piece, extra)
        edge_rows = pl.ds(length, EDGE)
        for n in range(slices):
            held[n, edge_rows, :] = (held[n, edge_rows, :].astype(f32) + extra).astype(bf16)
        for n in range(slices):
            blocks[n][...] = held[info_ref[3 + docs] ^ n]
    count, chunk = mine_ref.shape[0], mine_ref.shape[2]
    for c in range(2):

        @pl.when(info_ref[2 + docs] == c)
        def _():
            for n in range(count):
                at, other = (c * count + n) * chunk, ((1 - c) * count + n) * chunk
                mine_ref[n] = small[:, at : at + chunk]
                theirs_ref[n] = small[:, other : other + chunk].astype(bf16)


def backward(info, proj, tok, gain, dtw, vec, rates, entry, arrive, table, dt, inner, gs, deep4, ggate, ext,
             in_weight, wx, taps, docs, slices, chunks):
    length, width = inner.shape
    model = tok.shape[1]
    states = rates.shape[0]
    rank = dtw.shape[0]
    block = min(512, width)
    steps = length // SUBS
    rows = 2 * rank + 3 * states + taps + 4
    rows = -(-rows // EDGE) * EDGE
    shape = jax.ShapeDtypeStruct
    chunk = (chunks, rows, width // (2 * chunks))
    parts = max(slices, 1)
    return plain_call(
        functools.partial(backward_kernel, states, rank, taps, docs, slices),
        "backward",
        [shape(chunk, f32), shape(chunk, bf16), shape((length + EDGE, model), f32)]
        + [shape((length + EDGE, width // parts), bf16)] * parts,
        (info, proj, tok, gain, dtw, vec, rates, entry, arrive, table, dt, inner, gs, *deep4, ggate, ext, in_weight, wx),
        24,
        [
            pltpu.VMEM((length, 2 * states * LANES), f32),
            pltpu.VMEM((steps + 1, states, SUBS, LANES), f32),
            pltpu.VMEM((steps, states, SUBS, LANES), f32),
            pltpu.VMEM((taps, length, LANES), f32),
        ]
        + [pltpu.VMEM((length, LANES), f32)] * 4
        + [
            pltpu.VMEM((length, width), f32),
            pltpu.VMEM((length, width), bf16),
            pltpu.VMEM((length + EDGE, block), bf16),
            pltpu.VMEM((length, LANES), f32),
            pltpu.VMEM((length, LANES), bf16),
            pltpu.VMEM((rows, width), f32),
            pltpu.VMEM((parts, length + EDGE, width // parts), bf16),
        ],
        14,
    )


def finish_kernel(rim, info_ref, ngrad_ref, back_ref, tok_ref, cot_ref, gain_ref, gated_ref, wo_ref, grad_ref, mixed_ref):
    length = cot_ref.shape[0]
    x = tok_ref[pl.ds(0, length), :].astype(f32)
    mixed_ref[...] = turned((x + nn(gated_ref[...], wo_ref[...])).astype(bf16), True)
    inv = lax.rsqrt(jnp.mean(x * x, axis=-1, keepdims=True) + epsilon)
    scaled = x * inv
    row = lax.broadcasted_iota(jnp.int32, (SUBS, x.shape[1]), 0)
    pieces = [ngrad_ref[pl.ds(0, length - rim * SUBS), :]]
    for b in range(rim):
        late = jnp.where(row == SUBS - 1, back_ref[pl.ds(b, 1), :], 0.0)
        pieces.append(ngrad_ref[pl.ds(length - (rim - b) * SUBS, SUBS), :] + late)
    hat = jnp.concatenate(pieces, axis=0) * gain_ref[...]
    grad = cot_ref[...].astype(f32) + inv * (hat - scaled * jnp.mean(hat * scaled, axis=-1, keepdims=True))
    grad_ref[...] = turned(grad.astype(bf16), True)


def span_of(x, states):
    return x[2 * states : 2 * states + 1] + x[2 * states + 1 : 2 * states + 2] + x[2 * states + 2 : 2 * states + 3]


def span_rows(d):
    high = d.astype(bf16).astype(f32)
    middle = (d - high).astype(bf16).astype(f32)
    row = lax.broadcasted_iota(jnp.int32, (EDGE, d.shape[1]), 0)
    return jnp.where(row == 0, high, jnp.where(row == 1, middle, jnp.where(row == 2, d - high - middle, 0.0)))


def pair_parts(info_ref, mine, other, rates, states):
    first = info_ref[0] == 0
    near, far = jnp.where(first, mine, other), jnp.where(first, other, mine)
    d0, d1 = span_of(near, states), span_of(far, states)
    state = jnp.exp2(rates * d1) * near[:states] + far[:states]
    flow = near[states : 2 * states] + jnp.exp2(rates * d0) * far[states : 2 * states]
    return state, flow, span_rows(d0 + d1)


def pair_kernel(states, info_ref, mine_ref, other_ref, rates_ref, out_ref):
    state, flow, spans = pair_parts(
        info_ref, mine_ref[...].astype(f32), other_ref[...].astype(f32), rates_ref[...], states
    )
    out_ref[...] = jnp.concatenate([state, flow, spans], axis=0).astype(bf16)


def pair_half_kernel(states, info_ref, mine_ref, other_ref, rates_ref, *outs):
    half = rates_ref.shape[1] // 2
    at = tile_at(info_ref[0] * half, half)
    state, flow, spans = pair_parts(
        info_ref, mine_ref[:, at].astype(f32), other_ref[:, at].astype(f32), rates_ref[:, at], states
    )
    place = info_ref[2]
    for k, out in enumerate(outs):
        up = (place ^ (k + 1)) > place
        out[...] = jnp.concatenate([jnp.where(up, state, flow), spans], axis=0).astype(bf16)


def enter_half_kernel(states, count, info_ref, rates_ref, *rest):
    gots, (out_ref, held) = rest[: count - 1], rest[count - 1 :]
    half = rates_ref.shape[1] // 2
    rates = rates_ref[:, tile_at(info_ref[0] * half, half)]
    place = info_ref[2]
    for k, got in enumerate(gots):
        held[place ^ (k + 1)] = got[...].astype(f32)
    held[place] = jnp.zeros_like(held[0])
    entry, arrive = jnp.zeros_like(rates), jnp.zeros_like(rates)
    for k in range(count):
        x = held[k]
        whole = jnp.exp2(rates * (x[states : states + 1] + x[states + 1 : states + 2] + x[states + 2 : states + 3]))
        entry = jnp.where(k < place, whole * entry + x[:states], entry)
    for k in reversed(range(count)):
        x = held[k]
        whole = jnp.exp2(rates * (x[states : states + 1] + x[states + 1 : states + 2] + x[states + 2 : states + 3]))
        arrive = jnp.where(k > place, whole * arrive + x[:states], arrive)
    out_ref[...] = jnp.concatenate([entry, arrive], axis=0)


def enter_both_kernel(states, info_ref, other_ref, rates_ref, here_ref, there_ref, entry_ref, arrive_ref):
    core = info_ref[0]
    half = rates_ref.shape[1] // 2
    for part, side in ((here_ref, core), (there_ref, 1 - core)):
        at = tile_at(side * half, half)
        other = other_ref[:, at].astype(f32)
        whole = jnp.exp2(rates_ref[:, at] * span_of(other, states))
        entry, arrive = part[pl.ds(0, states), :], part[pl.ds(states, states), :]
        entry_ref[:, at] = jnp.where(core == 1, whole * entry + other[:states], entry)
        arrive_ref[:, at] = jnp.where(core == 0, whole * arrive + other[states : 2 * states], arrive)


def enter_kernel(states, count, info_ref, other_ref, rates_ref, chips_ref, entry_ref, arrive_ref):
    core, place = info_ref[0], info_ref[2]
    rates = rates_ref[...]

    def split(x):
        return x[:states], x[states : 2 * states], jnp.exp2(rates * span_of(x, states))

    def lap(k, carry):
        entry, arrive = carry
        s, _, whole = split(chips_ref[k].astype(f32))
        entry = jnp.where(k < place, whole * entry + s, entry)
        back = count - 1 - k
        _, f, whole = split(chips_ref[back].astype(f32))
        arrive = jnp.where(back > place, whole * arrive + f, arrive)
        return entry, arrive

    entry, arrive = lax.fori_loop(0, count, lap, (jnp.zeros_like(rates), jnp.zeros_like(rates)))
    s, f, whole = split(other_ref[...].astype(f32))
    entry_ref[...] = jnp.where(core == 1, whole * entry + s, entry)
    arrive_ref[...] = jnp.where(core == 0, whole * arrive + f, arrive)


def gate_out_kernel(size, chips, thin, info_ref, gain_ref, *rest):
    early, late, (normed_ref, mine_ref, theirs_ref) = rest[:size], rest[size : 2 * size], rest[2 * size :]
    model = gain_ref.shape[1]
    length = early[0].shape[0]
    width = late[0].shape[1] * size // (size + 1)
    for k in range(size):
        normed_ref[pl.ds(k * length, length), :] = normalise(early[k][:, :model], gain_ref[...])
    gate = tn(jnp.concatenate([x[:, width:] for x in late], axis=0), normed_ref[...])
    left = jnp.concatenate([x[:, model:] for x in early], axis=0)
    out = tn(left, jnp.concatenate([x[:, :width] for x in late], axis=0))
    half = LANES // 2
    for c in range(2):

        @pl.when(info_ref[0] == c)
        def _():
            for q in range(chips):
                for ref, side in ((mine_ref, c), (theirs_ref, 1 - c)):
                    at = q * LANES + side * half
                    ref[q, pl.ds(0, half), :] = gate[at : at + half].astype(ref.dtype)
                    at = (2 * q + side) * thin
                    for n in range(width // model):
                        piece = out[at : at + thin, n * model : (n + 1) * model]
                        ref[q, pl.ds(half + n * thin, thin), :] = piece.astype(ref.dtype)


def conv_kernel(size, chips, rim, info_ref, normed_ref, *rest):
    gots, (mine_ref, theirs_ref) = rest[:size], rest[size:]
    length, wide = gots[0].shape[0] - EDGE, gots[0].shape[1]
    model = normed_ref.shape[1]
    pieces = model // wide
    got = jnp.concatenate([got[pl.ds(0, length), :] for got in gots], axis=0)
    lefts, rights = [], []
    for k in range(size):
        edge = gots[k][pl.ds(length, EDGE), :].astype(f32)
        row = lax.broadcasted_iota(jnp.int32, (SUBS, model), 0)
        left = jnp.zeros((SUBS, model), f32)
        for b in range(rim):
            at = rim + b * pieces
            one = jnp.concatenate([edge[at + c : at + c + 1] for c in range(pieces)], axis=1)
            left = jnp.where(row == b, jnp.broadcast_to(one, left.shape), left)
        lefts.append(left)
        right = edge[:SUBS]
        rights.append(jnp.where(lax.broadcasted_iota(jnp.int32, right.shape, 0) < rim, right, 0.0))
    left, right = (jnp.concatenate(x, axis=0).astype(bf16) for x in (lefts, rights))
    conv = tn(got, normed_ref[...]) + tn(right, left)
    half = LANES // 2
    for c in range(2):

        @pl.when(info_ref[0] == c)
        def _():
            for q in range(chips):
                at = q * LANES
                mine_ref[q] = conv[at + c * half : at + (c + 1) * half]
                theirs_ref[q] = conv[at + (1 - c) * half : at + (2 - c) * half].astype(bf16)


def halve_kernel(which, bit, info_ref, mine_ref, got_ref, keep_ref, send_ref):
    place = (info_ref[which] >> bit) & 1
    for n in range(mine_ref.shape[0] // 2):
        stay, leave = 2 * n + place, 2 * n + 1 - place
        keep_ref[n] = mine_ref[stay] + got_ref[stay].astype(f32)
        send_ref[n] = (mine_ref[leave] + got_ref[leave].astype(f32)).astype(bf16)


def go_last_kernel(thin, info_ref, mine_ref, got_ref, gate_ref, out_ref):
    half, model = gate_ref.shape
    both = mine_ref[0] + got_ref[0].astype(f32)
    gate_ref[...] = both[:half]
    for n in range(out_ref.shape[1] // model):
        out_ref[:, n * model : (n + 1) * model] = both[half + n * thin : half + (n + 1) * thin]


def cross_kernel(info_ref, mine_ref, got_ref, gate_ref, keep_ref, send_ref):
    conv = mine_ref[0] + got_ref[0].astype(f32)
    first = info_ref[1] < 2
    keep_ref[...] = jnp.where(first, conv, gate_ref[...])
    send_ref[...] = jnp.where(first, gate_ref[...], conv).astype(bf16)


def in_last_kernel(info_ref, keep_ref, got_ref, out_ref):
    keep, got = keep_ref[...], got_ref[...].astype(f32)
    first = info_ref[1] < 2
    both = jnp.concatenate([jnp.where(first, keep, got), jnp.where(first, got, keep)], axis=0)
    out_ref[...] = both.T


def add_kernel(info_ref, mine_ref, got_ref, out_ref):
    mine = mine_ref[...].reshape(out_ref.shape).astype(bf16).astype(f32)
    out_ref[...] = (mine + got_ref[...].reshape(out_ref.shape).astype(f32)).astype(bf16)


def join_kernel(which, bit, info_ref, mine_ref, got_ref, out_ref):
    place = (info_ref[which] >> bit) & 1
    for n in range(mine_ref.shape[0]):
        out_ref[2 * n + place] = mine_ref[n]
        out_ref[2 * n + 1 - place] = got_ref[n]


def unpack_kernel(edges, info_ref, rates_ref, mine_ref, other_ref, *outs):
    size, chunk = mine_ref.shape[0], mine_ref.shape[2]
    for c, part in ((info_ref[0], mine_ref), (1 - info_ref[0], other_ref)):
        for k in range(size):
            at = tile_at((c * size + k) * chunk, chunk)
            block = part[k].astype(f32)
            for n, out in enumerate(outs):
                piece = block[edges[n] : edges[n + 1]]
                out[:, at] = piece * rates_ref[:, at] if n == 2 else piece


class Group:
    def __init__(self, axis, size, stride):
        self.axis, self.size, self.stride = axis, size, stride
        self.direct = size <= 4
        self.place = (lax.axis_index(axis) // stride) % size

    def lists(self):
        n = lax.axis_size(self.axis)
        span = self.stride * self.size
        return [
            [base + low + self.stride * k for k in range(self.size)]
            for base in range(0, n, span)
            for low in range(self.stride)
        ]

    def swap(self, x, k):
        n = lax.axis_size(self.axis)
        return lax.ppermute(x, self.axis, [(i, i ^ (k * self.stride)) for i in range(n)])

    def exchange(self, blocks):
        if not self.direct:
            got = lax.all_to_all(blocks, self.axis, 0, 0, axis_index_groups=self.lists(), tiled=True)
            return [got[k] for k in range(self.size)]
        pick = lambda k: lax.dynamic_index_in_dim(blocks, self.place ^ k, 0, keepdims=False)
        return [pick(0)] + [self.swap(pick(k), k) for k in range(1, self.size)]

    def trade(self, blocks):
        if not self.direct:
            return self.exchange(jnp.stack(blocks))
        return [blocks[0]] + [self.swap(blocks[k], k) for k in range(1, self.size)]

    def gather(self, x):
        if not self.direct:
            got = lax.all_gather(x, self.axis, axis_index_groups=self.lists())
            return [got[k] for k in range(self.size)]
        return [x] + [self.swap(x, k) for k in range(1, self.size)]

    def sender(self, k):
        return self.place ^ k if self.direct else k

    def in_order(self, parts):
        if not self.direct:
            return jnp.stack(parts)
        stacked = jnp.stack(parts)
        return jnp.stack(
            [lax.dynamic_index_in_dim(stacked, self.place ^ q, 0, keepdims=False) for q in range(self.size)]
        )


def total(parts):
    return functools.reduce(lambda a, b: a + b, [part.astype(f32) for part in parts])


def body(
    tokens,
    cotangent,
    doc_starts,
    in_weight,
    conv_weight,
    conv_bias,
    xproj_weight,
    dt_weight,
    dt_bias,
    a_log,
    skip_scale,
    out_weight,
    norm_gain,
):
    length, model = tokens.shape[1:]
    inner_width, states = a_log.shape
    low_rank = dt_weight.shape[0]
    taps = conv_weight.shape[1]
    docs = doc_starts.shape[1]
    rim = taps - 1
    dp_size, seq_size = lax.axis_size("dp"), lax.axis_size("seq")
    core, outer = Group("seq", 2, 1), Group("seq", seq_size // 2, 2)
    rows_group = Group("dp", dp_size, 1)
    width = in_weight.shape[1] // (dp_size * seq_size)
    half_rows = dp_size // 2
    thin = model // (dp_size * seq_size)
    part = inner_width // dp_size
    tiled = outer.size == 4 and dp_size == 4 and width == LANES and thin % EDGE == 0
    tiled = tiled and model % part == 0 and rim * (1 + model // part) <= EDGE
    chips, slices = outer.size, dp_size if tiled else 0
    shape = jax.ShapeDtypeStruct

    base = lax.axis_index("seq") * length
    as_int = lambda *v: jnp.stack([jnp.asarray(x, jnp.int32) for x in v])
    info = jnp.concatenate([as_int(base), doc_starts[0], as_int(outer.place, core.place, rows_group.place)])
    where = as_int(core.place, rows_group.place, outer.place)
    gain = norm_gain.astype(f32)[None]
    vec = jnp.concatenate(
        [conv_weight.T, conv_bias[None], dt_bias[None], skip_scale[None], jnp.zeros((1, inner_width), bf16)], axis=0
    ).astype(f32)
    decay_rates = -jnp.exp(a_log).T
    rates = jnp.minimum(decay_rates, -LEAST_RATE) / LN2

    left = lax.ppermute(tokens[0, length - rim :], "seq", [(i, i + 1) for i in range(seq_size - 1)])
    wx = xproj_weight.T
    tok, cot, ext, inner, gate, ggated, gs, dt, proj, table, mine, dx, ex, db, fx, *early = front(
        info, tokens[0], left, cotangent[0], gain, vec, rates, dt_weight, in_weight, out_weight, wx, taps, docs, dp_size
    )
    other = core.swap(mine, 1)
    half = shape((states + EDGE, inner_width // 2), bf16)
    entering = [shape(rates.shape, f32)] * 2
    if tiled:
        to_chips = plain_call(
            functools.partial(pair_half_kernel, states), "pair", [half] * (chips - 1), (where, mine, other, rates), 2
        )
        gots = [outer.swap(x, k + 1) for k, x in enumerate(to_chips)]
        (here,) = plain_call(
            functools.partial(enter_half_kernel, states, chips),
            "enter_half",
            [shape((2 * states, inner_width // 2), f32)],
            (where, rates, *gots),
            1,
            [pltpu.VMEM((chips, states + EDGE, inner_width // 2), f32)],
        )
        entry, arrive = plain_call(
            functools.partial(enter_both_kernel, states), "enter", entering, (where, other, rates, here, core.swap(here, 1)), 1
        )
    else:
        (chip,) = plain_call(
            functools.partial(pair_kernel, states), "pair", [shape(mine.shape, bf16)], (where, mine, other, rates), 2
        )
        got = outer.in_order(outer.gather(chip))
        entry, arrive = plain_call(
            functools.partial(enter_kernel, states, outer.size), "enter", entering, (where, other, rates, got), 2
        )
    early = rows_group.trade(early)
    if tiled:
        entry, early = lax.optimization_barrier((entry, early))
    gated, ggate, *late = forward(info, vec, rates, entry, table, dt, inner, gate, ggated, dx, ex, taps, docs, slices)
    late = rows_group.trade(late) if tiled else rows_group.gather(gated)
    small_mine, small_theirs, ngrad, *sent = backward(
        info, proj, tok, gain, dt_weight, vec, rates, entry, arrive, table, dt, inner, gs, (dx, ex, db, fx), ggate, ext,
        in_weight, wx, taps, docs, slices, dp_size,
    )
    sent, small_theirs, late = lax.optimization_barrier((sent, small_theirs, late))
    rows, chunk = small_mine.shape[1:]

    def call(kernel, name, outs, args, us=1, scratch=()):
        return plain_call(kernel, name, [shape(*x) for x in outs], (where, *args), us, scratch)

    def halve(group, bit, which, mine, got, name):
        count, *rest = mine.shape
        outs = [((count // 2, *rest), f32), ((count // 2, *rest), bf16)]
        keep, send = call(functools.partial(halve_kernel, which, bit), name, outs, (mine, got))
        return keep, group.swap(send, 1 << bit)

    conv_got = rows_group.trade(sent) if tiled else None
    small_got = core.swap(small_theirs, 1)
    small, got = halve(rows_group, 0, 1, small_mine, small_got, "small_row0")
    small, got = halve(rows_group, 1, 1, small, got, "small_row1")
    one = ((1, rows, chunk), bf16)
    (small,) = call(add_kernel, "small_add", [one], (small, got))
    if tiled:
        (small,) = call(add_kernel, "small_chip0", [one], (small, outer.swap(small, 1)))
        (small,) = call(add_kernel, "small_chip1", [one], (small, outer.swap(small, 2)))
    else:
        small = total(outer.gather(small)).astype(bf16)
    join = lambda bit, x, got, name: call(
        functools.partial(join_kernel, 1, bit), name, [((2 * x.shape[0], rows, chunk), bf16)], (x, got)
    )[0]
    small = join(1, small, rows_group.swap(small, 2), "small_join1")
    small = join(0, small, rows_group.swap(small, 1), "small_join0")
    sizes = [low_rank + 2 * states, low_rank, states, taps, 1, 1, 1, 1]
    edges = [sum(sizes[:k]) for k in range(len(sizes) + 1)]
    parts = call(
        functools.partial(unpack_kernel, edges),
        "unpack",
        [((size, inner_width), f32) for size in sizes],
        (decay_rates, small, core.swap(small, 1)),
        2,
    )

    back = lax.ppermute(ngrad[length:], "seq", [(i, i - 1) for i in range(1, seq_size)])
    tokens_grad, mixed = plain_call(
        functools.partial(finish_kernel, rim),
        "finish",
        [shape((length, model), bf16)] * 2,
        (where, ngrad, back, tok, cot, gain, gated, out_weight),
        3,
    )

    if tiled:
        block = (chips, LANES, model)
        normed, go_mine, go_theirs = call(
            functools.partial(gate_out_kernel, dp_size, chips, thin),
            "gate_out_columns",
            [((dp_size * length, model), bf16), (block, f32), (block, bf16)],
            (gain, *early, *late),
            5,
        )
        go, got = halve(outer, 0, 2, go_mine, core.swap(go_theirs, 1), "go_chip0")
        go, got = halve(outer, 1, 2, go, got, "go_chip1")
        half = LANES // 2
        gate_slice, out_share = call(
            functools.partial(go_last_kernel, thin),
            "go_last",
            [((half, model), f32), ((thin, inner_width), f32)],
            (go, got),
        )
        block = (chips, half, model)
        conv_mine, conv_theirs = call(
            functools.partial(conv_kernel, dp_size, chips, rim),
            "conv_columns",
            [(block, f32), (block, bf16)],
            (normed, *conv_got),
            3,
        )
        conv, got = halve(outer, 0, 2, conv_mine, core.swap(conv_theirs, 1), "conv_chip0")
        conv, got = halve(outer, 1, 2, conv, got, "conv_chip1")
        keep, send = call(cross_kernel, "cross", [((half, model), f32), ((half, model), bf16)], (conv, got, gate_slice))
        (in_share,) = call(in_last_kernel, "in_last", [((model, width), f32)], (keep, rows_group.swap(send, 2)))
    else:

        def normalised(x):
            wide = x.astype(f32)
            inv = lax.rsqrt(jnp.mean(wide * wide, axis=-1, keepdims=True) + epsilon)
            return (wide * inv * gain).astype(bf16)

        def summed(lefts, rights):
            return functools.reduce(lambda a, b: a + b, [tn(a, b) for a, b in zip(lefts, rights, strict=True)])

        def halved(x):
            return x.astype(bf16).reshape(model, 2, -1).swapaxes(0, 1)

        def by_chip(x):
            blocks = x.reshape(x.shape[0], half_rows, outer.size, 2, width)
            return outer.exchange(blocks.transpose(2, 0, 3, 1, 4).reshape(outer.size, x.shape[0], -1))

        normed_parts = [normalised(x) for x in outer.gather(tok)]
        gate_core = total(core.exchange(halved(summed([x[:length] for x in normed_parts], by_chip(ggate)))))
        conv_core = total(core.exchange(halved(summed(normed_parts, by_chip(sent[0])))))
        in_core = jnp.concatenate([conv_core, gate_core], axis=1).astype(bf16)
        in_share = total(rows_group.exchange(in_core.reshape(model, dp_size, width).swapaxes(0, 1)))
        out_sum = summed([x[:, model:] for x in early], late).astype(bf16)
        out_core = total(core.exchange(out_sum.reshape(outer.size, 2, thin, inner_width).swapaxes(0, 1)))
        out_share = total(outer.exchange(out_core.astype(bf16)))

    return (
        mixed[None],
        tokens_grad[None],
        in_share,
        parts[3].T,
        parts[6][0],
        parts[0].T,
        parts[1],
        parts[4][0],
        parts[2].T,
        parts[5][0],
        out_share.T,
        parts[7][0, :model],
    )


def solution(mesh):
    whole = (P(),) * 10
    row = P("dp", "seq", None)
    columns = P(None, ("dp", "seq"))
    return jax.shard_map(
        body,
        mesh=mesh,
        in_specs=(row, row, P("dp", None)) + whole,
        out_specs=(row, row, columns) + (P(),) * 7 + (columns, P()),
        check_vma=False,
    )
```

time: 294 us -> 166 us (0.56)
  matrix products: 55.8 us -> 0 us
  starting transfers between devices: 77.5 us -> 32 us
  Pallas kernels: 33 us -> 69.8 us
  local copies, waits for them, and re-layouts: 48.7 us -> 14.4 us
  other arithmetic: 26.7 us -> 1.74 us
    dot_general x23 -> x0, matrix products: 55.8 us -> none  [the longest x12 25.9 us: summed(): lax.dot_general(a, b, (((0,), (0,)), ((), ())), preferred_element_type=f32)]
    ppermute x41 -> x29, starting transfers between devices: 73.9 us -> 28.4 us  [swap(): lax.ppermute(x, self.axis, [(i, i ^ k * self.stride) for i in range(n)])]
    pallas_call x2 -> x24, Pallas kernels: 33 us -> 69.8 us  [plain_call(): pl.pallas_call(kernel, in_specs=[SMEM_SPEC] + [full(x) for x in args[1:]]...]
    convert_element_type x23 -> x1, other arithmetic: 11.9 us -> 0.01 us  [body(): vec = jnp.concatenate([conv_weight.T, conv_bias[None], dt_bias[None], ski...]
    concatenate x22 -> x2, local copies, waits for them, and re-layouts: 10.3 us -> 1.52 us  [the longest x1 0.78 us: body(): jnp.concatenate([conv_weight.T, conv_bias[None], dt_bias[None], skip_scal...]
    slice x22 -> x1, local copies, waits for them, and re-layouts: 8.04 us -> 0.01 us  [body(): ngrad[length:]]
    reshape x9 -> x0, local copies, waits for them, and re-layouts: 7.46 us -> none  [the longest x1 1.87 us: body(): summed([part[:length] for part in normed_parts], gate_got)]
    squeeze x7 -> x1, local copies, waits for them, and re-layouts: 5.08 us -> 0.73 us  [body(): tokens[0, length - rim:]]
  transfers between devices with their start and end apart: 43 -> 31, of which waited for: 11 -> 16; matrix products, arithmetic and copies ran while one was open for 35% -> 4% of each run, Pallas kernels for 7% -> 25%
where the time goes in v3:
time: 166 us
  Pallas kernels  69.8 us (42%)
  waiting for transfers between devices  46.7 us (28%)
  starting transfers between devices  32 us (19%)
  local copies, waits for them, and re-layouts  14.4 us (9%)
  other arithmetic  1.74 us (1%)
    pallas_call x24, Pallas kernels, plain_call(): pl.pallas_call(kernel, in_specs=[SMEM_SPEC] + [full(x) for x in args[1:]]...  69.8 us
    ppermute x29, waiting for transfers between devices, swap(): lax.ppermute(x, self.axis, [(i, i ^ k * self.stride) for i in range(n)])  46.7 us
    ppermute x29, starting transfers between devices, swap(): lax.ppermute(x, self.axis, [(i, i ^ k * self.stride) for i in range(n)])  28.4 us
    unnamed x22, local copies, waits for them, and re-layouts  9.44 us
  transfers between devices with their start and end apart: 31, of which 16 were waited for; matrix products, arithmetic and copies ran while one was open for 4% of the time, Pallas kernels for 25%

profile of v3, /device:TPU:0, one launch (start us, length us, event | category | flops | bytes accessed | tf_op | source)
XLA Modules:
  0.0 165.6 jit_solution(1609977854932190753)
XLA Ops:
  0.6 0.7 slice_bitcast_fusion
  1.4 2.3 %collective-permute-start = (bf16[3,1024]{1,0:T(4,128)(2,1)S(1)}, bf16[3,1024]{1,0:T(4,128)(2,1)S(1)}, u32[]{:S(2)}, u32[]{:S(2)}) collective-permute-start(bf16[3,1024]{1,0:T(4,128)(2,1)S(1)} %slice_bitcast_fusion), channel_id=1, source_target_pairs={{0,1},{1,2},{2,3},{3,4},{4,5},{5,6},{6,7},{8,9},{9,10},{10,11},{11... | collective-permute-start | bytes 18440 | tf_op jit(solution)/shard_map/ppermute | solution.py:909
  3.7 0.9 minimum_multiply_fusion.rates_ref
  4.7 0.7 broadcast_in_dim.31
  5.4 0.7 broadcast_in_dim.25
  6.1 0.7 broadcast_in_dim.26
  6.8 0.7 broadcast_in_dim.27
  7.5 0.8 concatenate.7
  8.3 0.7 concatenate.6.info_ref
  9.0 3.4 %copy-done = bf16[1024,4096]{1,0:T(8,128)(2,1)S(1)} copy-done((bf16[1024,4096]{1,0:T(8,128)(2,1)S(1)}, bf16[1024,4096]{1,0:T(8,128)(2,1)}, u32[]{:S(2)}) %copy-start) | copy-done | bytes 8388632
  12.4 2.2 %copy-done.2 = bf16[2048,1024]{1,0:T(8,128)(2,1)S(1)} copy-done((bf16[2048,1024]{1,0:T(8,128)(2,1)S(1)}, bf16[2048,1024]{1,0:T(8,128)(2,1)}, u32[]{:S(2)}) %copy-start.2) | copy-done | bytes 4194328
  14.6 1.0 copy-done.4
  15.6 0.9 copy-done.6
  16.6 0.9 copy-done.8
  17.5 0.9 copy-done.9
  18.5 17.7 %front.1 = (bf16[144,1024]{1,0:T(8,128)(2,1)S(1)}, bf16[128,1024]{1,0:T(8,128)(2,1)S(1)}, bf16[160,2048]{1,0:T(8,128)(2,1)S(1)}, bf16[128,2048]{1,0:T(8,128)(2,1...) custom-call(s32[8]{0:T(128)S(1)} %concatenate.6.info_ref, ...), custom_call_target="tpu_custom_call" | custom-call | bytes 64800000 | tf_op jit(solution)/shard_map/front/pallas_call | solution.py:36
  36.2 2.8 %collective-permute-start.1 = (bf16[48,2048]{1,0:T(8,128)(2,1)S(1)}, bf16[48,2048]{1,0:T(8,128)(2,1)S(1)}, u32[]{:S(2)}, u32[]{:S(2)}) collective-permute-start(bf16[48,2048]{1,0:T(8,128)(2,1)S(1)} %get-tuple-element.96.mine_ref), channel_id=1, source_target_pairs={{0,1},{1,0},{2,3},{3,2},{4,5},{5,4},{6,7},{7,6},{8,9},{9,8},{10,11... | collective-permute-start | bytes 589832 | tf_op jit(solution)/shard_map/ppermute | solution.py:829
  39.0 1.5 collective-permute-start.6
  40.5 1.5 collective-permute-start.7
  43.2 1.7 collective-permute-start.2
  44.8 1.1 collective-permute-start.3
  45.9 2.2 %collective-permute-done.2.rest_0_ = bf16[32,1024]{1,0:T(8,128)(2,1)S(1)} collective-permute-done((bf16[32,1024]{1,0:T(8,128)(2,1)S(1)}, bf16[32,1024]{1,0:T(8,128)(2,1)S(1)}, u32[]{:S(2)}, u32[]{:S(2)}) %collective-permute-start.2) | collective-permute-done | bytes 65568 | tf_op jit(solution)/shard_map/ppermute | solution.py:829
  48.1 1.4 collective-permute-start.4
  49.5 2.3 %collective-permute-done.3.rest_1_ = bf16[32,1024]{1,0:T(8,128)(2,1)S(1)} collective-permute-done((bf16[32,1024]{1,0:T(8,128)(2,1)S(1)}, bf16[32,1024]{1,0:T(8,128)(2,1)S(1)}, u32[]{:S(2)}, u32[]{:S(2)}) %collective-permute-start.3) | collective-permute-done | bytes 65568 | tf_op jit(solution)/shard_map/ppermute | solution.py:829
  51.9 2.3 %collective-permute-done.4.rest_2_ = bf16[32,1024]{1,0:T(8,128)(2,1)S(1)} collective-permute-done((bf16[32,1024]{1,0:T(8,128)(2,1)S(1)}, bf16[32,1024]{1,0:T(8,128)(2,1)S(1)}, u32[]{:S(2)}, u32[]{:S(2)}) %collective-permute-start.4) | collective-permute-done | bytes 65568 | tf_op jit(solution)/shard_map/ppermute | solution.py:829
  54.2 0.7 enter_half.1.here_ref
  54.9 1.3 collective-permute-done.5.there_ref
  56.9 6.6 %forward.1 = (bf16[128,2048]{1,0:T(8,128)(2,1)S(1)}, bf16[128,2048]{1,0:T(8,128)(2,1)S(1)}, bf16[128,2560]{1,0:T(8,128)(2,1)S(1)}, bf16[128,2560]{1,0:T(8,128)(2...) custom-call(s32[8]{0:T(128)S(1)} %concatenate.6.info_ref, ...), custom_call_target="tpu_custom_call" | custom-call | bytes 28800000 | tf_op jit(solution)/shard_map/forward/pallas_call | solution.py:36
  63.6 1.6 collective-permute-start.10
  65.2 1.5 collective-permute-start.11
  67.2 25.4 %backward.1 = (f32[4,192,256]{2,1,0:T(8,128)S(1)}, bf16[4,192,256]{2,1,0:T(8,128)(2,1)S(1)}, f32[144,1024]{1,0:T(8,128)S(1)}, bf16[144,512]{1,0:T(8,128)(2,1)S(1...) custom-call(s32[8]{0:T(128)S(1)} %concatenate.6.info_ref, ...), custom_call_target="tpu_custom_call" | custom-call | bytes 86400000 | tf_op jit(solution)/shard_map/backward/pallas_call | solution.py:36
  92.6 3.1 %collective-permute-done.11.rest_6_ = bf16[128,2560]{1,0:T(8,128)(2,1)S(1)} collective-permute-done((bf16[128,2560]{1,0:T(8,128)(2,1)S(1)}, bf16[128,2560]{1,0:T(8,128)(2,1)S(1)}, u32[]{:S(2)}, u32[]{:S(2)}) %collective-permute-start.11) | collective-permute-done | bytes 655392 | tf_op jit(solution)/shard_map/ppermute | solution.py:829
  95.7 2.3 %gate_out_columns.1 = (bf16[512,1024]{1,0:T(8,128)(2,1)S(1)}, f32[4,128,1024]{2,1,0:T(8,128)S(1)}, bf16[4,128,1024]{2,1,0:T(8,128)(2,1)S(1)}) custom-call(s32[3]{0:T(128)S(1)} %pad_add_fusion.info_ref, f32[1,1024]{1,0:T(1,128)S(1)} %bitcast.32, bf16[128,1280]{1,0:T(8,128)(2,1)S(1)} %get-tuple-element.124.rest_0_, ...), custom_call_target="tpu_custom_call" | custom-call | bytes 18000000 | tf_op jit(solution)/shard_map/gate_out_columns/pallas_call | solution.py:36
  98.6 1.2 collective-permute-start.13
  99.8 0.8 collective-permute-start.14
  100.7 1.4 collective-permute-start.15
  102.1 3.2 %collective-permute-done.13.rest_1_ = bf16[144,512]{1,0:T(8,128)(2,1)S(1)} collective-permute-done((bf16[144,512]{1,0:T(8,128)(2,1)S(1)}, bf16[144,512]{1,0:T(8,128)(2,1)S(1)}, u32[]{:S(2)}, u32[]{:S(2)}) %collective-permute-start.13) | collective-permute-done | bytes 147488 | tf_op jit(solution)/shard_map/ppermute | solution.py:829
  105.3 1.6 collective-permute-done.14.rest_2_
  106.9 1.6 collective-permute-done.15.rest_3_
  108.5 1.6 conv_columns.1
  110.9 0.9 collective-permute-start.24
  111.7 0.7 go_chip0.1
  112.9 5.4 %collective-permute-done.24.got_ref = bf16[2,192,256]{2,1,0:T(8,128)(2,1)S(1)} collective-permute-done((bf16[2,192,256]{2,1,0:T(8,128)(2,1)S(1)}, bf16[2,192,256]{2,1,0:T(8,128)(2,1)S(1)}, u32[]{:S(2)}, u32[]{:S(2)}) %collective-permute-start.24) | collective-permute-done | bytes 196640 | tf_op jit(solution)/shard_map/ppermute | solution.py:829
  118.8 0.9 collective-permute-start.25
  119.7 3.8 %collective-permute-done.25.got_ref = bf16[1,192,256]{2,1,0:T(8,128)(2,1)S(1)} collective-permute-done((bf16[1,192,256]{2,1,0:T(8,128)(2,1)S(1)}, bf16[1,192,256]{2,1,0:T(8,128)(2,1)S(1)}, u32[]{:S(2)}, u32[]{:S(2)}) %collective-permute-start.25) | collective-permute-done | bytes 98336 | tf_op jit(solution)/shard_map/ppermute | solution.py:829
  124.2 4.6 %collective-permute-done.26.got_ref = bf16[1,192,256]{2,1,0:T(8,128)(2,1)S(1)} collective-permute-done((bf16[1,192,256]{2,1,0:T(8,128)(2,1)S(1)}, bf16[1,192,256]{2,1,0:T(8,128)(2,1)S(1)}, u32[]{:S(2)}, u32[]{:S(2)}) %collective-permute-start.26) | collective-permute-done | bytes 98336 | tf_op jit(solution)/shard_map/ppermute | solution.py:829
  129.3 1.3 collective-permute-start.27
  130.7 0.7 conv_chip0.1
  131.3 0.9 collective-permute-start.17
  132.2 3.6 %collective-permute-done.27.got_ref = bf16[1,192,256]{2,1,0:T(8,128)(2,1)S(1)} collective-permute-done((bf16[1,192,256]{2,1,0:T(8,128)(2,1)S(1)}, bf16[1,192,256]{2,1,0:T(8,128)(2,1)S(1)}, u32[]{:S(2)}, u32[]{:S(2)}) %collective-permute-start.27) | collective-permute-done | bytes 98336 | tf_op jit(solution)/shard_map/ppermute | solution.py:829
  136.4 2.2 %collective-permute-start.28 = (bf16[1,192,256]{2,1,0:T(8,128)(2,1)S(1)}, bf16[1,192,256]{2,1,0:T(8,128)(2,1)S(1)}, u32[]{:S(2)}, u32[]{:S(2)}) collective-permute-start(bf16[1,192,256]{2,1,0:T(8,128)(2,1)S(1)} %small_chip1.1.mine_ref), channel_id=1, source_target_pairs={{0,16},{8,24},{16,0},{24,8},{1,17},{9,25},{17,1},{25,9},{2,18},{10... | collective-permute-start | bytes 294920 | tf_op jit(solution)/shard_map/ppermute | solution.py:829
  138.6 0.6 go_chip1.1
  139.5 1.9 %collective-permute-done.28.got_ref = bf16[1,192,256]{2,1,0:T(8,128)(2,1)S(1)} collective-permute-done((bf16[1,192,256]{2,1,0:T(8,128)(2,1)S(1)}, bf16[1,192,256]{2,1,0:T(8,128)(2,1)S(1)}, u32[]{:S(2)}, u32[]{:S(2)}) %collective-permute-start.28) | collective-permute-done | bytes 98336 | tf_op jit(solution)/shard_map/ppermute | solution.py:829
  142.0 1.3 collective-permute-start.29
  143.9 0.8 collective-permute-start.18
  144.7 1.3 collective-permute-start.9
  146.0 2.1 %collective-permute-done.29.got_ref = bf16[2,192,256]{2,1,0:T(8,128)(2,1)S(1)} collective-permute-done((bf16[2,192,256]{2,1,0:T(8,128)(2,1)S(1)}, bf16[2,192,256]{2,1,0:T(8,128)(2,1)S(1)}, u32[]{:S(2)}, u32[]{:S(2)}) %collective-permute-start.29) | collective-permute-done | bytes 196640 | tf_op jit(solution)/shard_map/ppermute | solution.py:829
  148.7 6.2 %collective-permute-done.21.got_ref = bf16[1,128,1024]{2,1,0:T(8,128)(2,1)S(1)} collective-permute-done((bf16[1,128,1024]{2,1,0:T(8,128)(2,1)S(1)}, bf16[1,128,1024]{2,1,0:T(8,128)(2,1)S(1)}, u32[]{:S(2)}, u32[]{:S(2)}) %collective-permute-start.21) | collective-permute-done | bytes 262176 | tf_op jit(solution)/shard_map/ppermute | solution.py:829
  154.9 1.3 go_last.1
  156.2 1.4 collective-permute-done.18.got_ref
  158.2 1.1 collective-permute-start.22
  159.4 2.4 %finish.1 = (bf16[128,1024]{1,0:T(8,128)(2,1)}, bf16[128,1024]{1,0:T(8,128)(2,1)}) custom-call(s32[3]{0:T(128)S(1)} %pad_add_fusion.info_ref, f32[144,1024]{1,0:T(8,128)S(1)} %get-tuple-element.119.ngrad_ref, f32[16,1024]{1,0:T(8,128)S(1)} %collective-permute-done.9.back_ref, bf16[144,1024]{1,0:T(8,128)(2,1)S(1)} %get-tuple-element.95.tok_ref, ...), custom_call_target="tpu_custom_call" | custom-call | bytes 10800000 | tf_op jit(solution)/shard_map/finish/pallas_call | solution.py:36
  161.7 1.8 %unpack.1 = (f32[96,2048]{1,0:T(8,128)}, f32[64,2048]{1,0:T(8,128)}, f32[16,2048]{1,0:T(8,128)}, f32[4,2048]{1,0:T(4,128)}, f32[1,2048]{1,0:T(1,128)}, /*index=5...) custom-call(s32[3]{0:T(128)S(1)} %pad_add_fusion.info_ref, f32[16,2048]{1,0:T(8,128)S(1)} %negate_bitcast_fusion.rates_ref, ...), custom_call_target="tpu_custom_call" | custom-call | bytes 7200000 | tf_op jit(solution)/shard_map/unpack/pallas_call | solution.py:36
  164.1 1.5 in_last.1
  (58 shorter events, 9.6 us)
Async XLA Ops:
  1.4 7.7 %collective-permute-start = (bf16[3,1024]{1,0:T(4,128)(2,1)S(1)}, bf16[3,1024]{1,0:T(4,128)(2,1)S(1)}, u32[]{:S(2)}, u32[]{:S(2)}) collective-permute-start(bf16[3,1024]{1,0:T(4,128)(2,1)S(1)} %slice_bitcast_fusion), channel_id=1, source_target_pairs={{0,1},{1,2},{2,3},{3,4},{4,5},{5,6},{6,7},{8,9},{9,10},{10,11},{11... | collective-permute-start | bytes 18440 | tf_op jit(solution)/shard_map/ppermute | solution.py:909
  9.0 3.4 %copy-start = (bf16[1024,4096]{1,0:T(8,128)(2,1)S(1)}, bf16[1024,4096]{1,0:T(8,128)(2,1)}, u32[]{:S(2)}) copy-start(bf16[1024,4096]{1,0:T(8,128)(2,1)} %win_ref.3) | copy-start | bytes 25165828
  12.4 2.2 %copy-start.2 = (bf16[2048,1024]{1,0:T(8,128)(2,1)S(1)}, bf16[2048,1024]{1,0:T(8,128)(2,1)}, u32[]{:S(2)}) copy-start(bf16[2048,1024]{1,0:T(8,128)(2,1)} %wo_ref.3) | copy-start | bytes 12582916
  14.6 1.0 copy-start.4
  15.6 0.9 copy-start.6
  16.6 0.9 copy-start.8
  17.5 0.9 copy-start.9
  36.2 6.3 %collective-permute-start.1 = (bf16[48,2048]{1,0:T(8,128)(2,1)S(1)}, bf16[48,2048]{1,0:T(8,128)(2,1)S(1)}, u32[]{:S(2)}, u32[]{:S(2)}) collective-permute-start(bf16[48,2048]{1,0:T(8,128)(2,1)S(1)} %get-tuple-element.96.mine_ref), channel_id=1, source_target_pairs={{0,1},{1,0},{2,3},{3,2},{4,5},{5,4},{6,7},{7,6},{8,9},{9,8},{10,11... | collective-permute-start | bytes 589832 | tf_op jit(solution)/shard_map/ppermute | solution.py:829
  39.0 18.0 %collective-permute-start.6 = (bf16[128,1280]{1,0:T(8,128)(2,1)S(1)}, bf16[128,1280]{1,0:T(8,128)(2,1)S(1)}, u32[]{:S(2)}, u32[]{:S(2)}) collective-permute-start(bf16[128,1280]{1,0:T(8,128)(2,1)S(1)} %get-tuple-element.102), channel_id=1, source_target_pairs={{0,8},{8,0},{16,24},{24,16},{1,9},{9,1},{17,25},{25,17},{2,10},{10... | collective-permute-start | bytes 983048 | tf_op jit(solution)/shard_map/ppermute | solution.py:829
  40.5 16.4 %collective-permute-start.7 = (bf16[128,1280]{1,0:T(8,128)(2,1)S(1)}, bf16[128,1280]{1,0:T(8,128)(2,1)S(1)}, u32[]{:S(2)}, u32[]{:S(2)}) collective-permute-start(bf16[128,1280]{1,0:T(8,128)(2,1)S(1)} %get-tuple-element.103), channel_id=1, source_target_pairs={{0,16},{8,24},{16,0},{24,8},{1,17},{9,25},{17,1},{25,9},{2,18},{10... | collective-permute-start | bytes 983048 | tf_op jit(solution)/shard_map/ppermute | solution.py:829
  42.0 14.9 %collective-permute-start.8 = (bf16[128,1280]{1,0:T(8,128)(2,1)S(1)}, bf16[128,1280]{1,0:T(8,128)(2,1)S(1)}, u32[]{:S(2)}, u32[]{:S(2)}) collective-permute-start(bf16[128,1280]{1,0:T(8,128)(2,1)S(1)} %get-tuple-element.104), channel_id=1, source_target_pairs={{0,24},{8,16},{16,8},{24,0},{1,25},{9,17},{17,9},{25,1},{2,26},{10... | collective-permute-start | bytes 983048 | tf_op jit(solution)/shard_map/ppermute | solution.py:829
  43.2 5.0 %collective-permute-start.2 = (bf16[32,1024]{1,0:T(8,128)(2,1)S(1)}, bf16[32,1024]{1,0:T(8,128)(2,1)S(1)}, u32[]{:S(2)}, u32[]{:S(2)}) collective-permute-start(bf16[32,1024]{1,0:T(8,128)(2,1)S(1)} %get-tuple-element.97), channel_id=1, source_target_pairs={{0,2},{1,3},{2,0},{3,1},{4,6},{5,7},{6,4},{7,5},{8,10},{9,11},{10,... | collective-permute-start | bytes 196616 | tf_op jit(solution)/shard_map/ppermute | solution.py:829
  44.8 7.1 %collective-permute-start.3 = (bf16[32,1024]{1,0:T(8,128)(2,1)S(1)}, bf16[32,1024]{1,0:T(8,128)(2,1)S(1)}, u32[]{:S(2)}, u32[]{:S(2)}) collective-permute-start(bf16[32,1024]{1,0:T(8,128)(2,1)S(1)} %get-tuple-element.98), channel_id=1, source_target_pairs={{0,4},{1,5},{2,6},{3,7},{4,0},{5,1},{6,2},{7,3},{8,12},{9,13},{10,... | collective-permute-start | bytes 196616 | tf_op jit(solution)/shard_map/ppermute | solution.py:829
  48.1 6.1 %collective-permute-start.4 = (bf16[32,1024]{1,0:T(8,128)(2,1)S(1)}, bf16[32,1024]{1,0:T(8,128)(2,1)S(1)}, u32[]{:S(2)}, u32[]{:S(2)}) collective-permute-start(bf16[32,1024]{1,0:T(8,128)(2,1)S(1)} %get-tuple-element.99), channel_id=1, source_target_pairs={{0,6},{1,7},{2,4},{3,5},{4,2},{5,3},{6,0},{7,1},{8,14},{9,15},{10,... | collective-permute-start | bytes 196616 | tf_op jit(solution)/shard_map/ppermute | solution.py:829
  54.2 13.0 %copy-start.7 = (bf16[64,2048]{1,0:T(8,128)(2,1)S(1)}, bf16[64,2048]{1,0:T(8,128)(2,1)}, u32[]{:S(2)}) copy-start(bf16[64,2048]{1,0:T(8,128)(2,1)} %dtw_ref.3) | copy-start | bytes 786436
  54.9 1.4 collective-permute-start.5
  56.3 10.9 %copy-start.1 = (bf16[1024,4096]{1,0:T(8,128)(2,1)S(1)}, bf16[1024,4096]{1,0:T(8,128)(2,1)}, u32[]{:S(2)}) copy-start(bf16[1024,4096]{1,0:T(8,128)(2,1)} %win_ref.3) | copy-start | bytes 25165828
  56.9 10.3 %copy-start.5 = (bf16[2048,96]{0,1:T(8,128)(2,1)S(1)}, bf16[2048,96]{0,1:T(8,128)(2,1)}, u32[]{:S(2)}) copy-start(bf16[2048,96]{0,1:T(8,128)(2,1)} %param.19) | copy-start | bytes 1179652
  63.6 29.0 %collective-permute-start.10 = (bf16[128,2560]{1,0:T(8,128)(2,1)S(1)}, bf16[128,2560]{1,0:T(8,128)(2,1)S(1)}, u32[]{:S(2)}, u32[]{:S(2)}) collective-permute-start(bf16[128,2560]{1,0:T(8,128)(2,1)S(1)} %get-tuple-element.134), channel_id=1, source_target_pairs={{0,8},{8,0},{16,24},{24,16},{1,9},{9,1},{17,25},{25,17},{2,10},{10... | collective-permute-start | bytes 1966088 | tf_op jit(solution)/shard_map/ppermute | solution.py:829
  65.2 30.6 %collective-permute-start.11 = (bf16[128,2560]{1,0:T(8,128)(2,1)S(1)}, bf16[128,2560]{1,0:T(8,128)(2,1)S(1)}, u32[]{:S(2)}, u32[]{:S(2)}) collective-permute-start(bf16[128,2560]{1,0:T(8,128)(2,1)S(1)} %get-tuple-element.135), channel_id=1, source_target_pairs={{0,16},{8,24},{16,0},{24,8},{1,17},{9,25},{17,1},{25,9},{2,18},{10... | collective-permute-start | bytes 1966088 | tf_op jit(solution)/shard_map/ppermute | solution.py:829
  66.7 29.0 %collective-permute-start.12 = (bf16[128,2560]{1,0:T(8,128)(2,1)S(1)}, bf16[128,2560]{1,0:T(8,128)(2,1)S(1)}, u32[]{:S(2)}, u32[]{:S(2)}) collective-permute-start(bf16[128,2560]{1,0:T(8,128)(2,1)S(1)} %get-tuple-element.136), channel_id=1, source_target_pairs={{0,24},{8,16},{16,8},{24,0},{1,25},{9,17},{17,9},{25,1},{2,26},{10... | collective-permute-start | bytes 1966088 | tf_op jit(solution)/shard_map/ppermute | solution.py:829
  98.0 13.7 %collective-permute-start.19 = (bf16[4,128,1024]{2,1,0:T(8,128)(2,1)S(1)}, bf16[4,128,1024]{2,1,0:T(8,128)(2,1)S(1)}, u32[]{:S(2)}, u32[]{:S(2)}) collective-permute-start(bf16[4,128,1024]{2,1,0:T(8,128)(2,1)S(1)} %get-tuple-element.153), channel_id=1, source_target_pairs={{0,1},{1,0},{2,3},{3,2},{4,5},{5,4},{6,7},{7,6},{8,9},{9,8},{10,11... | collective-permute-start | bytes 3145736 | tf_op jit(solution)/shard_map/ppermute | solution.py:829
  98.1 12.2 %collective-permute-start.23 = (bf16[4,192,256]{2,1,0:T(8,128)(2,1)S(1)}, bf16[4,192,256]{2,1,0:T(8,128)(2,1)S(1)}, u32[]{:S(2)}, u32[]{:S(2)}) collective-permute-start(bf16[4,192,256]{2,1,0:T(8,128)(2,1)S(1)} %get-tuple-element.162), channel_id=1, source_target_pairs={{0,1},{1,0},{2,3},{3,2},{4,5},{5,4},{6,7},{7,6},{8,9},{9,8},{10,11... | collective-permute-start | bytes 1179656 | tf_op jit(solution)/shard_map/ppermute | solution.py:829
  98.6 6.7 %collective-permute-start.13 = (bf16[144,512]{1,0:T(8,128)(2,1)S(1)}, bf16[144,512]{1,0:T(8,128)(2,1)S(1)}, u32[]{:S(2)}, u32[]{:S(2)}) collective-permute-start(bf16[144,512]{1,0:T(8,128)(2,1)S(1)} %get-tuple-element.143), channel_id=1, source_target_pairs={{0,8},{8,0},{16,24},{24,16},{1,9},{9,1},{17,25},{25,17},{2,10},{10... | collective-permute-start | bytes 442376 | tf_op jit(solution)/shard_map/ppermute | solution.py:829
  99.8 7.1 %collective-permute-start.14 = (bf16[144,512]{1,0:T(8,128)(2,1)S(1)}, bf16[144,512]{1,0:T(8,128)(2,1)S(1)}, u32[]{:S(2)}, u32[]{:S(2)}) collective-permute-start(bf16[144,512]{1,0:T(8,128)(2,1)S(1)} %get-tuple-element.144), channel_id=1, source_target_pairs={{0,16},{8,24},{16,0},{24,8},{1,17},{9,25},{17,1},{25,9},{2,18},{10... | collective-permute-start | bytes 442376 | tf_op jit(solution)/shard_map/ppermute | solution.py:829
  100.7 7.9 %collective-permute-start.15 = (bf16[144,512]{1,0:T(8,128)(2,1)S(1)}, bf16[144,512]{1,0:T(8,128)(2,1)S(1)}, u32[]{:S(2)}, u32[]{:S(2)}) collective-permute-start(bf16[144,512]{1,0:T(8,128)(2,1)S(1)} %get-tuple-element.145), channel_id=1, source_target_pairs={{0,24},{8,16},{16,8},{24,0},{1,25},{9,17},{17,9},{25,1},{2,26},{10... | collective-permute-start | bytes 442376 | tf_op jit(solution)/shard_map/ppermute | solution.py:829
  110.2 20.5 %collective-permute-start.16 = (bf16[4,64,1024]{2,1,0:T(8,128)(2,1)S(1)}, bf16[4,64,1024]{2,1,0:T(8,128)(2,1)S(1)}, u32[]{:S(2)}, u32[]{:S(2)}) collective-permute-start(bf16[4,64,1024]{2,1,0:T(8,128)(2,1)S(1)} %get-tuple-element.147), channel_id=1, source_target_pairs={{0,1},{1,0},{2,3},{3,2},{4,5},{5,4},{6,7},{7,6},{8,9},{9,8},{10,11... | collective-permute-start | bytes 1572872 | tf_op jit(solution)/shard_map/ppermute | solution.py:829
  110.9 7.4 %collective-permute-start.24 = (bf16[2,192,256]{2,1,0:T(8,128)(2,1)S(1)}, bf16[2,192,256]{2,1,0:T(8,128)(2,1)S(1)}, u32[]{:S(2)}, u32[]{:S(2)}) collective-permute-start(bf16[2,192,256]{2,1,0:T(8,128)(2,1)S(1)} %get-tuple-element.164), channel_id=1, source_target_pairs={{0,8},{8,0},{16,24},{24,16},{1,9},{9,1},{17,25},{25,17},{2,10},{10... | collective-permute-start | bytes 589832 | tf_op jit(solution)/shard_map/ppermute | solution.py:829
  112.5 46.9 %copy-start.10 = (f32[2048,16]{0,1:T(8,128)S(1)}, f32[2048,16]{0,1:T(8,128)}, u32[]{:S(2)}) copy-start(f32[2048,16]{0,1:T(8,128)} %param.22) | copy-start | bytes 393220
  112.5 26.2 %collective-permute-start.20 = (bf16[2,128,1024]{2,1,0:T(8,128)(2,1)S(1)}, bf16[2,128,1024]{2,1,0:T(8,128)(2,1)S(1)}, u32[]{:S(2)}, u32[]{:S(2)}) collective-permute-start(bf16[2,128,1024]{2,1,0:T(8,128)(2,1)S(1)} %get-tuple-element.155), channel_id=1, source_target_pairs={{0,2},{1,3},{2,0},{3,1},{4,6},{5,7},{6,4},{7,5},{8,10},{9,11},{10,... | collective-permute-start | bytes 1572872 | tf_op jit(solution)/shard_map/ppermute | solution.py:829
  118.2 41.1 %copy-start.3 = (bf16[2048,1024]{1,0:T(8,128)(2,1)S(1)}, bf16[2048,1024]{1,0:T(8,128)(2,1)}, u32[]{:S(2)}) copy-start(bf16[2048,1024]{1,0:T(8,128)(2,1)} %wo_ref.3) | copy-start | bytes 12582916
  118.8 4.7 %collective-permute-start.25 = (bf16[1,192,256]{2,1,0:T(8,128)(2,1)S(1)}, bf16[1,192,256]{2,1,0:T(8,128)(2,1)S(1)}, u32[]{:S(2)}, u32[]{:S(2)}) collective-permute-start(bf16[1,192,256]{2,1,0:T(8,128)(2,1)S(1)} %get-tuple-element.166), channel_id=1, source_target_pairs={{0,16},{8,24},{16,0},{24,8},{1,17},{9,25},{17,1},{25,9},{2,18},{10... | collective-permute-start | bytes 294920 | tf_op jit(solution)/shard_map/ppermute | solution.py:829
  124.1 4.7 %collective-permute-start.26 = (bf16[1,192,256]{2,1,0:T(8,128)(2,1)S(1)}, bf16[1,192,256]{2,1,0:T(8,128)(2,1)S(1)}, u32[]{:S(2)}, u32[]{:S(2)}) collective-permute-start(bf16[1,192,256]{2,1,0:T(8,128)(2,1)S(1)} %small_add.1.mine_ref), channel_id=1, source_target_pairs={{0,2},{1,3},{2,0},{3,1},{4,6},{5,7},{6,4},{7,5},{8,10},{9,11},{10,... | collective-permute-start | bytes 294920 | tf_op jit(solution)/shard_map/ppermute | solution.py:829
  129.3 6.5 %collective-permute-start.27 = (bf16[1,192,256]{2,1,0:T(8,128)(2,1)S(1)}, bf16[1,192,256]{2,1,0:T(8,128)(2,1)S(1)}, u32[]{:S(2)}, u32[]{:S(2)}) collective-permute-start(bf16[1,192,256]{2,1,0:T(8,128)(2,1)S(1)} %small_chip0.1.mine_ref), channel_id=1, source_target_pairs={{0,4},{1,5},{2,6},{3,7},{4,0},{5,1},{6,2},{7,3},{8,12},{9,13},{10,... | collective-permute-start | bytes 294920 | tf_op jit(solution)/shard_map/ppermute | solution.py:829
  131.3 11.9 %collective-permute-start.17 = (bf16[2,64,1024]{2,1,0:T(8,128)(2,1)S(1)}, bf16[2,64,1024]{2,1,0:T(8,128)(2,1)S(1)}, u32[]{:S(2)}, u32[]{:S(2)}) collective-permute-start(bf16[2,64,1024]{2,1,0:T(8,128)(2,1)S(1)} %get-tuple-element.149), channel_id=1, source_target_pairs={{0,2},{1,3},{2,0},{3,1},{4,6},{5,7},{6,4},{7,5},{8,10},{9,11},{10,... | collective-permute-start | bytes 786440 | tf_op jit(solution)/shard_map/ppermute | solution.py:829
  136.4 5.0 %collective-permute-start.28 = (bf16[1,192,256]{2,1,0:T(8,128)(2,1)S(1)}, bf16[1,192,256]{2,1,0:T(8,128)(2,1)S(1)}, u32[]{:S(2)}, u32[]{:S(2)}) collective-permute-start(bf16[1,192,256]{2,1,0:T(8,128)(2,1)S(1)} %small_chip1.1.mine_ref), channel_id=1, source_target_pairs={{0,16},{8,24},{16,0},{24,8},{1,17},{9,25},{17,1},{25,9},{2,18},{10... | collective-permute-start | bytes 294920 | tf_op jit(solution)/shard_map/ppermute | solution.py:829
  139.3 15.6 %collective-permute-start.21 = (bf16[1,128,1024]{2,1,0:T(8,128)(2,1)S(1)}, bf16[1,128,1024]{2,1,0:T(8,128)(2,1)S(1)}, u32[]{:S(2)}, u32[]{:S(2)}) collective-permute-start(bf16[1,128,1024]{2,1,0:T(8,128)(2,1)S(1)} %get-tuple-element.157), channel_id=1, source_target_pairs={{0,4},{1,5},{2,6},{3,7},{4,0},{5,1},{6,2},{7,3},{8,12},{9,13},{10,... | collective-permute-start | bytes 786440 | tf_op jit(solution)/shard_map/ppermute | solution.py:829
  142.0 6.1 %collective-permute-start.29 = (bf16[2,192,256]{2,1,0:T(8,128)(2,1)S(1)}, bf16[2,192,256]{2,1,0:T(8,128)(2,1)S(1)}, u32[]{:S(2)}, u32[]{:S(2)}) collective-permute-start(bf16[2,192,256]{2,1,0:T(8,128)(2,1)S(1)} %small_join1.1.mine_ref), channel_id=1, source_target_pairs={{0,8},{8,0},{16,24},{24,16},{1,9},{9,1},{17,25},{25,17},{2,10},{10... | collective-permute-start | bytes 589832 | tf_op jit(solution)/shard_map/ppermute | solution.py:829
  143.9 13.7 %collective-permute-start.18 = (bf16[1,64,1024]{2,1,0:T(8,128)(2,1)S(1)}, bf16[1,64,1024]{2,1,0:T(8,128)(2,1)S(1)}, u32[]{:S(2)}, u32[]{:S(2)}) collective-permute-start(bf16[1,64,1024]{2,1,0:T(8,128)(2,1)S(1)} %get-tuple-element.151), channel_id=1, source_target_pairs={{0,4},{1,5},{2,6},{3,7},{4,0},{5,1},{6,2},{7,3},{8,12},{9,13},{10,... | collective-permute-start | bytes 393224 | tf_op jit(solution)/shard_map/ppermute | solution.py:829
  144.7 14.7 %collective-permute-start.9 = (f32[16,1024]{1,0:T(8,128)S(1)}, f32[16,1024]{1,0:T(8,128)S(1)}, u32[]{:S(2)}, u32[]{:S(2)}) collective-permute-start(f32[16,1024]{1,0:T(8,128)S(1)} %slice.10), channel_id=1, source_target_pairs={{1,0},{2,1},{3,2},{4,3},{5,4},{6,5},{7,6},{9,8},{10,9},{11,10},{12... | collective-permute-start | bytes 196616 | tf_op jit(solution)/shard_map/ppermute | solution.py:988
  148.6 13.1 %collective-permute-start.30 = (bf16[4,192,256]{2,1,0:T(8,128)(2,1)S(1)}, bf16[4,192,256]{2,1,0:T(8,128)(2,1)S(1)}, u32[]{:S(2)}, u32[]{:S(2)}) collective-permute-start(bf16[4,192,256]{2,1,0:T(8,128)(2,1)S(1)} %small_join0.1.mine_ref), channel_id=1, source_target_pairs={{0,1},{1,0},{2,3},{3,2},{4,5},{5,4},{6,7},{7,6},{8,9},{9,8},{10,11... | collective-permute-start | bytes 1179656 | tf_op jit(solution)/shard_map/ppermute | solution.py:829
  158.2 5.9 %collective-permute-start.22 = (bf16[64,1024]{1,0:T(8,128)(2,1)S(1)}, bf16[64,1024]{1,0:T(8,128)(2,1)S(1)}, u32[]{:S(2)}, u32[]{:S(2)}) collective-permute-start(bf16[64,1024]{1,0:T(8,128)(2,1)S(1)} %get-tuple-element.160), channel_id=1, source_target_pairs={{0,16},{8,24},{16,0},{24,8},{1,17},{9,25},{17,1},{25,9},{2,18},{10... | collective-permute-start | bytes 393224 | tf_op jit(solution)/shard_map/ppermute | solution.py:829

commit v4 on v3

--- a/solution.py
+++ b/solution.py
@@ -16,7 +16,6 @@
 EDGE = 16
 UNROLL = 8
 bf16, f32 = jnp.bfloat16, jnp.float32
-SMEM_SPEC = pl.BlockSpec(memory_space=pltpu.SMEM)
 
 
 def nt(a, b):
@@ -31,16 +30,30 @@
     return jnp.dot(a, b, preferred_element_type=f32)
 
 
-def plain_call(kernel, name, out_shape, args, us, scratch=(), limit=12):
+ANY_SPEC = pl.BlockSpec(memory_space=pltpu.HBM)
+
+
+class Here:
+    def __getitem__(self, which):
+        if which == 1:
+            return lax.axis_index("dp")
+        seq = lax.axis_index("seq")
+        return seq % 2 if which == 0 else seq // 2
+
+
+def plain_call(kernel, name, out_shape, args, us, scratch=(), limit=12, specs=None):
+    specs = specs or []
     full = lambda x: pl.BlockSpec(x.shape, lambda: (0,) * len(x.shape))
+    stay = lambda n, x: pltpu.with_memory_space_constraint(x, pltpu.HBM) if specs[n : n + 1] == [ANY_SPEC] else x
+    args = [stay(n, x) for n, x in enumerate(args)]
     return pl.pallas_call(
-        kernel,
-        in_specs=[SMEM_SPEC] + [full(x) for x in args[1:]],
+        lambda *refs: kernel(Here(), *refs),
+        in_specs=list(specs) + [full(x) for x in args[len(specs) :]],
         out_specs=[full(x) for x in out_shape],
         out_shape=out_shape,
         scratch_shapes=list(scratch),
         compiler_params=pltpu.CompilerParams(vmem_limit_bytes=limit << 20),
-        cost_estimate=pl.CostEstimate(flops=0, bytes_accessed=int(us * 3.6e6), transcendentals=0),
+        cost_estimate=pl.CostEstimate(flops=int(us * 1e6), bytes_accessed=0, transcendentals=0),
         name=name,
     )(*args)
 
@@ -57,13 +70,13 @@
     return pl.ds(pl.multiple_of(t * SUBS, SUBS), SUBS)
 
 
-def tap_masks(info_ref, docs, taps, length):
+def tap_masks(starts_ref, taps, length):
     row = lax.broadcasted_iota(jnp.int32, (length, LANES), 0)
-    place = info_ref[0] + (row % SUBS) * (length // SUBS) + row // SUBS
+    place = lax.axis_index("seq") * length + (row % SUBS) * (length // SUBS) + row // SUBS
     begin = jnp.zeros_like(place)
     reset = jnp.zeros((length, LANES), f32)
-    for k in range(docs):
-        start = info_ref[1 + k]
+    for k in range(starts_ref.shape[1]):
+        start = starts_ref[0, k]
         begin = jnp.maximum(begin, jnp.where(place >= start, start, 0))
         reset = jnp.where(place == start, 1.0, reset)
     return [reset] + [jnp.where(begin <= place - j, 1.0, 0.0) for j in range(1, taps)]
@@ -124,21 +137,54 @@
 
 
 def front_kernel(
-    states, rank, taps, docs, rows_size,
-    info_ref, tok_ref, left_ref, cot_ref, gain_ref, vec_ref, rates_ref, dtw_ref, win_ref, wo_ref, wx_ref,
+    states, rank, taps, rows_size,
+    here, starts_hbm, tok_hbm, cot_hbm, gain_hbm, convw_hbm, convb_hbm, dtb_hbm, skip_hbm, alog_hbm, dtw_hbm, wx_hbm,
+    win_hbm, wo_hbm, left_ref,
     tok_out, cot_out, ext_ref, inner_ref, gate_ref, ggated_ref, gs_ref, dt_ref, proj_ref, table, pack_ref,
-    dx_ref, ex_ref, db_ref, fx_ref, *rest,
+    dx_ref, ex_ref, db_ref, fx_ref, vec_ref, rates_ref, gain_ref, masks, *rest,
 ):
-    blocks, (normed, masks, dtm_s, u_s, ends) = rest[:rows_size], rest[rows_size:]
+    blocks = rest[:rows_size]
+    (normed, dtm_s, u_s, ends, starts_ref, tok_ref, cot_ref, gain_s, convw_s, convb_s, dtb_s, skip_s, alog_s, dtw_ref, wx_ref,
+     win_ref, wo_ref, sems, wide_sems) = rest[rows_size:]
     length, model = cot_ref.shape
     width = rates_ref.shape[1]
     steps = length // SUBS
     rim = taps - 1
     maps = rank + 2 * states
-
+    block = min(512, width)
+    pairs = (
+        (tok_hbm.at[0], tok_ref), (gain_hbm, gain_s), (cot_hbm.at[0], cot_ref), (convw_hbm, convw_s),
+        (convb_hbm, convb_s), (dtb_hbm, dtb_s), (skip_hbm, skip_s), (alog_hbm, alog_s), (wx_hbm, wx_ref),
+        (dtw_hbm, dtw_ref), (starts_hbm, starts_ref),
+    )
+    loads = [pltpu.make_async_copy(a, b, sems.at[n]) for n, (a, b) in enumerate(pairs)]
+
+    def weights(j):
+        conv = tile_at(j * block, block)
+        gate = tile_at(width + j * block, block)
+        return [
+            pltpu.make_async_copy(win_hbm.at[:, conv], win_ref.at[:, conv], wide_sems.at[0, j]),
+            pltpu.make_async_copy(win_hbm.at[:, gate], win_ref.at[:, gate], wide_sems.at[1, j]),
+            pltpu.make_async_copy(wo_hbm.at[conv, :], wo_ref.at[conv, :], wide_sems.at[2, j]),
+        ]
+
+    for load in loads:
+        load.start()
+    for j in range(width // block):
+        for load in weights(j):
+            load.start()
+    for load in loads[:2]:
+        load.wait()
+    gain_ref[...] = gain_s[...].astype(f32).reshape(1, model)
     tok_out[pl.ds(0, length), :] = turned(tok_ref[...], False)
     left = left_ref[...].astype(f32)
     tok_out[pl.ds(length, EDGE), :] = jnp.concatenate([left, jnp.zeros((EDGE - rim, model), f32)], axis=0).astype(bf16)
+    for load in loads[2:]:
+        load.wait()
+    vec_ref[pl.ds(0, taps), :] = convw_s[...].astype(f32)
+    for n, ref in enumerate((convb_s, dtb_s, skip_s)):
+        vec_ref[pl.ds(taps + n, 1), :] = ref[...].astype(f32).reshape(1, width)
+    rates_ref[...] = jnp.minimum(-jnp.exp(alog_s[...]), -LEAST_RATE) * (1.0 / LN2)
     cot = turned(cot_ref[...], False)
     cot_out[...] = cot
     thin = model // rows_size
@@ -146,18 +192,19 @@
         blocks[k][:, :model] = tok_out[pl.ds(0, length), :]
         for q in range(rows_size):
 
-            @pl.when((info_ref[3 + docs] ^ k) == q)
+            @pl.when((here[1] ^ k) == q)
             def _():
                 blocks[k][:, model:] = cot[:, q * thin : (q + 1) * thin]
 
     normed[...] = normalise(tok_out[...], gain_ref[...])
-    for k, mask in enumerate(tap_masks(info_ref, docs, taps, length)):
+    for k, mask in enumerate(tap_masks(starts_ref, taps, length)):
         masks[k] = mask
     proj_ref[...] = jnp.zeros_like(proj_ref)
-    block = min(512, width)
 
     def project(j, _):
         wide = tile_at(j * block, block)
+        for load in weights(j):
+            load.wait()
         conv = nn(normed[...], win_ref[:, wide]).astype(bf16)
         gate = nn(normed[pl.ds(0, length), :], win_ref[:, tile_at(width + j * block, block)])
         ggated = nt(cot_out[...], wo_ref[wide, :])
@@ -239,10 +286,10 @@
     pack_ref[...] = ends[...].astype(bf16)
 
 
-def front(info, tok, left, cot, gain, vec, rates, dtw, in_weight, out_weight, wx, taps, docs, rows_size):
-    length, model = cot.shape
-    states, width = rates.shape
-    rank = dtw.shape[0]
+def front(starts, tok, cot, gain, convw, convb, dtb, skip, alog, dtw, wx, in_weight, out_weight, left, rows_size):
+    length, model = cot.shape[1:]
+    states, width = alog.shape
+    rank, taps = dtw.shape[0], convw.shape[0]
     pack_rows = 2 * states + EDGE
     shape = jax.ShapeDtypeStruct
     big = lambda dtype: shape((length, width), dtype)
@@ -250,17 +297,24 @@
         shape((length + EDGE, model), bf16), shape((length, model), bf16), shape((length + 2 * EDGE, width), bf16),
         big(bf16), big(f32), big(f32), big(f32), big(f32),
         shape((length, LANES), f32), shape((length, 2 * states * LANES), f32), shape((pack_rows, width), bf16),
-    ] + [shape((states, SUBS, width), f32)] * 4 + [shape((length, model + model // rows_size), bf16)] * rows_size
+    ] + [shape((states, SUBS, width), f32)] * 4 + [
+        shape((taps + 4, width), f32), shape((states, width), f32), shape((1, model), f32),
+        shape((taps, length, LANES), f32),
+    ] + [shape((length, model + model // rows_size), bf16)] * rows_size
+    args = (starts, tok, cot, gain, convw, convb, dtb, skip, alog, dtw, wx, in_weight, out_weight, left)
     scratch = [
         pltpu.VMEM((length + EDGE, model), bf16),
-        pltpu.VMEM((taps, length, LANES), f32),
         pltpu.VMEM((length, LANES), f32),
         pltpu.VMEM((length, LANES), f32),
         pltpu.VMEM((pack_rows, width), f32),
-    ]
+        pltpu.SMEM(starts.shape, jnp.int32),
+        pltpu.VMEM((length, model), bf16),
+        pltpu.VMEM((length, model), bf16),
+    ] + [pltpu.VMEM(x.shape, x.dtype) for x in args[3:13]]
+    scratch += [pltpu.SemaphoreType.DMA((11,)), pltpu.SemaphoreType.DMA((3, width // min(512, width)))]
     return plain_call(
-        functools.partial(front_kernel, states, rank, taps, docs, rows_size), "front", out,
-        (info, tok, left, cot, gain, vec, rates, dtw, in_weight, out_weight, wx), 18, scratch, 10,
+        functools.partial(front_kernel, states, rank, taps, rows_size), "front", out,
+        args, 20, scratch, 24, [ANY_SPEC] * 13,
     )
 
 
@@ -273,21 +327,20 @@
 
 
 def forward_kernel(
-    states, taps, docs, slices,
-    info_ref, vec_ref, rates_ref, entry_ref, table, dt_ref, inner_ref, gate_ref, ggated_ref, dx_ref, ex_ref,
+    states, taps, slices,
+    here, masks, vec_ref, rates_ref, entry_ref, table, dt_ref, inner_ref, gate_ref, ggated_ref, dx_ref, ex_ref,
     gated_ref, ggate_ref, *rest,
 ):
-    blocks, (reset, dtm_s, u_s, y_s, held) = rest[:slices], rest[slices:]
+    blocks, (dtm_s, u_s, y_s, held) = rest[:slices], rest[slices:]
     length, width = inner_ref.shape
     tiles, steps = width // LANES, length // SUBS
     zero = jnp.zeros((SUBS, LANES), f32)
-    reset[...] = tap_masks(info_ref, docs, 1, length)[0]
 
     def scan(tile, _):
         at = tile_at(tile * LANES)
         dt = dt_ref[:, at]
         x = inner_ref[:, at].astype(f32)
-        dtm_s[...] = jnp.where(reset[...] > 0.0, FAR, dt)
+        dtm_s[...] = jnp.where(masks[0] > 0.0, FAR, dt)
         u_s[...] = dt * x
 
         def wide(ref, n):
@@ -326,32 +379,32 @@
         held[side, :, at], held[side + 2, :, at] = halves_of(near, far)
     for n in range(slices):
         blocks[n][:, :width] = gated_ref[...]
-        blocks[n][:, width:] = held[info_ref[3 + docs] ^ n]
-
-
-def forward(info, vec, rates, entry, table, dt, inner, gate, ggated, dx, ex, taps, docs, slices):
+        blocks[n][:, width:] = held[here[1] ^ n]
+
+
+def forward(masks, vec, rates, entry, table, dt, inner, gate, ggated, dx, ex, taps, slices):
     length, width = inner.shape
     states = rates.shape[0]
     shape = jax.ShapeDtypeStruct
     return plain_call(
-        functools.partial(forward_kernel, states, taps, docs, slices),
+        functools.partial(forward_kernel, states, taps, slices),
         "forward",
         [shape((length, width), bf16)] * 2 + [shape((length, width + width // max(slices, 1)), bf16)] * slices,
-        (info, vec, rates, entry, table, dt, inner, gate, ggated, dx, ex),
+        (masks, vec, rates, entry, table, dt, inner, gate, ggated, dx, ex),
         8,
-        [pltpu.VMEM((length, LANES), f32)] * 4 + [pltpu.VMEM((max(slices, 1), length, width // max(slices, 1)), bf16)],
+        [pltpu.VMEM((length, LANES), f32)] * 3 + [pltpu.VMEM((max(slices, 1), length, width // max(slices, 1)), bf16)],
         8,
     )
 
 
 def backward_kernel(
-    states, rank, taps, docs, slices,
-    info_ref, proj_ref, tok_ref, gain_ref, dtw_ref, vec_ref, rates_ref, entry_ref, arrive_ref, table,
-    dt_ref, inner_ref, gs_ref, dx_ref, ex_ref, db_ref, fx_ref, ggate_ref, ext_ref, win_ref, wx_ref,
-    mine_ref, theirs_ref, ngrad, *rest,
+    states, rank, taps, slices,
+    here, win_hbm, dtw_hbm, wx_hbm, masks, proj_ref, tok_ref, gain_ref, vec_ref, rates_ref, entry_ref, arrive_ref,
+    table, dt_ref, inner_ref, gs_ref, dx_ref, ex_ref, db_ref, fx_ref, ggate_ref, ext_ref,
+    ngrad, *rest,
 ):
-    blocks = rest[: max(slices, 1)]
-    (acc, hs, decays, masks, dtm_s, u_s, s1_s, s2_s, isg, raw_s, sent_s, low_acc, pg, small, held) = rest[max(slices, 1) :]
+    blocks, rest = rest[: max(slices, 1)], rest[max(slices, 1) :]
+    (acc, hs, decays, dtm_s, u_s, s1_s, s2_s, isg, raw_s, sent_s, low_acc, pg, small, held, win_ref, dtw_ref, wx_ref, sems) = rest[-18:]
     length, width = inner_ref.shape
     model = tok_ref.shape[1]
     steps, tiles = length // SUBS, width // LANES
@@ -364,9 +417,10 @@
     zero = jnp.zeros((SUBS, LANES), f32)
     half = states // 2
     block = min(512, width)
-
-    for k, mask in enumerate(tap_masks(info_ref, docs, taps, length)):
-        masks[k] = mask
+    pairs = ((dtw_hbm, dtw_ref), (wx_hbm, wx_ref), (win_hbm, win_ref))
+    loads = [pltpu.make_async_copy(a, b, sems.at[n]) for n, (a, b) in enumerate(pairs)]
+    for load in loads:
+        load.start()
     low_acc[...] = jnp.zeros_like(low_acc)
     small[pl.ds(small.shape[0] - EDGE, EDGE), :] = jnp.zeros((EDGE, width), f32)
     low = proj_ref[:, :rank].astype(bf16)
@@ -376,6 +430,7 @@
         return 0
 
     lax.fori_loop(0, steps, clear, 0)
+    loads[0].wait()
 
     def scan(tile, _):
         at = tile_at(tile * LANES)
@@ -474,6 +529,8 @@
 
     lax.fori_loop(0, steps, gather_maps, 0)
     pg[...] = low_acc[...].astype(bf16)
+    for load in loads[1:]:
+        load.wait()
     ngrad[...] = jnp.zeros_like(ngrad)
 
     def close(j, _):
@@ -539,20 +596,21 @@
         for n in range(slices):
             held[n, edge_rows, :] = (held[n, edge_rows, :].astype(f32) + extra).astype(bf16)
         for n in range(slices):
-            blocks[n][...] = held[info_ref[3 + docs] ^ n]
-    count, chunk = mine_ref.shape[0], mine_ref.shape[2]
+            blocks[n][...] = held[here[1] ^ n]
+    mine_ref, theirs_ref = rest[:2]
+    chunk = mine_ref.shape[2]
     for c in range(2):
 
-        @pl.when(info_ref[2 + docs] == c)
+        @pl.when(here[0] == c)
         def _():
-            for n in range(count):
-                at, other = (c * count + n) * chunk, ((1 - c) * count + n) * chunk
+            for n in range(mine_ref.shape[0]):
+                at, other = (2 * n + c) * chunk, (2 * n + 1 - c) * chunk
                 mine_ref[n] = small[:, at : at + chunk]
                 theirs_ref[n] = small[:, other : other + chunk].astype(bf16)
 
 
-def backward(info, proj, tok, gain, dtw, vec, rates, entry, arrive, table, dt, inner, gs, deep4, ggate, ext,
-             in_weight, wx, taps, docs, slices, chunks):
+def backward(masks, in_weight, dtw, wx, proj, tok, gain, vec, rates, entry, arrive, table, dt, inner, gs, deep4,
+             ggate, ext, taps, slices, chunks):
     length, width = inner.shape
     model = tok.shape[1]
     states = rates.shape[0]
@@ -562,20 +620,20 @@
     rows = 2 * rank + 3 * states + taps + 4
     rows = -(-rows // EDGE) * EDGE
     shape = jax.ShapeDtypeStruct
+    parts = max(slices, 1)
     chunk = (chunks, rows, width // (2 * chunks))
-    parts = max(slices, 1)
     return plain_call(
-        functools.partial(backward_kernel, states, rank, taps, docs, slices),
+        functools.partial(backward_kernel, states, rank, taps, slices),
         "backward",
-        [shape(chunk, f32), shape(chunk, bf16), shape((length + EDGE, model), f32)]
-        + [shape((length + EDGE, width // parts), bf16)] * parts,
-        (info, proj, tok, gain, dtw, vec, rates, entry, arrive, table, dt, inner, gs, *deep4, ggate, ext, in_weight, wx),
+        [shape((length + EDGE, model), f32)]
+        + [shape((length + EDGE, width // parts), bf16)] * parts
+        + [shape(chunk, f32), shape(chunk, bf16)],
+        (in_weight, dtw, wx, masks, proj, tok, gain, vec, rates, entry, arrive, table, dt, inner, gs, *deep4, ggate, ext),
         24,
         [
             pltpu.VMEM((length, 2 * states * LANES), f32),
             pltpu.VMEM((steps + 1, states, SUBS, LANES), f32),
             pltpu.VMEM((steps, states, SUBS, LANES), f32),
-            pltpu.VMEM((taps, length, LANES), f32),
         ]
         + [pltpu.VMEM((length, LANES), f32)] * 4
         + [
@@ -586,12 +644,15 @@
             pltpu.VMEM((length, LANES), bf16),
             pltpu.VMEM((rows, width), f32),
             pltpu.VMEM((parts, length + EDGE, width // parts), bf16),
-        ],
-        14,
+        ]
+        + [pltpu.VMEM(x.shape, x.dtype) for x in (in_weight, dtw, wx)]
+        + [pltpu.SemaphoreType.DMA((3,))],
+        24,
+        [ANY_SPEC] * 3,
     )
 
 
-def finish_kernel(rim, info_ref, ngrad_ref, back_ref, tok_ref, cot_ref, gain_ref, gated_ref, wo_ref, grad_ref, mixed_ref):
+def finish_kernel(rim, here, ngrad_ref, back_ref, tok_ref, cot_ref, gain_ref, gated_ref, wo_ref, grad_ref, mixed_ref):
     length = cot_ref.shape[0]
     x = tok_ref[pl.ds(0, length), :].astype(f32)
     mixed_ref[...] = turned((x + nn(gated_ref[...], wo_ref[...])).astype(bf16), True)
@@ -618,8 +679,8 @@
     return jnp.where(row == 0, high, jnp.where(row == 1, middle, jnp.where(row == 2, d - high - middle, 0.0)))
 
 
-def pair_parts(info_ref, mine, other, rates, states):
-    first = info_ref[0] == 0
+def pair_parts(here, mine, other, rates, states):
+    first = here[0] == 0
     near, far = jnp.where(first, mine, other), jnp.where(first, other, mine)
     d0, d1 = span_of(near, states), span_of(far, states)
     state = jnp.exp2(rates * d1) * near[:states] + far[:states]
@@ -627,47 +688,47 @@
     return state, flow, span_rows(d0 + d1)
 
 
-def pair_kernel(states, info_ref, mine_ref, other_ref, rates_ref, out_ref):
+def pair_kernel(states, here, mine_ref, other_ref, rates_ref, out_ref):
     state, flow, spans = pair_parts(
-        info_ref, mine_ref[...].astype(f32), other_ref[...].astype(f32), rates_ref[...], states
+        here, mine_ref[...].astype(f32), other_ref[...].astype(f32), rates_ref[...], states
     )
     out_ref[...] = jnp.concatenate([state, flow, spans], axis=0).astype(bf16)
 
 
-def pair_half_kernel(states, info_ref, mine_ref, other_ref, rates_ref, *outs):
+def pair_half_kernel(states, here, mine_ref, other_ref, rates_ref, out_ref):
     half = rates_ref.shape[1] // 2
-    at = tile_at(info_ref[0] * half, half)
-    state, flow, spans = pair_parts(
-        info_ref, mine_ref[:, at].astype(f32), other_ref[:, at].astype(f32), rates_ref[:, at], states
-    )
-    place = info_ref[2]
-    for k, out in enumerate(outs):
-        up = (place ^ (k + 1)) > place
-        out[...] = jnp.concatenate([jnp.where(up, state, flow), spans], axis=0).astype(bf16)
-
-
-def enter_half_kernel(states, count, info_ref, rates_ref, *rest):
-    gots, (out_ref, held) = rest[: count - 1], rest[count - 1 :]
+    at = tile_at(here[0] * half, half)
+    parts = pair_parts(here, mine_ref[:, at].astype(f32), other_ref[:, at].astype(f32), rates_ref[:, at], states)
+    out_ref[...] = jnp.concatenate(parts, axis=0).astype(bf16)
+
+
+def quad_kernel(states, here, mine_ref, got_ref, rates_ref, near_ref, out_ref):
     half = rates_ref.shape[1] // 2
-    rates = rates_ref[:, tile_at(info_ref[0] * half, half)]
-    place = info_ref[2]
-    for k, got in enumerate(gots):
-        held[place ^ (k + 1)] = got[...].astype(f32)
-    held[place] = jnp.zeros_like(held[0])
-    entry, arrive = jnp.zeros_like(rates), jnp.zeros_like(rates)
-    for k in range(count):
-        x = held[k]
-        whole = jnp.exp2(rates * (x[states : states + 1] + x[states + 1 : states + 2] + x[states + 2 : states + 3]))
-        entry = jnp.where(k < place, whole * entry + x[:states], entry)
-    for k in reversed(range(count)):
-        x = held[k]
-        whole = jnp.exp2(rates * (x[states : states + 1] + x[states + 1 : states + 2] + x[states + 2 : states + 3]))
-        arrive = jnp.where(k > place, whole * arrive + x[:states], arrive)
+    rates = rates_ref[:, tile_at(here[0] * half, half)]
+    mine, got = mine_ref[...].astype(f32), got_ref[...].astype(f32)
+    first = here[2] % 2 == 0
+    low, high = jnp.where(first, mine, got), jnp.where(first, got, mine)
+    d0, d1 = span_of(low, states), span_of(high, states)
+    w0, w1 = jnp.exp2(rates * d0), jnp.exp2(rates * d1)
+    near_ref[pl.ds(0, states), :] = jnp.where(first, 0.0, low[:states])
+    near_ref[pl.ds(states, states), :] = jnp.where(first, high[states : 2 * states], 0.0)
+    near_ref[pl.ds(2 * states, states), :] = jnp.where(first, 1.0, w0)
+    near_ref[pl.ds(3 * states, states), :] = jnp.where(first, w1, 1.0)
+    state = w1 * low[:states] + high[:states]
+    flow = low[states : 2 * states] + w0 * high[states : 2 * states]
+    out_ref[...] = jnp.where(here[2] < 2, state, flow).astype(bf16)
+
+
+def enter_half_kernel(states, here, near_ref, got_ref, out_ref):
+    got = got_ref[...].astype(f32)
+    low = here[2] < 2
+    entry = near_ref[pl.ds(0, states), :] + jnp.where(low, 0.0, near_ref[pl.ds(2 * states, states), :] * got)
+    arrive = near_ref[pl.ds(states, states), :] + jnp.where(low, near_ref[pl.ds(3 * states, states), :] * got, 0.0)
     out_ref[...] = jnp.concatenate([entry, arrive], axis=0)
 
 
-def enter_both_kernel(states, info_ref, other_ref, rates_ref, here_ref, there_ref, entry_ref, arrive_ref):
-    core = info_ref[0]
+def enter_both_kernel(states, here, other_ref, rates_ref, here_ref, there_ref, entry_ref, arrive_ref):
+    core = here[0]
     half = rates_ref.shape[1] // 2
     for part, side in ((here_ref, core), (there_ref, 1 - core)):
         at = tile_at(side * half, half)
@@ -678,8 +739,8 @@
         arrive_ref[:, at] = jnp.where(core == 0, whole * arrive + other[states : 2 * states], arrive)
 
 
-def enter_kernel(states, count, info_ref, other_ref, rates_ref, chips_ref, entry_ref, arrive_ref):
-    core, place = info_ref[0], info_ref[2]
+def enter_kernel(states, count, here, other_ref, rates_ref, chips_ref, entry_ref, arrive_ref):
+    core, place = here[0], here[2]
     rates = rates_ref[...]
 
     def split(x):
@@ -700,39 +761,54 @@
     arrive_ref[...] = jnp.where(core == 0, whole * arrive + f, arrive)
 
 
-def gate_out_kernel(size, chips, thin, info_ref, gain_ref, *rest):
-    early, late, (normed_ref, mine_ref, theirs_ref) = rest[:size], rest[size : 2 * size], rest[2 * size :]
-    model = gain_ref.shape[1]
-    length = early[0].shape[0]
+def early_kernel(here, gain_ref, *rest):
+    early, (normed_ref, left_ref) = rest[:-2], rest[-2:]
+    length, model = early[0].shape[0], gain_ref.shape[1]
+    for k, x in enumerate(early):
+        at = pl.ds(k * length, length)
+        normed_ref[at, :] = normalise(x[:, :model], gain_ref[...])
+        left_ref[at, :] = x[:, model:]
+
+
+def gate_out_kernel(size, chips, thin, here, normed_ref, left_ref, *rest):
+    late, mine_ref, theirs = rest[:size], rest[size], rest[size + 1 :]
+    model = normed_ref.shape[1]
     width = late[0].shape[1] * size // (size + 1)
-    for k in range(size):
-        normed_ref[pl.ds(k * length, length), :] = normalise(early[k][:, :model], gain_ref[...])
     gate = tn(jnp.concatenate([x[:, width:] for x in late], axis=0), normed_ref[...])
-    left = jnp.concatenate([x[:, model:] for x in early], axis=0)
-    out = tn(left, jnp.concatenate([x[:, :width] for x in late], axis=0))
+    out = tn(left_ref[...], jnp.concatenate([x[:, :width] for x in late], axis=0))
     half = LANES // 2
     for c in range(2):
 
-        @pl.when(info_ref[0] == c)
+        @pl.when(here[0] == c)
         def _():
             for q in range(chips):
-                for ref, side in ((mine_ref, c), (theirs_ref, 1 - c)):
+                for ref, side in ((mine_ref.at[q], c), (theirs[q], 1 - c)):
                     at = q * LANES + side * half
-                    ref[q, pl.ds(0, half), :] = gate[at : at + half].astype(ref.dtype)
+                    ref[pl.ds(0, half), :] = gate[at : at + half].astype(ref.dtype)
                     at = (2 * q + side) * thin
                     for n in range(width // model):
                         piece = out[at : at + thin, n * model : (n + 1) * model]
-                        ref[q, pl.ds(half + n * thin, thin), :] = piece.astype(ref.dtype)
-
-
-def conv_kernel(size, chips, rim, info_ref, normed_ref, *rest):
-    gots, (mine_ref, theirs_ref) = rest[:size], rest[size:]
-    length, wide = gots[0].shape[0] - EDGE, gots[0].shape[1]
+                        ref[pl.ds(half + n * thin, thin), :] = piece.astype(ref.dtype)
+
+
+def flat(x, pieces):
+    rows = x.shape[0] // pieces
+    return jnp.concatenate([x[n * rows : (n + 1) * rows] for n in range(pieces)], axis=1)
+
+
+def tall(x, pieces):
+    lanes = x.shape[1] // pieces
+    return jnp.concatenate([x[:, n * lanes : (n + 1) * lanes] for n in range(pieces)], axis=0)
+
+
+def conv_kernel(length, chips, rim, here, normed_ref, *rest):
+    gots, (mine_ref, theirs_ref) = rest[:-2], rest[-2:]
+    wide = gots[0].shape[1]
     model = normed_ref.shape[1]
     pieces = model // wide
     got = jnp.concatenate([got[pl.ds(0, length), :] for got in gots], axis=0)
     lefts, rights = [], []
-    for k in range(size):
+    for k in range(len(gots)):
         edge = gots[k][pl.ds(length, EDGE), :].astype(f32)
         row = lax.broadcasted_iota(jnp.int32, (SUBS, model), 0)
         left = jnp.zeros((SUBS, model), f32)
@@ -748,23 +824,70 @@
     half = LANES // 2
     for c in range(2):
 
-        @pl.when(info_ref[0] == c)
+        @pl.when(here[0] == c)
         def _():
             for q in range(chips):
                 at = q * LANES
                 mine_ref[q] = conv[at + c * half : at + (c + 1) * half]
-                theirs_ref[q] = conv[at + (1 - c) * half : at + (2 - c) * half].astype(bf16)
-
-
-def halve_kernel(which, bit, info_ref, mine_ref, got_ref, keep_ref, send_ref):
-    place = (info_ref[which] >> bit) & 1
-    for n in range(mine_ref.shape[0] // 2):
+                theirs_ref[pl.ds(q * half, half), :] = conv[at + (1 - c) * half : at + (2 - c) * half].astype(bf16)
+
+
+def mix0_kernel(here, mine_ref, got_ref, small_ref, small_got, keep_ref, small_out, send_ref):
+    place = here[2] & 1
+    half, count = mine_ref.shape[1], mine_ref.shape[0] // 2
+    at = lambda n: pl.ds(pl.multiple_of(n * half, half), half)
+    for n in range(count):
         stay, leave = 2 * n + place, 2 * n + 1 - place
-        keep_ref[n] = mine_ref[stay] + got_ref[stay].astype(f32)
-        send_ref[n] = (mine_ref[leave] + got_ref[leave].astype(f32)).astype(bf16)
-
-
-def go_last_kernel(thin, info_ref, mine_ref, got_ref, gate_ref, out_ref):
+        keep_ref[n] = mine_ref[stay] + got_ref[at(stay), :].astype(f32)
+        send_ref[at(n), :] = (mine_ref[leave] + got_ref[at(leave), :].astype(f32)).astype(bf16)
+    small = small_ref[0] + small_got[0].astype(f32)
+    small = flat(small, mine_ref.shape[2] // small.shape[1]).astype(bf16)
+    small_out[...] = small
+    send_ref[pl.ds(count * half, small.shape[0]), :] = small
+
+
+def mix1_kernel(here, mine_ref, got_ref, small_ref, keep_ref, small_out, send_ref):
+    place = (here[2] >> 1) & 1
+    half = mine_ref.shape[1]
+    at = lambda n: pl.ds(pl.multiple_of(n * half, half), half)
+    keep_ref[...] = mine_ref[place] + got_ref[at(place), :].astype(f32)
+    send_ref[pl.ds(0, half), :] = (mine_ref[1 - place] + got_ref[at(1 - place), :].astype(f32)).astype(bf16)
+    rows = small_ref.shape[0]
+    small = (small_ref[...].astype(f32) + got_ref[pl.ds(2 * half, rows), :].astype(f32)).astype(bf16)
+    small_out[...] = small
+    send_ref[pl.ds(half, rows), :] = small
+
+
+def halve_kernel(which, bit, here, mine_ref, *rest):
+    gots, (keep_ref, send_ref) = rest[:-2], rest[-2:]
+    place = (here[which] >> bit) & 1
+    each = mine_ref.shape[0] // len(gots)
+    for n in range(mine_ref.shape[0]):
+        got = gots[n // each]
+        total = mine_ref[n] + (got[n % each] if len(got.shape) == 3 else got[...]).astype(f32)
+        for side in range(2):
+
+            @pl.when(place == side)
+            def _():
+                if n % 2 == side:
+                    keep_ref[n // 2] = total
+                else:
+                    send_ref[n // 2] = total.astype(bf16)
+
+
+def cross_kernel(here, mine_ref, got_ref, small_ref, gate_ref, keep_ref, small_out, send_ref):
+    half = mine_ref.shape[0]
+    conv = mine_ref[...] + got_ref[pl.ds(0, half), :].astype(f32)
+    first = here[1] < 2
+    keep_ref[...] = jnp.where(first, conv, gate_ref[...])
+    send_ref[pl.ds(0, half), :] = jnp.where(first, gate_ref[...], conv).astype(bf16)
+    rows = small_ref.shape[0]
+    small = (small_ref[...].astype(f32) + got_ref[pl.ds(half, rows), :].astype(f32)).astype(bf16)
+    small_out[...] = small
+    send_ref[pl.ds(half, rows), :] = small
+
+
+def go_last_kernel(thin, here, mine_ref, got_ref, gate_ref, out_ref):
     half, model = gate_ref.shape
     both = mine_ref[0] + got_ref[0].astype(f32)
     gate_ref[...] = both[:half]
@@ -772,38 +895,29 @@
         out_ref[:, n * model : (n + 1) * model] = both[half + n * thin : half + (n + 1) * thin]
 
 
-def cross_kernel(info_ref, mine_ref, got_ref, gate_ref, keep_ref, send_ref):
-    conv = mine_ref[0] + got_ref[0].astype(f32)
-    first = info_ref[1] < 2
-    keep_ref[...] = jnp.where(first, conv, gate_ref[...])
-    send_ref[...] = jnp.where(first, gate_ref[...], conv).astype(bf16)
-
-
-def in_last_kernel(info_ref, keep_ref, got_ref, out_ref):
-    keep, got = keep_ref[...], got_ref[...].astype(f32)
-    first = info_ref[1] < 2
+def in_last_kernel(here, keep_ref, got_ref, out_ref):
+    half = keep_ref.shape[0]
+    keep, got = keep_ref[...], got_ref[pl.ds(0, half), :].astype(f32)
+    first = here[1] < 2
     both = jnp.concatenate([jnp.where(first, keep, got), jnp.where(first, got, keep)], axis=0)
     out_ref[...] = both.T
 
 
-def add_kernel(info_ref, mine_ref, got_ref, out_ref):
-    mine = mine_ref[...].reshape(out_ref.shape).astype(bf16).astype(f32)
-    out_ref[...] = (mine + got_ref[...].reshape(out_ref.shape).astype(f32)).astype(bf16)
-
-
-def join_kernel(which, bit, info_ref, mine_ref, got_ref, out_ref):
-    place = (info_ref[which] >> bit) & 1
-    for n in range(mine_ref.shape[0]):
-        out_ref[2 * n + place] = mine_ref[n]
-        out_ref[2 * n + 1 - place] = got_ref[n]
-
-
-def unpack_kernel(edges, info_ref, rates_ref, mine_ref, other_ref, *outs):
-    size, chunk = mine_ref.shape[0], mine_ref.shape[2]
-    for c, part in ((info_ref[0], mine_ref), (1 - info_ref[0], other_ref)):
+def join_kernel(here, *refs):
+    parts, out_ref = refs[:-1], refs[-1]
+    rows = out_ref.shape[1]
+    for k, part in enumerate(parts):
+        out_ref[here[1] ^ k] = part[pl.ds(part.shape[0] - rows, rows), :]
+
+
+def unpack_kernel(edges, here, rates_ref, mine_ref, other_ref, *outs):
+    size = mine_ref.shape[0]
+    chunk = rates_ref.shape[1] // (2 * size)
+    pieces = mine_ref.shape[2] // chunk
+    for c, part in ((here[0], mine_ref), (1 - here[0], other_ref)):
         for k in range(size):
-            at = tile_at((c * size + k) * chunk, chunk)
-            block = part[k].astype(f32)
+            at = tile_at((2 * k + c) * chunk, chunk)
+            block = tall(part[k].astype(f32), pieces)
             for n, out in enumerate(outs):
                 piece = block[edges[n] : edges[n + 1]]
                 out[:, at] = piece * rates_ref[:, at] if n == 2 else piece
@@ -881,7 +995,6 @@
     inner_width, states = a_log.shape
     low_rank = dt_weight.shape[0]
     taps = conv_weight.shape[1]
-    docs = doc_starts.shape[1]
     rim = taps - 1
     dp_size, seq_size = lax.axis_size("dp"), lax.axis_size("seq")
     core, outer = Group("seq", 2, 1), Group("seq", seq_size // 2, 2)
@@ -895,136 +1008,146 @@
     chips, slices = outer.size, dp_size if tiled else 0
     shape = jax.ShapeDtypeStruct
 
-    base = lax.axis_index("seq") * length
-    as_int = lambda *v: jnp.stack([jnp.asarray(x, jnp.int32) for x in v])
-    info = jnp.concatenate([as_int(base), doc_starts[0], as_int(outer.place, core.place, rows_group.place)])
-    where = as_int(core.place, rows_group.place, outer.place)
-    gain = norm_gain.astype(f32)[None]
-    vec = jnp.concatenate(
-        [conv_weight.T, conv_bias[None], dt_bias[None], skip_scale[None], jnp.zeros((1, inner_width), bf16)], axis=0
-    ).astype(f32)
+    wx = xproj_weight.T
     decay_rates = -jnp.exp(a_log).T
-    rates = jnp.minimum(decay_rates, -LEAST_RATE) / LN2
 
     left = lax.ppermute(tokens[0, length - rim :], "seq", [(i, i + 1) for i in range(seq_size - 1)])
-    wx = xproj_weight.T
-    tok, cot, ext, inner, gate, ggated, gs, dt, proj, table, mine, dx, ex, db, fx, *early = front(
-        info, tokens[0], left, cotangent[0], gain, vec, rates, dt_weight, in_weight, out_weight, wx, taps, docs, dp_size
+    tok, cot, ext, inner, gate, ggated, gs, dt, proj, table, mine, dx, ex, db, fx, vec, rates, gain, masks, *early = front(
+        doc_starts, tokens, cotangent, norm_gain, conv_weight.T, conv_bias, dt_bias, skip_scale, a_log.T, dt_weight, wx,
+        in_weight, out_weight, left, dp_size,
     )
+    early = rows_group.trade(early)
     other = core.swap(mine, 1)
-    half = shape((states + EDGE, inner_width // 2), bf16)
     entering = [shape(rates.shape, f32)] * 2
     if tiled:
-        to_chips = plain_call(
-            functools.partial(pair_half_kernel, states), "pair", [half] * (chips - 1), (where, mine, other, rates), 2
+        half = inner_width // 2
+        (mine_half,) = plain_call(
+            functools.partial(pair_half_kernel, states),
+            "pair",
+            [shape((2 * states + EDGE, half), bf16)],
+            (mine, other, rates),
+            1,
         )
-        gots = [outer.swap(x, k + 1) for k, x in enumerate(to_chips)]
+        near, far = plain_call(
+            functools.partial(quad_kernel, states),
+            "quad",
+            [shape((4 * states, half), f32), shape((states, half), bf16)],
+            (mine_half, outer.swap(mine_half, 1), rates),
+            1,
+        )
         (here,) = plain_call(
-            functools.partial(enter_half_kernel, states, chips),
+            functools.partial(enter_half_kernel, states),
             "enter_half",
-            [shape((2 * states, inner_width // 2), f32)],
-            (where, rates, *gots),
+            [shape((2 * states, half), f32)],
+            (near, outer.swap(far, 2)),
             1,
-            [pltpu.VMEM((chips, states + EDGE, inner_width // 2), f32)],
         )
         entry, arrive = plain_call(
-            functools.partial(enter_both_kernel, states), "enter", entering, (where, other, rates, here, core.swap(here, 1)), 1
+            functools.partial(enter_both_kernel, states), "enter", entering, (other, rates, here, core.swap(here, 1)), 1
         )
     else:
         (chip,) = plain_call(
-            functools.partial(pair_kernel, states), "pair", [shape(mine.shape, bf16)], (where, mine, other, rates), 2
+            functools.partial(pair_kernel, states), "pair", [shape(mine.shape, bf16)], (mine, other, rates), 2
         )
         got = outer.in_order(outer.gather(chip))
         entry, arrive = plain_call(
-            functools.partial(enter_kernel, states, outer.size), "enter", entering, (where, other, rates, got), 2
+            functools.partial(enter_kernel, states, outer.size), "enter", entering, (other, rates, got), 2
         )
-    early = rows_group.trade(early)
+    entry, early = lax.optimization_barrier((entry, early))
+    gated, ggate, *late = forward(masks, vec, rates, entry, table, dt, inner, gate, ggated, dx, ex, taps, slices)
+    late = rows_group.trade(late) if tiled else rows_group.gather(gated)
     if tiled:
-        entry, early = lax.optimization_barrier((entry, early))
-    gated, ggate, *late = forward(info, vec, rates, entry, table, dt, inner, gate, ggated, dx, ex, taps, docs, slices)
-    late = rows_group.trade(late) if tiled else rows_group.gather(gated)
-    small_mine, small_theirs, ngrad, *sent = backward(
-        info, proj, tok, gain, dt_weight, vec, rates, entry, arrive, table, dt, inner, gs, (dx, ex, db, fx), ggate, ext,
-        in_weight, wx, taps, docs, slices, dp_size,
+        early, _ = lax.optimization_barrier((early, ggate))
+        normed, left_cols = plain_call(
+            early_kernel,
+            "early",
+            [shape((dp_size * length, model), bf16), shape((dp_size * length, model // dp_size), bf16)],
+            (gain, *early),
+            1,
+        )
+        arrive, _ = lax.optimization_barrier((arrive, normed))
+    ngrad, *sent, small, small_theirs = backward(
+        masks, in_weight, dt_weight, wx, proj, tok, gain, vec, rates, entry, arrive, table, dt, inner, gs,
+        (dx, ex, db, fx), ggate, ext, taps, slices, dp_size,
     )
-    sent, small_theirs, late = lax.optimization_barrier((sent, small_theirs, late))
-    rows, chunk = small_mine.shape[1:]
-
-    def call(kernel, name, outs, args, us=1, scratch=()):
-        return plain_call(kernel, name, [shape(*x) for x in outs], (where, *args), us, scratch)
+    rows, chunk = small.shape[1:]
+    turn = [ngrad]
+
+    def call(kernel, name, outs, args, us=1):
+        args, _ = lax.optimization_barrier((tuple(args), turn[0]))
+        got = plain_call(kernel, name, [shape(*x) for x in outs], args, us)
+        turn[0] = got[0]
+        return got
 
     def halve(group, bit, which, mine, got, name):
         count, *rest = mine.shape
         outs = [((count // 2, *rest), f32), ((count // 2, *rest), bf16)]
-        keep, send = call(functools.partial(halve_kernel, which, bit), name, outs, (mine, got))
-        return keep, group.swap(send, 1 << bit)
-
-    conv_got = rows_group.trade(sent) if tiled else None
-    small_got = core.swap(small_theirs, 1)
-    small, got = halve(rows_group, 0, 1, small_mine, small_got, "small_row0")
-    small, got = halve(rows_group, 1, 1, small, got, "small_row1")
-    one = ((1, rows, chunk), bf16)
-    (small,) = call(add_kernel, "small_add", [one], (small, got))
+        keep, send = call(functools.partial(halve_kernel, which, bit), name, outs, (mine, *got))
+        return keep, [group.swap(send, 1 << bit)]
+
+    half = LANES // 2
+    lines = rows * chunk // model
+    part = ((lines, model), bf16)
+    back = lax.ppermute(ngrad[length:], "seq", [(i, i - 1) for i in range(1, seq_size)])
+
+    def finished():
+        return call(
+            functools.partial(finish_kernel, rim),
+            "finish",
+            [((length, model), bf16)] * 2,
+            (ngrad, back, tok, cot, gain, gated, out_weight),
+        )
+
     if tiled:
-        (small,) = call(add_kernel, "small_chip0", [one], (small, outer.swap(small, 1)))
-        (small,) = call(add_kernel, "small_chip1", [one], (small, outer.swap(small, 2)))
+        small_got = [core.swap(small_theirs, 1)]
+        conv_got = rows_group.trade(sent)
+        small, small_got = halve(rows_group, 0, 1, small, small_got, "small_row0")
+        go, *theirs = call(
+            functools.partial(gate_out_kernel, dp_size, chips, thin),
+            "gate_out_columns",
+            [((chips, LANES, model), f32)] + [((LANES, model), bf16)] * chips,
+            (normed, left_cols, *late),
+        )
+        go_got = [core.swap(x, 1) for x in theirs]
+        go, go_got = halve(outer, 0, 2, go, go_got, "go_chip0")
+        small, small_got = halve(rows_group, 1, 1, small, small_got, "small_row1")
+        go, go_got = halve(outer, 1, 2, go, go_got, "go_chip1")
+        outs = [((chips, half, model), f32), ((chips * half, model), bf16)]
+        conv, theirs = call(functools.partial(conv_kernel, length, chips, rim), "conv_columns", outs, (normed, *conv_got))
+        got = core.swap(theirs, 1)
+        outs = [((chips // 2, half, model), f32), part, ((chips // 2 * half + lines, model), bf16)]
+        conv, small, send = call(mix0_kernel, "mix0", outs, (conv, got, small, *small_got))
+        got = outer.swap(send, 1)
+        outs = [((half, model), f32), ((thin, inner_width), f32)]
+        gate_slice, out_share = call(functools.partial(go_last_kernel, thin), "go_last", outs, (go, *go_got))
+        outs = [((half, model), f32), part, ((half + lines, model), bf16)]
+        conv, small, send = call(mix1_kernel, "mix1", outs, (conv, got, small))
+        got = outer.swap(send, 2)
+        tokens_grad, mixed = finished()
+        outs = [((half, model), f32), part, ((half + lines, model), bf16)]
+        keep, small, send = call(cross_kernel, "cross", outs, (conv, got, small, gate_slice))
+        in_got = rows_group.swap(send, 2)
+        smalls = [small, rows_group.swap(small, 1), in_got, rows_group.swap(small, 3)]
+        (small,) = call(join_kernel, "join", [((dp_size, lines, model), bf16)], smalls)
+        small_other = core.swap(small, 1)
+        (in_share,) = call(in_last_kernel, "in_last", [((model, width), f32)], (keep, in_got))
     else:
-        small = total(outer.gather(small)).astype(bf16)
-    join = lambda bit, x, got, name: call(
-        functools.partial(join_kernel, 1, bit), name, [((2 * x.shape[0], rows, chunk), bf16)], (x, got)
-    )[0]
-    small = join(1, small, rows_group.swap(small, 2), "small_join1")
-    small = join(0, small, rows_group.swap(small, 1), "small_join0")
+        tokens_grad, mixed = finished()
+        small = small + core.swap(small_theirs, 1).astype(f32)
+        small = total(rows_group.exchange(small.astype(bf16)))
+        small = total(outer.gather(small.astype(bf16))).astype(bf16)
+        small = small.reshape(rows // lines, lines, -1).swapaxes(0, 1).reshape(lines, model)
+        small = rows_group.in_order(rows_group.gather(small))
+        small_other = core.swap(small, 1)
     sizes = [low_rank + 2 * states, low_rank, states, taps, 1, 1, 1, 1]
     edges = [sum(sizes[:k]) for k in range(len(sizes) + 1)]
     parts = call(
         functools.partial(unpack_kernel, edges),
         "unpack",
         [((size, inner_width), f32) for size in sizes],
-        (decay_rates, small, core.swap(small, 1)),
-        2,
+        (decay_rates, small, small_other),
     )
-
-    back = lax.ppermute(ngrad[length:], "seq", [(i, i - 1) for i in range(1, seq_size)])
-    tokens_grad, mixed = plain_call(
-        functools.partial(finish_kernel, rim),
-        "finish",
-        [shape((length, model), bf16)] * 2,
-        (where, ngrad, back, tok, cot, gain, gated, out_weight),
-        3,
-    )
-
-    if tiled:
-        block = (chips, LANES, model)
-        normed, go_mine, go_theirs = call(
-            functools.partial(gate_out_kernel, dp_size, chips, thin),
-            "gate_out_columns",
-            [((dp_size * length, model), bf16), (block, f32), (block, bf16)],
-            (gain, *early, *late),
-            5,
-        )
-        go, got = halve(outer, 0, 2, go_mine, core.swap(go_theirs, 1), "go_chip0")
-        go, got = halve(outer, 1, 2, go, got, "go_chip1")
-        half = LANES // 2
-        gate_slice, out_share = call(
-            functools.partial(go_last_kernel, thin),
-            "go_last",
-            [((half, model), f32), ((thin, inner_width), f32)],
-            (go, got),
-        )
-        block = (chips, half, model)
-        conv_mine, conv_theirs = call(
-            functools.partial(conv_kernel, dp_size, chips, rim),
-            "conv_columns",
-            [(block, f32), (block, bf16)],
-            (normed, *conv_got),
-            3,
-        )
-        conv, got = halve(outer, 0, 2, conv_mine, core.swap(conv_theirs, 1), "conv_chip0")
-        conv, got = halve(outer, 1, 2, conv, got, "conv_chip1")
-        keep, send = call(cross_kernel, "cross", [((half, model), f32), ((half, model), bf16)], (conv, got, gate_slice))
-        (in_share,) = call(in_last_kernel, "in_last", [((model, width), f32)], (keep, rows_group.swap(send, 2)))
-    else:
+    if not tiled:
 
         def normalised(x):
             wide = x.astype(f32)

time: 166 us -> 152 us (0.916)
  local copies, waits for them, and re-layouts: 14.4 us -> 1.34 us
  starting transfers between devices: 32 us -> 39.5 us
  Pallas kernels: 69.8 us -> 62.9 us
  other arithmetic: 1.74 us -> 0.03 us
    unnamed x22 -> x4, local copies, waits for them, and re-layouts: 9.44 us -> 0.01 us
    ppermute x29, starting transfers between devices: 28.4 us -> 35.8 us  [swap(): lax.ppermute(x, self.axis, [(i, i ^ k * self.stride) for i in range(n)])]
    pallas_call x24 -> x22, Pallas kernels: 69.8 us -> 62.9 us  [plain_call(): pl.pallas_call(lambda *refs: kernel(Here(), *refs), in_specs=list(specs)...]
    ppermute x29, waiting for transfers between devices: 46.7 us -> 44.1 us  [swap(): lax.ppermute(x, self.axis, [(i, i ^ k * self.stride) for i in range(n)])]
    broadcast_in_dim x4 -> x0, local copies, waits for them, and re-layouts: 2.08 us -> none  [the longest x1 0.69 us: body(): conv_bias[None]]
    ppermute x1, waiting for transfers between devices: 0.01 us -> 1.85 us  [body(): lax.ppermute(ngrad[length:], 'seq', [(i, i - 1) for i in range(1, seq_siz...]
  transfers between devices with their start and end apart: 31 -> 31, of which waited for: 16 -> 21; matrix products, arithmetic and copies ran while one was open for 4% -> 0% of each run, Pallas kernels for 25% -> 20%
where the time goes in v4:
time: 152 us; the launch traced here: 151 us
  Pallas kernels  62.9 us (41%)
  waiting for transfers between devices  46.7 us (31%)
  starting transfers between devices  39.5 us (26%)
    pallas_call x22, Pallas kernels, plain_call(): pl.pallas_call(lambda *refs: kernel(Here(), *refs), in_specs=list(specs)...  62.9 us
    ppermute x29, waiting for transfers between devices, swap(): lax.ppermute(x, self.axis, [(i, i ^ k * self.stride) for i in range(n)])  44.1 us
    ppermute x29, starting transfers between devices, swap(): lax.ppermute(x, self.axis, [(i, i ^ k * self.stride) for i in range(n)])  35.8 us
  transfers between devices with their start and end apart: 31, of which 21 were waited for; matrix products, arithmetic and copies ran while one was open for 0% of the time, Pallas kernels for 20%

profile of v4, /device:TPU:0, one launch (start us, length us, event | category | flops | bytes accessed | tf_op | source)
XLA Modules:
  0.0 151.4 jit_solution(451918424205571435)
XLA Ops:
  0.6 0.7 slice_bitcast_fusion
  1.4 2.3 %collective-permute-start = (bf16[3,1024]{1,0:T(4,128)(2,1)S(1)}, bf16[3,1024]{1,0:T(4,128)(2,1)S(1)}, u32[]{:S(2)}, u32[]{:S(2)}) collective-permute-start(bf16[3,1024]{1,0:T(4,128)(2,1)S(1)} %slice_bitcast_fusion), channel_id=1, source_target_pairs={{0,1},{1,2},{2,3},{3,4},{4,5},{5,6},{6,7},{8,9},{9,10},{10,11},{11... | collective-permute-start | bytes 18440 | tf_op jit(solution)/shard_map/ppermute | solution.py:1014
  3.7 0.8 collective-permute-done.refs_13_
  4.5 21.8 %front.1 = (bf16[144,1024]{1,0:T(8,128)(2,1)S(1)}, bf16[128,1024]{1,0:T(8,128)(2,1)S(1)}, bf16[160,2048]{1,0:T(8,128)(2,1)S(1)}, bf16[128,2048]{1,0:T(8,128)(2,1...) custom-call(s32[1,4]{1,0:T(1,128)} %refs_0_.2, ...), custom_call_target="tpu_custom_call" | custom-call | flops 20000000 | tf_op jit(solution)/shard_map/front/pallas_call | solution.py:49
  26.3 2.7 %collective-permute-start.1 = (bf16[48,2048]{1,0:T(8,128)(2,1)S(1)}, bf16[48,2048]{1,0:T(8,128)(2,1)S(1)}, u32[]{:S(2)}, u32[]{:S(2)}) collective-permute-start(bf16[48,2048]{1,0:T(8,128)(2,1)S(1)} %get-tuple-element.157.refs_0_), channel_id=1, source_target_pairs={{0,1},{1,0},{2,3},{3,2},{4,5},{5,4},{6,7},{7,6},{8,9},{9,8},{10,11... | collective-permute-start | bytes 589832 | tf_op jit(solution)/shard_map/ppermute | solution.py:943
  29.0 1.5 %collective-permute-start.5 = (bf16[128,1280]{1,0:T(8,128)(2,1)S(1)}, bf16[128,1280]{1,0:T(8,128)(2,1)S(1)}, u32[]{:S(2)}, u32[]{:S(2)}) collective-permute-start(bf16[128,1280]{1,0:T(8,128)(2,1)S(1)} %get-tuple-element.162), channel_id=1, source_target_pairs={{0,8},{8,0},{16,24},{24,16},{1,9},{9,1},{17,25},{25,17},{2,10},{10... | collective-permute-start | bytes 983048 | tf_op jit(solution)/shard_map/ppermute | solution.py:943
  30.5 1.5 collective-permute-start.6
  32.0 0.5 collective-permute-start.7
  32.6 2.3 %collective-permute-start.2 = (bf16[48,1024]{1,0:T(8,128)(2,1)S(1)}, bf16[48,1024]{1,0:T(8,128)(2,1)S(1)}, u32[]{:S(2)}, u32[]{:S(2)}) collective-permute-start(bf16[48,1024]{1,0:T(8,128)(2,1)S(1)} %pair.1.refs_0_), channel_id=1, source_target_pairs={{0,2},{1,3},{2,0},{3,1},{4,6},{5,7},{6,4},{7,5},{8,10},{9,11},{10,... | collective-permute-start | bytes 294920 | tf_op jit(solution)/shard_map/ppermute | solution.py:943
  34.9 2.6 %collective-permute-done.2.refs_1_ = bf16[48,1024]{1,0:T(8,128)(2,1)S(1)} collective-permute-done((bf16[48,1024]{1,0:T(8,128)(2,1)S(1)}, bf16[48,1024]{1,0:T(8,128)(2,1)S(1)}, u32[]{:S(2)}, u32[]{:S(2)}) %collective-permute-start.2) | collective-permute-done | bytes 98336 | tf_op jit(solution)/shard_map/ppermute | solution.py:943
  37.6 3.1 %collective-permute-start.3 = (bf16[16,1024]{1,0:T(8,128)(2,1)S(1)}, bf16[16,1024]{1,0:T(8,128)(2,1)S(1)}, u32[]{:S(2)}, u32[]{:S(2)}) collective-permute-start(bf16[16,1024]{1,0:T(8,128)(2,1)S(1)} %get-tuple-element.159), channel_id=1, source_target_pairs={{0,4},{1,5},{2,6},{3,7},{4,0},{5,1},{6,2},{7,3},{8,12},{9,13},{10,... | collective-permute-start | bytes 98312 | tf_op jit(solution)/shard_map/ppermute | solution.py:943
  40.7 1.9 %collective-permute-done.3.refs_1_ = bf16[16,1024]{1,0:T(8,128)(2,1)S(1)} collective-permute-done((bf16[16,1024]{1,0:T(8,128)(2,1)S(1)}, bf16[16,1024]{1,0:T(8,128)(2,1)S(1)}, u32[]{:S(2)}, u32[]{:S(2)}) %collective-permute-start.3) | collective-permute-done | bytes 32800 | tf_op jit(solution)/shard_map/ppermute | solution.py:943
  42.7 1.3 collective-permute-done.4.refs_3_
  44.1 2.8 %collective-permute-done.6.refs_3_ = bf16[128,1280]{1,0:T(8,128)(2,1)S(1)} collective-permute-done((bf16[128,1280]{1,0:T(8,128)(2,1)S(1)}, bf16[128,1280]{1,0:T(8,128)(2,1)S(1)}, u32[]{:S(2)}, u32[]{:S(2)}) %collective-permute-start.6) | collective-permute-done | bytes 327712 | tf_op jit(solution)/shard_map/ppermute | solution.py:943
  47.0 6.0 %forward.1 = (bf16[128,2048]{1,0:T(8,128)(2,1)S(1)}, bf16[128,2048]{1,0:T(8,128)(2,1)S(1)}, bf16[128,2560]{1,0:T(8,128)(2,1)S(1)}, bf16[128,2560]{1,0:T(8,128)(2...) custom-call(f32[4,128,128]{2,1,0:T(8,128)S(1)} %get-tuple-element.151.refs_0_.refs_3_, ...), custom_call_target="tpu_custom_call" | custom-call | flops 8000000 | tf_op jit(solution)/shard_map/forward/pallas_call | solution.py:49
  53.0 1.3 collective-permute-start.12
  54.3 0.8 collective-permute-start.13
  55.1 1.4 collective-permute-start.14
  56.5 0.4 early.1
  56.9 26.1 %backward.1 = (f32[144,1024]{1,0:T(8,128)S(1)}, bf16[144,512]{1,0:T(8,128)(2,1)S(1)}, bf16[144,512]{1,0:T(8,128)(2,1)S(1)}, bf16[144,512]{1,0:T(8,128)(2,1)S(1)}...) custom-call(bf16[1024,4096]{1,0:T(8,128)(2,1)} %refs_0_.3, ...), custom_call_target="tpu_custom_call" | custom-call | flops 24000000 | tf_op jit(solution)/shard_map/backward/pallas_call | solution.py:49
  83.1 1.7 %collective-permute-done.15.refs_1_ = bf16[4,192,256]{2,1,0:T(8,128)(2,1)S(1)} collective-permute-done((bf16[4,192,256]{2,1,0:T(8,128)(2,1)S(1)}, bf16[4,192,256]{2,1,0:T(8,128)(2,1)S(1)}, u32[]{:S(2)}, u32[]{:S(2)}) %collective-permute-start.15) | collective-permute-done | bytes 393248 | tf_op jit(solution)/shard_map/ppermute | solution.py:943
  84.8 0.1 small_row0.1
  85.0 1.5 gate_out_columns.1
  86.5 0.2 collective-permute-start.16
  86.7 0.3 collective-permute-start.17
  87.0 0.2 collective-permute-start.18
  87.2 0.3 collective-permute-start.19
  87.6 0.5 collective-permute-done.16.refs_1_
  88.1 0.4 collective-permute-done.17.refs_2_
  88.4 0.4 collective-permute-done.18.refs_3_
  88.8 0.4 collective-permute-done.19.refs_4_
  89.2 0.4 go_chip0.1
  89.6 2.7 %collective-permute-start.20 = (bf16[2,128,1024]{2,1,0:T(8,128)(2,1)S(1)}, bf16[2,128,1024]{2,1,0:T(8,128)(2,1)S(1)}, u32[]{:S(2)}, u32[]{:S(2)}) collective-permute-start(bf16[2,128,1024]{2,1,0:T(8,128)(2,1)S(1)} %get-tuple-element.223), channel_id=1, source_target_pairs={{0,2},{1,3},{2,0},{3,1},{4,6},{5,7},{6,4},{7,5},{8,10},{9,11},{10,... | collective-permute-start | bytes 1572872 | tf_op jit(solution)/shard_map/ppermute | solution.py:943
  92.3 1.2 collective-permute-start.21
  93.5 0.8 collective-permute-start.10
  94.3 1.4 collective-permute-start.11
  95.8 1.2 collective-permute-start.9
  97.0 3.1 %collective-permute-done.21.refs_1_ = bf16[2,192,256]{2,1,0:T(8,128)(2,1)S(1)} collective-permute-done((bf16[2,192,256]{2,1,0:T(8,128)(2,1)S(1)}, bf16[2,192,256]{2,1,0:T(8,128)(2,1)S(1)}, u32[]{:S(2)}, u32[]{:S(2)}) %collective-permute-start.21) | collective-permute-done | bytes 196640 | tf_op jit(solution)/shard_map/ppermute | solution.py:943
  100.1 4.4 %collective-permute-done.20.refs_1_ = bf16[2,128,1024]{2,1,0:T(8,128)(2,1)S(1)} collective-permute-done((bf16[2,128,1024]{2,1,0:T(8,128)(2,1)S(1)}, bf16[2,128,1024]{2,1,0:T(8,128)(2,1)S(1)}, u32[]{:S(2)}, u32[]{:S(2)}) %collective-permute-start.20) | collective-permute-done | bytes 524320 | tf_op jit(solution)/shard_map/ppermute | solution.py:943
  104.5 0.2 go_chip1.1
  104.7 0.6 collective-permute-done.9.refs_2_
  105.3 1.1 conv_columns.1
  106.5 1.6 %collective-permute-start.23 = (bf16[1,192,256]{2,1,0:T(8,128)(2,1)S(1)}, bf16[1,192,256]{2,1,0:T(8,128)(2,1)S(1)}, u32[]{:S(2)}, u32[]{:S(2)}) collective-permute-start(bf16[1,192,256]{2,1,0:T(8,128)(2,1)S(1)} %get-tuple-element.238), channel_id=1, source_target_pairs={{0,16},{8,24},{16,0},{24,8},{1,17},{9,25},{17,1},{25,9},{2,18},{10... | collective-permute-start | bytes 294920 | tf_op jit(solution)/shard_map/ppermute | solution.py:943
  108.0 3.6 %collective-permute-done.23.refs_3_ = bf16[1,192,256]{2,1,0:T(8,128)(2,1)S(1)} collective-permute-done((bf16[1,192,256]{2,1,0:T(8,128)(2,1)S(1)}, bf16[1,192,256]{2,1,0:T(8,128)(2,1)S(1)}, u32[]{:S(2)}, u32[]{:S(2)}) %collective-permute-start.23) | collective-permute-done | bytes 98336 | tf_op jit(solution)/shard_map/ppermute | solution.py:943
  111.7 0.1 mix0.1
  111.8 1.3 collective-permute-start.24
  113.0 2.6 %collective-permute-start.25 = (bf16[1,128,1024]{2,1,0:T(8,128)(2,1)S(1)}, bf16[1,128,1024]{2,1,0:T(8,128)(2,1)S(1)}, u32[]{:S(2)}, u32[]{:S(2)}) collective-permute-start(bf16[1,128,1024]{2,1,0:T(8,128)(2,1)S(1)} %get-tuple-element.246), channel_id=1, source_target_pairs={{0,4},{1,5},{2,6},{3,7},{4,0},{5,1},{6,2},{7,3},{8,12},{9,13},{10,... | collective-permute-start | bytes 786440 | tf_op jit(solution)/shard_map/ppermute | solution.py:943
  115.6 10.5 %collective-permute-done.25.refs_1_ = bf16[1,128,1024]{2,1,0:T(8,128)(2,1)S(1)} collective-permute-done((bf16[1,128,1024]{2,1,0:T(8,128)(2,1)S(1)}, bf16[1,128,1024]{2,1,0:T(8,128)(2,1)S(1)}, u32[]{:S(2)}, u32[]{:S(2)}) %collective-permute-start.25) | collective-permute-done | bytes 262176 | tf_op jit(solution)/shard_map/ppermute | solution.py:943
  126.2 0.7 go_last.1
  126.9 0.5 collective-permute-done.24.refs_1_
  127.5 2.9 %collective-permute-start.26 = (bf16[112,1024]{1,0:T(8,128)(2,1)S(1)}, bf16[112,1024]{1,0:T(8,128)(2,1)S(1)}, u32[]{:S(2)}, u32[]{:S(2)}) collective-permute-start(bf16[112,1024]{1,0:T(8,128)(2,1)S(1)} %get-tuple-element.263), channel_id=1, source_target_pairs={{0,4},{1,5},{2,6},{3,7},{4,0},{5,1},{6,2},{7,3},{8,12},{9,13},{10,... | collective-permute-start | bytes 688136 | tf_op jit(solution)/shard_map/ppermute | solution.py:943
  130.4 1.3 collective-permute-start.8
  131.7 1.8 %collective-permute-done.8.refs_1_ = f32[16,1024]{1,0:T(8,128)S(1)} collective-permute-done((f32[16,1024]{1,0:T(8,128)S(1)}, f32[16,1024]{1,0:T(8,128)S(1)}, u32[]{:S(2)}, u32[]{:S(2)}) %collective-permute-start.8) | collective-permute-done | bytes 65568 | tf_op jit(solution)/shard_map/ppermute | solution.py:1091
  133.6 1.8 %finish.1 = (bf16[128,1024]{1,0:T(8,128)(2,1)}, bf16[128,1024]{1,0:T(8,128)(2,1)}) custom-call(f32[144,1024]{1,0:T(8,128)S(1)} %get-tuple-element.254.refs_0_, f32[16,1024]{1,0:T(8,128)S(1)} %collective-permute-done.8.refs_1_, bf16[144,1024]{1,0:T(8,128)(2,1)S(1)} %get-tuple-element.256.refs_5_.refs_2_, bf16[128,1024]{1,0:T(8,128)(2,1)S(1)} %get-tuple-element.257.refs_3_, ...), custom_call_target="tpu_custom_call" | custom-call | flops 1000000 | tf_op jit(solution)/shard_map/finish/pallas_call | solution.py:49
  135.4 4.5 %collective-permute-done.26.refs_1_ = bf16[112,1024]{1,0:T(8,128)(2,1)S(1)} collective-permute-done((bf16[112,1024]{1,0:T(8,128)(2,1)S(1)}, bf16[112,1024]{1,0:T(8,128)(2,1)S(1)}, u32[]{:S(2)}, u32[]{:S(2)}) %collective-permute-start.26) | collective-permute-done | bytes 229408 | tf_op jit(solution)/shard_map/ppermute | solution.py:943
  140.0 1.6 %collective-permute-start.27 = (bf16[112,1024]{1,0:T(8,128)(2,1)S(1)}, bf16[112,1024]{1,0:T(8,128)(2,1)S(1)}, u32[]{:S(2)}, u32[]{:S(2)}) collective-permute-start(bf16[112,1024]{1,0:T(8,128)(2,1)S(1)} %get-tuple-element.270), channel_id=1, source_target_pairs={{0,16},{8,24},{16,0},{24,8},{1,17},{9,25},{17,1},{25,9},{2,18},{10... | collective-permute-start | bytes 688136 | tf_op jit(solution)/shard_map/ppermute | solution.py:943
  141.6 0.5 collective-permute-start.28
  142.1 1.4 collective-permute-start.29
  143.5 2.6 %collective-permute-done.28.refs_1_ = bf16[48,1024]{1,0:T(8,128)(2,1)S(1)} collective-permute-done((bf16[48,1024]{1,0:T(8,128)(2,1)S(1)}, bf16[48,1024]{1,0:T(8,128)(2,1)S(1)}, u32[]{:S(2)}, u32[]{:S(2)}) %collective-permute-start.28) | collective-permute-done | bytes 98336 | tf_op jit(solution)/shard_map/ppermute | solution.py:943
  146.2 1.5 %collective-permute-done.29.refs_3_ = bf16[48,1024]{1,0:T(8,128)(2,1)S(1)} collective-permute-done((bf16[48,1024]{1,0:T(8,128)(2,1)S(1)}, bf16[48,1024]{1,0:T(8,128)(2,1)S(1)}, u32[]{:S(2)}, u32[]{:S(2)}) %collective-permute-start.29) | collective-permute-done | bytes 98336 | tf_op jit(solution)/shard_map/ppermute | solution.py:943
  147.9 1.0 in_last.1
  148.9 0.7 collective-permute-done.30.refs_2_
  149.6 1.2 unpack.1
  150.8 0.6 slice.11
  (28 shorter events, 0.9 us)
Async XLA Ops:
  1.4 3.2 %collective-permute-start = (bf16[3,1024]{1,0:T(4,128)(2,1)S(1)}, bf16[3,1024]{1,0:T(4,128)(2,1)S(1)}, u32[]{:S(2)}, u32[]{:S(2)}) collective-permute-start(bf16[3,1024]{1,0:T(4,128)(2,1)S(1)} %slice_bitcast_fusion), channel_id=1, source_target_pairs={{0,1},{1,2},{2,3},{3,4},{4,5},{5,6},{6,7},{8,9},{9,10},{10,11},{11... | collective-permute-start | bytes 18440 | tf_op jit(solution)/shard_map/ppermute | solution.py:1014
  26.3 6.2 %collective-permute-start.1 = (bf16[48,2048]{1,0:T(8,128)(2,1)S(1)}, bf16[48,2048]{1,0:T(8,128)(2,1)S(1)}, u32[]{:S(2)}, u32[]{:S(2)}) collective-permute-start(bf16[48,2048]{1,0:T(8,128)(2,1)S(1)} %get-tuple-element.157.refs_0_), channel_id=1, source_target_pairs={{0,1},{1,0},{2,3},{3,2},{4,5},{5,4},{6,7},{7,6},{8,9},{9,8},{10,11... | collective-permute-start | bytes 589832 | tf_op jit(solution)/shard_map/ppermute | solution.py:943
  29.0 15.1 %collective-permute-start.5 = (bf16[128,1280]{1,0:T(8,128)(2,1)S(1)}, bf16[128,1280]{1,0:T(8,128)(2,1)S(1)}, u32[]{:S(2)}, u32[]{:S(2)}) collective-permute-start(bf16[128,1280]{1,0:T(8,128)(2,1)S(1)} %get-tuple-element.162), channel_id=1, source_target_pairs={{0,8},{8,0},{16,24},{24,16},{1,9},{9,1},{17,25},{25,17},{2,10},{10... | collective-permute-start | bytes 983048 | tf_op jit(solution)/shard_map/ppermute | solution.py:943
  30.5 16.4 %collective-permute-start.6 = (bf16[128,1280]{1,0:T(8,128)(2,1)S(1)}, bf16[128,1280]{1,0:T(8,128)(2,1)S(1)}, u32[]{:S(2)}, u32[]{:S(2)}) collective-permute-start(bf16[128,1280]{1,0:T(8,128)(2,1)S(1)} %get-tuple-element.163), channel_id=1, source_target_pairs={{0,16},{8,24},{16,0},{24,8},{1,17},{9,25},{17,1},{25,9},{2,18},{10... | collective-permute-start | bytes 983048 | tf_op jit(solution)/shard_map/ppermute | solution.py:943
  32.0 14.9 %collective-permute-start.7 = (bf16[128,1280]{1,0:T(8,128)(2,1)S(1)}, bf16[128,1280]{1,0:T(8,128)(2,1)S(1)}, u32[]{:S(2)}, u32[]{:S(2)}) collective-permute-start(bf16[128,1280]{1,0:T(8,128)(2,1)S(1)} %get-tuple-element.164), channel_id=1, source_target_pairs={{0,24},{8,16},{16,8},{24,0},{1,25},{9,17},{17,9},{25,1},{2,26},{10... | collective-permute-start | bytes 983048 | tf_op jit(solution)/shard_map/ppermute | solution.py:943
  32.6 4.9 %collective-permute-start.2 = (bf16[48,1024]{1,0:T(8,128)(2,1)S(1)}, bf16[48,1024]{1,0:T(8,128)(2,1)S(1)}, u32[]{:S(2)}, u32[]{:S(2)}) collective-permute-start(bf16[48,1024]{1,0:T(8,128)(2,1)S(1)} %pair.1.refs_0_), channel_id=1, source_target_pairs={{0,2},{1,3},{2,0},{3,1},{4,6},{5,7},{6,4},{7,5},{8,10},{9,11},{10,... | collective-permute-start | bytes 294920 | tf_op jit(solution)/shard_map/ppermute | solution.py:943
  37.6 5.0 %collective-permute-start.3 = (bf16[16,1024]{1,0:T(8,128)(2,1)S(1)}, bf16[16,1024]{1,0:T(8,128)(2,1)S(1)}, u32[]{:S(2)}, u32[]{:S(2)}) collective-permute-start(bf16[16,1024]{1,0:T(8,128)(2,1)S(1)} %get-tuple-element.159), channel_id=1, source_target_pairs={{0,4},{1,5},{2,6},{3,7},{4,0},{5,1},{6,2},{7,3},{8,12},{9,13},{10,... | collective-permute-start | bytes 98312 | tf_op jit(solution)/shard_map/ppermute | solution.py:943
  42.6 1.4 collective-permute-start.4
  53.0 32.0 %collective-permute-start.12 = (bf16[128,2560]{1,0:T(8,128)(2,1)S(1)}, bf16[128,2560]{1,0:T(8,128)(2,1)S(1)}, u32[]{:S(2)}, u32[]{:S(2)}) collective-permute-start(bf16[128,2560]{1,0:T(8,128)(2,1)S(1)} %get-tuple-element.198), channel_id=1, source_target_pairs={{0,8},{8,0},{16,24},{24,16},{1,9},{9,1},{17,25},{25,17},{2,10},{10... | collective-permute-start | bytes 1966088 | tf_op jit(solution)/shard_map/ppermute | solution.py:943
  54.3 30.7 %collective-permute-start.13 = (bf16[128,2560]{1,0:T(8,128)(2,1)S(1)}, bf16[128,2560]{1,0:T(8,128)(2,1)S(1)}, u32[]{:S(2)}, u32[]{:S(2)}) collective-permute-start(bf16[128,2560]{1,0:T(8,128)(2,1)S(1)} %get-tuple-element.199), channel_id=1, source_target_pairs={{0,16},{8,24},{16,0},{24,8},{1,17},{9,25},{17,1},{25,9},{2,18},{10... | collective-permute-start | bytes 1966088 | tf_op jit(solution)/shard_map/ppermute | solution.py:943
  55.1 29.9 %collective-permute-start.14 = (bf16[128,2560]{1,0:T(8,128)(2,1)S(1)}, bf16[128,2560]{1,0:T(8,128)(2,1)S(1)}, u32[]{:S(2)}, u32[]{:S(2)}) collective-permute-start(bf16[128,2560]{1,0:T(8,128)(2,1)S(1)} %get-tuple-element.200), channel_id=1, source_target_pairs={{0,24},{8,16},{16,8},{24,0},{1,25},{9,17},{17,9},{25,1},{2,26},{10... | collective-permute-start | bytes 1966088 | tf_op jit(solution)/shard_map/ppermute | solution.py:943
  83.0 1.8 %collective-permute-start.15 = (bf16[4,192,256]{2,1,0:T(8,128)(2,1)S(1)}, bf16[4,192,256]{2,1,0:T(8,128)(2,1)S(1)}, u32[]{:S(2)}, u32[]{:S(2)}) collective-permute-start(bf16[4,192,256]{2,1,0:T(8,128)(2,1)S(1)} %get-tuple-element.202), channel_id=1, source_target_pairs={{0,1},{1,0},{2,3},{3,2},{4,5},{5,4},{6,7},{7,6},{8,9},{9,8},{10,11... | collective-permute-start | bytes 1179656 | tf_op jit(solution)/shard_map/ppermute | solution.py:943
  86.5 1.6 %collective-permute-start.16 = (bf16[128,1024]{1,0:T(8,128)(2,1)S(1)}, bf16[128,1024]{1,0:T(8,128)(2,1)S(1)}, u32[]{:S(2)}, u32[]{:S(2)}) collective-permute-start(bf16[128,1024]{1,0:T(8,128)(2,1)S(1)} %get-tuple-element.213), channel_id=1, source_target_pairs={{0,1},{1,0},{2,3},{3,2},{4,5},{5,4},{6,7},{7,6},{8,9},{9,8},{10,11... | collective-permute-start | bytes 786440 | tf_op jit(solution)/shard_map/ppermute | solution.py:943
  86.7 1.7 %collective-permute-start.17 = (bf16[128,1024]{1,0:T(8,128)(2,1)S(1)}, bf16[128,1024]{1,0:T(8,128)(2,1)S(1)}, u32[]{:S(2)}, u32[]{:S(2)}) collective-permute-start(bf16[128,1024]{1,0:T(8,128)(2,1)S(1)} %get-tuple-element.214), channel_id=1, source_target_pairs={{0,1},{1,0},{2,3},{3,2},{4,5},{5,4},{6,7},{7,6},{8,9},{9,8},{10,11... | collective-permute-start | bytes 786440 | tf_op jit(solution)/shard_map/ppermute | solution.py:943
  87.0 1.8 %collective-permute-start.18 = (bf16[128,1024]{1,0:T(8,128)(2,1)S(1)}, bf16[128,1024]{1,0:T(8,128)(2,1)S(1)}, u32[]{:S(2)}, u32[]{:S(2)}) collective-permute-start(bf16[128,1024]{1,0:T(8,128)(2,1)S(1)} %get-tuple-element.215), channel_id=1, source_target_pairs={{0,1},{1,0},{2,3},{3,2},{4,5},{5,4},{6,7},{7,6},{8,9},{9,8},{10,11... | collective-permute-start | bytes 786440 | tf_op jit(solution)/shard_map/ppermute | solution.py:943
  87.2 2.0 %collective-permute-start.19 = (bf16[128,1024]{1,0:T(8,128)(2,1)S(1)}, bf16[128,1024]{1,0:T(8,128)(2,1)S(1)}, u32[]{:S(2)}, u32[]{:S(2)}) collective-permute-start(bf16[128,1024]{1,0:T(8,128)(2,1)S(1)} %get-tuple-element.216), channel_id=1, source_target_pairs={{0,1},{1,0},{2,3},{3,2},{4,5},{5,4},{6,7},{7,6},{8,9},{9,8},{10,11... | collective-permute-start | bytes 786440 | tf_op jit(solution)/shard_map/ppermute | solution.py:943
  89.6 44.0 %copy-start = (bf16[2048,1024]{1,0:T(8,128)(2,1)S(1)}, bf16[2048,1024]{1,0:T(8,128)(2,1)}, u32[]{:S(2)}) copy-start(bf16[2048,1024]{1,0:T(8,128)(2,1)} %refs_6_.2) | copy-start | bytes 12582916
  89.6 15.0 %collective-permute-start.20 = (bf16[2,128,1024]{2,1,0:T(8,128)(2,1)S(1)}, bf16[2,128,1024]{2,1,0:T(8,128)(2,1)S(1)}, u32[]{:S(2)}, u32[]{:S(2)}) collective-permute-start(bf16[2,128,1024]{2,1,0:T(8,128)(2,1)S(1)} %get-tuple-element.223), channel_id=1, source_target_pairs={{0,2},{1,3},{2,0},{3,1},{4,6},{5,7},{6,4},{7,5},{8,10},{9,11},{10,... | collective-permute-start | bytes 1572872 | tf_op jit(solution)/shard_map/ppermute | solution.py:943
  92.3 7.8 %collective-permute-start.21 = (bf16[2,192,256]{2,1,0:T(8,128)(2,1)S(1)}, bf16[2,192,256]{2,1,0:T(8,128)(2,1)S(1)}, u32[]{:S(2)}, u32[]{:S(2)}) collective-permute-start(bf16[2,192,256]{2,1,0:T(8,128)(2,1)S(1)} %get-tuple-element.224), channel_id=1, source_target_pairs={{0,8},{8,0},{16,24},{24,16},{1,9},{9,1},{17,25},{25,17},{2,10},{10... | collective-permute-start | bytes 589832 | tf_op jit(solution)/shard_map/ppermute | solution.py:943
  93.5 11.2 %collective-permute-start.10 = (bf16[144,512]{1,0:T(8,128)(2,1)S(1)}, bf16[144,512]{1,0:T(8,128)(2,1)S(1)}, u32[]{:S(2)}, u32[]{:S(2)}) collective-permute-start(bf16[144,512]{1,0:T(8,128)(2,1)S(1)} %get-tuple-element.194), channel_id=1, source_target_pairs={{0,16},{8,24},{16,0},{24,8},{1,17},{9,25},{17,1},{25,9},{2,18},{10... | collective-permute-start | bytes 442376 | tf_op jit(solution)/shard_map/ppermute | solution.py:943
  94.3 10.4 %collective-permute-start.11 = (bf16[144,512]{1,0:T(8,128)(2,1)S(1)}, bf16[144,512]{1,0:T(8,128)(2,1)S(1)}, u32[]{:S(2)}, u32[]{:S(2)}) collective-permute-start(bf16[144,512]{1,0:T(8,128)(2,1)S(1)} %get-tuple-element.195), channel_id=1, source_target_pairs={{0,24},{8,16},{16,8},{24,0},{1,25},{9,17},{17,9},{25,1},{2,26},{10... | collective-permute-start | bytes 442376 | tf_op jit(solution)/shard_map/ppermute | solution.py:943
  95.8 9.5 %collective-permute-start.9 = (bf16[144,512]{1,0:T(8,128)(2,1)S(1)}, bf16[144,512]{1,0:T(8,128)(2,1)S(1)}, u32[]{:S(2)}, u32[]{:S(2)}) collective-permute-start(bf16[144,512]{1,0:T(8,128)(2,1)S(1)} %get-tuple-element.193), channel_id=1, source_target_pairs={{0,8},{8,0},{16,24},{24,16},{1,9},{9,1},{17,25},{25,17},{2,10},{10... | collective-permute-start | bytes 442376 | tf_op jit(solution)/shard_map/ppermute | solution.py:943
  106.4 5.3 %collective-permute-start.22 = (bf16[256,1024]{1,0:T(8,128)(2,1)S(1)}, bf16[256,1024]{1,0:T(8,128)(2,1)S(1)}, u32[]{:S(2)}, u32[]{:S(2)}) collective-permute-start(bf16[256,1024]{1,0:T(8,128)(2,1)S(1)} %get-tuple-element.237), channel_id=1, source_target_pairs={{0,1},{1,0},{2,3},{3,2},{4,5},{5,4},{6,7},{7,6},{8,9},{9,8},{10,11... | collective-permute-start | bytes 1572872 | tf_op jit(solution)/shard_map/ppermute | solution.py:943
  106.5 5.2 %collective-permute-start.23 = (bf16[1,192,256]{2,1,0:T(8,128)(2,1)S(1)}, bf16[1,192,256]{2,1,0:T(8,128)(2,1)S(1)}, u32[]{:S(2)}, u32[]{:S(2)}) collective-permute-start(bf16[1,192,256]{2,1,0:T(8,128)(2,1)S(1)} %get-tuple-element.238), channel_id=1, source_target_pairs={{0,16},{8,24},{16,0},{24,8},{1,17},{9,25},{17,1},{25,9},{2,18},{10... | collective-permute-start | bytes 294920 | tf_op jit(solution)/shard_map/ppermute | solution.py:943
  111.8 15.7 %collective-permute-start.24 = (bf16[176,1024]{1,0:T(8,128)(2,1)S(1)}, bf16[176,1024]{1,0:T(8,128)(2,1)S(1)}, u32[]{:S(2)}, u32[]{:S(2)}) collective-permute-start(bf16[176,1024]{1,0:T(8,128)(2,1)S(1)} %get-tuple-element.244), channel_id=1, source_target_pairs={{0,2},{1,3},{2,0},{3,1},{4,6},{5,7},{6,4},{7,5},{8,10},{9,11},{10,... | collective-permute-start | bytes 1081352 | tf_op jit(solution)/shard_map/ppermute | solution.py:943
  113.0 13.1 %collective-permute-start.25 = (bf16[1,128,1024]{2,1,0:T(8,128)(2,1)S(1)}, bf16[1,128,1024]{2,1,0:T(8,128)(2,1)S(1)}, u32[]{:S(2)}, u32[]{:S(2)}) collective-permute-start(bf16[1,128,1024]{2,1,0:T(8,128)(2,1)S(1)} %get-tuple-element.246), channel_id=1, source_target_pairs={{0,4},{1,5},{2,6},{3,7},{4,0},{5,1},{6,2},{7,3},{8,12},{9,13},{10,... | collective-permute-start | bytes 786440 | tf_op jit(solution)/shard_map/ppermute | solution.py:943
  127.4 20.4 %copy-start.1 = (f32[2048,16]{0,1:T(8,128)S(1)}, f32[2048,16]{0,1:T(8,128)}, u32[]{:S(2)}) copy-start(f32[2048,16]{0,1:T(8,128)} %param.22) | copy-start | bytes 393220
  127.5 12.4 %collective-permute-start.26 = (bf16[112,1024]{1,0:T(8,128)(2,1)S(1)}, bf16[112,1024]{1,0:T(8,128)(2,1)S(1)}, u32[]{:S(2)}, u32[]{:S(2)}) collective-permute-start(bf16[112,1024]{1,0:T(8,128)(2,1)S(1)} %get-tuple-element.263), channel_id=1, source_target_pairs={{0,4},{1,5},{2,6},{3,7},{4,0},{5,1},{6,2},{7,3},{8,12},{9,13},{10,... | collective-permute-start | bytes 688136 | tf_op jit(solution)/shard_map/ppermute | solution.py:943
  130.4 3.1 %collective-permute-start.8 = (f32[16,1024]{1,0:T(8,128)S(1)}, f32[16,1024]{1,0:T(8,128)S(1)}, u32[]{:S(2)}, u32[]{:S(2)}) collective-permute-start(f32[16,1024]{1,0:T(8,128)S(1)} %slice.10), channel_id=1, source_target_pairs={{1,0},{2,1},{3,2},{4,3},{5,4},{6,5},{7,6},{9,8},{10,9},{11,10},{12... | collective-permute-start | bytes 196616 | tf_op jit(solution)/shard_map/ppermute | solution.py:1091
  140.0 7.7 %collective-permute-start.27 = (bf16[112,1024]{1,0:T(8,128)(2,1)S(1)}, bf16[112,1024]{1,0:T(8,128)(2,1)S(1)}, u32[]{:S(2)}, u32[]{:S(2)}) collective-permute-start(bf16[112,1024]{1,0:T(8,128)(2,1)S(1)} %get-tuple-element.270), channel_id=1, source_target_pairs={{0,16},{8,24},{16,0},{24,8},{1,17},{9,25},{17,1},{25,9},{2,18},{10... | collective-permute-start | bytes 688136 | tf_op jit(solution)/shard_map/ppermute | solution.py:943
  141.6 4.6 %collective-permute-start.28 = (bf16[48,1024]{1,0:T(8,128)(2,1)S(1)}, bf16[48,1024]{1,0:T(8,128)(2,1)S(1)}, u32[]{:S(2)}, u32[]{:S(2)}) collective-permute-start(bf16[48,1024]{1,0:T(8,128)(2,1)S(1)} %get-tuple-element.272.refs_0_), channel_id=1, source_target_pairs={{0,8},{8,0},{16,24},{24,16},{1,9},{9,1},{17,25},{25,17},{2,10},{10... | collective-permute-start | bytes 294920 | tf_op jit(solution)/shard_map/ppermute | solution.py:943
  142.1 5.6 %collective-permute-start.29 = (bf16[48,1024]{1,0:T(8,128)(2,1)S(1)}, bf16[48,1024]{1,0:T(8,128)(2,1)S(1)}, u32[]{:S(2)}, u32[]{:S(2)}) collective-permute-start(bf16[48,1024]{1,0:T(8,128)(2,1)S(1)} %get-tuple-element.272.refs_0_), channel_id=1, source_target_pairs={{0,24},{8,16},{16,8},{24,0},{1,25},{9,17},{17,9},{25,1},{2,26},{10... | collective-permute-start | bytes 294920 | tf_op jit(solution)/shard_map/ppermute | solution.py:943
  147.8 1.8 %collective-permute-start.30 = (bf16[4,48,1024]{2,1,0:T(8,128)(2,1)S(1)}, bf16[4,48,1024]{2,1,0:T(8,128)(2,1)S(1)}, u32[]{:S(2)}, u32[]{:S(2)}) collective-permute-start(bf16[4,48,1024]{2,1,0:T(8,128)(2,1)S(1)} %join.1.refs_1_), channel_id=1, source_target_pairs={{0,1},{1,0},{2,3},{3,2},{4,5},{5,4},{6,7},{7,6},{8,9},{9,8},{10,11... | collective-permute-start | bytes 1179656 | tf_op jit(solution)/shard_map/ppermute | solution.py:943

commit v5 on v4

--- a/solution.py
+++ b/solution.py
@@ -14,7 +14,7 @@
 LEAST_RATE = 1e-33
 LN2 = 0.6931471805599453
 EDGE = 16
-UNROLL = 8
+UNROLL = 16
 bf16, f32 = jnp.bfloat16, jnp.float32
 
 
@@ -53,7 +53,7 @@
         out_shape=out_shape,
         scratch_shapes=list(scratch),
         compiler_params=pltpu.CompilerParams(vmem_limit_bytes=limit << 20),
-        cost_estimate=pl.CostEstimate(flops=int(us * 1e6), bytes_accessed=0, transcendentals=0),
+        cost_estimate=pl.CostEstimate(flops=int(us * 1.1e9), bytes_accessed=0, transcendentals=0),
         name=name,
     )(*args)
 
@@ -137,15 +137,14 @@
 
 
 def front_kernel(
-    states, rank, taps, rows_size,
+    states, rank, taps,
     here, starts_hbm, tok_hbm, cot_hbm, gain_hbm, convw_hbm, convb_hbm, dtb_hbm, skip_hbm, alog_hbm, dtw_hbm, wx_hbm,
     win_hbm, wo_hbm, left_ref,
     tok_out, cot_out, ext_ref, inner_ref, gate_ref, ggated_ref, gs_ref, dt_ref, proj_ref, table, pack_ref,
     dx_ref, ex_ref, db_ref, fx_ref, vec_ref, rates_ref, gain_ref, masks, *rest,
 ):
-    blocks = rest[:rows_size]
     (normed, dtm_s, u_s, ends, starts_ref, tok_ref, cot_ref, gain_s, convw_s, convb_s, dtb_s, skip_s, alog_s, dtw_ref, wx_ref,
-     win_ref, wo_ref, sems, wide_sems) = rest[rows_size:]
+     win_ref, wo_ref, sems, wide_sems) = rest
     length, model = cot_ref.shape
     width = rates_ref.shape[1]
     steps = length // SUBS
@@ -170,7 +169,7 @@
 
     for load in loads:
         load.start()
-    for j in range(width // block):
+    for j in range(min(2, width // block)):
         for load in weights(j):
             load.start()
     for load in loads[:2]:
@@ -187,15 +186,6 @@
     rates_ref[...] = jnp.minimum(-jnp.exp(alog_s[...]), -LEAST_RATE) * (1.0 / LN2)
     cot = turned(cot_ref[...], False)
     cot_out[...] = cot
-    thin = model // rows_size
-    for k in range(rows_size):
-        blocks[k][:, :model] = tok_out[pl.ds(0, length), :]
-        for q in range(rows_size):
-
-            @pl.when((here[1] ^ k) == q)
-            def _():
-                blocks[k][:, model:] = cot[:, q * thin : (q + 1) * thin]
-
     normed[...] = normalise(tok_out[...], gain_ref[...])
     for k, mask in enumerate(tap_masks(starts_ref, taps, length)):
         masks[k] = mask
@@ -205,6 +195,12 @@
         wide = tile_at(j * block, block)
         for load in weights(j):
             load.wait()
+
+        @pl.when(j + 2 < width // block)
+        def _():
+            for load in weights(j + 2):
+                load.start()
+
         conv = nn(normed[...], win_ref[:, wide]).astype(bf16)
         gate = nn(normed[pl.ds(0, length), :], win_ref[:, tile_at(width + j * block, block)])
         ggated = nt(cot_out[...], wo_ref[wide, :])
@@ -286,7 +282,7 @@
     pack_ref[...] = ends[...].astype(bf16)
 
 
-def front(starts, tok, cot, gain, convw, convb, dtb, skip, alog, dtw, wx, in_weight, out_weight, left, rows_size):
+def front(starts, tok, cot, gain, convw, convb, dtb, skip, alog, dtw, wx, in_weight, out_weight, left):
     length, model = cot.shape[1:]
     states, width = alog.shape
     rank, taps = dtw.shape[0], convw.shape[0]
@@ -300,7 +296,7 @@
     ] + [shape((states, SUBS, width), f32)] * 4 + [
         shape((taps + 4, width), f32), shape((states, width), f32), shape((1, model), f32),
         shape((taps, length, LANES), f32),
-    ] + [shape((length, model + model // rows_size), bf16)] * rows_size
+    ]
     args = (starts, tok, cot, gain, convw, convb, dtb, skip, alog, dtw, wx, in_weight, out_weight, left)
     scratch = [
         pltpu.VMEM((length + EDGE, model), bf16),
@@ -313,25 +309,22 @@
     ] + [pltpu.VMEM(x.shape, x.dtype) for x in args[3:13]]
     scratch += [pltpu.SemaphoreType.DMA((11,)), pltpu.SemaphoreType.DMA((3, width // min(512, width)))]
     return plain_call(
-        functools.partial(front_kernel, states, rank, taps, rows_size), "front", out,
+        functools.partial(front_kernel, states, rank, taps), "front", out,
         args, 20, scratch, 24, [ANY_SPEC] * 13,
     )
 
 
-def halves_of(near, far):
-    lane = lax.broadcasted_iota(jnp.int32, near.shape, 1)
-    half = LANES // 2
-    low = jnp.where(lane < half, near, pltpu.roll(far, half, 1))
-    high = jnp.where(lane < half, pltpu.roll(near, half, 1), far)
-    return low.astype(bf16), high.astype(bf16)
+def chip_spot(tile, chips, tiles):
+    half, chip, core = tile // (2 * chips), (tile // 2) % chips, tile % 2
+    return chip, core * (tiles // (2 * chips)) + half
 
 
 def forward_kernel(
-    states, taps, slices,
-    here, masks, vec_ref, rates_ref, entry_ref, table, dt_ref, inner_ref, gate_ref, ggated_ref, dx_ref, ex_ref,
+    states, taps, chips, rows_size,
+    here, masks, cot_ref, vec_ref, rates_ref, entry_ref, table, dt_ref, inner_ref, gate_ref, ggated_ref, dx_ref, ex_ref,
     gated_ref, ggate_ref, *rest,
 ):
-    blocks, (dtm_s, u_s, y_s, held) = rest[:slices], rest[slices:]
+    lines, blocks, (dtm_s, u_s, y_s, held) = rest[:rows_size], rest[rows_size:-4], rest[-4:]
     length, width = inner_ref.shape
     tiles, steps = width // LANES, length // SUBS
     zero = jnp.zeros((SUBS, LANES), f32)
@@ -367,43 +360,44 @@
         gated_ref[:, at] = (scanned * gate * sig).astype(bf16)
         ggate = (ggated_ref[:, at] * scanned * (sig * (1.0 + gate * (1.0 - sig)))).astype(bf16)
         ggate_ref[:, at] = ggate
+        if chips:
+            chip, spot = chip_spot(tile, chips, tiles)
+            held[chip, :, tile_at(spot * LANES)] = ggate
         return 0
 
     lax.fori_loop(0, tiles, scan, 0)
-    if not slices:
-        return
-    for pair in range(tiles // 2):
-        side, spot = pair // (tiles // 4), pair % (tiles // 4)
-        near, far = (ggate_ref[:, (2 * pair + n) * LANES : (2 * pair + n + 1) * LANES].astype(f32) for n in range(2))
-        at = pl.ds(spot * LANES, LANES)
-        held[side, :, at], held[side + 2, :, at] = halves_of(near, far)
-    for n in range(slices):
-        blocks[n][:, :width] = gated_ref[...]
-        blocks[n][:, width:] = held[here[1] ^ n]
-
-
-def forward(masks, vec, rates, entry, table, dt, inner, gate, ggated, dx, ex, taps, slices):
+    for n in range(chips):
+        blocks[n][...] = held[here[2] ^ n]
+    thin = cot_ref.shape[1] // rows_size
+    for n in range(rows_size):
+        lines[n][:, :width] = gated_ref[...]
+        lines[n][:, width:] = cot_ref[:, tile_at((here[1] ^ n) * thin, thin)]
+
+
+def forward(masks, cot, vec, rates, entry, table, dt, inner, gate, ggated, dx, ex, taps, chips, rows_size):
     length, width = inner.shape
     states = rates.shape[0]
     shape = jax.ShapeDtypeStruct
     return plain_call(
-        functools.partial(forward_kernel, states, taps, slices),
+        functools.partial(forward_kernel, states, taps, chips, rows_size),
         "forward",
-        [shape((length, width), bf16)] * 2 + [shape((length, width + width // max(slices, 1)), bf16)] * slices,
-        (masks, vec, rates, entry, table, dt, inner, gate, ggated, dx, ex),
+        [shape((length, width), bf16)] * 2
+        + [shape((length, width + cot.shape[1] // rows_size), bf16)] * rows_size
+        + [shape((length, width // max(chips, 1)), bf16)] * chips,
+        (masks, cot, vec, rates, entry, table, dt, inner, gate, ggated, dx, ex),
         8,
-        [pltpu.VMEM((length, LANES), f32)] * 3 + [pltpu.VMEM((max(slices, 1), length, width // max(slices, 1)), bf16)],
+        [pltpu.VMEM((length, LANES), f32)] * 3 + [pltpu.VMEM((max(chips, 1), length, width // max(chips, 1)), bf16)],
         8,
     )
 
 
 def backward_kernel(
-    states, rank, taps, slices,
+    states, rank, taps, chips,
     here, win_hbm, dtw_hbm, wx_hbm, masks, proj_ref, tok_ref, gain_ref, vec_ref, rates_ref, entry_ref, arrive_ref,
     table, dt_ref, inner_ref, gs_ref, dx_ref, ex_ref, db_ref, fx_ref, ggate_ref, ext_ref,
     ngrad, *rest,
 ):
-    blocks, rest = rest[: max(slices, 1)], rest[max(slices, 1) :]
+    blocks, rest = rest[: max(chips, 1)], rest[max(chips, 1) :]
     (acc, hs, decays, dtm_s, u_s, s1_s, s2_s, isg, raw_s, sent_s, low_acc, pg, small, held, win_ref, dtw_ref, wx_ref, sems) = rest[-18:]
     length, width = inner_ref.shape
     model = tok_ref.shape[1]
@@ -516,18 +510,11 @@
         return 0
 
     lax.fori_loop(0, width // block, low_part, 0)
-    lane = lax.broadcasted_iota(jnp.int32, (SUBS, LANES), 1)
-
-    def gather_maps(t, _):
-        rows = step_rows(t)
-        out = low_acc[rows, :]
-        for n in range(2 * states):
-            part = jnp.sum(acc[rows, n * LANES : (n + 1) * LANES], axis=1, keepdims=True)
-            out = jnp.where(lane == rank + n, part, out)
-        low_acc[rows, :] = out
-        return 0
-
-    lax.fori_loop(0, steps, gather_maps, 0)
+    wide_row = lax.broadcasted_iota(jnp.int32, (2 * states * LANES, LANES), 0)
+    wide_lane = lax.broadcasted_iota(jnp.int32, (2 * states * LANES, LANES), 1)
+    ones = jnp.where(wide_lane == rank + wide_row // LANES, 1.0, 0.0).astype(bf16)
+    high = acc[...].astype(bf16)
+    low_acc[...] += nn(high, ones) + nn((acc[...] - high.astype(f32)).astype(bf16), ones)
     pg[...] = low_acc[...].astype(bf16)
     for load in loads[1:]:
         load.wait()
@@ -568,13 +555,11 @@
                 edge = jnp.where(row == b, jnp.broadcast_to(head[b][:1], (SUBS, LANES)), edge)
             sent = jnp.concatenate(near + [edge, zero], axis=0)
             sent_s[:, tile * LANES : (tile + 1) * LANES] = sent.astype(bf16)
-            if not slices:
+            if chips:
+                chip, spot = chip_spot(j * (block // LANES) + tile, chips, tiles)
+                held[chip, :, tile_at(spot * LANES)] = sent.astype(bf16)
+            else:
                 blocks[0][:, far] = sent.astype(bf16)
-            elif tile % 2 == 1:
-                pair = j * (block // LANES // 2) + tile // 2
-                side, spot = pair // (tiles // 4), tile_at(pair % (tiles // 4) * LANES)
-                held[side, :, spot], held[side + 2, :, spot] = halves_of(last, sent)
-            last = sent
         ngrad[...] += nt(sent_s[...], win_ref[:, wide])
         return 0
 
@@ -582,8 +567,8 @@
     x = tok_ref[...].astype(f32)
     inv = lax.rsqrt(jnp.mean(x * x, axis=-1, keepdims=True) + epsilon)
     small[pl.ds(row_gain, 1), pl.ds(0, model)] = jnp.sum(ngrad[...] * (x * inv), axis=0, keepdims=True)
-    if slices:
-        part = width // slices
+    if chips:
+        part = width // chips
         row = lax.broadcasted_iota(jnp.int32, (EDGE, part), 0)
         extra = jnp.zeros((EDGE, part), f32)
         normed = x[length:] * inv[length:] * gain_ref[...]
@@ -593,10 +578,10 @@
                 piece = jnp.broadcast_to(normed[b : b + 1, c * part : (c + 1) * part], (EDGE, part))
                 extra = jnp.where(row == rim + b * count + c, piece, extra)
         edge_rows = pl.ds(length, EDGE)
-        for n in range(slices):
+        for n in range(chips):
             held[n, edge_rows, :] = (held[n, edge_rows, :].astype(f32) + extra).astype(bf16)
-        for n in range(slices):
-            blocks[n][...] = held[here[1] ^ n]
+        for n in range(chips):
+            blocks[n][...] = held[here[2] ^ n]
     mine_ref, theirs_ref = rest[:2]
     chunk = mine_ref.shape[2]
     for c in range(2):
@@ -610,7 +595,7 @@
 
 
 def backward(masks, in_weight, dtw, wx, proj, tok, gain, vec, rates, entry, arrive, table, dt, inner, gs, deep4,
-             ggate, ext, taps, slices, chunks):
+             ggate, ext, taps, chips, chunks):
     length, width = inner.shape
     model = tok.shape[1]
     states = rates.shape[0]
@@ -620,10 +605,10 @@
     rows = 2 * rank + 3 * states + taps + 4
     rows = -(-rows // EDGE) * EDGE
     shape = jax.ShapeDtypeStruct
-    parts = max(slices, 1)
+    parts = max(chips, 1)
     chunk = (chunks, rows, width // (2 * chunks))
     return plain_call(
-        functools.partial(backward_kernel, states, rank, taps, slices),
+        functools.partial(backward_kernel, states, rank, taps, chips),
         "backward",
         [shape((length + EDGE, model), f32)]
         + [shape((length + EDGE, width // parts), bf16)] * parts
@@ -761,34 +746,42 @@
     arrive_ref[...] = jnp.where(core == 0, whole * arrive + f, arrive)
 
 
-def early_kernel(here, gain_ref, *rest):
-    early, (normed_ref, left_ref) = rest[:-2], rest[-2:]
-    length, model = early[0].shape[0], gain_ref.shape[1]
-    for k, x in enumerate(early):
-        at = pl.ds(k * length, length)
-        normed_ref[at, :] = normalise(x[:, :model], gain_ref[...])
-        left_ref[at, :] = x[:, model:]
-
-
-def gate_out_kernel(size, chips, thin, here, normed_ref, left_ref, *rest):
-    late, mine_ref, theirs = rest[:size], rest[size], rest[size + 1 :]
-    model = normed_ref.shape[1]
-    width = late[0].shape[1] * size // (size + 1)
-    gate = tn(jnp.concatenate([x[:, width:] for x in late], axis=0), normed_ref[...])
-    out = tn(left_ref[...], jnp.concatenate([x[:, :width] for x in late], axis=0))
-    half = LANES // 2
+def out_kernel(size, chips, thin, here, *rest):
+    parts, (mine_ref, theirs_ref) = rest[:size], rest[size:]
+    model = mine_ref.shape[2]
+    width = parts[0].shape[1] - 2 * chips * thin
+    left = jnp.concatenate([x[:, width:] for x in parts], axis=0)
+    out = tn(left, jnp.concatenate([x[:, :width] for x in parts], axis=0))
     for c in range(2):
 
         @pl.when(here[0] == c)
         def _():
             for q in range(chips):
-                for ref, side in ((mine_ref.at[q], c), (theirs[q], 1 - c)):
-                    at = q * LANES + side * half
-                    ref[pl.ds(0, half), :] = gate[at : at + half].astype(ref.dtype)
+                for ref, side in ((mine_ref, c), (theirs_ref, 1 - c)):
                     at = (2 * q + side) * thin
                     for n in range(width // model):
                         piece = out[at : at + thin, n * model : (n + 1) * model]
-                        ref[pl.ds(half + n * thin, thin), :] = piece.astype(ref.dtype)
+                        ref[q, pl.ds(n * thin, thin), :] = piece.astype(ref.dtype)
+
+
+def split_cores(here, x, mine_ref, theirs_ref):
+    count, rows = mine_ref.shape[:2]
+    for c in range(2):
+
+        @pl.when(here[0] == c)
+        def _():
+            for n in range(count):
+                mine_ref[n] = x[(c * count + n) * rows : (c * count + n + 1) * rows]
+                theirs_ref[n] = x[((1 - c) * count + n) * rows : ((1 - c) * count + n + 1) * rows].astype(bf16)
+
+
+def gate_kernel(size, here, gain_ref, *rest):
+    toks, gots, (normed_ref, mine_ref, theirs_ref) = rest[:size], rest[size:-3], rest[-3:]
+    length = toks[0].shape[0]
+    for k, x in enumerate(toks):
+        normed_ref[pl.ds(k * length, length), :] = normalise(turned(x[...], False), gain_ref[...])
+    got = jnp.concatenate([x[...] for x in gots], axis=0)
+    split_cores(here, tn(got, normed_ref[...]), mine_ref, theirs_ref)
 
 
 def flat(x, pieces):
@@ -801,7 +794,7 @@
     return jnp.concatenate([x[:, n * lanes : (n + 1) * lanes] for n in range(pieces)], axis=0)
 
 
-def conv_kernel(length, chips, rim, here, normed_ref, *rest):
+def conv_kernel(length, rim, here, normed_ref, *rest):
     gots, (mine_ref, theirs_ref) = rest[:-2], rest[-2:]
     wide = gots[0].shape[1]
     model = normed_ref.shape[1]
@@ -821,93 +814,58 @@
         rights.append(jnp.where(lax.broadcasted_iota(jnp.int32, right.shape, 0) < rim, right, 0.0))
     left, right = (jnp.concatenate(x, axis=0).astype(bf16) for x in (lefts, rights))
     conv = tn(got, normed_ref[...]) + tn(right, left)
-    half = LANES // 2
-    for c in range(2):
-
-        @pl.when(here[0] == c)
-        def _():
-            for q in range(chips):
-                at = q * LANES
-                mine_ref[q] = conv[at + c * half : at + (c + 1) * half]
-                theirs_ref[pl.ds(q * half, half), :] = conv[at + (1 - c) * half : at + (2 - c) * half].astype(bf16)
-
-
-def mix0_kernel(here, mine_ref, got_ref, small_ref, small_got, keep_ref, small_out, send_ref):
-    place = here[2] & 1
-    half, count = mine_ref.shape[1], mine_ref.shape[0] // 2
-    at = lambda n: pl.ds(pl.multiple_of(n * half, half), half)
-    for n in range(count):
+    split_cores(here, conv, mine_ref, theirs_ref)
+
+
+def halve_kernel(which, bit, here, mine_ref, got_ref, keep_ref, send_ref):
+    place = (here[which] >> bit) & 1
+    for n in range(mine_ref.shape[0] // 2):
         stay, leave = 2 * n + place, 2 * n + 1 - place
-        keep_ref[n] = mine_ref[stay] + got_ref[at(stay), :].astype(f32)
-        send_ref[at(n), :] = (mine_ref[leave] + got_ref[at(leave), :].astype(f32)).astype(bf16)
-    small = small_ref[0] + small_got[0].astype(f32)
-    small = flat(small, mine_ref.shape[2] // small.shape[1]).astype(bf16)
-    small_out[...] = small
-    send_ref[pl.ds(count * half, small.shape[0]), :] = small
-
-
-def mix1_kernel(here, mine_ref, got_ref, small_ref, keep_ref, small_out, send_ref):
-    place = (here[2] >> 1) & 1
-    half = mine_ref.shape[1]
-    at = lambda n: pl.ds(pl.multiple_of(n * half, half), half)
-    keep_ref[...] = mine_ref[place] + got_ref[at(place), :].astype(f32)
-    send_ref[pl.ds(0, half), :] = (mine_ref[1 - place] + got_ref[at(1 - place), :].astype(f32)).astype(bf16)
-    rows = small_ref.shape[0]
-    small = (small_ref[...].astype(f32) + got_ref[pl.ds(2 * half, rows), :].astype(f32)).astype(bf16)
-    small_out[...] = small
-    send_ref[pl.ds(half, rows), :] = small
-
-
-def halve_kernel(which, bit, here, mine_ref, *rest):
-    gots, (keep_ref, send_ref) = rest[:-2], rest[-2:]
-    place = (here[which] >> bit) & 1
-    each = mine_ref.shape[0] // len(gots)
-    for n in range(mine_ref.shape[0]):
-        got = gots[n // each]
-        total = mine_ref[n] + (got[n % each] if len(got.shape) == 3 else got[...]).astype(f32)
-        for side in range(2):
-
-            @pl.when(place == side)
-            def _():
-                if n % 2 == side:
-                    keep_ref[n // 2] = total
-                else:
-                    send_ref[n // 2] = total.astype(bf16)
-
-
-def cross_kernel(here, mine_ref, got_ref, small_ref, gate_ref, keep_ref, small_out, send_ref):
-    half = mine_ref.shape[0]
-    conv = mine_ref[...] + got_ref[pl.ds(0, half), :].astype(f32)
-    first = here[1] < 2
-    keep_ref[...] = jnp.where(first, conv, gate_ref[...])
-    send_ref[pl.ds(0, half), :] = jnp.where(first, gate_ref[...], conv).astype(bf16)
-    rows = small_ref.shape[0]
-    small = (small_ref[...].astype(f32) + got_ref[pl.ds(half, rows), :].astype(f32)).astype(bf16)
-    small_out[...] = small
-    send_ref[pl.ds(half, rows), :] = small
-
-
-def go_last_kernel(thin, here, mine_ref, got_ref, gate_ref, out_ref):
-    half, model = gate_ref.shape
+        keep_ref[n] = mine_ref[stay] + got_ref[stay].astype(f32)
+        send_ref[n] = (mine_ref[leave] + got_ref[leave].astype(f32)).astype(bf16)
+
+
+def small_last_kernel(here, mine_ref, got_ref, out_ref):
+    small = mine_ref[0] + got_ref[0].astype(f32)
+    out_ref[...] = flat(small, out_ref.shape[1] // small.shape[1]).astype(bf16)
+
+
+def add_kernel(here, mine_ref, got_ref, out_ref):
+    out_ref[...] = (mine_ref[...].astype(f32) + got_ref[...].astype(f32)).astype(bf16)
+
+
+def in_merge_kernel(here, conv_mine, conv_got, gate_mine, gate_got, small_ref, own_ref, *parts):
+    count, rows = conv_mine.shape[:2]
+    for part in parts:
+        part[pl.ds(rows, small_ref.shape[0]), :] = small_ref[...]
+    for mine, got, first in ((conv_mine, conv_got, 0), (gate_mine, gate_got, count)):
+        for n in range(count):
+            both = mine[n] + got[n].astype(f32)
+            for k in range(2 * count):
+
+                @pl.when((here[1] ^ k) == first + n)
+                def _():
+                    if k == 0:
+                        own_ref[...] = both
+                    else:
+                        parts[k - 1][pl.ds(0, rows), :] = both.astype(bf16)
+
+
+def in_last_kernel(here, own_ref, small_ref, *rest):
+    gots, (out_ref, small_out) = rest[:-2], rest[-2:]
+    both, rows = own_ref[...], own_ref.shape[0]
+    small_out[here[1]] = small_ref[...]
+    for k, got in enumerate(gots):
+        both = both + got[pl.ds(0, rows), :].astype(f32)
+        small_out[here[1] ^ (k + 1)] = got[pl.ds(rows, small_ref.shape[0]), :]
+    out_ref[...] = both.T
+
+
+def out_last_kernel(here, mine_ref, got_ref, out_ref):
+    thin, model = out_ref.shape[0], mine_ref.shape[2]
     both = mine_ref[0] + got_ref[0].astype(f32)
-    gate_ref[...] = both[:half]
     for n in range(out_ref.shape[1] // model):
-        out_ref[:, n * model : (n + 1) * model] = both[half + n * thin : half + (n + 1) * thin]
-
-
-def in_last_kernel(here, keep_ref, got_ref, out_ref):
-    half = keep_ref.shape[0]
-    keep, got = keep_ref[...], got_ref[pl.ds(0, half), :].astype(f32)
-    first = here[1] < 2
-    both = jnp.concatenate([jnp.where(first, keep, got), jnp.where(first, got, keep)], axis=0)
-    out_ref[...] = both.T
-
-
-def join_kernel(here, *refs):
-    parts, out_ref = refs[:-1], refs[-1]
-    rows = out_ref.shape[1]
-    for k, part in enumerate(parts):
-        out_ref[here[1] ^ k] = part[pl.ds(part.shape[0] - rows, rows), :]
+        out_ref[:, n * model : (n + 1) * model] = both[n * thin : (n + 1) * thin]
 
 
 def unpack_kernel(edges, here, rates_ref, mine_ref, other_ref, *outs):
@@ -920,7 +878,8 @@
             block = tall(part[k].astype(f32), pieces)
             for n, out in enumerate(outs):
                 piece = block[edges[n] : edges[n + 1]]
-                out[:, at] = piece * rates_ref[:, at] if n == 2 else piece
+                if (2 * k + 1) * chunk < out.shape[1]:
+                    out[:, at] = piece * rates_ref[:, at] if n == 2 else piece
 
 
 class Group:
@@ -1002,21 +961,24 @@
     width = in_weight.shape[1] // (dp_size * seq_size)
     half_rows = dp_size // 2
     thin = model // (dp_size * seq_size)
-    part = inner_width // dp_size
+    part = inner_width // outer.size
     tiled = outer.size == 4 and dp_size == 4 and width == LANES and thin % EDGE == 0
     tiled = tiled and model % part == 0 and rim * (1 + model // part) <= EDGE
-    chips, slices = outer.size, dp_size if tiled else 0
+    chips = outer.size if tiled else 0
     shape = jax.ShapeDtypeStruct
 
     wx = xproj_weight.T
     decay_rates = -jnp.exp(a_log).T
 
     left = lax.ppermute(tokens[0, length - rim :], "seq", [(i, i + 1) for i in range(seq_size - 1)])
-    tok, cot, ext, inner, gate, ggated, gs, dt, proj, table, mine, dx, ex, db, fx, vec, rates, gain, masks, *early = front(
+    tok, cot, ext, inner, gate, ggated, gs, dt, proj, table, mine, dx, ex, db, fx, vec, rates, gain, masks = front(
         doc_starts, tokens, cotangent, norm_gain, conv_weight.T, conv_bias, dt_bias, skip_scale, a_log.T, dt_weight, wx,
-        in_weight, out_weight, left, dp_size,
+        in_weight, out_weight, left,
     )
-    early = rows_group.trade(early)
+    if tiled:
+        after, _ = lax.optimization_barrier((tokens[0], left))
+        tok_parts = outer.gather(after)
+        mine, tok_parts = lax.optimization_barrier((mine, tok_parts))
     other = core.swap(mine, 1)
     entering = [shape(rates.shape, f32)] * 2
     if tiled:
@@ -1053,28 +1015,19 @@
         entry, arrive = plain_call(
             functools.partial(enter_kernel, states, outer.size), "enter", entering, (other, rates, got), 2
         )
-    entry, early = lax.optimization_barrier((entry, early))
-    gated, ggate, *late = forward(masks, vec, rates, entry, table, dt, inner, gate, ggated, dx, ex, taps, slices)
-    late = rows_group.trade(late) if tiled else rows_group.gather(gated)
-    if tiled:
-        early, _ = lax.optimization_barrier((early, ggate))
-        normed, left_cols = plain_call(
-            early_kernel,
-            "early",
-            [shape((dp_size * length, model), bf16), shape((dp_size * length, model // dp_size), bf16)],
-            (gain, *early),
-            1,
-        )
-        arrive, _ = lax.optimization_barrier((arrive, normed))
+    gated, ggate, *late = forward(masks, cot, vec, rates, entry, table, dt, inner, gate, ggated, dx, ex, taps, chips, dp_size)
+    lines_got = rows_group.trade(late[:dp_size])
+    gate_got = outer.trade(late[dp_size:]) if tiled else None
+
     ngrad, *sent, small, small_theirs = backward(
         masks, in_weight, dt_weight, wx, proj, tok, gain, vec, rates, entry, arrive, table, dt, inner, gs,
-        (dx, ex, db, fx), ggate, ext, taps, slices, dp_size,
+        (dx, ex, db, fx), ggate, ext, taps, chips, dp_size,
     )
     rows, chunk = small.shape[1:]
     turn = [ngrad]
 
-    def call(kernel, name, outs, args, us=1):
-        args, _ = lax.optimization_barrier((tuple(args), turn[0]))
+    def call(kernel, name, outs, args, us=2):
+        args = tuple(args)
         got = plain_call(kernel, name, [shape(*x) for x in outs], args, us)
         turn[0] = got[0]
         return got
@@ -1082,10 +1035,9 @@
     def halve(group, bit, which, mine, got, name):
         count, *rest = mine.shape
         outs = [((count // 2, *rest), f32), ((count // 2, *rest), bf16)]
-        keep, send = call(functools.partial(halve_kernel, which, bit), name, outs, (mine, *got))
-        return keep, [group.swap(send, 1 << bit)]
-
-    half = LANES // 2
+        keep, send = call(functools.partial(halve_kernel, which, bit), name, outs, (mine, got))
+        return keep, group.swap(send, 1 << bit)
+
     lines = rows * chunk // model
     part = ((lines, model), bf16)
     back = lax.ppermute(ngrad[length:], "seq", [(i, i - 1) for i in range(1, seq_size)])
@@ -1099,38 +1051,52 @@
         )
 
     if tiled:
-        small_got = [core.swap(small_theirs, 1)]
-        conv_got = rows_group.trade(sent)
+        blocks = (half_rows, width, model)
+        sent, small_theirs, *early_got = lax.optimization_barrier((sent, small_theirs, *lines_got, *gate_got[:-1]))
+        lines_got, gate_got = early_got[:dp_size], early_got[dp_size:] + gate_got[-1:]
+        small_got = core.swap(small_theirs, 1)
+        conv_got = outer.trade(sent)
         small, small_got = halve(rows_group, 0, 1, small, small_got, "small_row0")
-        go, *theirs = call(
-            functools.partial(gate_out_kernel, dp_size, chips, thin),
-            "gate_out_columns",
-            [((chips, LANES, model), f32)] + [((LANES, model), bf16)] * chips,
-            (normed, left_cols, *late),
+        block = (chips, LANES // 2, model)
+        out, theirs = call(
+            functools.partial(out_kernel, dp_size, chips, thin),
+            "out_columns",
+            [(block, f32), (block, bf16)],
+            lines_got,
         )
-        go_got = [core.swap(x, 1) for x in theirs]
-        go, go_got = halve(outer, 0, 2, go, go_got, "go_chip0")
+        out_got = core.swap(theirs, 1)
         small, small_got = halve(rows_group, 1, 1, small, small_got, "small_row1")
-        go, go_got = halve(outer, 1, 2, go, go_got, "go_chip1")
-        outs = [((chips, half, model), f32), ((chips * half, model), bf16)]
-        conv, theirs = call(functools.partial(conv_kernel, length, chips, rim), "conv_columns", outs, (normed, *conv_got))
-        got = core.swap(theirs, 1)
-        outs = [((chips // 2, half, model), f32), part, ((chips // 2 * half + lines, model), bf16)]
-        conv, small, send = call(mix0_kernel, "mix0", outs, (conv, got, small, *small_got))
-        got = outer.swap(send, 1)
-        outs = [((half, model), f32), ((thin, inner_width), f32)]
-        gate_slice, out_share = call(functools.partial(go_last_kernel, thin), "go_last", outs, (go, *go_got))
-        outs = [((half, model), f32), part, ((half + lines, model), bf16)]
-        conv, small, send = call(mix1_kernel, "mix1", outs, (conv, got, small))
-        got = outer.swap(send, 2)
+        normed, gate, theirs = call(
+            functools.partial(gate_kernel, chips),
+            "gate_columns",
+            [((chips * length, model), bf16), (blocks, f32), (blocks, bf16)],
+            (gain, *tok_parts, *gate_got),
+        )
+        gate_got = core.swap(theirs, 1)
+        (small,) = call(small_last_kernel, "small_last", [part], (small, small_got))
+        small_got = outer.swap(small, 1)
+        conv, theirs = call(
+            functools.partial(conv_kernel, length, rim), "conv_columns", [(blocks, f32), (blocks, bf16)], (normed, *conv_got)
+        )
+        conv_got = core.swap(theirs, 1)
+        (small,) = call(add_kernel, "small_chip0", [part], (small, small_got))
+        small_got = outer.swap(small, 2)
+        (small,) = call(add_kernel, "small_chip1", [part], (small, small_got))
+        slab = (width, model)
+        in_own, *sends = call(
+            in_merge_kernel,
+            "in_merge",
+            [(slab, f32)] + [((width + lines, model), bf16)] * (dp_size - 1),
+            (conv, conv_got, gate, gate_got, small),
+        )
+        in_own, *in_gots = rows_group.trade([in_own] + sends)
+        out, out_got = halve(outer, 0, 2, out, out_got, "out_chip0")
         tokens_grad, mixed = finished()
-        outs = [((half, model), f32), part, ((half + lines, model), bf16)]
-        keep, small, send = call(cross_kernel, "cross", outs, (conv, got, small, gate_slice))
-        in_got = rows_group.swap(send, 2)
-        smalls = [small, rows_group.swap(small, 1), in_got, rows_group.swap(small, 3)]
-        (small,) = call(join_kernel, "join", [((dp_size, lines, model), bf16)], smalls)
+        out, out_got = halve(outer, 1, 2, out, out_got, "out_chip1")
+        outs = [((model, width), f32), ((dp_size, lines, model), bf16)]
+        in_share, small = call(in_last_kernel, "in_last", outs, (in_own, small, *in_gots))
         small_other = core.swap(small, 1)
-        (in_share,) = call(in_last_kernel, "in_last", [((model, width), f32)], (keep, in_got))
+        (out_share,) = call(out_last_kernel, "out_last", [((thin, inner_width), f32)], (out, out_got))
     else:
         tokens_grad, mixed = finished()
         small = small + core.swap(small_theirs, 1).astype(f32)
@@ -1144,7 +1110,7 @@
     parts = call(
         functools.partial(unpack_kernel, edges),
         "unpack",
-        [((size, inner_width), f32) for size in sizes],
+        [((size, inner_width), f32) for size in sizes[:-1]] + [((1, model), f32)],
         (decay_rates, small, small_other),
     )
     if not tiled:
@@ -1169,7 +1135,7 @@
         conv_core = total(core.exchange(halved(summed(normed_parts, by_chip(sent[0])))))
         in_core = jnp.concatenate([conv_core, gate_core], axis=1).astype(bf16)
         in_share = total(rows_group.exchange(in_core.reshape(model, dp_size, width).swapaxes(0, 1)))
-        out_sum = summed([x[:, model:] for x in early], late).astype(bf16)
+        out_sum = summed([x[:, inner_width:] for x in lines_got], [x[:, :inner_width] for x in lines_got]).astype(bf16)
         out_core = total(core.exchange(out_sum.reshape(outer.size, 2, thin, inner_width).swapaxes(0, 1)))
         out_share = total(outer.exchange(out_core.astype(bf16)))
 
@@ -1185,7 +1151,7 @@
         parts[2].T,
         parts[5][0],
         out_share.T,
-        parts[7][0, :model],
+        parts[7][0],
     )
 
 

time: 152 us -> 135 us (0.89)
  waiting for transfers between devices: 46.7 us -> 31.1 us
  Pallas kernels: 62.9 us -> 57 us
  starting transfers between devices: 39.5 us -> 45 us
    ppermute x29 -> x30, waiting for transfers between devices: 44.1 us -> 30.3 us  [swap(): lax.ppermute(x, self.axis, [(i, i ^ k * self.stride) for i in range(n)])]
    pallas_call x22, Pallas kernels: 62.9 us -> 57 us  [plain_call(): pl.pallas_call(lambda *refs: kernel(Here(), *refs), in_specs=list(specs)...]
    ppermute x29 -> x30, starting transfers between devices: 35.8 us -> 41.4 us  [swap(): lax.ppermute(x, self.axis, [(i, i ^ k * self.stride) for i in range(n)])]
    ppermute x1, waiting for transfers between devices: 1.85 us -> 0.01 us  [body(): lax.ppermute(ngrad[length:], 'seq', [(i, i - 1) for i in range(1, seq_siz...]
  transfers between devices with their start and end apart: 31 -> 32, of which waited for: 21 -> 15; matrix products, arithmetic and copies ran while one was open for 0% -> 0% of each run, Pallas kernels for 20% -> 37%
where the time goes in v5:
time: 135 us
  Pallas kernels  57 us (42%)
  starting transfers between devices  45 us (33%)
  waiting for transfers between devices  31.1 us (23%)
    pallas_call x22, Pallas kernels, plain_call(): pl.pallas_call(lambda *refs: kernel(Here(), *refs), in_specs=list(specs)...  57 us
    ppermute x30, starting transfers between devices, swap(): lax.ppermute(x, self.axis, [(i, i ^ k * self.stride) for i in range(n)])  41.4 us
    ppermute x30, waiting for transfers between devices, swap(): lax.ppermute(x, self.axis, [(i, i ^ k * self.stride) for i in range(n)])  30.3 us
  transfers between devices with their start and end apart: 32, of which 15 were waited for; matrix products, arithmetic and copies ran while one was open for 0% of the time, Pallas kernels for 37%

profile of v5, /device:TPU:0, one launch (start us, length us, event | category | flops | bytes accessed | tf_op | source)
XLA Modules:
  0.0 134.9 jit_solution(6528809702085551710)
XLA Ops:
  0.6 0.7 slice_bitcast_fusion
  1.4 2.3 %collective-permute-start = (bf16[3,1024]{1,0:T(4,128)(2,1)S(1)}, bf16[3,1024]{1,0:T(4,128)(2,1)S(1)}, u32[]{:S(2)}, u32[]{:S(2)}) collective-permute-start(bf16[3,1024]{1,0:T(4,128)(2,1)S(1)} %slice_bitcast_fusion), channel_id=1, source_target_pairs={{0,1},{1,2},{2,3},{3,4},{4,5},{5,6},{6,7},{8,9},{9,10},{10,11},{11... | collective-permute-start | bytes 18440 | tf_op jit(solution)/shard_map/ppermute | solution.py:973
  3.7 0.8 collective-permute-done.refs_13_
  4.5 4.8 %collective-permute-start.1 = (bf16[128,1024]{1,0:T(8,128)(2,1)}, bf16[128,1024]{1,0:T(8,128)(2,1)S(1)}, u32[]{:S(2)}, u32[]{:S(2)}) collective-permute-start(bf16[128,1024]{1,0:T(8,128)(2,1)} %bitcast.18), channel_id=1, source_target_pairs={{0,2},{1,3},{2,0},{3,1},{4,6},{5,7},{6,4},{7,5},{8,10},{9,11},{10,... | collective-permute-start | bytes 786440 | tf_op jit(solution)/shard_map/ppermute | solution.py:902
  9.4 2.6 %collective-permute-start.2 = (bf16[128,1024]{1,0:T(8,128)(2,1)}, bf16[128,1024]{1,0:T(8,128)(2,1)S(1)}, u32[]{:S(2)}, u32[]{:S(2)}) collective-permute-start(bf16[128,1024]{1,0:T(8,128)(2,1)} %bitcast.19), channel_id=1, source_target_pairs={{0,4},{1,5},{2,6},{3,7},{4,0},{5,1},{6,2},{7,3},{8,12},{9,13},{10,... | collective-permute-start | bytes 786440 | tf_op jit(solution)/shard_map/ppermute | solution.py:902
  11.9 18.6 %front.1 = (bf16[144,1024]{1,0:T(8,128)(2,1)S(1)}, bf16[128,1024]{1,0:T(8,128)(2,1)S(1)}, bf16[160,2048]{1,0:T(8,128)(2,1)S(1)}, bf16[128,2048]{1,0:T(8,128)(2,1...) custom-call(s32[1,4]{1,0:T(1,128)} %refs_0_.2, ...), custom_call_target="tpu_custom_call" | custom-call | flops 22000001024 | tf_op jit(solution)/shard_map/front/pallas_call | solution.py:49
  30.6 0.3 collective-permute-done.2.refs_3_
  30.9 1.4 %collective-permute-done.4.refs_1_.refs_0_ = bf16[48,2048]{1,0:T(8,128)(2,1)S(1)} collective-permute-done((bf16[48,2048]{1,0:T(8,128)(2,1)S(1)}, bf16[48,2048]{1,0:T(8,128)(2,1)S(1)}, u32[]{:S(2)}, u32[]{:S(2)}) %collective-permute-start.4) | collective-permute-done | bytes 196640 | tf_op jit(solution)/shard_map/ppermute | solution.py:902
  32.4 0.1 pair.1.refs_0_
  32.5 4.4 %collective-permute-start.5 = (bf16[48,1024]{1,0:T(8,128)(2,1)S(1)}, bf16[48,1024]{1,0:T(8,128)(2,1)S(1)}, u32[]{:S(2)}, u32[]{:S(2)}) collective-permute-start(bf16[48,1024]{1,0:T(8,128)(2,1)S(1)} %pair.1.refs_0_), channel_id=1, source_target_pairs={{0,2},{1,3},{2,0},{3,1},{4,6},{5,7},{6,4},{7,5},{8,10},{9,11},{10,... | collective-permute-start | bytes 294920 | tf_op jit(solution)/shard_map/ppermute | solution.py:902
  36.9 3.1 %collective-permute-done.5.refs_1_ = bf16[48,1024]{1,0:T(8,128)(2,1)S(1)} collective-permute-done((bf16[48,1024]{1,0:T(8,128)(2,1)S(1)}, bf16[48,1024]{1,0:T(8,128)(2,1)S(1)}, u32[]{:S(2)}, u32[]{:S(2)}) %collective-permute-start.5) | collective-permute-done | bytes 98336 | tf_op jit(solution)/shard_map/ppermute | solution.py:902
  40.0 0.1 quad.1
  40.1 2.8 %collective-permute-start.6 = (bf16[16,1024]{1,0:T(8,128)(2,1)S(1)}, bf16[16,1024]{1,0:T(8,128)(2,1)S(1)}, u32[]{:S(2)}, u32[]{:S(2)}) collective-permute-start(bf16[16,1024]{1,0:T(8,128)(2,1)S(1)} %get-tuple-element.111), channel_id=1, source_target_pairs={{0,4},{1,5},{2,6},{3,7},{4,0},{5,1},{6,2},{7,3},{8,12},{9,13},{10,... | collective-permute-start | bytes 98312 | tf_op jit(solution)/shard_map/ppermute | solution.py:902
  42.9 2.1 %collective-permute-done.6.refs_1_ = bf16[16,1024]{1,0:T(8,128)(2,1)S(1)} collective-permute-done((bf16[16,1024]{1,0:T(8,128)(2,1)S(1)}, bf16[16,1024]{1,0:T(8,128)(2,1)S(1)}, u32[]{:S(2)}, u32[]{:S(2)}) %collective-permute-start.6) | collective-permute-done | bytes 32800 | tf_op jit(solution)/shard_map/ppermute | solution.py:902
  45.0 0.1 collective-permute-start.7
  45.0 1.3 collective-permute-done.7.refs_3_
  46.4 0.1 enter.1
  46.4 5.4 %forward.1 = (bf16[128,2048]{1,0:T(8,128)(2,1)S(1)}, bf16[128,2048]{1,0:T(8,128)(2,1)S(1)}, bf16[128,2304]{1,0:T(8,128)(2,1)S(1)}, bf16[128,2304]{1,0:T(8,128)(2...) custom-call(f32[4,128,128]{2,1,0:T(8,128)S(1)} %get-tuple-element.10, ...), custom_call_target="tpu_custom_call" | custom-call | flops 8800000000 | tf_op jit(solution)/shard_map/forward/pallas_call | solution.py:49
  51.8 1.6 %collective-permute-start.10 = (bf16[128,2304]{1,0:T(8,128)(2,1)S(1)}, bf16[128,2304]{1,0:T(8,128)(2,1)S(1)}, u32[]{:S(2)}, u32[]{:S(2)}) collective-permute-start(bf16[128,2304]{1,0:T(8,128)(2,1)S(1)} %get-tuple-element.142), channel_id=1, source_target_pairs={{0,16},{8,24},{16,0},{24,8},{1,17},{9,25},{17,1},{25,9},{2,18},{10... | collective-permute-start | bytes 1769480 | tf_op jit(solution)/shard_map/ppermute | solution.py:902
  53.4 1.4 %collective-permute-start.11 = (bf16[128,2304]{1,0:T(8,128)(2,1)S(1)}, bf16[128,2304]{1,0:T(8,128)(2,1)S(1)}, u32[]{:S(2)}, u32[]{:S(2)}) collective-permute-start(bf16[128,2304]{1,0:T(8,128)(2,1)S(1)} %get-tuple-element.143), channel_id=1, source_target_pairs={{0,24},{8,16},{16,8},{24,0},{1,25},{9,17},{17,9},{25,1},{2,26},{10... | collective-permute-start | bytes 1769480 | tf_op jit(solution)/shard_map/ppermute | solution.py:902
  54.8 0.5 collective-permute-start.9
  55.4 1.7 %collective-permute-start.12 = (bf16[128,512]{1,0:T(8,128)(2,1)S(1)}, bf16[128,512]{1,0:T(8,128)(2,1)S(1)}, u32[]{:S(2)}, u32[]{:S(2)}) collective-permute-start(bf16[128,512]{1,0:T(8,128)(2,1)S(1)} %get-tuple-element.145), channel_id=1, source_target_pairs={{0,2},{1,3},{2,0},{3,1},{4,6},{5,7},{6,4},{7,5},{8,10},{9,11},{10,... | collective-permute-start | bytes 393224 | tf_op jit(solution)/shard_map/ppermute | solution.py:902
  57.1 1.3 collective-permute-start.13
  58.4 24.0 %backward.1 = (f32[144,1024]{1,0:T(8,128)S(1)}, bf16[144,512]{1,0:T(8,128)(2,1)S(1)}, bf16[144,512]{1,0:T(8,128)(2,1)S(1)}, bf16[144,512]{1,0:T(8,128)(2,1)S(1)}...) custom-call(bf16[1024,4096]{1,0:T(8,128)(2,1)} %refs_0_.3, ...), custom_call_target="tpu_custom_call" | custom-call | flops 26400000000 | tf_op jit(solution)/shard_map/backward/pallas_call | solution.py:49
  82.4 0.1 collective-permute-start.20
  82.5 1.4 %collective-permute-start.14 = (bf16[128,512]{1,0:T(8,128)(2,1)S(1)}, bf16[128,512]{1,0:T(8,128)(2,1)S(1)}, u32[]{:S(2)}, u32[]{:S(2)}) collective-permute-start(bf16[128,512]{1,0:T(8,128)(2,1)S(1)} %get-tuple-element.150), channel_id=1, source_target_pairs={{0,6},{1,7},{2,4},{3,5},{4,2},{5,3},{6,0},{7,1},{8,14},{9,15},{10,... | collective-permute-start | bytes 393224 | tf_op jit(solution)/shard_map/ppermute | solution.py:902
  83.9 0.3 collective-permute-done.20.refs_1_
  84.2 0.1 small_row0.1
  84.3 1.6 %collective-permute-start.21 = (bf16[2,192,256]{2,1,0:T(8,128)(2,1)S(1)}, bf16[2,192,256]{2,1,0:T(8,128)(2,1)S(1)}, u32[]{:S(2)}, u32[]{:S(2)}) collective-permute-start(bf16[2,192,256]{2,1,0:T(8,128)(2,1)S(1)} %get-tuple-element.163), channel_id=1, source_target_pairs={{0,8},{8,0},{16,24},{24,16},{1,9},{9,1},{17,25},{25,17},{2,10},{10... | collective-permute-start | bytes 589832 | tf_op jit(solution)/shard_map/ppermute | solution.py:902
  85.8 0.8 out_columns.1
  86.7 0.0 copy-start
  86.7 0.1 collective-permute-start.29
  86.7 1.8 %collective-permute-start.15 = (bf16[144,512]{1,0:T(8,128)(2,1)S(1)}, bf16[144,512]{1,0:T(8,128)(2,1)S(1)}, u32[]{:S(2)}, u32[]{:S(2)}) collective-permute-start(bf16[144,512]{1,0:T(8,128)(2,1)S(1)} %get-tuple-element.153), channel_id=1, source_target_pairs={{0,2},{1,3},{2,0},{3,1},{4,6},{5,7},{6,4},{7,5},{8,10},{9,11},{10,... | collective-permute-start | bytes 442376 | tf_op jit(solution)/shard_map/ppermute | solution.py:902
  88.6 1.0 collective-permute-start.16
  89.6 1.7 %collective-permute-done.21.refs_1_ = bf16[2,192,256]{2,1,0:T(8,128)(2,1)S(1)} collective-permute-done((bf16[2,192,256]{2,1,0:T(8,128)(2,1)S(1)}, bf16[2,192,256]{2,1,0:T(8,128)(2,1)S(1)}, u32[]{:S(2)}, u32[]{:S(2)}) %collective-permute-start.21) | collective-permute-done | bytes 196640 | tf_op jit(solution)/shard_map/ppermute | solution.py:902
  91.3 2.2 %collective-permute-start.17 = (bf16[144,512]{1,0:T(8,128)(2,1)S(1)}, bf16[144,512]{1,0:T(8,128)(2,1)S(1)}, u32[]{:S(2)}, u32[]{:S(2)}) collective-permute-start(bf16[144,512]{1,0:T(8,128)(2,1)S(1)} %get-tuple-element.155), channel_id=1, source_target_pairs={{0,6},{1,7},{2,4},{3,5},{4,2},{5,3},{6,0},{7,1},{8,14},{9,15},{10,... | collective-permute-start | bytes 442376 | tf_op jit(solution)/shard_map/ppermute | solution.py:902
  93.6 1.6 %collective-permute-start.22 = (bf16[1,192,256]{2,1,0:T(8,128)(2,1)S(1)}, bf16[1,192,256]{2,1,0:T(8,128)(2,1)S(1)}, u32[]{:S(2)}, u32[]{:S(2)}) collective-permute-start(bf16[1,192,256]{2,1,0:T(8,128)(2,1)S(1)} %get-tuple-element.165), channel_id=1, source_target_pairs={{0,16},{8,24},{16,0},{24,8},{1,17},{9,25},{17,1},{25,9},{2,18},{10... | collective-permute-start | bytes 294920 | tf_op jit(solution)/shard_map/ppermute | solution.py:902
  95.1 1.3 gate_columns.1
  96.4 1.8 %collective-permute-done.22.refs_1_ = bf16[1,192,256]{2,1,0:T(8,128)(2,1)S(1)} collective-permute-done((bf16[1,192,256]{2,1,0:T(8,128)(2,1)S(1)}, bf16[1,192,256]{2,1,0:T(8,128)(2,1)S(1)}, u32[]{:S(2)}, u32[]{:S(2)}) %collective-permute-start.22) | collective-permute-done | bytes 98336 | tf_op jit(solution)/shard_map/ppermute | solution.py:902
  98.3 0.1 collective-permute-start.23
  98.4 4.2 %collective-permute-done.16.refs_3_ = bf16[144,512]{1,0:T(8,128)(2,1)S(1)} collective-permute-done((bf16[144,512]{1,0:T(8,128)(2,1)S(1)}, bf16[144,512]{1,0:T(8,128)(2,1)S(1)}, u32[]{:S(2)}, u32[]{:S(2)}) %collective-permute-start.16) | collective-permute-done | bytes 147488 | tf_op jit(solution)/shard_map/ppermute | solution.py:902
  102.5 1.3 conv_columns.1
  103.8 0.1 collective-permute-start.18
  103.9 0.2 collective-permute-done.23.refs_1_
  104.1 2.9 %collective-permute-start.24 = (bf16[48,1024]{1,0:T(8,128)(2,1)S(1)}, bf16[48,1024]{1,0:T(8,128)(2,1)S(1)}, u32[]{:S(2)}, u32[]{:S(2)}) collective-permute-start(bf16[48,1024]{1,0:T(8,128)(2,1)S(1)} %small_chip0.1.refs_0_), channel_id=1, source_target_pairs={{0,4},{1,5},{2,6},{3,7},{4,0},{5,1},{6,2},{7,3},{8,12},{9,13},{10,... | collective-permute-start | bytes 294920 | tf_op jit(solution)/shard_map/ppermute | solution.py:902
  107.0 0.1 out_chip0.1
  107.1 0.2 collective-permute-start.30
  107.3 3.2 %collective-permute-done.24.refs_1_ = bf16[48,1024]{1,0:T(8,128)(2,1)S(1)} collective-permute-done((bf16[48,1024]{1,0:T(8,128)(2,1)S(1)}, bf16[48,1024]{1,0:T(8,128)(2,1)S(1)}, u32[]{:S(2)}, u32[]{:S(2)}) %collective-permute-start.24) | collective-permute-done | bytes 98336 | tf_op jit(solution)/shard_map/ppermute | solution.py:902
  110.5 0.0 copy-start.2
  110.6 0.4 in_merge.1
  111.0 1.5 %collective-permute-start.25 = (bf16[176,1024]{1,0:T(8,128)(2,1)S(1)}, bf16[176,1024]{1,0:T(8,128)(2,1)S(1)}, u32[]{:S(2)}, u32[]{:S(2)}) collective-permute-start(bf16[176,1024]{1,0:T(8,128)(2,1)S(1)} %get-tuple-element.167), channel_id=1, source_target_pairs={{0,8},{8,0},{16,24},{24,16},{1,9},{9,1},{17,25},{25,17},{2,10},{10... | collective-permute-start | bytes 1081352 | tf_op jit(solution)/shard_map/ppermute | solution.py:902
  112.5 1.5 %collective-permute-start.26 = (bf16[176,1024]{1,0:T(8,128)(2,1)S(1)}, bf16[176,1024]{1,0:T(8,128)(2,1)S(1)}, u32[]{:S(2)}, u32[]{:S(2)}) collective-permute-start(bf16[176,1024]{1,0:T(8,128)(2,1)S(1)} %get-tuple-element.168), channel_id=1, source_target_pairs={{0,16},{8,24},{16,0},{24,8},{1,17},{9,25},{17,1},{25,9},{2,18},{10... | collective-permute-start | bytes 1081352 | tf_op jit(solution)/shard_map/ppermute | solution.py:902
  114.0 0.5 collective-permute-start.27
  114.6 1.3 collective-permute-start.8
  115.9 0.2 collective-permute-done.30.refs_1_
  116.1 0.1 out_chip1.1
  116.1 0.0 copy-start.1
  116.1 3.6 %collective-permute-start.31 = (bf16[1,64,1024]{2,1,0:T(8,128)(2,1)S(1)}, bf16[1,64,1024]{2,1,0:T(8,128)(2,1)S(1)}, u32[]{:S(2)}, u32[]{:S(2)}) collective-permute-start(bf16[1,64,1024]{2,1,0:T(8,128)(2,1)S(1)} %get-tuple-element.188), channel_id=1, source_target_pairs={{0,4},{1,5},{2,6},{3,7},{4,0},{5,1},{6,2},{7,3},{8,12},{9,13},{10,... | collective-permute-start | bytes 393224 | tf_op jit(solution)/shard_map/ppermute | solution.py:902
  119.7 2.6 %collective-permute-done.25.refs_2_ = bf16[176,1024]{1,0:T(8,128)(2,1)S(1)} collective-permute-done((bf16[176,1024]{1,0:T(8,128)(2,1)S(1)}, bf16[176,1024]{1,0:T(8,128)(2,1)S(1)}, u32[]{:S(2)}, u32[]{:S(2)}) %collective-permute-start.25) | collective-permute-done | bytes 360480 | tf_op jit(solution)/shard_map/ppermute | solution.py:902
  122.4 7.7 %collective-permute-done.26.refs_3_ = bf16[176,1024]{1,0:T(8,128)(2,1)S(1)} collective-permute-done((bf16[176,1024]{1,0:T(8,128)(2,1)S(1)}, bf16[176,1024]{1,0:T(8,128)(2,1)S(1)}, u32[]{:S(2)}, u32[]{:S(2)}) %collective-permute-start.26) | collective-permute-done | bytes 360480 | tf_op jit(solution)/shard_map/ppermute | solution.py:902
  130.1 1.0 in_last.1
  131.1 1.8 %finish.1 = (bf16[128,1024]{1,0:T(8,128)(2,1)}, bf16[128,1024]{1,0:T(8,128)(2,1)}) custom-call(f32[144,1024]{1,0:T(8,128)S(1)} %get-tuple-element.127.refs_0_, f32[16,1024]{1,0:T(8,128)S(1)} %collective-permute-done.8.refs_1_, bf16[144,1024]{1,0:T(8,128)(2,1)S(1)} %get-tuple-element.103.refs_5_.refs_2_, ...), custom_call_target="tpu_custom_call" | custom-call | flops 2200000000 | tf_op jit(solution)/shard_map/finish/pallas_call | solution.py:49
  132.9 0.7 out_last.1
  133.6 1.2 unpack.1
  (31 shorter events, 0.2 us)
Async XLA Ops:
  1.4 3.2 %collective-permute-start = (bf16[3,1024]{1,0:T(4,128)(2,1)S(1)}, bf16[3,1024]{1,0:T(4,128)(2,1)S(1)}, u32[]{:S(2)}, u32[]{:S(2)}) collective-permute-start(bf16[3,1024]{1,0:T(4,128)(2,1)S(1)} %slice_bitcast_fusion), channel_id=1, source_target_pairs={{0,1},{1,2},{2,3},{3,4},{4,5},{5,6},{6,7},{8,9},{9,10},{10,11},{11... | collective-permute-start | bytes 18440 | tf_op jit(solution)/shard_map/ppermute | solution.py:973
  4.5 26.1 %collective-permute-start.1 = (bf16[128,1024]{1,0:T(8,128)(2,1)}, bf16[128,1024]{1,0:T(8,128)(2,1)S(1)}, u32[]{:S(2)}, u32[]{:S(2)}) collective-permute-start(bf16[128,1024]{1,0:T(8,128)(2,1)} %bitcast.18), channel_id=1, source_target_pairs={{0,2},{1,3},{2,0},{3,1},{4,6},{5,7},{6,4},{7,5},{8,10},{9,11},{10,... | collective-permute-start | bytes 786440 | tf_op jit(solution)/shard_map/ppermute | solution.py:902
  9.4 21.6 %collective-permute-start.2 = (bf16[128,1024]{1,0:T(8,128)(2,1)}, bf16[128,1024]{1,0:T(8,128)(2,1)S(1)}, u32[]{:S(2)}, u32[]{:S(2)}) collective-permute-start(bf16[128,1024]{1,0:T(8,128)(2,1)} %bitcast.19), channel_id=1, source_target_pairs={{0,4},{1,5},{2,6},{3,7},{4,0},{5,1},{6,2},{7,3},{8,12},{9,13},{10,... | collective-permute-start | bytes 786440 | tf_op jit(solution)/shard_map/ppermute | solution.py:902
  11.9 19.0 %collective-permute-start.3 = (bf16[128,1024]{1,0:T(8,128)(2,1)}, bf16[128,1024]{1,0:T(8,128)(2,1)S(1)}, u32[]{:S(2)}, u32[]{:S(2)}) collective-permute-start(bf16[128,1024]{1,0:T(8,128)(2,1)} %bitcast.20), channel_id=1, source_target_pairs={{0,6},{1,7},{2,4},{3,5},{4,2},{5,3},{6,0},{7,1},{8,14},{9,15},{10,... | collective-permute-start | bytes 786440 | tf_op jit(solution)/shard_map/ppermute | solution.py:902
  30.9 1.4 %collective-permute-start.4 = (bf16[48,2048]{1,0:T(8,128)(2,1)S(1)}, bf16[48,2048]{1,0:T(8,128)(2,1)S(1)}, u32[]{:S(2)}, u32[]{:S(2)}) collective-permute-start(bf16[48,2048]{1,0:T(8,128)(2,1)S(1)} %get-tuple-element.109.refs_0_), channel_id=1, source_target_pairs={{0,1},{1,0},{2,3},{3,2},{4,5},{5,4},{6,7},{7,6},{8,9},{9,8},{10,11... | collective-permute-start | bytes 589832 | tf_op jit(solution)/shard_map/ppermute | solution.py:902
  32.5 7.5 %collective-permute-start.5 = (bf16[48,1024]{1,0:T(8,128)(2,1)S(1)}, bf16[48,1024]{1,0:T(8,128)(2,1)S(1)}, u32[]{:S(2)}, u32[]{:S(2)}) collective-permute-start(bf16[48,1024]{1,0:T(8,128)(2,1)S(1)} %pair.1.refs_0_), channel_id=1, source_target_pairs={{0,2},{1,3},{2,0},{3,1},{4,6},{5,7},{6,4},{7,5},{8,10},{9,11},{10,... | collective-permute-start | bytes 294920 | tf_op jit(solution)/shard_map/ppermute | solution.py:902
  40.1 4.9 %collective-permute-start.6 = (bf16[16,1024]{1,0:T(8,128)(2,1)S(1)}, bf16[16,1024]{1,0:T(8,128)(2,1)S(1)}, u32[]{:S(2)}, u32[]{:S(2)}) collective-permute-start(bf16[16,1024]{1,0:T(8,128)(2,1)S(1)} %get-tuple-element.111), channel_id=1, source_target_pairs={{0,4},{1,5},{2,6},{3,7},{4,0},{5,1},{6,2},{7,3},{8,12},{9,13},{10,... | collective-permute-start | bytes 98312 | tf_op jit(solution)/shard_map/ppermute | solution.py:902
  45.0 1.4 %collective-permute-start.7 = (f32[32,1024]{1,0:T(8,128)S(1)}, f32[32,1024]{1,0:T(8,128)S(1)}, u32[]{:S(2)}, u32[]{:S(2)}) collective-permute-start(f32[32,1024]{1,0:T(8,128)S(1)} %enter_half.1.refs_2_), channel_id=1, source_target_pairs={{0,1},{1,0},{2,3},{3,2},{4,5},{5,4},{6,7},{7,6},{8,9},{9,8},{10,11... | collective-permute-start | bytes 393224 | tf_op jit(solution)/shard_map/ppermute | solution.py:902
  51.8 30.6 %collective-permute-start.10 = (bf16[128,2304]{1,0:T(8,128)(2,1)S(1)}, bf16[128,2304]{1,0:T(8,128)(2,1)S(1)}, u32[]{:S(2)}, u32[]{:S(2)}) collective-permute-start(bf16[128,2304]{1,0:T(8,128)(2,1)S(1)} %get-tuple-element.142), channel_id=1, source_target_pairs={{0,16},{8,24},{16,0},{24,8},{1,17},{9,25},{17,1},{25,9},{2,18},{10... | collective-permute-start | bytes 1769480 | tf_op jit(solution)/shard_map/ppermute | solution.py:902
  53.4 29.0 %collective-permute-start.11 = (bf16[128,2304]{1,0:T(8,128)(2,1)S(1)}, bf16[128,2304]{1,0:T(8,128)(2,1)S(1)}, u32[]{:S(2)}, u32[]{:S(2)}) collective-permute-start(bf16[128,2304]{1,0:T(8,128)(2,1)S(1)} %get-tuple-element.143), channel_id=1, source_target_pairs={{0,24},{8,16},{16,8},{24,0},{1,25},{9,17},{17,9},{25,1},{2,26},{10... | collective-permute-start | bytes 1769480 | tf_op jit(solution)/shard_map/ppermute | solution.py:902
  54.8 27.6 %collective-permute-start.9 = (bf16[128,2304]{1,0:T(8,128)(2,1)S(1)}, bf16[128,2304]{1,0:T(8,128)(2,1)S(1)}, u32[]{:S(2)}, u32[]{:S(2)}) collective-permute-start(bf16[128,2304]{1,0:T(8,128)(2,1)S(1)} %get-tuple-element.141), channel_id=1, source_target_pairs={{0,8},{8,0},{16,24},{24,16},{1,9},{9,1},{17,25},{25,17},{2,10},{10... | collective-permute-start | bytes 1769480 | tf_op jit(solution)/shard_map/ppermute | solution.py:902
  55.4 27.0 %collective-permute-start.12 = (bf16[128,512]{1,0:T(8,128)(2,1)S(1)}, bf16[128,512]{1,0:T(8,128)(2,1)S(1)}, u32[]{:S(2)}, u32[]{:S(2)}) collective-permute-start(bf16[128,512]{1,0:T(8,128)(2,1)S(1)} %get-tuple-element.145), channel_id=1, source_target_pairs={{0,2},{1,3},{2,0},{3,1},{4,6},{5,7},{6,4},{7,5},{8,10},{9,11},{10,... | collective-permute-start | bytes 393224 | tf_op jit(solution)/shard_map/ppermute | solution.py:902
  57.1 25.3 %collective-permute-start.13 = (bf16[128,512]{1,0:T(8,128)(2,1)S(1)}, bf16[128,512]{1,0:T(8,128)(2,1)S(1)}, u32[]{:S(2)}, u32[]{:S(2)}) collective-permute-start(bf16[128,512]{1,0:T(8,128)(2,1)S(1)} %get-tuple-element.146), channel_id=1, source_target_pairs={{0,4},{1,5},{2,6},{3,7},{4,0},{5,1},{6,2},{7,3},{8,12},{9,13},{10,... | collective-permute-start | bytes 393224 | tf_op jit(solution)/shard_map/ppermute | solution.py:902
  82.4 1.8 %collective-permute-start.20 = (bf16[4,192,256]{2,1,0:T(8,128)(2,1)S(1)}, bf16[4,192,256]{2,1,0:T(8,128)(2,1)S(1)}, u32[]{:S(2)}, u32[]{:S(2)}) collective-permute-start(bf16[4,192,256]{2,1,0:T(8,128)(2,1)S(1)} %get-tuple-element.161), channel_id=1, source_target_pairs={{0,1},{1,0},{2,3},{3,2},{4,5},{5,4},{6,7},{7,6},{8,9},{9,8},{10,11... | collective-permute-start | bytes 1179656 | tf_op jit(solution)/shard_map/ppermute | solution.py:902
  82.5 11.0 %collective-permute-start.14 = (bf16[128,512]{1,0:T(8,128)(2,1)S(1)}, bf16[128,512]{1,0:T(8,128)(2,1)S(1)}, u32[]{:S(2)}, u32[]{:S(2)}) collective-permute-start(bf16[128,512]{1,0:T(8,128)(2,1)S(1)} %get-tuple-element.150), channel_id=1, source_target_pairs={{0,6},{1,7},{2,4},{3,5},{4,2},{5,3},{6,0},{7,1},{8,14},{9,15},{10,... | collective-permute-start | bytes 393224 | tf_op jit(solution)/shard_map/ppermute | solution.py:902
  84.3 7.0 %collective-permute-start.21 = (bf16[2,192,256]{2,1,0:T(8,128)(2,1)S(1)}, bf16[2,192,256]{2,1,0:T(8,128)(2,1)S(1)}, u32[]{:S(2)}, u32[]{:S(2)}) collective-permute-start(bf16[2,192,256]{2,1,0:T(8,128)(2,1)S(1)} %get-tuple-element.163), channel_id=1, source_target_pairs={{0,8},{8,0},{16,24},{24,16},{1,9},{9,1},{17,25},{25,17},{2,10},{10... | collective-permute-start | bytes 589832 | tf_op jit(solution)/shard_map/ppermute | solution.py:902
  86.7 8.5 %copy-start = (bf16[1,128,1024]{2,1,0:T(8,128)(2,1)S(1)}, bf16[1,128,1024]{2,1,0:T(8,128)(2,1)}, u32[]{:S(2)}) copy-start(bf16[1,128,1024]{2,1,0:T(8,128)(2,1)} %refs_1_.2) | copy-start | bytes 786436
  86.7 20.3 %collective-permute-start.29 = (bf16[4,64,1024]{2,1,0:T(8,128)(2,1)S(1)}, bf16[4,64,1024]{2,1,0:T(8,128)(2,1)S(1)}, u32[]{:S(2)}, u32[]{:S(2)}) collective-permute-start(bf16[4,64,1024]{2,1,0:T(8,128)(2,1)S(1)} %get-tuple-element.184), channel_id=1, source_target_pairs={{0,1},{1,0},{2,3},{3,2},{4,5},{5,4},{6,7},{7,6},{8,9},{9,8},{10,11... | collective-permute-start | bytes 1572872 | tf_op jit(solution)/shard_map/ppermute | solution.py:902
  86.7 11.5 %collective-permute-start.15 = (bf16[144,512]{1,0:T(8,128)(2,1)S(1)}, bf16[144,512]{1,0:T(8,128)(2,1)S(1)}, u32[]{:S(2)}, u32[]{:S(2)}) collective-permute-start(bf16[144,512]{1,0:T(8,128)(2,1)S(1)} %get-tuple-element.153), channel_id=1, source_target_pairs={{0,2},{1,3},{2,0},{3,1},{4,6},{5,7},{6,4},{7,5},{8,10},{9,11},{10,... | collective-permute-start | bytes 442376 | tf_op jit(solution)/shard_map/ppermute | solution.py:902
  88.6 14.0 %collective-permute-start.16 = (bf16[144,512]{1,0:T(8,128)(2,1)S(1)}, bf16[144,512]{1,0:T(8,128)(2,1)S(1)}, u32[]{:S(2)}, u32[]{:S(2)}) collective-permute-start(bf16[144,512]{1,0:T(8,128)(2,1)S(1)} %get-tuple-element.154), channel_id=1, source_target_pairs={{0,4},{1,5},{2,6},{3,7},{4,0},{5,1},{6,2},{7,3},{8,12},{9,13},{10,... | collective-permute-start | bytes 442376 | tf_op jit(solution)/shard_map/ppermute | solution.py:902
  91.3 11.2 %collective-permute-start.17 = (bf16[144,512]{1,0:T(8,128)(2,1)S(1)}, bf16[144,512]{1,0:T(8,128)(2,1)S(1)}, u32[]{:S(2)}, u32[]{:S(2)}) collective-permute-start(bf16[144,512]{1,0:T(8,128)(2,1)S(1)} %get-tuple-element.155), channel_id=1, source_target_pairs={{0,6},{1,7},{2,4},{3,5},{4,2},{5,3},{6,0},{7,1},{8,14},{9,15},{10,... | collective-permute-start | bytes 442376 | tf_op jit(solution)/shard_map/ppermute | solution.py:902
  93.6 4.7 %collective-permute-start.22 = (bf16[1,192,256]{2,1,0:T(8,128)(2,1)S(1)}, bf16[1,192,256]{2,1,0:T(8,128)(2,1)S(1)}, u32[]{:S(2)}, u32[]{:S(2)}) collective-permute-start(bf16[1,192,256]{2,1,0:T(8,128)(2,1)S(1)} %get-tuple-element.165), channel_id=1, source_target_pairs={{0,16},{8,24},{16,0},{24,8},{1,17},{9,25},{17,1},{25,9},{2,18},{10... | collective-permute-start | bytes 294920 | tf_op jit(solution)/shard_map/ppermute | solution.py:902
  98.2 12.3 %collective-permute-start.19 = (bf16[2,128,1024]{2,1,0:T(8,128)(2,1)S(1)}, bf16[2,128,1024]{2,1,0:T(8,128)(2,1)S(1)}, u32[]{:S(2)}, u32[]{:S(2)}) collective-permute-start(bf16[2,128,1024]{2,1,0:T(8,128)(2,1)S(1)} %get-tuple-element.159), channel_id=1, source_target_pairs={{0,1},{1,0},{2,3},{3,2},{4,5},{5,4},{6,7},{7,6},{8,9},{9,8},{10,11... | collective-permute-start | bytes 1572872 | tf_op jit(solution)/shard_map/ppermute | solution.py:902
  98.3 5.8 %collective-permute-start.23 = (bf16[48,1024]{1,0:T(8,128)(2,1)S(1)}, bf16[48,1024]{1,0:T(8,128)(2,1)S(1)}, u32[]{:S(2)}, u32[]{:S(2)}) collective-permute-start(bf16[48,1024]{1,0:T(8,128)(2,1)S(1)} %small_last.1.refs_0_), channel_id=1, source_target_pairs={{0,2},{1,3},{2,0},{3,1},{4,6},{5,7},{6,4},{7,5},{8,10},{9,11},{10,... | collective-permute-start | bytes 294920 | tf_op jit(solution)/shard_map/ppermute | solution.py:902
  103.8 6.8 %collective-permute-start.18 = (bf16[2,128,1024]{2,1,0:T(8,128)(2,1)S(1)}, bf16[2,128,1024]{2,1,0:T(8,128)(2,1)S(1)}, u32[]{:S(2)}, u32[]{:S(2)}) collective-permute-start(bf16[2,128,1024]{2,1,0:T(8,128)(2,1)S(1)} %get-tuple-element.157), channel_id=1, source_target_pairs={{0,1},{1,0},{2,3},{3,2},{4,5},{5,4},{6,7},{7,6},{8,9},{9,8},{10,11... | collective-permute-start | bytes 1572872 | tf_op jit(solution)/shard_map/ppermute | solution.py:902
  104.1 6.4 %collective-permute-start.24 = (bf16[48,1024]{1,0:T(8,128)(2,1)S(1)}, bf16[48,1024]{1,0:T(8,128)(2,1)S(1)}, u32[]{:S(2)}, u32[]{:S(2)}) collective-permute-start(bf16[48,1024]{1,0:T(8,128)(2,1)S(1)} %small_chip0.1.refs_0_), channel_id=1, source_target_pairs={{0,4},{1,5},{2,6},{3,7},{4,0},{5,1},{6,2},{7,3},{8,12},{9,13},{10,... | collective-permute-start | bytes 294920 | tf_op jit(solution)/shard_map/ppermute | solution.py:902
  107.1 9.0 %collective-permute-start.30 = (bf16[2,64,1024]{2,1,0:T(8,128)(2,1)S(1)}, bf16[2,64,1024]{2,1,0:T(8,128)(2,1)S(1)}, u32[]{:S(2)}, u32[]{:S(2)}) collective-permute-start(bf16[2,64,1024]{2,1,0:T(8,128)(2,1)S(1)} %get-tuple-element.186), channel_id=1, source_target_pairs={{0,2},{1,3},{2,0},{3,1},{4,6},{5,7},{6,4},{7,5},{8,10},{9,11},{10,... | collective-permute-start | bytes 786440 | tf_op jit(solution)/shard_map/ppermute | solution.py:902
  110.5 4.0 %copy-start.2 = (f32[2048,16]{0,1:T(8,128)S(1)}, f32[2048,16]{0,1:T(8,128)}, u32[]{:S(2)}) copy-start(f32[2048,16]{0,1:T(8,128)} %param.22) | copy-start | bytes 393220
  111.0 11.4 %collective-permute-start.25 = (bf16[176,1024]{1,0:T(8,128)(2,1)S(1)}, bf16[176,1024]{1,0:T(8,128)(2,1)S(1)}, u32[]{:S(2)}, u32[]{:S(2)}) collective-permute-start(bf16[176,1024]{1,0:T(8,128)(2,1)S(1)} %get-tuple-element.167), channel_id=1, source_target_pairs={{0,8},{8,0},{16,24},{24,16},{1,9},{9,1},{17,25},{25,17},{2,10},{10... | collective-permute-start | bytes 1081352 | tf_op jit(solution)/shard_map/ppermute | solution.py:902
  112.5 17.6 %collective-permute-start.26 = (bf16[176,1024]{1,0:T(8,128)(2,1)S(1)}, bf16[176,1024]{1,0:T(8,128)(2,1)S(1)}, u32[]{:S(2)}, u32[]{:S(2)}) collective-permute-start(bf16[176,1024]{1,0:T(8,128)(2,1)S(1)} %get-tuple-element.168), channel_id=1, source_target_pairs={{0,16},{8,24},{16,0},{24,8},{1,17},{9,25},{17,1},{25,9},{2,18},{10... | collective-permute-start | bytes 1081352 | tf_op jit(solution)/shard_map/ppermute | solution.py:902
  114.0 16.1 %collective-permute-start.27 = (bf16[176,1024]{1,0:T(8,128)(2,1)S(1)}, bf16[176,1024]{1,0:T(8,128)(2,1)S(1)}, u32[]{:S(2)}, u32[]{:S(2)}) collective-permute-start(bf16[176,1024]{1,0:T(8,128)(2,1)S(1)} %get-tuple-element.169), channel_id=1, source_target_pairs={{0,24},{8,16},{16,8},{24,0},{1,25},{9,17},{17,9},{25,1},{2,26},{10... | collective-permute-start | bytes 1081352 | tf_op jit(solution)/shard_map/ppermute | solution.py:902
  114.6 16.5 %collective-permute-start.8 = (f32[16,1024]{1,0:T(8,128)S(1)}, f32[16,1024]{1,0:T(8,128)S(1)}, u32[]{:S(2)}, u32[]{:S(2)}) collective-permute-start(f32[16,1024]{1,0:T(8,128)S(1)} %slice.7), channel_id=1, source_target_pairs={{1,0},{2,1},{3,2},{4,3},{5,4},{6,5},{7,6},{9,8},{10,9},{11,10},{12... | collective-permute-start | bytes 196616 | tf_op jit(solution)/shard_map/ppermute | solution.py:1043
  116.1 15.0 %copy-start.1 = (bf16[2048,1024]{1,0:T(8,128)(2,1)S(1)}, bf16[2048,1024]{1,0:T(8,128)(2,1)}, u32[]{:S(2)}) copy-start(bf16[2048,1024]{1,0:T(8,128)(2,1)} %refs_6_.3) | copy-start | bytes 12582916
  116.1 16.8 %collective-permute-start.31 = (bf16[1,64,1024]{2,1,0:T(8,128)(2,1)S(1)}, bf16[1,64,1024]{2,1,0:T(8,128)(2,1)S(1)}, u32[]{:S(2)}, u32[]{:S(2)}) collective-permute-start(bf16[1,64,1024]{2,1,0:T(8,128)(2,1)S(1)} %get-tuple-element.188), channel_id=1, source_target_pairs={{0,4},{1,5},{2,6},{3,7},{4,0},{5,1},{6,2},{7,3},{8,12},{9,13},{10,... | collective-permute-start | bytes 393224 | tf_op jit(solution)/shard_map/ppermute | solution.py:902
  131.1 2.5 %collective-permute-start.28 = (bf16[4,48,1024]{2,1,0:T(8,128)(2,1)S(1)}, bf16[4,48,1024]{2,1,0:T(8,128)(2,1)S(1)}, u32[]{:S(2)}, u32[]{:S(2)}) collective-permute-start(bf16[4,48,1024]{2,1,0:T(8,128)(2,1)S(1)} %get-tuple-element.171.refs_1_), channel_id=1, source_target_pairs={{0,1},{1,0},{2,3},{3,2},{4,5},{5,4},{6,7},{7,6},{8,9},{9,8},{10,11... | collective-permute-start | bytes 1179656 | tf_op jit(solution)/shard_map/ppermute | solution.py:902

commit v6 on v5

--- a/solution.py
+++ b/solution.py
@@ -321,7 +321,7 @@
 
 def forward_kernel(
     states, taps, chips, rows_size,
-    here, masks, cot_ref, vec_ref, rates_ref, entry_ref, table, dt_ref, inner_ref, gate_ref, ggated_ref, dx_ref, ex_ref,
+    here, masks, cot_ref, tok_ref, far_ref, vec_ref, rates_ref, entry_ref, table, dt_ref, inner_ref, gate_ref, ggated_ref, dx_ref, ex_ref,
     gated_ref, ggate_ref, *rest,
 ):
     lines, blocks, (dtm_s, u_s, y_s, held) = rest[:rows_size], rest[rows_size:-4], rest[-4:]
@@ -367,14 +367,19 @@
 
     lax.fori_loop(0, tiles, scan, 0)
     for n in range(chips):
-        blocks[n][...] = held[here[2] ^ n]
+        part = held.shape[2]
+        blocks[n][:, :part] = held[here[2] ^ n]
+        if n == 1:
+            model = cot_ref.shape[1]
+            blocks[n][:, part : part + model] = tok_ref[pl.ds(0, length), :]
+            blocks[n][:, part + model :] = turned(far_ref[...], False)
     thin = cot_ref.shape[1] // rows_size
     for n in range(rows_size):
         lines[n][:, :width] = gated_ref[...]
         lines[n][:, width:] = cot_ref[:, tile_at((here[1] ^ n) * thin, thin)]
 
 
-def forward(masks, cot, vec, rates, entry, table, dt, inner, gate, ggated, dx, ex, taps, chips, rows_size):
+def forward(masks, cot, tok, far, vec, rates, entry, table, dt, inner, gate, ggated, dx, ex, taps, chips, rows_size):
     length, width = inner.shape
     states = rates.shape[0]
     shape = jax.ShapeDtypeStruct
@@ -383,8 +388,8 @@
         "forward",
         [shape((length, width), bf16)] * 2
         + [shape((length, width + cot.shape[1] // rows_size), bf16)] * rows_size
-        + [shape((length, width // max(chips, 1)), bf16)] * chips,
-        (masks, cot, vec, rates, entry, table, dt, inner, gate, ggated, dx, ex),
+        + [shape((length, width // max(chips, 1) + 2 * cot.shape[1] * (n == 1)), bf16) for n in range(chips)],
+        (masks, cot, tok, far, vec, rates, entry, table, dt, inner, gate, ggated, dx, ex),
         8,
         [pltpu.VMEM((length, LANES), f32)] * 3 + [pltpu.VMEM((max(chips, 1), length, width // max(chips, 1)), bf16)],
         8,
@@ -775,12 +780,20 @@
                 theirs_ref[n] = x[((1 - c) * count + n) * rows : ((1 - c) * count + n + 1) * rows].astype(bf16)
 
 
-def gate_kernel(size, here, gain_ref, *rest):
-    toks, gots, (normed_ref, mine_ref, theirs_ref) = rest[:size], rest[size:-3], rest[-3:]
-    length = toks[0].shape[0]
+def gate_kernel(here, gain_ref, tok_ref, far_ref, *rest):
+    gots, (normed_ref, mine_ref, theirs_ref) = rest[:-3], rest[-3:]
+    length, part = gots[0].shape
+    model = gain_ref.shape[1]
+    near = gots[1]
+    toks = (
+        tok_ref[pl.ds(0, length), :],
+        near[:, part : part + model],
+        turned(far_ref[...], False),
+        near[:, part + model :],
+    )
     for k, x in enumerate(toks):
-        normed_ref[pl.ds(k * length, length), :] = normalise(turned(x[...], False), gain_ref[...])
-    got = jnp.concatenate([x[...] for x in gots], axis=0)
+        normed_ref[pl.ds(k * length, length), :] = normalise(x, gain_ref[...])
+    got = jnp.concatenate([x[:, :part] for x in gots], axis=0)
     split_cores(here, tn(got, normed_ref[...]), mine_ref, theirs_ref)
 
 
@@ -970,15 +983,17 @@
     wx = xproj_weight.T
     decay_rates = -jnp.exp(a_log).T
 
-    left = lax.ppermute(tokens[0, length - rim :], "seq", [(i, i + 1) for i in range(seq_size - 1)])
+    edge = tokens[0, length - rim :]
+    left = lax.ppermute(edge, "seq", [(i, i + 1) for i in range(seq_size - 1)])
     tok, cot, ext, inner, gate, ggated, gs, dt, proj, table, mine, dx, ex, db, fx, vec, rates, gain, masks = front(
         doc_starts, tokens, cotangent, norm_gain, conv_weight.T, conv_bias, dt_bias, skip_scale, a_log.T, dt_weight, wx,
         in_weight, out_weight, left,
     )
+    beyond = cot
     if tiled:
-        after, _ = lax.optimization_barrier((tokens[0], left))
-        tok_parts = outer.gather(after)
-        mine, tok_parts = lax.optimization_barrier((mine, tok_parts))
+        after, _ = lax.optimization_barrier((tokens[0], edge))
+        beyond = outer.swap(after, 2)
+        mine, beyond = lax.optimization_barrier((mine, beyond))
     other = core.swap(mine, 1)
     entering = [shape(rates.shape, f32)] * 2
     if tiled:
@@ -1015,7 +1030,7 @@
         entry, arrive = plain_call(
             functools.partial(enter_kernel, states, outer.size), "enter", entering, (other, rates, got), 2
         )
-    gated, ggate, *late = forward(masks, cot, vec, rates, entry, table, dt, inner, gate, ggated, dx, ex, taps, chips, dp_size)
+    gated, ggate, *late = forward(masks, cot, tok, beyond, vec, rates, entry, table, dt, inner, gate, ggated, dx, ex, taps, chips, dp_size)
     lines_got = rows_group.trade(late[:dp_size])
     gate_got = outer.trade(late[dp_size:]) if tiled else None
 
@@ -1067,10 +1082,10 @@
         out_got = core.swap(theirs, 1)
         small, small_got = halve(rows_group, 1, 1, small, small_got, "small_row1")
         normed, gate, theirs = call(
-            functools.partial(gate_kernel, chips),
+            gate_kernel,
             "gate_columns",
             [((chips * length, model), bf16), (blocks, f32), (blocks, bf16)],
-            (gain, *tok_parts, *gate_got),
+            (gain, tok, beyond, *gate_got),
         )
         gate_got = core.swap(theirs, 1)
         (small,) = call(small_last_kernel, "small_last", [part], (small, small_got))

time: 135 us -> 131 us (0.970)
  starting transfers between devices: 45 us -> 36.1 us
  waiting for transfers between devices: 31.1 us -> 35.9 us
    ppermute x30 -> x28, starting transfers between devices: 41.4 us -> 32.5 us  [swap(): lax.ppermute(x, self.axis, [(i, i ^ k * self.stride) for i in range(n)])]
    ppermute x30 -> x28, waiting for transfers between devices: 30.3 us -> 35.9 us  [swap(): lax.ppermute(x, self.axis, [(i, i ^ k * self.stride) for i in range(n)])]
  transfers between devices with their start and end apart: 32 -> 30, of which waited for: 15 -> 13; matrix products, arithmetic and copies ran while one was open for 0% -> 0% of each run, Pallas kernels for 37% -> 38%
where the time goes in v6:
time: 131 us
  Pallas kernels  57.1 us (44%)
  starting transfers between devices  36.1 us (28%)
  waiting for transfers between devices  35.9 us (27%)
    pallas_call x22, Pallas kernels, plain_call(): pl.pallas_call(lambda *refs: kernel(Here(), *refs), in_specs=list(specs)...  57.1 us
    ppermute x28, waiting for transfers between devices, swap(): lax.ppermute(x, self.axis, [(i, i ^ k * self.stride) for i in range(n)])  35.9 us
    ppermute x28, starting transfers between devices, swap(): lax.ppermute(x, self.axis, [(i, i ^ k * self.stride) for i in range(n)])  32.5 us
  transfers between devices with their start and end apart: 30, of which 13 were waited for; matrix products, arithmetic and copies ran while one was open for 0% of the time, Pallas kernels for 38%

profile of v6, /device:TPU:0, one launch (start us, length us, event | category | flops | bytes accessed | tf_op | source)
XLA Modules:
  0.0 130.8 jit_solution(11717508019613543737)
XLA Ops:
  0.6 0.7 slice_bitcast_fusion
  1.4 2.3 %collective-permute-start = (bf16[3,1024]{1,0:T(4,128)(2,1)S(1)}, bf16[3,1024]{1,0:T(4,128)(2,1)S(1)}, u32[]{:S(2)}, u32[]{:S(2)}) collective-permute-start(bf16[3,1024]{1,0:T(4,128)(2,1)S(1)} %slice_bitcast_fusion), channel_id=1, source_target_pairs={{0,1},{1,2},{2,3},{3,4},{4,5},{5,6},{6,7},{8,9},{9,10},{10,11},{11... | collective-permute-start | bytes 18440 | tf_op jit(solution)/shard_map/ppermute | solution.py:987
  3.7 3.7 %collective-permute-start.1 = (bf16[128,1024]{1,0:T(8,128)(2,1)}, bf16[128,1024]{1,0:T(8,128)(2,1)S(1)}, u32[]{:S(2)}, u32[]{:S(2)}) collective-permute-start(bf16[128,1024]{1,0:T(8,128)(2,1)} %bitcast.19), channel_id=1, source_target_pairs={{0,4},{1,5},{2,6},{3,7},{4,0},{5,1},{6,2},{7,3},{8,12},{9,13},{10,... | collective-permute-start | bytes 786440 | tf_op jit(solution)/shard_map/ppermute | solution.py:915
  7.4 0.0 collective-permute-done.refs_13_
  7.4 18.6 %front.1 = (bf16[144,1024]{1,0:T(8,128)(2,1)S(1)}, bf16[128,1024]{1,0:T(8,128)(2,1)S(1)}, bf16[160,2048]{1,0:T(8,128)(2,1)S(1)}, bf16[128,2048]{1,0:T(8,128)(2,1...) custom-call(s32[1,4]{1,0:T(1,128)} %refs_0_.2, ...), custom_call_target="tpu_custom_call" | custom-call | flops 22000001024 | tf_op jit(solution)/shard_map/front/pallas_call | solution.py:49
  26.0 0.0 collective-permute-done.1.refs_3_.refs_2_
  26.0 1.5 %collective-permute-start.2 = (bf16[48,2048]{1,0:T(8,128)(2,1)S(1)}, bf16[48,2048]{1,0:T(8,128)(2,1)S(1)}, u32[]{:S(2)}, u32[]{:S(2)}) collective-permute-start(bf16[48,2048]{1,0:T(8,128)(2,1)S(1)} %get-tuple-element.106.refs_0_), channel_id=1, source_target_pairs={{0,1},{1,0},{2,3},{3,2},{4,5},{5,4},{6,7},{7,6},{8,9},{9,8},{10,11... | collective-permute-start | bytes 589832 | tf_op jit(solution)/shard_map/ppermute | solution.py:915
  27.5 1.1 collective-permute-done.2.refs_1_.refs_0_
  28.6 0.1 pair.1.refs_0_
  28.7 1.0 collective-permute-start.3
  29.7 4.1 %collective-permute-done.3.refs_1_ = bf16[48,1024]{1,0:T(8,128)(2,1)S(1)} collective-permute-done((bf16[48,1024]{1,0:T(8,128)(2,1)S(1)}, bf16[48,1024]{1,0:T(8,128)(2,1)S(1)}, u32[]{:S(2)}, u32[]{:S(2)}) %collective-permute-start.3) | collective-permute-done | bytes 98336 | tf_op jit(solution)/shard_map/ppermute | solution.py:915
  33.8 0.1 quad.1
  33.9 1.8 %collective-permute-start.4 = (bf16[16,1024]{1,0:T(8,128)(2,1)S(1)}, bf16[16,1024]{1,0:T(8,128)(2,1)S(1)}, u32[]{:S(2)}, u32[]{:S(2)}) collective-permute-start(bf16[16,1024]{1,0:T(8,128)(2,1)S(1)} %get-tuple-element.108), channel_id=1, source_target_pairs={{0,4},{1,5},{2,6},{3,7},{4,0},{5,1},{6,2},{7,3},{8,12},{9,13},{10,... | collective-permute-start | bytes 98312 | tf_op jit(solution)/shard_map/ppermute | solution.py:915
  35.7 3.5 %collective-permute-done.4.refs_1_ = bf16[16,1024]{1,0:T(8,128)(2,1)S(1)} collective-permute-done((bf16[16,1024]{1,0:T(8,128)(2,1)S(1)}, bf16[16,1024]{1,0:T(8,128)(2,1)S(1)}, u32[]{:S(2)}, u32[]{:S(2)}) %collective-permute-start.4) | collective-permute-done | bytes 32800 | tf_op jit(solution)/shard_map/ppermute | solution.py:915
  39.1 0.1 collective-permute-start.5
  39.2 1.3 %collective-permute-done.5.refs_3_ = f32[32,1024]{1,0:T(8,128)S(1)} collective-permute-done((f32[32,1024]{1,0:T(8,128)S(1)}, f32[32,1024]{1,0:T(8,128)S(1)}, u32[]{:S(2)}, u32[]{:S(2)}) %collective-permute-start.5) | collective-permute-done | bytes 131104 | tf_op jit(solution)/shard_map/ppermute | solution.py:915
  40.6 0.1 enter.1
  40.6 5.5 %forward.1 = (bf16[128,2048]{1,0:T(8,128)(2,1)S(1)}, bf16[128,2048]{1,0:T(8,128)(2,1)S(1)}, bf16[128,2304]{1,0:T(8,128)(2,1)S(1)}, bf16[128,2304]{1,0:T(8,128)(2...) custom-call(f32[4,128,128]{2,1,0:T(8,128)S(1)} %get-tuple-element.98, ...), custom_call_target="tpu_custom_call" | custom-call | flops 8800000000 | tf_op jit(solution)/shard_map/forward/pallas_call | solution.py:49
  46.1 0.5 collective-permute-start.10
  46.6 1.5 %collective-permute-start.7 = (bf16[128,2304]{1,0:T(8,128)(2,1)S(1)}, bf16[128,2304]{1,0:T(8,128)(2,1)S(1)}, u32[]{:S(2)}, u32[]{:S(2)}) collective-permute-start(bf16[128,2304]{1,0:T(8,128)(2,1)S(1)} %get-tuple-element.135), channel_id=1, source_target_pairs={{0,8},{8,0},{16,24},{24,16},{1,9},{9,1},{17,25},{25,17},{2,10},{10... | collective-permute-start | bytes 1769480 | tf_op jit(solution)/shard_map/ppermute | solution.py:915
  48.1 1.5 %collective-permute-start.8 = (bf16[128,2304]{1,0:T(8,128)(2,1)S(1)}, bf16[128,2304]{1,0:T(8,128)(2,1)S(1)}, u32[]{:S(2)}, u32[]{:S(2)}) collective-permute-start(bf16[128,2304]{1,0:T(8,128)(2,1)S(1)} %get-tuple-element.136), channel_id=1, source_target_pairs={{0,16},{8,24},{16,0},{24,8},{1,17},{9,25},{17,1},{25,9},{2,18},{10... | collective-permute-start | bytes 1769480 | tf_op jit(solution)/shard_map/ppermute | solution.py:915
  49.7 0.5 collective-permute-start.9
  50.1 2.7 %collective-permute-start.11 = (bf16[128,512]{1,0:T(8,128)(2,1)S(1)}, bf16[128,512]{1,0:T(8,128)(2,1)S(1)}, u32[]{:S(2)}, u32[]{:S(2)}) collective-permute-start(bf16[128,512]{1,0:T(8,128)(2,1)S(1)} %get-tuple-element.140), channel_id=1, source_target_pairs={{0,4},{1,5},{2,6},{3,7},{4,0},{5,1},{6,2},{7,3},{8,12},{9,13},{10,... | collective-permute-start | bytes 393224 | tf_op jit(solution)/shard_map/ppermute | solution.py:915
  52.9 24.0 %backward.1 = (f32[144,1024]{1,0:T(8,128)S(1)}, bf16[144,512]{1,0:T(8,128)(2,1)S(1)}, bf16[144,512]{1,0:T(8,128)(2,1)S(1)}, bf16[144,512]{1,0:T(8,128)(2,1)S(1)}...) custom-call(bf16[1024,4096]{1,0:T(8,128)(2,1)} %refs_0_.3, ...), custom_call_target="tpu_custom_call" | custom-call | flops 26400000000 | tf_op jit(solution)/shard_map/backward/pallas_call | solution.py:49
  76.9 0.0 collective-permute-done.8.refs_2_
  76.9 0.1 collective-permute-start.18
  77.0 1.3 collective-permute-start.12
  78.3 0.4 collective-permute-done.18.refs_1_
  78.7 0.1 small_row0.1
  78.8 1.6 %collective-permute-start.19 = (bf16[2,192,256]{2,1,0:T(8,128)(2,1)S(1)}, bf16[2,192,256]{2,1,0:T(8,128)(2,1)S(1)}, u32[]{:S(2)}, u32[]{:S(2)}) collective-permute-start(bf16[2,192,256]{2,1,0:T(8,128)(2,1)S(1)} %get-tuple-element.157), channel_id=1, source_target_pairs={{0,8},{8,0},{16,24},{24,16},{1,9},{9,1},{17,25},{25,17},{2,10},{10... | collective-permute-start | bytes 589832 | tf_op jit(solution)/shard_map/ppermute | solution.py:915
  80.3 0.8 out_columns.1
  81.1 0.1 collective-permute-start.27
  81.2 0.3 collective-permute-start.13
  81.5 2.5 %collective-permute-start.14 = (bf16[144,512]{1,0:T(8,128)(2,1)S(1)}, bf16[144,512]{1,0:T(8,128)(2,1)S(1)}, u32[]{:S(2)}, u32[]{:S(2)}) collective-permute-start(bf16[144,512]{1,0:T(8,128)(2,1)S(1)} %get-tuple-element.148), channel_id=1, source_target_pairs={{0,4},{1,5},{2,6},{3,7},{4,0},{5,1},{6,2},{7,3},{8,12},{9,13},{10,... | collective-permute-start | bytes 442376 | tf_op jit(solution)/shard_map/ppermute | solution.py:915
  84.0 1.7 %collective-permute-done.19.refs_1_ = bf16[2,192,256]{2,1,0:T(8,128)(2,1)S(1)} collective-permute-done((bf16[2,192,256]{2,1,0:T(8,128)(2,1)S(1)}, bf16[2,192,256]{2,1,0:T(8,128)(2,1)S(1)}, u32[]{:S(2)}, u32[]{:S(2)}) %collective-permute-start.19) | collective-permute-done | bytes 196640 | tf_op jit(solution)/shard_map/ppermute | solution.py:915
  85.8 2.2 %collective-permute-start.15 = (bf16[144,512]{1,0:T(8,128)(2,1)S(1)}, bf16[144,512]{1,0:T(8,128)(2,1)S(1)}, u32[]{:S(2)}, u32[]{:S(2)}) collective-permute-start(bf16[144,512]{1,0:T(8,128)(2,1)S(1)} %get-tuple-element.149), channel_id=1, source_target_pairs={{0,6},{1,7},{2,4},{3,5},{4,2},{5,3},{6,0},{7,1},{8,14},{9,15},{10,... | collective-permute-start | bytes 442376 | tf_op jit(solution)/shard_map/ppermute | solution.py:915
  88.0 1.6 %collective-permute-start.20 = (bf16[1,192,256]{2,1,0:T(8,128)(2,1)S(1)}, bf16[1,192,256]{2,1,0:T(8,128)(2,1)S(1)}, u32[]{:S(2)}, u32[]{:S(2)}) collective-permute-start(bf16[1,192,256]{2,1,0:T(8,128)(2,1)S(1)} %get-tuple-element.159), channel_id=1, source_target_pairs={{0,16},{8,24},{16,0},{24,8},{1,17},{9,25},{17,1},{25,9},{2,18},{10... | collective-permute-start | bytes 294920 | tf_op jit(solution)/shard_map/ppermute | solution.py:915
  89.6 1.1 gate_columns.1
  90.8 2.0 %collective-permute-done.20.refs_1_ = bf16[1,192,256]{2,1,0:T(8,128)(2,1)S(1)} collective-permute-done((bf16[1,192,256]{2,1,0:T(8,128)(2,1)S(1)}, bf16[1,192,256]{2,1,0:T(8,128)(2,1)S(1)}, u32[]{:S(2)}, u32[]{:S(2)}) %collective-permute-start.20) | collective-permute-done | bytes 98336 | tf_op jit(solution)/shard_map/ppermute | solution.py:915
  92.8 0.1 collective-permute-start.21
  92.8 2.6 %collective-permute-done.14.refs_3_ = bf16[144,512]{1,0:T(8,128)(2,1)S(1)} collective-permute-done((bf16[144,512]{1,0:T(8,128)(2,1)S(1)}, bf16[144,512]{1,0:T(8,128)(2,1)S(1)}, u32[]{:S(2)}, u32[]{:S(2)}) %collective-permute-start.14) | collective-permute-done | bytes 147488 | tf_op jit(solution)/shard_map/ppermute | solution.py:915
  95.4 1.1 conv_columns.1
  96.5 0.1 collective-permute-start.16
  96.6 1.4 %collective-permute-done.21.refs_1_ = bf16[48,1024]{1,0:T(8,128)(2,1)S(1)} collective-permute-done((bf16[48,1024]{1,0:T(8,128)(2,1)S(1)}, bf16[48,1024]{1,0:T(8,128)(2,1)S(1)}, u32[]{:S(2)}, u32[]{:S(2)}) %collective-permute-start.21) | collective-permute-done | bytes 98336 | tf_op jit(solution)/shard_map/ppermute | solution.py:915
  98.1 2.9 %collective-permute-start.22 = (bf16[48,1024]{1,0:T(8,128)(2,1)S(1)}, bf16[48,1024]{1,0:T(8,128)(2,1)S(1)}, u32[]{:S(2)}, u32[]{:S(2)}) collective-permute-start(bf16[48,1024]{1,0:T(8,128)(2,1)S(1)} %small_chip0.1.refs_0_), channel_id=1, source_target_pairs={{0,4},{1,5},{2,6},{3,7},{4,0},{5,1},{6,2},{7,3},{8,12},{9,13},{10,... | collective-permute-start | bytes 294920 | tf_op jit(solution)/shard_map/ppermute | solution.py:915
  101.0 0.1 out_chip0.1
  101.1 0.1 collective-permute-start.28
  101.1 5.5 %collective-permute-done.22.refs_1_ = bf16[48,1024]{1,0:T(8,128)(2,1)S(1)} collective-permute-done((bf16[48,1024]{1,0:T(8,128)(2,1)S(1)}, bf16[48,1024]{1,0:T(8,128)(2,1)S(1)}, u32[]{:S(2)}, u32[]{:S(2)}) %collective-permute-start.22) | collective-permute-done | bytes 98336 | tf_op jit(solution)/shard_map/ppermute | solution.py:915
  106.6 0.0 copy-start.1
  106.7 0.6 in_merge.1
  107.3 1.3 collective-permute-start.23
  108.6 0.8 collective-permute-start.24
  109.4 1.4 %collective-permute-start.25 = (bf16[176,1024]{1,0:T(8,128)(2,1)S(1)}, bf16[176,1024]{1,0:T(8,128)(2,1)S(1)}, u32[]{:S(2)}, u32[]{:S(2)}) collective-permute-start(bf16[176,1024]{1,0:T(8,128)(2,1)S(1)} %get-tuple-element.163), channel_id=1, source_target_pairs={{0,24},{8,16},{16,8},{24,0},{1,25},{9,17},{17,9},{25,1},{2,26},{10... | collective-permute-start | bytes 1081352 | tf_op jit(solution)/shard_map/ppermute | solution.py:915
  110.9 1.3 collective-permute-start.6
  112.2 0.1 out_chip1.1
  112.3 0.0 copy-start
  112.3 1.5 %collective-permute-start.29 = (bf16[1,64,1024]{2,1,0:T(8,128)(2,1)S(1)}, bf16[1,64,1024]{2,1,0:T(8,128)(2,1)S(1)}, u32[]{:S(2)}, u32[]{:S(2)}) collective-permute-start(bf16[1,64,1024]{2,1,0:T(8,128)(2,1)S(1)} %get-tuple-element.182), channel_id=1, source_target_pairs={{0,4},{1,5},{2,6},{3,7},{4,0},{5,1},{6,2},{7,3},{8,12},{9,13},{10,... | collective-permute-start | bytes 393224 | tf_op jit(solution)/shard_map/ppermute | solution.py:915
  113.8 4.9 %collective-permute-done.23.refs_2_ = bf16[176,1024]{1,0:T(8,128)(2,1)S(1)} collective-permute-done((bf16[176,1024]{1,0:T(8,128)(2,1)S(1)}, bf16[176,1024]{1,0:T(8,128)(2,1)S(1)}, u32[]{:S(2)}, u32[]{:S(2)}) %collective-permute-start.23) | collective-permute-done | bytes 360480 | tf_op jit(solution)/shard_map/ppermute | solution.py:915
  118.7 0.4 collective-permute-done.24.refs_3_
  119.1 6.9 %collective-permute-done.25.refs_4_ = bf16[176,1024]{1,0:T(8,128)(2,1)S(1)} collective-permute-done((bf16[176,1024]{1,0:T(8,128)(2,1)S(1)}, bf16[176,1024]{1,0:T(8,128)(2,1)S(1)}, u32[]{:S(2)}, u32[]{:S(2)}) %collective-permute-start.25) | collective-permute-done | bytes 360480 | tf_op jit(solution)/shard_map/ppermute | solution.py:915
  126.0 1.0 in_last.1
  127.0 1.8 %finish.1 = (bf16[128,1024]{1,0:T(8,128)(2,1)}, bf16[128,1024]{1,0:T(8,128)(2,1)}) custom-call(f32[144,1024]{1,0:T(8,128)S(1)} %get-tuple-element.125.refs_0_, f32[16,1024]{1,0:T(8,128)S(1)} %collective-permute-done.6.refs_1_, bf16[144,1024]{1,0:T(8,128)(2,1)S(1)} %get-tuple-element.100.refs_2_.refs_5_.refs_1_, ...), custom_call_target="tpu_custom_call" | custom-call | flops 2200000000 | tf_op jit(solution)/shard_map/finish/pallas_call | solution.py:49
  128.8 0.7 out_last.1
  129.6 1.2 unpack.1
  (25 shorter events, 0.2 us)
Async XLA Ops:
  1.4 6.0 %collective-permute-start = (bf16[3,1024]{1,0:T(4,128)(2,1)S(1)}, bf16[3,1024]{1,0:T(4,128)(2,1)S(1)}, u32[]{:S(2)}, u32[]{:S(2)}) collective-permute-start(bf16[3,1024]{1,0:T(4,128)(2,1)S(1)} %slice_bitcast_fusion), channel_id=1, source_target_pairs={{0,1},{1,2},{2,3},{3,4},{4,5},{5,6},{6,7},{8,9},{9,10},{10,11},{11... | collective-permute-start | bytes 18440 | tf_op jit(solution)/shard_map/ppermute | solution.py:987
  3.7 22.3 %collective-permute-start.1 = (bf16[128,1024]{1,0:T(8,128)(2,1)}, bf16[128,1024]{1,0:T(8,128)(2,1)S(1)}, u32[]{:S(2)}, u32[]{:S(2)}) collective-permute-start(bf16[128,1024]{1,0:T(8,128)(2,1)} %bitcast.19), channel_id=1, source_target_pairs={{0,4},{1,5},{2,6},{3,7},{4,0},{5,1},{6,2},{7,3},{8,12},{9,13},{10,... | collective-permute-start | bytes 786440 | tf_op jit(solution)/shard_map/ppermute | solution.py:915
  26.0 2.5 %collective-permute-start.2 = (bf16[48,2048]{1,0:T(8,128)(2,1)S(1)}, bf16[48,2048]{1,0:T(8,128)(2,1)S(1)}, u32[]{:S(2)}, u32[]{:S(2)}) collective-permute-start(bf16[48,2048]{1,0:T(8,128)(2,1)S(1)} %get-tuple-element.106.refs_0_), channel_id=1, source_target_pairs={{0,1},{1,0},{2,3},{3,2},{4,5},{5,4},{6,7},{7,6},{8,9},{9,8},{10,11... | collective-permute-start | bytes 589832 | tf_op jit(solution)/shard_map/ppermute | solution.py:915
  28.7 5.1 %collective-permute-start.3 = (bf16[48,1024]{1,0:T(8,128)(2,1)S(1)}, bf16[48,1024]{1,0:T(8,128)(2,1)S(1)}, u32[]{:S(2)}, u32[]{:S(2)}) collective-permute-start(bf16[48,1024]{1,0:T(8,128)(2,1)S(1)} %pair.1.refs_0_), channel_id=1, source_target_pairs={{0,2},{1,3},{2,0},{3,1},{4,6},{5,7},{6,4},{7,5},{8,10},{9,11},{10,... | collective-permute-start | bytes 294920 | tf_op jit(solution)/shard_map/ppermute | solution.py:915
  33.9 5.2 %collective-permute-start.4 = (bf16[16,1024]{1,0:T(8,128)(2,1)S(1)}, bf16[16,1024]{1,0:T(8,128)(2,1)S(1)}, u32[]{:S(2)}, u32[]{:S(2)}) collective-permute-start(bf16[16,1024]{1,0:T(8,128)(2,1)S(1)} %get-tuple-element.108), channel_id=1, source_target_pairs={{0,4},{1,5},{2,6},{3,7},{4,0},{5,1},{6,2},{7,3},{8,12},{9,13},{10,... | collective-permute-start | bytes 98312 | tf_op jit(solution)/shard_map/ppermute | solution.py:915
  39.1 1.4 %collective-permute-start.5 = (f32[32,1024]{1,0:T(8,128)S(1)}, f32[32,1024]{1,0:T(8,128)S(1)}, u32[]{:S(2)}, u32[]{:S(2)}) collective-permute-start(f32[32,1024]{1,0:T(8,128)S(1)} %enter_half.1.refs_2_), channel_id=1, source_target_pairs={{0,1},{1,0},{2,3},{3,2},{4,5},{5,4},{6,7},{7,6},{8,9},{9,8},{10,11... | collective-permute-start | bytes 393224 | tf_op jit(solution)/shard_map/ppermute | solution.py:915
  46.1 30.8 %collective-permute-start.10 = (bf16[128,2560]{1,0:T(8,128)(2,1)S(1)}, bf16[128,2560]{1,0:T(8,128)(2,1)S(1)}, u32[]{:S(2)}, u32[]{:S(2)}) collective-permute-start(bf16[128,2560]{1,0:T(8,128)(2,1)S(1)} %get-tuple-element.139), channel_id=1, source_target_pairs={{0,2},{1,3},{2,0},{3,1},{4,6},{5,7},{6,4},{7,5},{8,10},{9,11},{10,... | collective-permute-start | bytes 1966088 | tf_op jit(solution)/shard_map/ppermute | solution.py:915
  46.6 30.2 %collective-permute-start.7 = (bf16[128,2304]{1,0:T(8,128)(2,1)S(1)}, bf16[128,2304]{1,0:T(8,128)(2,1)S(1)}, u32[]{:S(2)}, u32[]{:S(2)}) collective-permute-start(bf16[128,2304]{1,0:T(8,128)(2,1)S(1)} %get-tuple-element.135), channel_id=1, source_target_pairs={{0,8},{8,0},{16,24},{24,16},{1,9},{9,1},{17,25},{25,17},{2,10},{10... | collective-permute-start | bytes 1769480 | tf_op jit(solution)/shard_map/ppermute | solution.py:915
  48.1 28.8 %collective-permute-start.8 = (bf16[128,2304]{1,0:T(8,128)(2,1)S(1)}, bf16[128,2304]{1,0:T(8,128)(2,1)S(1)}, u32[]{:S(2)}, u32[]{:S(2)}) collective-permute-start(bf16[128,2304]{1,0:T(8,128)(2,1)S(1)} %get-tuple-element.136), channel_id=1, source_target_pairs={{0,16},{8,24},{16,0},{24,8},{1,17},{9,25},{17,1},{25,9},{2,18},{10... | collective-permute-start | bytes 1769480 | tf_op jit(solution)/shard_map/ppermute | solution.py:915
  49.7 27.2 %collective-permute-start.9 = (bf16[128,2304]{1,0:T(8,128)(2,1)S(1)}, bf16[128,2304]{1,0:T(8,128)(2,1)S(1)}, u32[]{:S(2)}, u32[]{:S(2)}) collective-permute-start(bf16[128,2304]{1,0:T(8,128)(2,1)S(1)} %get-tuple-element.137), channel_id=1, source_target_pairs={{0,24},{8,16},{16,8},{24,0},{1,25},{9,17},{17,9},{25,1},{2,26},{10... | collective-permute-start | bytes 1769480 | tf_op jit(solution)/shard_map/ppermute | solution.py:915
  50.1 26.7 %collective-permute-start.11 = (bf16[128,512]{1,0:T(8,128)(2,1)S(1)}, bf16[128,512]{1,0:T(8,128)(2,1)S(1)}, u32[]{:S(2)}, u32[]{:S(2)}) collective-permute-start(bf16[128,512]{1,0:T(8,128)(2,1)S(1)} %get-tuple-element.140), channel_id=1, source_target_pairs={{0,4},{1,5},{2,6},{3,7},{4,0},{5,1},{6,2},{7,3},{8,12},{9,13},{10,... | collective-permute-start | bytes 393224 | tf_op jit(solution)/shard_map/ppermute | solution.py:915
  76.9 1.8 %collective-permute-start.18 = (bf16[4,192,256]{2,1,0:T(8,128)(2,1)S(1)}, bf16[4,192,256]{2,1,0:T(8,128)(2,1)S(1)}, u32[]{:S(2)}, u32[]{:S(2)}) collective-permute-start(bf16[4,192,256]{2,1,0:T(8,128)(2,1)S(1)} %get-tuple-element.155), channel_id=1, source_target_pairs={{0,1},{1,0},{2,3},{3,2},{4,5},{5,4},{6,7},{7,6},{8,9},{9,8},{10,11... | collective-permute-start | bytes 1179656 | tf_op jit(solution)/shard_map/ppermute | solution.py:915
  77.0 11.1 %collective-permute-start.12 = (bf16[128,512]{1,0:T(8,128)(2,1)S(1)}, bf16[128,512]{1,0:T(8,128)(2,1)S(1)}, u32[]{:S(2)}, u32[]{:S(2)}) collective-permute-start(bf16[128,512]{1,0:T(8,128)(2,1)S(1)} %get-tuple-element.144), channel_id=1, source_target_pairs={{0,6},{1,7},{2,4},{3,5},{4,2},{5,3},{6,0},{7,1},{8,14},{9,15},{10,... | collective-permute-start | bytes 393224 | tf_op jit(solution)/shard_map/ppermute | solution.py:915
  78.8 7.0 %collective-permute-start.19 = (bf16[2,192,256]{2,1,0:T(8,128)(2,1)S(1)}, bf16[2,192,256]{2,1,0:T(8,128)(2,1)S(1)}, u32[]{:S(2)}, u32[]{:S(2)}) collective-permute-start(bf16[2,192,256]{2,1,0:T(8,128)(2,1)S(1)} %get-tuple-element.157), channel_id=1, source_target_pairs={{0,8},{8,0},{16,24},{24,16},{1,9},{9,1},{17,25},{25,17},{2,10},{10... | collective-permute-start | bytes 589832 | tf_op jit(solution)/shard_map/ppermute | solution.py:915
  81.1 19.8 %collective-permute-start.27 = (bf16[4,64,1024]{2,1,0:T(8,128)(2,1)S(1)}, bf16[4,64,1024]{2,1,0:T(8,128)(2,1)S(1)}, u32[]{:S(2)}, u32[]{:S(2)}) collective-permute-start(bf16[4,64,1024]{2,1,0:T(8,128)(2,1)S(1)} %get-tuple-element.178), channel_id=1, source_target_pairs={{0,1},{1,0},{2,3},{3,2},{4,5},{5,4},{6,7},{7,6},{8,9},{9,8},{10,11... | collective-permute-start | bytes 1572872 | tf_op jit(solution)/shard_map/ppermute | solution.py:915
  81.2 11.5 %collective-permute-start.13 = (bf16[144,512]{1,0:T(8,128)(2,1)S(1)}, bf16[144,512]{1,0:T(8,128)(2,1)S(1)}, u32[]{:S(2)}, u32[]{:S(2)}) collective-permute-start(bf16[144,512]{1,0:T(8,128)(2,1)S(1)} %get-tuple-element.147), channel_id=1, source_target_pairs={{0,2},{1,3},{2,0},{3,1},{4,6},{5,7},{6,4},{7,5},{8,10},{9,11},{10,... | collective-permute-start | bytes 442376 | tf_op jit(solution)/shard_map/ppermute | solution.py:915
  81.5 13.9 %collective-permute-start.14 = (bf16[144,512]{1,0:T(8,128)(2,1)S(1)}, bf16[144,512]{1,0:T(8,128)(2,1)S(1)}, u32[]{:S(2)}, u32[]{:S(2)}) collective-permute-start(bf16[144,512]{1,0:T(8,128)(2,1)S(1)} %get-tuple-element.148), channel_id=1, source_target_pairs={{0,4},{1,5},{2,6},{3,7},{4,0},{5,1},{6,2},{7,3},{8,12},{9,13},{10,... | collective-permute-start | bytes 442376 | tf_op jit(solution)/shard_map/ppermute | solution.py:915
  85.8 9.7 %collective-permute-start.15 = (bf16[144,512]{1,0:T(8,128)(2,1)S(1)}, bf16[144,512]{1,0:T(8,128)(2,1)S(1)}, u32[]{:S(2)}, u32[]{:S(2)}) collective-permute-start(bf16[144,512]{1,0:T(8,128)(2,1)S(1)} %get-tuple-element.149), channel_id=1, source_target_pairs={{0,6},{1,7},{2,4},{3,5},{4,2},{5,3},{6,0},{7,1},{8,14},{9,15},{10,... | collective-permute-start | bytes 442376 | tf_op jit(solution)/shard_map/ppermute | solution.py:915
  88.0 4.7 %collective-permute-start.20 = (bf16[1,192,256]{2,1,0:T(8,128)(2,1)S(1)}, bf16[1,192,256]{2,1,0:T(8,128)(2,1)S(1)}, u32[]{:S(2)}, u32[]{:S(2)}) collective-permute-start(bf16[1,192,256]{2,1,0:T(8,128)(2,1)S(1)} %get-tuple-element.159), channel_id=1, source_target_pairs={{0,16},{8,24},{16,0},{24,8},{1,17},{9,25},{17,1},{25,9},{2,18},{10... | collective-permute-start | bytes 294920 | tf_op jit(solution)/shard_map/ppermute | solution.py:915
  92.7 13.9 %collective-permute-start.17 = (bf16[2,128,1024]{2,1,0:T(8,128)(2,1)S(1)}, bf16[2,128,1024]{2,1,0:T(8,128)(2,1)S(1)}, u32[]{:S(2)}, u32[]{:S(2)}) collective-permute-start(bf16[2,128,1024]{2,1,0:T(8,128)(2,1)S(1)} %get-tuple-element.153), channel_id=1, source_target_pairs={{0,1},{1,0},{2,3},{3,2},{4,5},{5,4},{6,7},{7,6},{8,9},{9,8},{10,11... | collective-permute-start | bytes 1572872 | tf_op jit(solution)/shard_map/ppermute | solution.py:915
  92.8 5.3 %collective-permute-start.21 = (bf16[48,1024]{1,0:T(8,128)(2,1)S(1)}, bf16[48,1024]{1,0:T(8,128)(2,1)S(1)}, u32[]{:S(2)}, u32[]{:S(2)}) collective-permute-start(bf16[48,1024]{1,0:T(8,128)(2,1)S(1)} %small_last.1.refs_0_), channel_id=1, source_target_pairs={{0,2},{1,3},{2,0},{3,1},{4,6},{5,7},{6,4},{7,5},{8,10},{9,11},{10,... | collective-permute-start | bytes 294920 | tf_op jit(solution)/shard_map/ppermute | solution.py:915
  96.5 10.2 %collective-permute-start.16 = (bf16[2,128,1024]{2,1,0:T(8,128)(2,1)S(1)}, bf16[2,128,1024]{2,1,0:T(8,128)(2,1)S(1)}, u32[]{:S(2)}, u32[]{:S(2)}) collective-permute-start(bf16[2,128,1024]{2,1,0:T(8,128)(2,1)S(1)} %get-tuple-element.151), channel_id=1, source_target_pairs={{0,1},{1,0},{2,3},{3,2},{4,5},{5,4},{6,7},{7,6},{8,9},{9,8},{10,11... | collective-permute-start | bytes 1572872 | tf_op jit(solution)/shard_map/ppermute | solution.py:915
  98.1 8.6 %collective-permute-start.22 = (bf16[48,1024]{1,0:T(8,128)(2,1)S(1)}, bf16[48,1024]{1,0:T(8,128)(2,1)S(1)}, u32[]{:S(2)}, u32[]{:S(2)}) collective-permute-start(bf16[48,1024]{1,0:T(8,128)(2,1)S(1)} %small_chip0.1.refs_0_), channel_id=1, source_target_pairs={{0,4},{1,5},{2,6},{3,7},{4,0},{5,1},{6,2},{7,3},{8,12},{9,13},{10,... | collective-permute-start | bytes 294920 | tf_op jit(solution)/shard_map/ppermute | solution.py:915
  101.1 11.1 %collective-permute-start.28 = (bf16[2,64,1024]{2,1,0:T(8,128)(2,1)S(1)}, bf16[2,64,1024]{2,1,0:T(8,128)(2,1)S(1)}, u32[]{:S(2)}, u32[]{:S(2)}) collective-permute-start(bf16[2,64,1024]{2,1,0:T(8,128)(2,1)S(1)} %get-tuple-element.180), channel_id=1, source_target_pairs={{0,2},{1,3},{2,0},{3,1},{4,6},{5,7},{6,4},{7,5},{8,10},{9,11},{10,... | collective-permute-start | bytes 786440 | tf_op jit(solution)/shard_map/ppermute | solution.py:915
  106.6 4.2 %copy-start.1 = (f32[2048,16]{0,1:T(8,128)S(1)}, f32[2048,16]{0,1:T(8,128)}, u32[]{:S(2)}) copy-start(f32[2048,16]{0,1:T(8,128)} %param.22) | copy-start | bytes 393220
  107.3 11.4 %collective-permute-start.23 = (bf16[176,1024]{1,0:T(8,128)(2,1)S(1)}, bf16[176,1024]{1,0:T(8,128)(2,1)S(1)}, u32[]{:S(2)}, u32[]{:S(2)}) collective-permute-start(bf16[176,1024]{1,0:T(8,128)(2,1)S(1)} %get-tuple-element.161), channel_id=1, source_target_pairs={{0,8},{8,0},{16,24},{24,16},{1,9},{9,1},{17,25},{25,17},{2,10},{10... | collective-permute-start | bytes 1081352 | tf_op jit(solution)/shard_map/ppermute | solution.py:915
  108.6 10.5 %collective-permute-start.24 = (bf16[176,1024]{1,0:T(8,128)(2,1)S(1)}, bf16[176,1024]{1,0:T(8,128)(2,1)S(1)}, u32[]{:S(2)}, u32[]{:S(2)}) collective-permute-start(bf16[176,1024]{1,0:T(8,128)(2,1)S(1)} %get-tuple-element.162), channel_id=1, source_target_pairs={{0,16},{8,24},{16,0},{24,8},{1,17},{9,25},{17,1},{25,9},{2,18},{10... | collective-permute-start | bytes 1081352 | tf_op jit(solution)/shard_map/ppermute | solution.py:915
  109.4 16.6 %collective-permute-start.25 = (bf16[176,1024]{1,0:T(8,128)(2,1)S(1)}, bf16[176,1024]{1,0:T(8,128)(2,1)S(1)}, u32[]{:S(2)}, u32[]{:S(2)}) collective-permute-start(bf16[176,1024]{1,0:T(8,128)(2,1)S(1)} %get-tuple-element.163), channel_id=1, source_target_pairs={{0,24},{8,16},{16,8},{24,0},{1,25},{9,17},{17,9},{25,1},{2,26},{10... | collective-permute-start | bytes 1081352 | tf_op jit(solution)/shard_map/ppermute | solution.py:915
  110.9 16.2 %collective-permute-start.6 = (f32[16,1024]{1,0:T(8,128)S(1)}, f32[16,1024]{1,0:T(8,128)S(1)}, u32[]{:S(2)}, u32[]{:S(2)}) collective-permute-start(f32[16,1024]{1,0:T(8,128)S(1)} %slice.7), channel_id=1, source_target_pairs={{1,0},{2,1},{3,2},{4,3},{5,4},{6,5},{7,6},{9,8},{10,9},{11,10},{12... | collective-permute-start | bytes 196616 | tf_op jit(solution)/shard_map/ppermute | solution.py:1058
  112.3 14.8 %copy-start = (bf16[2048,1024]{1,0:T(8,128)(2,1)S(1)}, bf16[2048,1024]{1,0:T(8,128)(2,1)}, u32[]{:S(2)}) copy-start(bf16[2048,1024]{1,0:T(8,128)(2,1)} %refs_6_.3) | copy-start | bytes 12582916
  112.3 16.6 %collective-permute-start.29 = (bf16[1,64,1024]{2,1,0:T(8,128)(2,1)S(1)}, bf16[1,64,1024]{2,1,0:T(8,128)(2,1)S(1)}, u32[]{:S(2)}, u32[]{:S(2)}) collective-permute-start(bf16[1,64,1024]{2,1,0:T(8,128)(2,1)S(1)} %get-tuple-element.182), channel_id=1, source_target_pairs={{0,4},{1,5},{2,6},{3,7},{4,0},{5,1},{6,2},{7,3},{8,12},{9,13},{10,... | collective-permute-start | bytes 393224 | tf_op jit(solution)/shard_map/ppermute | solution.py:915
  127.0 2.5 %collective-permute-start.26 = (bf16[4,48,1024]{2,1,0:T(8,128)(2,1)S(1)}, bf16[4,48,1024]{2,1,0:T(8,128)(2,1)S(1)}, u32[]{:S(2)}, u32[]{:S(2)}) collective-permute-start(bf16[4,48,1024]{2,1,0:T(8,128)(2,1)S(1)} %get-tuple-element.165.refs_1_), channel_id=1, source_target_pairs={{0,1},{1,0},{2,3},{3,2},{4,5},{5,4},{6,7},{7,6},{8,9},{9,8},{10,11... | collective-permute-start | bytes 1179656 | tf_op jit(solution)/shard_map/ppermute | solution.py:915

commit v7 on v6

--- a/solution.py
+++ b/solution.py
@@ -324,6 +324,7 @@
     here, masks, cot_ref, tok_ref, far_ref, vec_ref, rates_ref, entry_ref, table, dt_ref, inner_ref, gate_ref, ggated_ref, dx_ref, ex_ref,
     gated_ref, ggate_ref, *rest,
 ):
+    hs_refs, rest = rest[:8], rest[8:]
     lines, blocks, (dtm_s, u_s, y_s, held) = rest[:rows_size], rest[rows_size:-4], rest[-4:]
     length, width = inner_ref.shape
     tiles, steps = width // LANES, length // SUBS
@@ -341,6 +342,8 @@
 
         rates = [wide(rates_ref, n) for n in range(states)]
         start = tuple(dx_ref[n, :, at] * wide(entry_ref, n) + ex_ref[n, :, at] for n in range(states))
+        for n in range(states):
+            hs_refs[n * 8 // states][tile, 0, n % (states // 8)] = start[n]
 
         def lap(t, h):
             rows = step_rows(t)
@@ -348,6 +351,7 @@
             new, y = [], [zero, zero]
             for n in range(states):
                 now = jnp.exp2(d * rates[n]) * h[n] + u * table[rows, n * LANES : (n + 1) * LANES]
+                hs_refs[n * 8 // states][tile, t + 1, n % (states // 8)] = now
                 y[n % 2] = y[n % 2] + now * table[rows, (states + n) * LANES : (states + n + 1) * LANES]
                 new.append(now)
             y_s[rows, :] = y[0] + y[1]
@@ -387,23 +391,24 @@
         functools.partial(forward_kernel, states, taps, chips, rows_size),
         "forward",
         [shape((length, width), bf16)] * 2
+        + [shape((width // LANES, length // SUBS + 1, states // 8, SUBS, LANES), f32)] * 8
         + [shape((length, width + cot.shape[1] // rows_size), bf16)] * rows_size
         + [shape((length, width // max(chips, 1) + 2 * cot.shape[1] * (n == 1)), bf16) for n in range(chips)],
         (masks, cot, tok, far, vec, rates, entry, table, dt, inner, gate, ggated, dx, ex),
         8,
         [pltpu.VMEM((length, LANES), f32)] * 3 + [pltpu.VMEM((max(chips, 1), length, width // max(chips, 1)), bf16)],
-        8,
+        4,
     )
 
 
 def backward_kernel(
     states, rank, taps, chips,
-    here, win_hbm, dtw_hbm, wx_hbm, masks, proj_ref, tok_ref, gain_ref, vec_ref, rates_ref, entry_ref, arrive_ref,
-    table, dt_ref, inner_ref, gs_ref, dx_ref, ex_ref, db_ref, fx_ref, ggate_ref, ext_ref,
+    here, win_hbm, dtw_hbm, wx_hbm, masks, proj_ref, tok_ref, gain_ref, vec_ref, rates_ref, arrive_ref,
+    table, dt_ref, inner_ref, gs_ref, hs0, hs1, hs2, hs3, hs4, hs5, hs6, hs7, db_ref, fx_ref, ggate_ref, ext_ref,
     ngrad, *rest,
 ):
     blocks, rest = rest[: max(chips, 1)], rest[max(chips, 1) :]
-    (acc, hs, decays, dtm_s, u_s, s1_s, s2_s, isg, raw_s, sent_s, low_acc, pg, small, held, win_ref, dtw_ref, wx_ref, sems) = rest[-18:]
+    (acc, dtm_s, u_s, s1_s, s2_s, isg, raw_s, sent_s, low_acc, pg, small, held, win_ref, dtw_ref, wx_ref, sems) = rest[-16:]
     length, width = inner_ref.shape
     model = tok_ref.shape[1]
     steps, tiles = length // SUBS, width // LANES
@@ -415,11 +420,25 @@
     row_dtb, row_skip, row_cb, row_gain = (row_taps + taps + k for k in range(4))
     zero = jnp.zeros((SUBS, LANES), f32)
     half = states // 2
+    hs_refs = (hs0, hs1, hs2, hs3, hs4, hs5, hs6, hs7)
     block = min(512, width)
-    pairs = ((dtw_hbm, dtw_ref), (wx_hbm, wx_ref), (win_hbm, win_ref))
+    pairs = ((dtw_hbm, dtw_ref), (wx_hbm, wx_ref))
     loads = [pltpu.make_async_copy(a, b, sems.at[n]) for n, (a, b) in enumerate(pairs)]
+
+    def weights(j):
+        slot = j % 2
+        return [
+            pltpu.make_async_copy(
+                win_hbm.at[:, tile_at(n * width + j * block, block)], win_ref.at[slot, n], sems.at[2 + 2 * slot + n]
+            )
+            for n in range(2)
+        ]
+
     for load in loads:
         load.start()
+    for j in range(min(2, width // block)):
+        for load in weights(j):
+            load.start()
     low_acc[...] = jnp.zeros_like(low_acc)
     small[pl.ds(small.shape[0] - EDGE, EDGE), :] = jnp.zeros((EDGE, width), f32)
     low = proj_ref[:, :rank].astype(bf16)
@@ -442,25 +461,6 @@
             return jnp.broadcast_to(ref[pl.ds(n, 1), at], (SUBS, LANES))
 
         rates = [wide(rates_ref, n) for n in range(states)]
-        start = []
-        for n in range(states):
-            h0 = dx_ref[n, :, at] * wide(entry_ref, n) + ex_ref[n, :, at]
-            hs[0, n] = h0
-            start.append(h0)
-
-        def lap(t, h):
-            rows = step_rows(t)
-            d, u = dtm_s[rows, :], u_s[rows, :]
-            new = []
-            for n in range(states):
-                a = jnp.exp2(d * rates[n])
-                decays[t, n] = a
-                now = a * h[n] + u * table[rows, n * LANES : (n + 1) * LANES]
-                hs[t + 1, n] = now
-                new.append(now)
-            return tuple(new)
-
-        lax.fori_loop(0, steps, lap, tuple(start), unroll=UNROLL)
         for first in range(0, states, half):
             some = rates[first : first + half]
 
@@ -468,18 +468,18 @@
                 f, r = carry
                 t = steps - 1 - k
                 rows = step_rows(t)
-                dtt, g, u = dt_ref[rows, at], gs_ref[rows, at], u_s[rows, :]
+                dtt, g, u, d = dt_ref[rows, at], gs_ref[rows, at], u_s[rows, :], dtm_s[rows, :]
                 fn, rn, s1, s2 = [], [], zero, zero
                 for k in range(half):
                     n = first + k
                     into, out = (slice(m * LANES, (m + 1) * LANES) for m in (n, states + n))
                     adj = g * table[rows, out] + f[k]
                     acc[rows, into] += adj * u
-                    acc[rows, out] += g * hs[t + 1, n]
+                    acc[rows, out] += g * hs_refs[n * 8 // states][tile, t + 1, n % (states // 8)]
                     s1 = s1 + adj * table[rows, into]
-                    flow = decays[t, n] * adj
+                    flow = jnp.exp2(d * some[k]) * adj
                     fn.append(flow)
-                    flow = flow * hs[t, n]
+                    flow = flow * hs_refs[n * 8 // states][tile, t, n % (states // 8)]
                     s2 = s2 + flow * some[k]
                     rn.append(r[k] + flow * dtt)
                 if first == 0:
@@ -527,7 +527,9 @@
 
     def close(j, _):
         wide = tile_at(j * block, block)
-        ngrad[pl.ds(0, length), :] += nt(ggate_ref[:, wide], win_ref[:, tile_at(width + j * block, block)])
+        for load in weights(j):
+            load.wait()
+        ngrad[pl.ds(0, length), :] += nt(ggate_ref[:, wide], win_ref[j % 2, 1])
         small[pl.ds(0, maps), wide] = tn(pg[...], inner_ref[:, wide])[:maps]
         inner_grad = isg[:, wide] + nn(pg[:, :maps], wx_ref[:, wide])
         mask = [masks[k] for k in range(taps)]
@@ -565,7 +567,13 @@
                 held[chip, :, tile_at(spot * LANES)] = sent.astype(bf16)
             else:
                 blocks[0][:, far] = sent.astype(bf16)
-        ngrad[...] += nt(sent_s[...], win_ref[:, wide])
+        ngrad[...] += nt(sent_s[...], win_ref[j % 2, 0])
+
+        @pl.when(j + 2 < width // block)
+        def _():
+            for load in weights(j + 2):
+                load.start()
+
         return 0
 
     lax.fori_loop(0, width // block, close, 0)
@@ -599,7 +607,7 @@
                 theirs_ref[n] = small[:, other : other + chunk].astype(bf16)
 
 
-def backward(masks, in_weight, dtw, wx, proj, tok, gain, vec, rates, entry, arrive, table, dt, inner, gs, deep4,
+def backward(masks, in_weight, dtw, wx, proj, tok, gain, vec, rates, arrive, table, dt, inner, gs, deep3,
              ggate, ext, taps, chips, chunks):
     length, width = inner.shape
     model = tok.shape[1]
@@ -618,12 +626,10 @@
         [shape((length + EDGE, model), f32)]
         + [shape((length + EDGE, width // parts), bf16)] * parts
         + [shape(chunk, f32), shape(chunk, bf16)],
-        (in_weight, dtw, wx, masks, proj, tok, gain, vec, rates, entry, arrive, table, dt, inner, gs, *deep4, ggate, ext),
+        (in_weight, dtw, wx, masks, proj, tok, gain, vec, rates, arrive, table, dt, inner, gs, *deep3, ggate, ext),
         24,
         [
             pltpu.VMEM((length, 2 * states * LANES), f32),
-            pltpu.VMEM((steps + 1, states, SUBS, LANES), f32),
-            pltpu.VMEM((steps, states, SUBS, LANES), f32),
         ]
         + [pltpu.VMEM((length, LANES), f32)] * 4
         + [
@@ -635,9 +641,10 @@
             pltpu.VMEM((rows, width), f32),
             pltpu.VMEM((parts, length + EDGE, width // parts), bf16),
         ]
-        + [pltpu.VMEM(x.shape, x.dtype) for x in (in_weight, dtw, wx)]
-        + [pltpu.SemaphoreType.DMA((3,))],
-        24,
+        + [pltpu.VMEM((2, 2, model, block), bf16)]
+        + [pltpu.VMEM(x.shape, x.dtype) for x in (dtw, wx)]
+        + [pltpu.SemaphoreType.DMA((6,))],
+        16,
         [ANY_SPEC] * 3,
     )
 
@@ -864,14 +871,20 @@
                         parts[k - 1][pl.ds(0, rows), :] = both.astype(bf16)
 
 
-def in_last_kernel(here, own_ref, small_ref, *rest):
-    gots, (out_ref, small_out) = rest[:-2], rest[-2:]
+def in_last_kernel(here, own_ref, *rest):
+    gots, out_ref = rest[:-1], rest[-1]
     both, rows = own_ref[...], own_ref.shape[0]
+    for got in gots:
+        both = both + got[pl.ds(0, rows), :].astype(f32)
+    out_ref[...] = both.T
+
+
+def join_kernel(here, small_ref, *rest):
+    gots, small_out = rest[:-1], rest[-1]
+    rows = small_ref.shape[0]
     small_out[here[1]] = small_ref[...]
     for k, got in enumerate(gots):
-        both = both + got[pl.ds(0, rows), :].astype(f32)
-        small_out[here[1] ^ (k + 1)] = got[pl.ds(rows, small_ref.shape[0]), :]
-    out_ref[...] = both.T
+        small_out[here[1] ^ (k + 1)] = got[pl.ds(got.shape[0] - rows, rows), :]
 
 
 def out_last_kernel(here, mine_ref, got_ref, out_ref):
@@ -1031,12 +1044,13 @@
             functools.partial(enter_kernel, states, outer.size), "enter", entering, (other, rates, got), 2
         )
     gated, ggate, *late = forward(masks, cot, tok, beyond, vec, rates, entry, table, dt, inner, gate, ggated, dx, ex, taps, chips, dp_size)
+    hs, late = late[:8], late[8:]
     lines_got = rows_group.trade(late[:dp_size])
     gate_got = outer.trade(late[dp_size:]) if tiled else None
 
     ngrad, *sent, small, small_theirs = backward(
-        masks, in_weight, dt_weight, wx, proj, tok, gain, vec, rates, entry, arrive, table, dt, inner, gs,
-        (dx, ex, db, fx), ggate, ext, taps, chips, dp_size,
+        masks, in_weight, dt_weight, wx, proj, tok, gain, vec, rates, arrive, table, dt, inner, gs,
+        (*hs, db, fx), ggate, ext, taps, chips, dp_size,
     )
     rows, chunk = small.shape[1:]
     turn = [ngrad]
@@ -1108,9 +1122,10 @@
         out, out_got = halve(outer, 0, 2, out, out_got, "out_chip0")
         tokens_grad, mixed = finished()
         out, out_got = halve(outer, 1, 2, out, out_got, "out_chip1")
-        outs = [((model, width), f32), ((dp_size, lines, model), bf16)]
-        in_share, small = call(in_last_kernel, "in_last", outs, (in_own, small, *in_gots))
+        (small,) = call(join_kernel, "join", [((dp_size, lines, model), bf16)], (small, *in_gots))
         small_other = core.swap(small, 1)
+        tied, _ = lax.optimization_barrier(((in_own, *in_gots), small))
+        (in_share,) = call(in_last_kernel, "in_last", [((model, width), f32)], tied)
         (out_share,) = call(out_last_kernel, "out_last", [((thin, inner_width), f32)], (out, out_got))
     else:
         tokens_grad, mixed = finished()

time: 131 us -> 128 us (0.977)
  Pallas kernels: 57.1 us -> 54.4 us
  starting transfers between devices: 36.1 us -> 34.4 us
    pallas_call x22 -> x23, Pallas kernels: 57.1 us -> 54.4 us  [plain_call(): pl.pallas_call(lambda *refs: kernel(Here(), *refs), in_specs=list(specs)...]
    ppermute x28, starting transfers between devices: 32.5 us -> 30.8 us  [swap(): lax.ppermute(x, self.axis, [(i, i ^ k * self.stride) for i in range(n)])]
  transfers between devices with their start and end apart: 30 -> 30, of which waited for: 13 -> 13; matrix products, arithmetic and copies ran while one was open for 0% -> 0% of each run, Pallas kernels for 38% -> 37%
where the time goes in v7:
time: 128 us; the launch traced here: 127 us
  Pallas kernels  54.4 us (42%)
  waiting for transfers between devices  36.7 us (29%)
  starting transfers between devices  34.4 us (27%)
    pallas_call x23, Pallas kernels, plain_call(): pl.pallas_call(lambda *refs: kernel(Here(), *refs), in_specs=list(specs)...  54.4 us
    ppermute x28, waiting for transfers between devices, swap(): lax.ppermute(x, self.axis, [(i, i ^ k * self.stride) for i in range(n)])  36.7 us
    ppermute x28, starting transfers between devices, swap(): lax.ppermute(x, self.axis, [(i, i ^ k * self.stride) for i in range(n)])  30.8 us
  transfers between devices with their start and end apart: 30, of which 13 were waited for; matrix products, arithmetic and copies ran while one was open for 0% of the time, Pallas kernels for 37%

profile of v7, /device:TPU:0, one launch (start us, length us, event | category | flops | bytes accessed | tf_op | source)
XLA Modules:
  0.0 127.2 jit_solution(17680171752294289645)
XLA Ops:
  0.6 0.7 slice_bitcast_fusion
  1.4 2.3 %collective-permute-start = (bf16[3,1024]{1,0:T(4,128)(2,1)S(1)}, bf16[3,1024]{1,0:T(4,128)(2,1)S(1)}, u32[]{:S(2)}, u32[]{:S(2)}) collective-permute-start(bf16[3,1024]{1,0:T(4,128)(2,1)S(1)} %slice_bitcast_fusion), channel_id=1, source_target_pairs={{0,1},{1,2},{2,3},{3,4},{4,5},{5,6},{6,7},{8,9},{9,10},{10,11},{11... | collective-permute-start | bytes 18440 | tf_op jit(solution)/shard_map/ppermute | solution.py:1000
  3.7 3.7 %collective-permute-start.1 = (bf16[128,1024]{1,0:T(8,128)(2,1)}, bf16[128,1024]{1,0:T(8,128)(2,1)S(1)}, u32[]{:S(2)}, u32[]{:S(2)}) collective-permute-start(bf16[128,1024]{1,0:T(8,128)(2,1)} %bitcast.19), channel_id=1, source_target_pairs={{0,4},{1,5},{2,6},{3,7},{4,0},{5,1},{6,2},{7,3},{8,12},{9,13},{10,... | collective-permute-start | bytes 786440 | tf_op jit(solution)/shard_map/ppermute | solution.py:928
  7.4 0.0 collective-permute-done.refs_13_
  7.4 18.6 %front.1 = (bf16[144,1024]{1,0:T(8,128)(2,1)S(1)}, bf16[128,1024]{1,0:T(8,128)(2,1)S(1)}, bf16[160,2048]{1,0:T(8,128)(2,1)S(1)}, bf16[128,2048]{1,0:T(8,128)(2,1...) custom-call(s32[1,4]{1,0:T(1,128)} %refs_0_.2, ...), custom_call_target="tpu_custom_call" | custom-call | flops 22000001024 | tf_op jit(solution)/shard_map/front/pallas_call | solution.py:49
  26.0 0.0 collective-permute-done.1.refs_3_.refs_2_
  26.0 1.5 %collective-permute-start.2 = (bf16[48,2048]{1,0:T(8,128)(2,1)S(1)}, bf16[48,2048]{1,0:T(8,128)(2,1)S(1)}, u32[]{:S(2)}, u32[]{:S(2)}) collective-permute-start(bf16[48,2048]{1,0:T(8,128)(2,1)S(1)} %get-tuple-element.116.refs_0_), channel_id=1, source_target_pairs={{0,1},{1,0},{2,3},{3,2},{4,5},{5,4},{6,7},{7,6},{8,9},{9,8},{10,11... | collective-permute-start | bytes 589832 | tf_op jit(solution)/shard_map/ppermute | solution.py:928
  27.5 1.1 collective-permute-done.2.refs_1_.refs_0_
  28.6 0.1 pair.1.refs_0_
  28.6 1.0 collective-permute-start.3
  29.6 4.1 %collective-permute-done.3.refs_1_ = bf16[48,1024]{1,0:T(8,128)(2,1)S(1)} collective-permute-done((bf16[48,1024]{1,0:T(8,128)(2,1)S(1)}, bf16[48,1024]{1,0:T(8,128)(2,1)S(1)}, u32[]{:S(2)}, u32[]{:S(2)}) %collective-permute-start.3) | collective-permute-done | bytes 98336 | tf_op jit(solution)/shard_map/ppermute | solution.py:928
  33.8 0.1 quad.1
  33.9 1.8 %collective-permute-start.4 = (bf16[16,1024]{1,0:T(8,128)(2,1)S(1)}, bf16[16,1024]{1,0:T(8,128)(2,1)S(1)}, u32[]{:S(2)}, u32[]{:S(2)}) collective-permute-start(bf16[16,1024]{1,0:T(8,128)(2,1)S(1)} %get-tuple-element.118), channel_id=1, source_target_pairs={{0,4},{1,5},{2,6},{3,7},{4,0},{5,1},{6,2},{7,3},{8,12},{9,13},{10,... | collective-permute-start | bytes 98312 | tf_op jit(solution)/shard_map/ppermute | solution.py:928
  35.7 3.5 %collective-permute-done.4.refs_1_ = bf16[16,1024]{1,0:T(8,128)(2,1)S(1)} collective-permute-done((bf16[16,1024]{1,0:T(8,128)(2,1)S(1)}, bf16[16,1024]{1,0:T(8,128)(2,1)S(1)}, u32[]{:S(2)}, u32[]{:S(2)}) %collective-permute-start.4) | collective-permute-done | bytes 32800 | tf_op jit(solution)/shard_map/ppermute | solution.py:928
  39.1 0.1 collective-permute-start.5
  39.2 1.3 %collective-permute-done.5.refs_3_ = f32[32,1024]{1,0:T(8,128)S(1)} collective-permute-done((f32[32,1024]{1,0:T(8,128)S(1)}, f32[32,1024]{1,0:T(8,128)S(1)}, u32[]{:S(2)}, u32[]{:S(2)}) %collective-permute-start.5) | collective-permute-done | bytes 131104 | tf_op jit(solution)/shard_map/ppermute | solution.py:928
  40.5 0.1 enter.1
  40.6 5.5 %forward.1 = (bf16[128,2048]{1,0:T(8,128)(2,1)S(1)}, bf16[128,2048]{1,0:T(8,128)(2,1)S(1)}, f32[16,17,2,8,128]{4,3,2,1,0:T(8,128)S(1)}, f32[16,17,2,8,128]{4,3,2...) custom-call(f32[4,128,128]{2,1,0:T(8,128)S(1)} %get-tuple-element.10, ...), custom_call_target="tpu_custom_call" | custom-call | flops 8800000000 | tf_op jit(solution)/shard_map/forward/pallas_call | solution.py:49
  46.1 1.6 %collective-permute-start.7 = (bf16[128,2304]{1,0:T(8,128)(2,1)S(1)}, bf16[128,2304]{1,0:T(8,128)(2,1)S(1)}, u32[]{:S(2)}, u32[]{:S(2)}) collective-permute-start(bf16[128,2304]{1,0:T(8,128)(2,1)S(1)} %get-tuple-element.153), channel_id=1, source_target_pairs={{0,8},{8,0},{16,24},{24,16},{1,9},{9,1},{17,25},{25,17},{2,10},{10... | collective-permute-start | bytes 1769480 | tf_op jit(solution)/shard_map/ppermute | solution.py:928
  47.7 1.5 %collective-permute-start.8 = (bf16[128,2304]{1,0:T(8,128)(2,1)S(1)}, bf16[128,2304]{1,0:T(8,128)(2,1)S(1)}, u32[]{:S(2)}, u32[]{:S(2)}) collective-permute-start(bf16[128,2304]{1,0:T(8,128)(2,1)S(1)} %get-tuple-element.154), channel_id=1, source_target_pairs={{0,16},{8,24},{16,0},{24,8},{1,17},{9,25},{17,1},{25,9},{2,18},{10... | collective-permute-start | bytes 1769480 | tf_op jit(solution)/shard_map/ppermute | solution.py:928
  49.2 0.5 collective-permute-start.9
  49.7 0.4 collective-permute-start.10
  50.1 2.7 %collective-permute-start.11 = (bf16[128,512]{1,0:T(8,128)(2,1)S(1)}, bf16[128,512]{1,0:T(8,128)(2,1)S(1)}, u32[]{:S(2)}, u32[]{:S(2)}) collective-permute-start(bf16[128,512]{1,0:T(8,128)(2,1)S(1)} %get-tuple-element.158), channel_id=1, source_target_pairs={{0,4},{1,5},{2,6},{3,7},{4,0},{5,1},{6,2},{7,3},{8,12},{9,13},{10,... | collective-permute-start | bytes 393224 | tf_op jit(solution)/shard_map/ppermute | solution.py:928
  52.9 21.5 %backward.1 = (f32[144,1024]{1,0:T(8,128)S(1)}, bf16[144,512]{1,0:T(8,128)(2,1)S(1)}, bf16[144,512]{1,0:T(8,128)(2,1)S(1)}, bf16[144,512]{1,0:T(8,128)(2,1)S(1)}...) custom-call(bf16[1024,4096]{1,0:T(8,128)(2,1)} %refs_0_.3, ...), custom_call_target="tpu_custom_call" | custom-call | flops 26400000000 | tf_op jit(solution)/shard_map/backward/pallas_call | solution.py:49
  74.4 0.0 collective-permute-done.7.refs_1_
  74.4 1.1 collective-permute-done.8.refs_2_
  75.4 0.0 collective-permute-done.9.refs_3_
  75.5 0.0 collective-permute-done.10.refs_4_
  75.5 1.3 %collective-permute-start.6 = (f32[16,1024]{1,0:T(8,128)S(1)}, f32[16,1024]{1,0:T(8,128)S(1)}, u32[]{:S(2)}, u32[]{:S(2)}) collective-permute-start(f32[16,1024]{1,0:T(8,128)S(1)} %slice.7), channel_id=1, source_target_pairs={{1,0},{2,1},{3,2},{4,3},{5,4},{6,5},{7,6},{9,8},{10,9},{11,10},{12... | collective-permute-start | bytes 196616 | tf_op jit(solution)/shard_map/ppermute | solution.py:1072
  76.8 3.6 %collective-permute-start.12 = (bf16[128,512]{1,0:T(8,128)(2,1)S(1)}, bf16[128,512]{1,0:T(8,128)(2,1)S(1)}, u32[]{:S(2)}, u32[]{:S(2)}) collective-permute-start(bf16[128,512]{1,0:T(8,128)(2,1)S(1)} %get-tuple-element.162), channel_id=1, source_target_pairs={{0,6},{1,7},{2,4},{3,5},{4,2},{5,3},{6,0},{7,1},{8,14},{9,15},{10,... | collective-permute-start | bytes 393224 | tf_op jit(solution)/shard_map/ppermute | solution.py:928
  80.4 0.0 collective-permute-start.13
  80.5 0.8 collective-permute-start.14
  81.3 0.1 small_row0.1
  81.3 1.3 %collective-permute-start.19 = (bf16[2,192,256]{2,1,0:T(8,128)(2,1)S(1)}, bf16[2,192,256]{2,1,0:T(8,128)(2,1)S(1)}, u32[]{:S(2)}, u32[]{:S(2)}) collective-permute-start(bf16[2,192,256]{2,1,0:T(8,128)(2,1)S(1)} %get-tuple-element.175), channel_id=1, source_target_pairs={{0,8},{8,0},{16,24},{24,16},{1,9},{9,1},{17,25},{25,17},{2,10},{10... | collective-permute-start | bytes 589832 | tf_op jit(solution)/shard_map/ppermute | solution.py:928
  82.6 0.8 out_columns.1
  83.5 5.0 %collective-permute-done.19.refs_1_ = bf16[2,192,256]{2,1,0:T(8,128)(2,1)S(1)} collective-permute-done((bf16[2,192,256]{2,1,0:T(8,128)(2,1)S(1)}, bf16[2,192,256]{2,1,0:T(8,128)(2,1)S(1)}, u32[]{:S(2)}, u32[]{:S(2)}) %collective-permute-start.19) | collective-permute-done | bytes 196640 | tf_op jit(solution)/shard_map/ppermute | solution.py:928
  88.5 2.6 %collective-permute-start.15 = (bf16[144,512]{1,0:T(8,128)(2,1)S(1)}, bf16[144,512]{1,0:T(8,128)(2,1)S(1)}, u32[]{:S(2)}, u32[]{:S(2)}) collective-permute-start(bf16[144,512]{1,0:T(8,128)(2,1)S(1)} %get-tuple-element.167), channel_id=1, source_target_pairs={{0,6},{1,7},{2,4},{3,5},{4,2},{5,3},{6,0},{7,1},{8,14},{9,15},{10,... | collective-permute-start | bytes 442376 | tf_op jit(solution)/shard_map/ppermute | solution.py:928
  91.2 1.6 %collective-permute-start.20 = (bf16[1,192,256]{2,1,0:T(8,128)(2,1)S(1)}, bf16[1,192,256]{2,1,0:T(8,128)(2,1)S(1)}, u32[]{:S(2)}, u32[]{:S(2)}) collective-permute-start(bf16[1,192,256]{2,1,0:T(8,128)(2,1)S(1)} %get-tuple-element.177), channel_id=1, source_target_pairs={{0,16},{8,24},{16,0},{24,8},{1,17},{9,25},{17,1},{25,9},{2,18},{10... | collective-permute-start | bytes 294920 | tf_op jit(solution)/shard_map/ppermute | solution.py:928
  92.8 1.1 gate_columns.1
  93.9 1.9 %collective-permute-done.20.refs_1_ = bf16[1,192,256]{2,1,0:T(8,128)(2,1)S(1)} collective-permute-done((bf16[1,192,256]{2,1,0:T(8,128)(2,1)S(1)}, bf16[1,192,256]{2,1,0:T(8,128)(2,1)S(1)}, u32[]{:S(2)}, u32[]{:S(2)}) %collective-permute-start.20) | collective-permute-done | bytes 98336 | tf_op jit(solution)/shard_map/ppermute | solution.py:928
  95.9 0.6 collective-permute-start.17
  96.5 1.1 collective-permute-done.14.refs_3_
  97.6 1.1 conv_columns.1
  98.7 0.1 collective-permute-start.16
  98.7 3.4 %collective-permute-done.21.refs_1_ = bf16[48,1024]{1,0:T(8,128)(2,1)S(1)} collective-permute-done((bf16[48,1024]{1,0:T(8,128)(2,1)S(1)}, bf16[48,1024]{1,0:T(8,128)(2,1)S(1)}, u32[]{:S(2)}, u32[]{:S(2)}) %collective-permute-start.21) | collective-permute-done | bytes 98336 | tf_op jit(solution)/shard_map/ppermute | solution.py:928
  102.2 0.1 collective-permute-start.22
  102.3 0.1 out_chip0.1
  102.4 1.5 %collective-permute-start.28 = (bf16[2,64,1024]{2,1,0:T(8,128)(2,1)S(1)}, bf16[2,64,1024]{2,1,0:T(8,128)(2,1)S(1)}, u32[]{:S(2)}, u32[]{:S(2)}) collective-permute-start(bf16[2,64,1024]{2,1,0:T(8,128)(2,1)S(1)} %get-tuple-element.200), channel_id=1, source_target_pairs={{0,2},{1,3},{2,0},{3,1},{4,6},{5,7},{6,4},{7,5},{8,10},{9,11},{10,... | collective-permute-start | bytes 786440 | tf_op jit(solution)/shard_map/ppermute | solution.py:928
  103.9 4.8 %collective-permute-done.22.refs_1_ = bf16[48,1024]{1,0:T(8,128)(2,1)S(1)} collective-permute-done((bf16[48,1024]{1,0:T(8,128)(2,1)S(1)}, bf16[48,1024]{1,0:T(8,128)(2,1)S(1)}, u32[]{:S(2)}, u32[]{:S(2)}) %collective-permute-start.22) | collective-permute-done | bytes 98336 | tf_op jit(solution)/shard_map/ppermute | solution.py:928
  108.7 0.0 copy-start
  108.8 0.4 in_merge.1
  109.2 1.3 collective-permute-start.23
  110.4 0.8 collective-permute-start.24
  111.3 1.4 %collective-permute-start.25 = (bf16[176,1024]{1,0:T(8,128)(2,1)S(1)}, bf16[176,1024]{1,0:T(8,128)(2,1)S(1)}, u32[]{:S(2)}, u32[]{:S(2)}) collective-permute-start(bf16[176,1024]{1,0:T(8,128)(2,1)S(1)} %get-tuple-element.181), channel_id=1, source_target_pairs={{0,24},{8,16},{16,8},{24,0},{1,25},{9,17},{17,9},{25,1},{2,26},{10... | collective-permute-start | bytes 1081352 | tf_op jit(solution)/shard_map/ppermute | solution.py:928
  112.7 1.8 %finish.1 = (bf16[128,1024]{1,0:T(8,128)(2,1)}, bf16[128,1024]{1,0:T(8,128)(2,1)}) custom-call(f32[144,1024]{1,0:T(8,128)S(1)} %get-tuple-element.143.refs_0_, f32[16,1024]{1,0:T(8,128)S(1)} %collective-permute-done.6.refs_1_, bf16[144,1024]{1,0:T(8,128)(2,1)S(1)} %get-tuple-element.110.refs_2_.refs_5_.refs_1_, ...), custom_call_target="tpu_custom_call" | custom-call | flops 2200000000 | tf_op jit(solution)/shard_map/finish/pallas_call | solution.py:49
  114.5 0.1 out_chip1.1
  114.6 0.3 collective-permute-start.29
  114.8 4.4 %collective-permute-done.23.refs_1_ = bf16[176,1024]{1,0:T(8,128)(2,1)S(1)} collective-permute-done((bf16[176,1024]{1,0:T(8,128)(2,1)S(1)}, bf16[176,1024]{1,0:T(8,128)(2,1)S(1)}, u32[]{:S(2)}, u32[]{:S(2)}) %collective-permute-start.23) | collective-permute-done | bytes 360480 | tf_op jit(solution)/shard_map/ppermute | solution.py:928
  119.3 1.0 collective-permute-done.24.refs_2_
  120.3 3.9 %collective-permute-done.25.refs_3_ = bf16[176,1024]{1,0:T(8,128)(2,1)S(1)} collective-permute-done((bf16[176,1024]{1,0:T(8,128)(2,1)S(1)}, bf16[176,1024]{1,0:T(8,128)(2,1)S(1)}, u32[]{:S(2)}, u32[]{:S(2)}) %collective-permute-start.25) | collective-permute-done | bytes 360480 | tf_op jit(solution)/shard_map/ppermute | solution.py:928
  124.2 0.1 collective-permute-start.26
  124.3 0.7 out_last.1
  125.0 1.0 in_last.1
  126.0 1.2 unpack.1
  (26 shorter events, 0.3 us)
Async XLA Ops:
  1.4 6.0 %collective-permute-start = (bf16[3,1024]{1,0:T(4,128)(2,1)S(1)}, bf16[3,1024]{1,0:T(4,128)(2,1)S(1)}, u32[]{:S(2)}, u32[]{:S(2)}) collective-permute-start(bf16[3,1024]{1,0:T(4,128)(2,1)S(1)} %slice_bitcast_fusion), channel_id=1, source_target_pairs={{0,1},{1,2},{2,3},{3,4},{4,5},{5,6},{6,7},{8,9},{9,10},{10,11},{11... | collective-permute-start | bytes 18440 | tf_op jit(solution)/shard_map/ppermute | solution.py:1000
  3.7 22.3 %collective-permute-start.1 = (bf16[128,1024]{1,0:T(8,128)(2,1)}, bf16[128,1024]{1,0:T(8,128)(2,1)S(1)}, u32[]{:S(2)}, u32[]{:S(2)}) collective-permute-start(bf16[128,1024]{1,0:T(8,128)(2,1)} %bitcast.19), channel_id=1, source_target_pairs={{0,4},{1,5},{2,6},{3,7},{4,0},{5,1},{6,2},{7,3},{8,12},{9,13},{10,... | collective-permute-start | bytes 786440 | tf_op jit(solution)/shard_map/ppermute | solution.py:928
  26.0 2.5 %collective-permute-start.2 = (bf16[48,2048]{1,0:T(8,128)(2,1)S(1)}, bf16[48,2048]{1,0:T(8,128)(2,1)S(1)}, u32[]{:S(2)}, u32[]{:S(2)}) collective-permute-start(bf16[48,2048]{1,0:T(8,128)(2,1)S(1)} %get-tuple-element.116.refs_0_), channel_id=1, source_target_pairs={{0,1},{1,0},{2,3},{3,2},{4,5},{5,4},{6,7},{7,6},{8,9},{9,8},{10,11... | collective-permute-start | bytes 589832 | tf_op jit(solution)/shard_map/ppermute | solution.py:928
  28.6 5.1 %collective-permute-start.3 = (bf16[48,1024]{1,0:T(8,128)(2,1)S(1)}, bf16[48,1024]{1,0:T(8,128)(2,1)S(1)}, u32[]{:S(2)}, u32[]{:S(2)}) collective-permute-start(bf16[48,1024]{1,0:T(8,128)(2,1)S(1)} %pair.1.refs_0_), channel_id=1, source_target_pairs={{0,2},{1,3},{2,0},{3,1},{4,6},{5,7},{6,4},{7,5},{8,10},{9,11},{10,... | collective-permute-start | bytes 294920 | tf_op jit(solution)/shard_map/ppermute | solution.py:928
  33.9 5.2 %collective-permute-start.4 = (bf16[16,1024]{1,0:T(8,128)(2,1)S(1)}, bf16[16,1024]{1,0:T(8,128)(2,1)S(1)}, u32[]{:S(2)}, u32[]{:S(2)}) collective-permute-start(bf16[16,1024]{1,0:T(8,128)(2,1)S(1)} %get-tuple-element.118), channel_id=1, source_target_pairs={{0,4},{1,5},{2,6},{3,7},{4,0},{5,1},{6,2},{7,3},{8,12},{9,13},{10,... | collective-permute-start | bytes 98312 | tf_op jit(solution)/shard_map/ppermute | solution.py:928
  39.1 1.4 %collective-permute-start.5 = (f32[32,1024]{1,0:T(8,128)S(1)}, f32[32,1024]{1,0:T(8,128)S(1)}, u32[]{:S(2)}, u32[]{:S(2)}) collective-permute-start(f32[32,1024]{1,0:T(8,128)S(1)} %enter_half.1.refs_2_), channel_id=1, source_target_pairs={{0,1},{1,0},{2,3},{3,2},{4,5},{5,4},{6,7},{7,6},{8,9},{9,8},{10,11... | collective-permute-start | bytes 393224 | tf_op jit(solution)/shard_map/ppermute | solution.py:928
  46.1 28.2 %collective-permute-start.7 = (bf16[128,2304]{1,0:T(8,128)(2,1)S(1)}, bf16[128,2304]{1,0:T(8,128)(2,1)S(1)}, u32[]{:S(2)}, u32[]{:S(2)}) collective-permute-start(bf16[128,2304]{1,0:T(8,128)(2,1)S(1)} %get-tuple-element.153), channel_id=1, source_target_pairs={{0,8},{8,0},{16,24},{24,16},{1,9},{9,1},{17,25},{25,17},{2,10},{10... | collective-permute-start | bytes 1769480 | tf_op jit(solution)/shard_map/ppermute | solution.py:928
  47.7 27.7 %collective-permute-start.8 = (bf16[128,2304]{1,0:T(8,128)(2,1)S(1)}, bf16[128,2304]{1,0:T(8,128)(2,1)S(1)}, u32[]{:S(2)}, u32[]{:S(2)}) collective-permute-start(bf16[128,2304]{1,0:T(8,128)(2,1)S(1)} %get-tuple-element.154), channel_id=1, source_target_pairs={{0,16},{8,24},{16,0},{24,8},{1,17},{9,25},{17,1},{25,9},{2,18},{10... | collective-permute-start | bytes 1769480 | tf_op jit(solution)/shard_map/ppermute | solution.py:928
  49.2 26.2 %collective-permute-start.9 = (bf16[128,2304]{1,0:T(8,128)(2,1)S(1)}, bf16[128,2304]{1,0:T(8,128)(2,1)S(1)}, u32[]{:S(2)}, u32[]{:S(2)}) collective-permute-start(bf16[128,2304]{1,0:T(8,128)(2,1)S(1)} %get-tuple-element.155), channel_id=1, source_target_pairs={{0,24},{8,16},{16,8},{24,0},{1,25},{9,17},{17,9},{25,1},{2,26},{10... | collective-permute-start | bytes 1769480 | tf_op jit(solution)/shard_map/ppermute | solution.py:928
  49.7 25.8 %collective-permute-start.10 = (bf16[128,2560]{1,0:T(8,128)(2,1)S(1)}, bf16[128,2560]{1,0:T(8,128)(2,1)S(1)}, u32[]{:S(2)}, u32[]{:S(2)}) collective-permute-start(bf16[128,2560]{1,0:T(8,128)(2,1)S(1)} %get-tuple-element.157), channel_id=1, source_target_pairs={{0,2},{1,3},{2,0},{3,1},{4,6},{5,7},{6,4},{7,5},{8,10},{9,11},{10,... | collective-permute-start | bytes 1966088 | tf_op jit(solution)/shard_map/ppermute | solution.py:928
  50.1 24.2 %collective-permute-start.11 = (bf16[128,512]{1,0:T(8,128)(2,1)S(1)}, bf16[128,512]{1,0:T(8,128)(2,1)S(1)}, u32[]{:S(2)}, u32[]{:S(2)}) collective-permute-start(bf16[128,512]{1,0:T(8,128)(2,1)S(1)} %get-tuple-element.158), channel_id=1, source_target_pairs={{0,4},{1,5},{2,6},{3,7},{4,0},{5,1},{6,2},{7,3},{8,12},{9,13},{10,... | collective-permute-start | bytes 393224 | tf_op jit(solution)/shard_map/ppermute | solution.py:928
  52.9 22.6 %copy-start.1 = (f32[2048,16]{0,1:T(8,128)S(1)}, f32[2048,16]{0,1:T(8,128)}, u32[]{:S(2)}) copy-start(f32[2048,16]{0,1:T(8,128)} %param.22) | copy-start | bytes 393220
  75.5 5.8 %collective-permute-start.18 = (bf16[4,192,256]{2,1,0:T(8,128)(2,1)S(1)}, bf16[4,192,256]{2,1,0:T(8,128)(2,1)S(1)}, u32[]{:S(2)}, u32[]{:S(2)}) collective-permute-start(bf16[4,192,256]{2,1,0:T(8,128)(2,1)S(1)} %get-tuple-element.173), channel_id=1, source_target_pairs={{0,1},{1,0},{2,3},{3,2},{4,5},{5,4},{6,7},{7,6},{8,9},{9,8},{10,11... | collective-permute-start | bytes 1179656 | tf_op jit(solution)/shard_map/ppermute | solution.py:928
  75.5 37.2 %collective-permute-start.6 = (f32[16,1024]{1,0:T(8,128)S(1)}, f32[16,1024]{1,0:T(8,128)S(1)}, u32[]{:S(2)}, u32[]{:S(2)}) collective-permute-start(f32[16,1024]{1,0:T(8,128)S(1)} %slice.7), channel_id=1, source_target_pairs={{1,0},{2,1},{3,2},{4,3},{5,4},{6,5},{7,6},{9,8},{10,9},{11,10},{12... | collective-permute-start | bytes 196616 | tf_op jit(solution)/shard_map/ppermute | solution.py:1072
  76.8 14.3 %collective-permute-start.12 = (bf16[128,512]{1,0:T(8,128)(2,1)S(1)}, bf16[128,512]{1,0:T(8,128)(2,1)S(1)}, u32[]{:S(2)}, u32[]{:S(2)}) collective-permute-start(bf16[128,512]{1,0:T(8,128)(2,1)S(1)} %get-tuple-element.162), channel_id=1, source_target_pairs={{0,6},{1,7},{2,4},{3,5},{4,2},{5,3},{6,0},{7,1},{8,14},{9,15},{10,... | collective-permute-start | bytes 393224 | tf_op jit(solution)/shard_map/ppermute | solution.py:928
  80.4 15.4 %collective-permute-start.13 = (bf16[144,512]{1,0:T(8,128)(2,1)S(1)}, bf16[144,512]{1,0:T(8,128)(2,1)S(1)}, u32[]{:S(2)}, u32[]{:S(2)}) collective-permute-start(bf16[144,512]{1,0:T(8,128)(2,1)S(1)} %get-tuple-element.165), channel_id=1, source_target_pairs={{0,2},{1,3},{2,0},{3,1},{4,6},{5,7},{6,4},{7,5},{8,10},{9,11},{10,... | collective-permute-start | bytes 442376 | tf_op jit(solution)/shard_map/ppermute | solution.py:928
  80.5 17.1 %collective-permute-start.14 = (bf16[144,512]{1,0:T(8,128)(2,1)S(1)}, bf16[144,512]{1,0:T(8,128)(2,1)S(1)}, u32[]{:S(2)}, u32[]{:S(2)}) collective-permute-start(bf16[144,512]{1,0:T(8,128)(2,1)S(1)} %get-tuple-element.166), channel_id=1, source_target_pairs={{0,4},{1,5},{2,6},{3,7},{4,0},{5,1},{6,2},{7,3},{8,12},{9,13},{10,... | collective-permute-start | bytes 442376 | tf_op jit(solution)/shard_map/ppermute | solution.py:928
  81.3 7.2 %collective-permute-start.19 = (bf16[2,192,256]{2,1,0:T(8,128)(2,1)S(1)}, bf16[2,192,256]{2,1,0:T(8,128)(2,1)S(1)}, u32[]{:S(2)}, u32[]{:S(2)}) collective-permute-start(bf16[2,192,256]{2,1,0:T(8,128)(2,1)S(1)} %get-tuple-element.175), channel_id=1, source_target_pairs={{0,8},{8,0},{16,24},{24,16},{1,9},{9,1},{17,25},{25,17},{2,10},{10... | collective-permute-start | bytes 589832 | tf_op jit(solution)/shard_map/ppermute | solution.py:928
  88.5 9.1 %collective-permute-start.15 = (bf16[144,512]{1,0:T(8,128)(2,1)S(1)}, bf16[144,512]{1,0:T(8,128)(2,1)S(1)}, u32[]{:S(2)}, u32[]{:S(2)}) collective-permute-start(bf16[144,512]{1,0:T(8,128)(2,1)S(1)} %get-tuple-element.167), channel_id=1, source_target_pairs={{0,6},{1,7},{2,4},{3,5},{4,2},{5,3},{6,0},{7,1},{8,14},{9,15},{10,... | collective-permute-start | bytes 442376 | tf_op jit(solution)/shard_map/ppermute | solution.py:928
  91.2 4.7 %collective-permute-start.20 = (bf16[1,192,256]{2,1,0:T(8,128)(2,1)S(1)}, bf16[1,192,256]{2,1,0:T(8,128)(2,1)S(1)}, u32[]{:S(2)}, u32[]{:S(2)}) collective-permute-start(bf16[1,192,256]{2,1,0:T(8,128)(2,1)S(1)} %get-tuple-element.177), channel_id=1, source_target_pairs={{0,16},{8,24},{16,0},{24,8},{1,17},{9,25},{17,1},{25,9},{2,18},{10... | collective-permute-start | bytes 294920 | tf_op jit(solution)/shard_map/ppermute | solution.py:928
  95.9 6.4 %collective-permute-start.27 = (bf16[4,64,1024]{2,1,0:T(8,128)(2,1)S(1)}, bf16[4,64,1024]{2,1,0:T(8,128)(2,1)S(1)}, u32[]{:S(2)}, u32[]{:S(2)}) collective-permute-start(bf16[4,64,1024]{2,1,0:T(8,128)(2,1)S(1)} %get-tuple-element.198), channel_id=1, source_target_pairs={{0,1},{1,0},{2,3},{3,2},{4,5},{5,4},{6,7},{7,6},{8,9},{9,8},{10,11... | collective-permute-start | bytes 1572872 | tf_op jit(solution)/shard_map/ppermute | solution.py:928
  95.9 12.8 %collective-permute-start.17 = (bf16[2,128,1024]{2,1,0:T(8,128)(2,1)S(1)}, bf16[2,128,1024]{2,1,0:T(8,128)(2,1)S(1)}, u32[]{:S(2)}, u32[]{:S(2)}) collective-permute-start(bf16[2,128,1024]{2,1,0:T(8,128)(2,1)S(1)} %get-tuple-element.171), channel_id=1, source_target_pairs={{0,1},{1,0},{2,3},{3,2},{4,5},{5,4},{6,7},{7,6},{8,9},{9,8},{10,11... | collective-permute-start | bytes 1572872 | tf_op jit(solution)/shard_map/ppermute | solution.py:928
  97.6 4.6 %collective-permute-start.21 = (bf16[48,1024]{1,0:T(8,128)(2,1)S(1)}, bf16[48,1024]{1,0:T(8,128)(2,1)S(1)}, u32[]{:S(2)}, u32[]{:S(2)}) collective-permute-start(bf16[48,1024]{1,0:T(8,128)(2,1)S(1)} %small_last.1.refs_0_), channel_id=1, source_target_pairs={{0,2},{1,3},{2,0},{3,1},{4,6},{5,7},{6,4},{7,5},{8,10},{9,11},{10,... | collective-permute-start | bytes 294920 | tf_op jit(solution)/shard_map/ppermute | solution.py:928
  98.7 10.1 %collective-permute-start.16 = (bf16[2,128,1024]{2,1,0:T(8,128)(2,1)S(1)}, bf16[2,128,1024]{2,1,0:T(8,128)(2,1)S(1)}, u32[]{:S(2)}, u32[]{:S(2)}) collective-permute-start(bf16[2,128,1024]{2,1,0:T(8,128)(2,1)S(1)} %get-tuple-element.169), channel_id=1, source_target_pairs={{0,1},{1,0},{2,3},{3,2},{4,5},{5,4},{6,7},{7,6},{8,9},{9,8},{10,11... | collective-permute-start | bytes 1572872 | tf_op jit(solution)/shard_map/ppermute | solution.py:928
  102.2 6.5 %collective-permute-start.22 = (bf16[48,1024]{1,0:T(8,128)(2,1)S(1)}, bf16[48,1024]{1,0:T(8,128)(2,1)S(1)}, u32[]{:S(2)}, u32[]{:S(2)}) collective-permute-start(bf16[48,1024]{1,0:T(8,128)(2,1)S(1)} %small_chip0.1.refs_0_), channel_id=1, source_target_pairs={{0,4},{1,5},{2,6},{3,7},{4,0},{5,1},{6,2},{7,3},{8,12},{9,13},{10,... | collective-permute-start | bytes 294920 | tf_op jit(solution)/shard_map/ppermute | solution.py:928
  102.4 12.1 %collective-permute-start.28 = (bf16[2,64,1024]{2,1,0:T(8,128)(2,1)S(1)}, bf16[2,64,1024]{2,1,0:T(8,128)(2,1)S(1)}, u32[]{:S(2)}, u32[]{:S(2)}) collective-permute-start(bf16[2,64,1024]{2,1,0:T(8,128)(2,1)S(1)} %get-tuple-element.200), channel_id=1, source_target_pairs={{0,2},{1,3},{2,0},{3,1},{4,6},{5,7},{6,4},{7,5},{8,10},{9,11},{10,... | collective-permute-start | bytes 786440 | tf_op jit(solution)/shard_map/ppermute | solution.py:928
  108.7 4.0 %copy-start = (bf16[2048,1024]{1,0:T(8,128)(2,1)S(1)}, bf16[2048,1024]{1,0:T(8,128)(2,1)}, u32[]{:S(2)}) copy-start(bf16[2048,1024]{1,0:T(8,128)(2,1)} %refs_6_.3) | copy-start | bytes 12582916
  109.2 10.1 %collective-permute-start.23 = (bf16[176,1024]{1,0:T(8,128)(2,1)S(1)}, bf16[176,1024]{1,0:T(8,128)(2,1)S(1)}, u32[]{:S(2)}, u32[]{:S(2)}) collective-permute-start(bf16[176,1024]{1,0:T(8,128)(2,1)S(1)} %get-tuple-element.179), channel_id=1, source_target_pairs={{0,8},{8,0},{16,24},{24,16},{1,9},{9,1},{17,25},{25,17},{2,10},{10... | collective-permute-start | bytes 1081352 | tf_op jit(solution)/shard_map/ppermute | solution.py:928
  110.4 9.9 %collective-permute-start.24 = (bf16[176,1024]{1,0:T(8,128)(2,1)S(1)}, bf16[176,1024]{1,0:T(8,128)(2,1)S(1)}, u32[]{:S(2)}, u32[]{:S(2)}) collective-permute-start(bf16[176,1024]{1,0:T(8,128)(2,1)S(1)} %get-tuple-element.180), channel_id=1, source_target_pairs={{0,16},{8,24},{16,0},{24,8},{1,17},{9,25},{17,1},{25,9},{2,18},{10... | collective-permute-start | bytes 1081352 | tf_op jit(solution)/shard_map/ppermute | solution.py:928
  111.3 12.9 %collective-permute-start.25 = (bf16[176,1024]{1,0:T(8,128)(2,1)S(1)}, bf16[176,1024]{1,0:T(8,128)(2,1)S(1)}, u32[]{:S(2)}, u32[]{:S(2)}) collective-permute-start(bf16[176,1024]{1,0:T(8,128)(2,1)S(1)} %get-tuple-element.181), channel_id=1, source_target_pairs={{0,24},{8,16},{16,8},{24,0},{1,25},{9,17},{17,9},{25,1},{2,26},{10... | collective-permute-start | bytes 1081352 | tf_op jit(solution)/shard_map/ppermute | solution.py:928
  114.6 9.7 %collective-permute-start.29 = (bf16[1,64,1024]{2,1,0:T(8,128)(2,1)S(1)}, bf16[1,64,1024]{2,1,0:T(8,128)(2,1)S(1)}, u32[]{:S(2)}, u32[]{:S(2)}) collective-permute-start(bf16[1,64,1024]{2,1,0:T(8,128)(2,1)S(1)} %get-tuple-element.202), channel_id=1, source_target_pairs={{0,4},{1,5},{2,6},{3,7},{4,0},{5,1},{6,2},{7,3},{8,12},{9,13},{10,... | collective-permute-start | bytes 393224 | tf_op jit(solution)/shard_map/ppermute | solution.py:928
  124.2 1.8 %collective-permute-start.26 = (bf16[4,48,1024]{2,1,0:T(8,128)(2,1)S(1)}, bf16[4,48,1024]{2,1,0:T(8,128)(2,1)S(1)}, u32[]{:S(2)}, u32[]{:S(2)}) collective-permute-start(bf16[4,48,1024]{2,1,0:T(8,128)(2,1)S(1)} %join.1.refs_1_), channel_id=1, source_target_pairs={{0,1},{1,0},{2,3},{3,2},{4,5},{5,4},{6,7},{7,6},{8,9},{9,8},{10,11... | collective-permute-start | bytes 1179656 | tf_op jit(solution)/shard_map/ppermute | solution.py:928

commit v8 on v7

--- a/solution.py
+++ b/solution.py
@@ -529,7 +529,6 @@
         wide = tile_at(j * block, block)
         for load in weights(j):
             load.wait()
-        ngrad[pl.ds(0, length), :] += nt(ggate_ref[:, wide], win_ref[j % 2, 1])
         small[pl.ds(0, maps), wide] = tn(pg[...], inner_ref[:, wide])[:maps]
         inner_grad = isg[:, wide] + nn(pg[:, :maps], wx_ref[:, wide])
         mask = [masks[k] for k in range(taps)]
@@ -567,7 +566,9 @@
                 held[chip, :, tile_at(spot * LANES)] = sent.astype(bf16)
             else:
                 blocks[0][:, far] = sent.astype(bf16)
-        ngrad[...] += nt(sent_s[...], win_ref[j % 2, 0])
+        part = nt(sent_s[...], win_ref[j % 2, 0])
+        ngrad[pl.ds(0, length), :] += part[:length] + nt(ggate_ref[:, wide], win_ref[j % 2, 1])
+        ngrad[pl.ds(length, EDGE), :] += part[length:]
 
         @pl.when(j + 2 < width // block)
         def _():

time: 128 us -> 128 us (level)
  no operation moved by 1% of the time
where the time goes in v8:
time: 128 us; the launch traced here: 127 us
  Pallas kernels  54.5 us (43%)
  waiting for transfers between devices  36.7 us (29%)
  starting transfers between devices  34.4 us (27%)
    pallas_call x23, Pallas kernels, plain_call(): pl.pallas_call(lambda *refs: kernel(Here(), *refs), in_specs=list(specs)...  54.5 us
    ppermute x28, waiting for transfers between devices, swap(): lax.ppermute(x, self.axis, [(i, i ^ k * self.stride) for i in range(n)])  36.6 us
    ppermute x28, starting transfers between devices, swap(): lax.ppermute(x, self.axis, [(i, i ^ k * self.stride) for i in range(n)])  30.7 us
  transfers between devices with their start and end apart: 30, of which 13 were waited for; matrix products, arithmetic and copies ran while one was open for 0% of the time, Pallas kernels for 37%

profile of v8, /device:TPU:0, one launch (start us, length us, event | category | flops | bytes accessed | tf_op | source)
XLA Modules:
  0.0 127.2 jit_solution(13539047118696478637)
XLA Ops:
  0.6 0.7 slice_bitcast_fusion
  1.4 2.3 %collective-permute-start = (bf16[3,1024]{1,0:T(4,128)(2,1)S(1)}, bf16[3,1024]{1,0:T(4,128)(2,1)S(1)}, u32[]{:S(2)}, u32[]{:S(2)}) collective-permute-start(bf16[3,1024]{1,0:T(4,128)(2,1)S(1)} %slice_bitcast_fusion), channel_id=1, source_target_pairs={{0,1},{1,2},{2,3},{3,4},{4,5},{5,6},{6,7},{8,9},{9,10},{10,11},{11... | collective-permute-start | bytes 18440 | tf_op jit(solution)/shard_map/ppermute | solution.py:1001
  3.7 3.7 %collective-permute-start.1 = (bf16[128,1024]{1,0:T(8,128)(2,1)}, bf16[128,1024]{1,0:T(8,128)(2,1)S(1)}, u32[]{:S(2)}, u32[]{:S(2)}) collective-permute-start(bf16[128,1024]{1,0:T(8,128)(2,1)} %bitcast.19), channel_id=1, source_target_pairs={{0,4},{1,5},{2,6},{3,7},{4,0},{5,1},{6,2},{7,3},{8,12},{9,13},{10,... | collective-permute-start | bytes 786440 | tf_op jit(solution)/shard_map/ppermute | solution.py:929
  7.4 0.0 collective-permute-done.refs_13_
  7.4 18.6 %front.1 = (bf16[144,1024]{1,0:T(8,128)(2,1)S(1)}, bf16[128,1024]{1,0:T(8,128)(2,1)S(1)}, bf16[160,2048]{1,0:T(8,128)(2,1)S(1)}, bf16[128,2048]{1,0:T(8,128)(2,1...) custom-call(s32[1,4]{1,0:T(1,128)} %refs_0_.2, ...), custom_call_target="tpu_custom_call" | custom-call | flops 22000001024 | tf_op jit(solution)/shard_map/front/pallas_call | solution.py:49
  26.0 0.0 collective-permute-done.1.refs_3_.refs_2_
  26.0 1.5 %collective-permute-start.2 = (bf16[48,2048]{1,0:T(8,128)(2,1)S(1)}, bf16[48,2048]{1,0:T(8,128)(2,1)S(1)}, u32[]{:S(2)}, u32[]{:S(2)}) collective-permute-start(bf16[48,2048]{1,0:T(8,128)(2,1)S(1)} %get-tuple-element.116.refs_0_), channel_id=1, source_target_pairs={{0,1},{1,0},{2,3},{3,2},{4,5},{5,4},{6,7},{7,6},{8,9},{9,8},{10,11... | collective-permute-start | bytes 589832 | tf_op jit(solution)/shard_map/ppermute | solution.py:929
  27.5 1.1 collective-permute-done.2.refs_1_.refs_0_
  28.6 0.1 pair.1.refs_0_
  28.6 1.0 collective-permute-start.3
  29.6 4.1 %collective-permute-done.3.refs_1_ = bf16[48,1024]{1,0:T(8,128)(2,1)S(1)} collective-permute-done((bf16[48,1024]{1,0:T(8,128)(2,1)S(1)}, bf16[48,1024]{1,0:T(8,128)(2,1)S(1)}, u32[]{:S(2)}, u32[]{:S(2)}) %collective-permute-start.3) | collective-permute-done | bytes 98336 | tf_op jit(solution)/shard_map/ppermute | solution.py:929
  33.8 0.1 quad.1
  33.9 1.8 %collective-permute-start.4 = (bf16[16,1024]{1,0:T(8,128)(2,1)S(1)}, bf16[16,1024]{1,0:T(8,128)(2,1)S(1)}, u32[]{:S(2)}, u32[]{:S(2)}) collective-permute-start(bf16[16,1024]{1,0:T(8,128)(2,1)S(1)} %get-tuple-element.118), channel_id=1, source_target_pairs={{0,4},{1,5},{2,6},{3,7},{4,0},{5,1},{6,2},{7,3},{8,12},{9,13},{10,... | collective-permute-start | bytes 98312 | tf_op jit(solution)/shard_map/ppermute | solution.py:929
  35.7 3.5 %collective-permute-done.4.refs_1_ = bf16[16,1024]{1,0:T(8,128)(2,1)S(1)} collective-permute-done((bf16[16,1024]{1,0:T(8,128)(2,1)S(1)}, bf16[16,1024]{1,0:T(8,128)(2,1)S(1)}, u32[]{:S(2)}, u32[]{:S(2)}) %collective-permute-start.4) | collective-permute-done | bytes 32800 | tf_op jit(solution)/shard_map/ppermute | solution.py:929
  39.1 0.1 collective-permute-start.5
  39.2 1.3 %collective-permute-done.5.refs_3_ = f32[32,1024]{1,0:T(8,128)S(1)} collective-permute-done((f32[32,1024]{1,0:T(8,128)S(1)}, f32[32,1024]{1,0:T(8,128)S(1)}, u32[]{:S(2)}, u32[]{:S(2)}) %collective-permute-start.5) | collective-permute-done | bytes 131104 | tf_op jit(solution)/shard_map/ppermute | solution.py:929
  40.5 0.1 enter.1
  40.6 5.5 %forward.1 = (bf16[128,2048]{1,0:T(8,128)(2,1)S(1)}, bf16[128,2048]{1,0:T(8,128)(2,1)S(1)}, f32[16,17,2,8,128]{4,3,2,1,0:T(8,128)S(1)}, f32[16,17,2,8,128]{4,3,2...) custom-call(f32[4,128,128]{2,1,0:T(8,128)S(1)} %get-tuple-element.10, ...), custom_call_target="tpu_custom_call" | custom-call | flops 8800000000 | tf_op jit(solution)/shard_map/forward/pallas_call | solution.py:49
  46.1 1.6 %collective-permute-start.7 = (bf16[128,2304]{1,0:T(8,128)(2,1)S(1)}, bf16[128,2304]{1,0:T(8,128)(2,1)S(1)}, u32[]{:S(2)}, u32[]{:S(2)}) collective-permute-start(bf16[128,2304]{1,0:T(8,128)(2,1)S(1)} %get-tuple-element.153), channel_id=1, source_target_pairs={{0,8},{8,0},{16,24},{24,16},{1,9},{9,1},{17,25},{25,17},{2,10},{10... | collective-permute-start | bytes 1769480 | tf_op jit(solution)/shard_map/ppermute | solution.py:929
  47.7 1.5 %collective-permute-start.8 = (bf16[128,2304]{1,0:T(8,128)(2,1)S(1)}, bf16[128,2304]{1,0:T(8,128)(2,1)S(1)}, u32[]{:S(2)}, u32[]{:S(2)}) collective-permute-start(bf16[128,2304]{1,0:T(8,128)(2,1)S(1)} %get-tuple-element.154), channel_id=1, source_target_pairs={{0,16},{8,24},{16,0},{24,8},{1,17},{9,25},{17,1},{25,9},{2,18},{10... | collective-permute-start | bytes 1769480 | tf_op jit(solution)/shard_map/ppermute | solution.py:929
  49.2 0.5 collective-permute-start.9
  49.7 0.4 collective-permute-start.10
  50.1 2.7 %collective-permute-start.11 = (bf16[128,512]{1,0:T(8,128)(2,1)S(1)}, bf16[128,512]{1,0:T(8,128)(2,1)S(1)}, u32[]{:S(2)}, u32[]{:S(2)}) collective-permute-start(bf16[128,512]{1,0:T(8,128)(2,1)S(1)} %get-tuple-element.158), channel_id=1, source_target_pairs={{0,4},{1,5},{2,6},{3,7},{4,0},{5,1},{6,2},{7,3},{8,12},{9,13},{10,... | collective-permute-start | bytes 393224 | tf_op jit(solution)/shard_map/ppermute | solution.py:929
  52.9 21.5 %backward.1 = (f32[144,1024]{1,0:T(8,128)S(1)}, bf16[144,512]{1,0:T(8,128)(2,1)S(1)}, bf16[144,512]{1,0:T(8,128)(2,1)S(1)}, bf16[144,512]{1,0:T(8,128)(2,1)S(1)}...) custom-call(bf16[1024,4096]{1,0:T(8,128)(2,1)} %refs_0_.3, ...), custom_call_target="tpu_custom_call" | custom-call | flops 26400000000 | tf_op jit(solution)/shard_map/backward/pallas_call | solution.py:49
  74.4 0.0 collective-permute-done.7.refs_1_
  74.4 1.0 collective-permute-done.8.refs_2_
  75.4 0.0 collective-permute-done.9.refs_3_
  75.5 0.0 collective-permute-done.10.refs_4_
  75.5 1.3 %collective-permute-start.6 = (f32[16,1024]{1,0:T(8,128)S(1)}, f32[16,1024]{1,0:T(8,128)S(1)}, u32[]{:S(2)}, u32[]{:S(2)}) collective-permute-start(f32[16,1024]{1,0:T(8,128)S(1)} %slice.7), channel_id=1, source_target_pairs={{1,0},{2,1},{3,2},{4,3},{5,4},{6,5},{7,6},{9,8},{10,9},{11,10},{12... | collective-permute-start | bytes 196616 | tf_op jit(solution)/shard_map/ppermute | solution.py:1073
  76.8 3.6 %collective-permute-start.12 = (bf16[128,512]{1,0:T(8,128)(2,1)S(1)}, bf16[128,512]{1,0:T(8,128)(2,1)S(1)}, u32[]{:S(2)}, u32[]{:S(2)}) collective-permute-start(bf16[128,512]{1,0:T(8,128)(2,1)S(1)} %get-tuple-element.162), channel_id=1, source_target_pairs={{0,6},{1,7},{2,4},{3,5},{4,2},{5,3},{6,0},{7,1},{8,14},{9,15},{10,... | collective-permute-start | bytes 393224 | tf_op jit(solution)/shard_map/ppermute | solution.py:929
  80.4 0.0 collective-permute-start.13
  80.5 0.8 collective-permute-start.14
  81.3 0.1 small_row0.1
  81.3 1.3 %collective-permute-start.19 = (bf16[2,192,256]{2,1,0:T(8,128)(2,1)S(1)}, bf16[2,192,256]{2,1,0:T(8,128)(2,1)S(1)}, u32[]{:S(2)}, u32[]{:S(2)}) collective-permute-start(bf16[2,192,256]{2,1,0:T(8,128)(2,1)S(1)} %get-tuple-element.175), channel_id=1, source_target_pairs={{0,8},{8,0},{16,24},{24,16},{1,9},{9,1},{17,25},{25,17},{2,10},{10... | collective-permute-start | bytes 589832 | tf_op jit(solution)/shard_map/ppermute | solution.py:929
  82.6 0.8 out_columns.1
  83.5 5.0 %collective-permute-done.19.refs_1_ = bf16[2,192,256]{2,1,0:T(8,128)(2,1)S(1)} collective-permute-done((bf16[2,192,256]{2,1,0:T(8,128)(2,1)S(1)}, bf16[2,192,256]{2,1,0:T(8,128)(2,1)S(1)}, u32[]{:S(2)}, u32[]{:S(2)}) %collective-permute-start.19) | collective-permute-done | bytes 196640 | tf_op jit(solution)/shard_map/ppermute | solution.py:929
  88.5 2.6 %collective-permute-start.15 = (bf16[144,512]{1,0:T(8,128)(2,1)S(1)}, bf16[144,512]{1,0:T(8,128)(2,1)S(1)}, u32[]{:S(2)}, u32[]{:S(2)}) collective-permute-start(bf16[144,512]{1,0:T(8,128)(2,1)S(1)} %get-tuple-element.167), channel_id=1, source_target_pairs={{0,6},{1,7},{2,4},{3,5},{4,2},{5,3},{6,0},{7,1},{8,14},{9,15},{10,... | collective-permute-start | bytes 442376 | tf_op jit(solution)/shard_map/ppermute | solution.py:929
  91.2 1.6 %collective-permute-start.20 = (bf16[1,192,256]{2,1,0:T(8,128)(2,1)S(1)}, bf16[1,192,256]{2,1,0:T(8,128)(2,1)S(1)}, u32[]{:S(2)}, u32[]{:S(2)}) collective-permute-start(bf16[1,192,256]{2,1,0:T(8,128)(2,1)S(1)} %get-tuple-element.177), channel_id=1, source_target_pairs={{0,16},{8,24},{16,0},{24,8},{1,17},{9,25},{17,1},{25,9},{2,18},{10... | collective-permute-start | bytes 294920 | tf_op jit(solution)/shard_map/ppermute | solution.py:929
  92.8 1.1 gate_columns.1
  93.9 1.9 %collective-permute-done.20.refs_1_ = bf16[1,192,256]{2,1,0:T(8,128)(2,1)S(1)} collective-permute-done((bf16[1,192,256]{2,1,0:T(8,128)(2,1)S(1)}, bf16[1,192,256]{2,1,0:T(8,128)(2,1)S(1)}, u32[]{:S(2)}, u32[]{:S(2)}) %collective-permute-start.20) | collective-permute-done | bytes 98336 | tf_op jit(solution)/shard_map/ppermute | solution.py:929
  95.9 0.6 collective-permute-start.17
  96.5 1.1 collective-permute-done.14.refs_3_
  97.6 1.1 conv_columns.1
  98.7 0.1 collective-permute-start.16
  98.7 3.4 %collective-permute-done.21.refs_1_ = bf16[48,1024]{1,0:T(8,128)(2,1)S(1)} collective-permute-done((bf16[48,1024]{1,0:T(8,128)(2,1)S(1)}, bf16[48,1024]{1,0:T(8,128)(2,1)S(1)}, u32[]{:S(2)}, u32[]{:S(2)}) %collective-permute-start.21) | collective-permute-done | bytes 98336 | tf_op jit(solution)/shard_map/ppermute | solution.py:929
  102.2 0.1 collective-permute-start.22
  102.3 0.1 out_chip0.1
  102.4 1.5 %collective-permute-start.28 = (bf16[2,64,1024]{2,1,0:T(8,128)(2,1)S(1)}, bf16[2,64,1024]{2,1,0:T(8,128)(2,1)S(1)}, u32[]{:S(2)}, u32[]{:S(2)}) collective-permute-start(bf16[2,64,1024]{2,1,0:T(8,128)(2,1)S(1)} %get-tuple-element.200), channel_id=1, source_target_pairs={{0,2},{1,3},{2,0},{3,1},{4,6},{5,7},{6,4},{7,5},{8,10},{9,11},{10,... | collective-permute-start | bytes 786440 | tf_op jit(solution)/shard_map/ppermute | solution.py:929
  103.9 4.8 %collective-permute-done.22.refs_1_ = bf16[48,1024]{1,0:T(8,128)(2,1)S(1)} collective-permute-done((bf16[48,1024]{1,0:T(8,128)(2,1)S(1)}, bf16[48,1024]{1,0:T(8,128)(2,1)S(1)}, u32[]{:S(2)}, u32[]{:S(2)}) %collective-permute-start.22) | collective-permute-done | bytes 98336 | tf_op jit(solution)/shard_map/ppermute | solution.py:929
  108.7 0.0 copy-start
  108.8 0.4 in_merge.1
  109.2 1.3 collective-permute-start.23
  110.4 0.9 collective-permute-start.24
  111.3 1.4 %collective-permute-start.25 = (bf16[176,1024]{1,0:T(8,128)(2,1)S(1)}, bf16[176,1024]{1,0:T(8,128)(2,1)S(1)}, u32[]{:S(2)}, u32[]{:S(2)}) collective-permute-start(bf16[176,1024]{1,0:T(8,128)(2,1)S(1)} %get-tuple-element.181), channel_id=1, source_target_pairs={{0,24},{8,16},{16,8},{24,0},{1,25},{9,17},{17,9},{25,1},{2,26},{10... | collective-permute-start | bytes 1081352 | tf_op jit(solution)/shard_map/ppermute | solution.py:929
  112.7 1.8 %finish.1 = (bf16[128,1024]{1,0:T(8,128)(2,1)}, bf16[128,1024]{1,0:T(8,128)(2,1)}) custom-call(f32[144,1024]{1,0:T(8,128)S(1)} %get-tuple-element.143.refs_0_, f32[16,1024]{1,0:T(8,128)S(1)} %collective-permute-done.6.refs_1_, bf16[144,1024]{1,0:T(8,128)(2,1)S(1)} %get-tuple-element.110.refs_2_.refs_5_.refs_1_, ...), custom_call_target="tpu_custom_call" | custom-call | flops 2200000000 | tf_op jit(solution)/shard_map/finish/pallas_call | solution.py:49
  114.5 0.1 out_chip1.1
  114.6 0.2 collective-permute-start.29
  114.8 4.4 %collective-permute-done.23.refs_1_ = bf16[176,1024]{1,0:T(8,128)(2,1)S(1)} collective-permute-done((bf16[176,1024]{1,0:T(8,128)(2,1)S(1)}, bf16[176,1024]{1,0:T(8,128)(2,1)S(1)}, u32[]{:S(2)}, u32[]{:S(2)}) %collective-permute-start.23) | collective-permute-done | bytes 360480 | tf_op jit(solution)/shard_map/ppermute | solution.py:929
  119.3 1.0 collective-permute-done.24.refs_2_
  120.3 3.9 %collective-permute-done.25.refs_3_ = bf16[176,1024]{1,0:T(8,128)(2,1)S(1)} collective-permute-done((bf16[176,1024]{1,0:T(8,128)(2,1)S(1)}, bf16[176,1024]{1,0:T(8,128)(2,1)S(1)}, u32[]{:S(2)}, u32[]{:S(2)}) %collective-permute-start.25) | collective-permute-done | bytes 360480 | tf_op jit(solution)/shard_map/ppermute | solution.py:929
  124.2 0.1 collective-permute-start.26
  124.3 0.7 out_last.1
  125.0 1.0 in_last.1
  126.0 1.2 unpack.1
  (26 shorter events, 0.3 us)
Async XLA Ops:
  1.4 6.0 %collective-permute-start = (bf16[3,1024]{1,0:T(4,128)(2,1)S(1)}, bf16[3,1024]{1,0:T(4,128)(2,1)S(1)}, u32[]{:S(2)}, u32[]{:S(2)}) collective-permute-start(bf16[3,1024]{1,0:T(4,128)(2,1)S(1)} %slice_bitcast_fusion), channel_id=1, source_target_pairs={{0,1},{1,2},{2,3},{3,4},{4,5},{5,6},{6,7},{8,9},{9,10},{10,11},{11... | collective-permute-start | bytes 18440 | tf_op jit(solution)/shard_map/ppermute | solution.py:1001
  3.7 22.3 %collective-permute-start.1 = (bf16[128,1024]{1,0:T(8,128)(2,1)}, bf16[128,1024]{1,0:T(8,128)(2,1)S(1)}, u32[]{:S(2)}, u32[]{:S(2)}) collective-permute-start(bf16[128,1024]{1,0:T(8,128)(2,1)} %bitcast.19), channel_id=1, source_target_pairs={{0,4},{1,5},{2,6},{3,7},{4,0},{5,1},{6,2},{7,3},{8,12},{9,13},{10,... | collective-permute-start | bytes 786440 | tf_op jit(solution)/shard_map/ppermute | solution.py:929
  26.0 2.5 %collective-permute-start.2 = (bf16[48,2048]{1,0:T(8,128)(2,1)S(1)}, bf16[48,2048]{1,0:T(8,128)(2,1)S(1)}, u32[]{:S(2)}, u32[]{:S(2)}) collective-permute-start(bf16[48,2048]{1,0:T(8,128)(2,1)S(1)} %get-tuple-element.116.refs_0_), channel_id=1, source_target_pairs={{0,1},{1,0},{2,3},{3,2},{4,5},{5,4},{6,7},{7,6},{8,9},{9,8},{10,11... | collective-permute-start | bytes 589832 | tf_op jit(solution)/shard_map/ppermute | solution.py:929
  28.6 5.1 %collective-permute-start.3 = (bf16[48,1024]{1,0:T(8,128)(2,1)S(1)}, bf16[48,1024]{1,0:T(8,128)(2,1)S(1)}, u32[]{:S(2)}, u32[]{:S(2)}) collective-permute-start(bf16[48,1024]{1,0:T(8,128)(2,1)S(1)} %pair.1.refs_0_), channel_id=1, source_target_pairs={{0,2},{1,3},{2,0},{3,1},{4,6},{5,7},{6,4},{7,5},{8,10},{9,11},{10,... | collective-permute-start | bytes 294920 | tf_op jit(solution)/shard_map/ppermute | solution.py:929
  33.9 5.2 %collective-permute-start.4 = (bf16[16,1024]{1,0:T(8,128)(2,1)S(1)}, bf16[16,1024]{1,0:T(8,128)(2,1)S(1)}, u32[]{:S(2)}, u32[]{:S(2)}) collective-permute-start(bf16[16,1024]{1,0:T(8,128)(2,1)S(1)} %get-tuple-element.118), channel_id=1, source_target_pairs={{0,4},{1,5},{2,6},{3,7},{4,0},{5,1},{6,2},{7,3},{8,12},{9,13},{10,... | collective-permute-start | bytes 98312 | tf_op jit(solution)/shard_map/ppermute | solution.py:929
  39.1 1.4 %collective-permute-start.5 = (f32[32,1024]{1,0:T(8,128)S(1)}, f32[32,1024]{1,0:T(8,128)S(1)}, u32[]{:S(2)}, u32[]{:S(2)}) collective-permute-start(f32[32,1024]{1,0:T(8,128)S(1)} %enter_half.1.refs_2_), channel_id=1, source_target_pairs={{0,1},{1,0},{2,3},{3,2},{4,5},{5,4},{6,7},{7,6},{8,9},{9,8},{10,11... | collective-permute-start | bytes 393224 | tf_op jit(solution)/shard_map/ppermute | solution.py:929
  46.1 28.3 %collective-permute-start.7 = (bf16[128,2304]{1,0:T(8,128)(2,1)S(1)}, bf16[128,2304]{1,0:T(8,128)(2,1)S(1)}, u32[]{:S(2)}, u32[]{:S(2)}) collective-permute-start(bf16[128,2304]{1,0:T(8,128)(2,1)S(1)} %get-tuple-element.153), channel_id=1, source_target_pairs={{0,8},{8,0},{16,24},{24,16},{1,9},{9,1},{17,25},{25,17},{2,10},{10... | collective-permute-start | bytes 1769480 | tf_op jit(solution)/shard_map/ppermute | solution.py:929
  47.7 27.7 %collective-permute-start.8 = (bf16[128,2304]{1,0:T(8,128)(2,1)S(1)}, bf16[128,2304]{1,0:T(8,128)(2,1)S(1)}, u32[]{:S(2)}, u32[]{:S(2)}) collective-permute-start(bf16[128,2304]{1,0:T(8,128)(2,1)S(1)} %get-tuple-element.154), channel_id=1, source_target_pairs={{0,16},{8,24},{16,0},{24,8},{1,17},{9,25},{17,1},{25,9},{2,18},{10... | collective-permute-start | bytes 1769480 | tf_op jit(solution)/shard_map/ppermute | solution.py:929
  49.2 26.2 %collective-permute-start.9 = (bf16[128,2304]{1,0:T(8,128)(2,1)S(1)}, bf16[128,2304]{1,0:T(8,128)(2,1)S(1)}, u32[]{:S(2)}, u32[]{:S(2)}) collective-permute-start(bf16[128,2304]{1,0:T(8,128)(2,1)S(1)} %get-tuple-element.155), channel_id=1, source_target_pairs={{0,24},{8,16},{16,8},{24,0},{1,25},{9,17},{17,9},{25,1},{2,26},{10... | collective-permute-start | bytes 1769480 | tf_op jit(solution)/shard_map/ppermute | solution.py:929
  49.7 25.8 %collective-permute-start.10 = (bf16[128,2560]{1,0:T(8,128)(2,1)S(1)}, bf16[128,2560]{1,0:T(8,128)(2,1)S(1)}, u32[]{:S(2)}, u32[]{:S(2)}) collective-permute-start(bf16[128,2560]{1,0:T(8,128)(2,1)S(1)} %get-tuple-element.157), channel_id=1, source_target_pairs={{0,2},{1,3},{2,0},{3,1},{4,6},{5,7},{6,4},{7,5},{8,10},{9,11},{10,... | collective-permute-start | bytes 1966088 | tf_op jit(solution)/shard_map/ppermute | solution.py:929
  50.1 24.3 %collective-permute-start.11 = (bf16[128,512]{1,0:T(8,128)(2,1)S(1)}, bf16[128,512]{1,0:T(8,128)(2,1)S(1)}, u32[]{:S(2)}, u32[]{:S(2)}) collective-permute-start(bf16[128,512]{1,0:T(8,128)(2,1)S(1)} %get-tuple-element.158), channel_id=1, source_target_pairs={{0,4},{1,5},{2,6},{3,7},{4,0},{5,1},{6,2},{7,3},{8,12},{9,13},{10,... | collective-permute-start | bytes 393224 | tf_op jit(solution)/shard_map/ppermute | solution.py:929
  52.9 22.6 %copy-start.1 = (f32[2048,16]{0,1:T(8,128)S(1)}, f32[2048,16]{0,1:T(8,128)}, u32[]{:S(2)}) copy-start(f32[2048,16]{0,1:T(8,128)} %param.22) | copy-start | bytes 393220
  75.5 5.8 %collective-permute-start.18 = (bf16[4,192,256]{2,1,0:T(8,128)(2,1)S(1)}, bf16[4,192,256]{2,1,0:T(8,128)(2,1)S(1)}, u32[]{:S(2)}, u32[]{:S(2)}) collective-permute-start(bf16[4,192,256]{2,1,0:T(8,128)(2,1)S(1)} %get-tuple-element.173), channel_id=1, source_target_pairs={{0,1},{1,0},{2,3},{3,2},{4,5},{5,4},{6,7},{7,6},{8,9},{9,8},{10,11... | collective-permute-start | bytes 1179656 | tf_op jit(solution)/shard_map/ppermute | solution.py:929
  75.5 37.2 %collective-permute-start.6 = (f32[16,1024]{1,0:T(8,128)S(1)}, f32[16,1024]{1,0:T(8,128)S(1)}, u32[]{:S(2)}, u32[]{:S(2)}) collective-permute-start(f32[16,1024]{1,0:T(8,128)S(1)} %slice.7), channel_id=1, source_target_pairs={{1,0},{2,1},{3,2},{4,3},{5,4},{6,5},{7,6},{9,8},{10,9},{11,10},{12... | collective-permute-start | bytes 196616 | tf_op jit(solution)/shard_map/ppermute | solution.py:1073
  76.8 14.3 %collective-permute-start.12 = (bf16[128,512]{1,0:T(8,128)(2,1)S(1)}, bf16[128,512]{1,0:T(8,128)(2,1)S(1)}, u32[]{:S(2)}, u32[]{:S(2)}) collective-permute-start(bf16[128,512]{1,0:T(8,128)(2,1)S(1)} %get-tuple-element.162), channel_id=1, source_target_pairs={{0,6},{1,7},{2,4},{3,5},{4,2},{5,3},{6,0},{7,1},{8,14},{9,15},{10,... | collective-permute-start | bytes 393224 | tf_op jit(solution)/shard_map/ppermute | solution.py:929
  80.4 15.4 %collective-permute-start.13 = (bf16[144,512]{1,0:T(8,128)(2,1)S(1)}, bf16[144,512]{1,0:T(8,128)(2,1)S(1)}, u32[]{:S(2)}, u32[]{:S(2)}) collective-permute-start(bf16[144,512]{1,0:T(8,128)(2,1)S(1)} %get-tuple-element.165), channel_id=1, source_target_pairs={{0,2},{1,3},{2,0},{3,1},{4,6},{5,7},{6,4},{7,5},{8,10},{9,11},{10,... | collective-permute-start | bytes 442376 | tf_op jit(solution)/shard_map/ppermute | solution.py:929
  80.5 17.1 %collective-permute-start.14 = (bf16[144,512]{1,0:T(8,128)(2,1)S(1)}, bf16[144,512]{1,0:T(8,128)(2,1)S(1)}, u32[]{:S(2)}, u32[]{:S(2)}) collective-permute-start(bf16[144,512]{1,0:T(8,128)(2,1)S(1)} %get-tuple-element.166), channel_id=1, source_target_pairs={{0,4},{1,5},{2,6},{3,7},{4,0},{5,1},{6,2},{7,3},{8,12},{9,13},{10,... | collective-permute-start | bytes 442376 | tf_op jit(solution)/shard_map/ppermute | solution.py:929
  81.3 7.2 %collective-permute-start.19 = (bf16[2,192,256]{2,1,0:T(8,128)(2,1)S(1)}, bf16[2,192,256]{2,1,0:T(8,128)(2,1)S(1)}, u32[]{:S(2)}, u32[]{:S(2)}) collective-permute-start(bf16[2,192,256]{2,1,0:T(8,128)(2,1)S(1)} %get-tuple-element.175), channel_id=1, source_target_pairs={{0,8},{8,0},{16,24},{24,16},{1,9},{9,1},{17,25},{25,17},{2,10},{10... | collective-permute-start | bytes 589832 | tf_op jit(solution)/shard_map/ppermute | solution.py:929
  88.5 9.1 %collective-permute-start.15 = (bf16[144,512]{1,0:T(8,128)(2,1)S(1)}, bf16[144,512]{1,0:T(8,128)(2,1)S(1)}, u32[]{:S(2)}, u32[]{:S(2)}) collective-permute-start(bf16[144,512]{1,0:T(8,128)(2,1)S(1)} %get-tuple-element.167), channel_id=1, source_target_pairs={{0,6},{1,7},{2,4},{3,5},{4,2},{5,3},{6,0},{7,1},{8,14},{9,15},{10,... | collective-permute-start | bytes 442376 | tf_op jit(solution)/shard_map/ppermute | solution.py:929
  91.2 4.7 %collective-permute-start.20 = (bf16[1,192,256]{2,1,0:T(8,128)(2,1)S(1)}, bf16[1,192,256]{2,1,0:T(8,128)(2,1)S(1)}, u32[]{:S(2)}, u32[]{:S(2)}) collective-permute-start(bf16[1,192,256]{2,1,0:T(8,128)(2,1)S(1)} %get-tuple-element.177), channel_id=1, source_target_pairs={{0,16},{8,24},{16,0},{24,8},{1,17},{9,25},{17,1},{25,9},{2,18},{10... | collective-permute-start | bytes 294920 | tf_op jit(solution)/shard_map/ppermute | solution.py:929
  95.9 6.4 %collective-permute-start.27 = (bf16[4,64,1024]{2,1,0:T(8,128)(2,1)S(1)}, bf16[4,64,1024]{2,1,0:T(8,128)(2,1)S(1)}, u32[]{:S(2)}, u32[]{:S(2)}) collective-permute-start(bf16[4,64,1024]{2,1,0:T(8,128)(2,1)S(1)} %get-tuple-element.198), channel_id=1, source_target_pairs={{0,1},{1,0},{2,3},{3,2},{4,5},{5,4},{6,7},{7,6},{8,9},{9,8},{10,11... | collective-permute-start | bytes 1572872 | tf_op jit(solution)/shard_map/ppermute | solution.py:929
  95.9 12.8 %collective-permute-start.17 = (bf16[2,128,1024]{2,1,0:T(8,128)(2,1)S(1)}, bf16[2,128,1024]{2,1,0:T(8,128)(2,1)S(1)}, u32[]{:S(2)}, u32[]{:S(2)}) collective-permute-start(bf16[2,128,1024]{2,1,0:T(8,128)(2,1)S(1)} %get-tuple-element.171), channel_id=1, source_target_pairs={{0,1},{1,0},{2,3},{3,2},{4,5},{5,4},{6,7},{7,6},{8,9},{9,8},{10,11... | collective-permute-start | bytes 1572872 | tf_op jit(solution)/shard_map/ppermute | solution.py:929
  97.6 4.6 %collective-permute-start.21 = (bf16[48,1024]{1,0:T(8,128)(2,1)S(1)}, bf16[48,1024]{1,0:T(8,128)(2,1)S(1)}, u32[]{:S(2)}, u32[]{:S(2)}) collective-permute-start(bf16[48,1024]{1,0:T(8,128)(2,1)S(1)} %small_last.1.refs_0_), channel_id=1, source_target_pairs={{0,2},{1,3},{2,0},{3,1},{4,6},{5,7},{6,4},{7,5},{8,10},{9,11},{10,... | collective-permute-start | bytes 294920 | tf_op jit(solution)/shard_map/ppermute | solution.py:929
  98.7 10.1 %collective-permute-start.16 = (bf16[2,128,1024]{2,1,0:T(8,128)(2,1)S(1)}, bf16[2,128,1024]{2,1,0:T(8,128)(2,1)S(1)}, u32[]{:S(2)}, u32[]{:S(2)}) collective-permute-start(bf16[2,128,1024]{2,1,0:T(8,128)(2,1)S(1)} %get-tuple-element.169), channel_id=1, source_target_pairs={{0,1},{1,0},{2,3},{3,2},{4,5},{5,4},{6,7},{7,6},{8,9},{9,8},{10,11... | collective-permute-start | bytes 1572872 | tf_op jit(solution)/shard_map/ppermute | solution.py:929
  102.2 6.5 %collective-permute-start.22 = (bf16[48,1024]{1,0:T(8,128)(2,1)S(1)}, bf16[48,1024]{1,0:T(8,128)(2,1)S(1)}, u32[]{:S(2)}, u32[]{:S(2)}) collective-permute-start(bf16[48,1024]{1,0:T(8,128)(2,1)S(1)} %small_chip0.1.refs_0_), channel_id=1, source_target_pairs={{0,4},{1,5},{2,6},{3,7},{4,0},{5,1},{6,2},{7,3},{8,12},{9,13},{10,... | collective-permute-start | bytes 294920 | tf_op jit(solution)/shard_map/ppermute | solution.py:929
  102.4 12.1 %collective-permute-start.28 = (bf16[2,64,1024]{2,1,0:T(8,128)(2,1)S(1)}, bf16[2,64,1024]{2,1,0:T(8,128)(2,1)S(1)}, u32[]{:S(2)}, u32[]{:S(2)}) collective-permute-start(bf16[2,64,1024]{2,1,0:T(8,128)(2,1)S(1)} %get-tuple-element.200), channel_id=1, source_target_pairs={{0,2},{1,3},{2,0},{3,1},{4,6},{5,7},{6,4},{7,5},{8,10},{9,11},{10,... | collective-permute-start | bytes 786440 | tf_op jit(solution)/shard_map/ppermute | solution.py:929
  108.7 4.0 %copy-start = (bf16[2048,1024]{1,0:T(8,128)(2,1)S(1)}, bf16[2048,1024]{1,0:T(8,128)(2,1)}, u32[]{:S(2)}) copy-start(bf16[2048,1024]{1,0:T(8,128)(2,1)} %refs_6_.3) | copy-start | bytes 12582916
  109.2 10.1 %collective-permute-start.23 = (bf16[176,1024]{1,0:T(8,128)(2,1)S(1)}, bf16[176,1024]{1,0:T(8,128)(2,1)S(1)}, u32[]{:S(2)}, u32[]{:S(2)}) collective-permute-start(bf16[176,1024]{1,0:T(8,128)(2,1)S(1)} %get-tuple-element.179), channel_id=1, source_target_pairs={{0,8},{8,0},{16,24},{24,16},{1,9},{9,1},{17,25},{25,17},{2,10},{10... | collective-permute-start | bytes 1081352 | tf_op jit(solution)/shard_map/ppermute | solution.py:929
  110.4 9.9 %collective-permute-start.24 = (bf16[176,1024]{1,0:T(8,128)(2,1)S(1)}, bf16[176,1024]{1,0:T(8,128)(2,1)S(1)}, u32[]{:S(2)}, u32[]{:S(2)}) collective-permute-start(bf16[176,1024]{1,0:T(8,128)(2,1)S(1)} %get-tuple-element.180), channel_id=1, source_target_pairs={{0,16},{8,24},{16,0},{24,8},{1,17},{9,25},{17,1},{25,9},{2,18},{10... | collective-permute-start | bytes 1081352 | tf_op jit(solution)/shard_map/ppermute | solution.py:929
  111.3 12.8 %collective-permute-start.25 = (bf16[176,1024]{1,0:T(8,128)(2,1)S(1)}, bf16[176,1024]{1,0:T(8,128)(2,1)S(1)}, u32[]{:S(2)}, u32[]{:S(2)}) collective-permute-start(bf16[176,1024]{1,0:T(8,128)(2,1)S(1)} %get-tuple-element.181), channel_id=1, source_target_pairs={{0,24},{8,16},{16,8},{24,0},{1,25},{9,17},{17,9},{25,1},{2,26},{10... | collective-permute-start | bytes 1081352 | tf_op jit(solution)/shard_map/ppermute | solution.py:929
  114.6 9.7 %collective-permute-start.29 = (bf16[1,64,1024]{2,1,0:T(8,128)(2,1)S(1)}, bf16[1,64,1024]{2,1,0:T(8,128)(2,1)S(1)}, u32[]{:S(2)}, u32[]{:S(2)}) collective-permute-start(bf16[1,64,1024]{2,1,0:T(8,128)(2,1)S(1)} %get-tuple-element.202), channel_id=1, source_target_pairs={{0,4},{1,5},{2,6},{3,7},{4,0},{5,1},{6,2},{7,3},{8,12},{9,13},{10,... | collective-permute-start | bytes 393224 | tf_op jit(solution)/shard_map/ppermute | solution.py:929
  124.2 1.8 %collective-permute-start.26 = (bf16[4,48,1024]{2,1,0:T(8,128)(2,1)S(1)}, bf16[4,48,1024]{2,1,0:T(8,128)(2,1)S(1)}, u32[]{:S(2)}, u32[]{:S(2)}) collective-permute-start(bf16[4,48,1024]{2,1,0:T(8,128)(2,1)S(1)} %join.1.refs_1_), channel_id=1, source_target_pairs={{0,1},{1,0},{2,3},{3,2},{4,5},{5,4},{6,7},{7,6},{8,9},{9,8},{10,11... | collective-permute-start | bytes 1179656 | tf_op jit(solution)/shard_map/ppermute | solution.py:929
